TPU v7x, 512 devices: a whole 4x8x8 slice. The times are simulated.
512 devices in a mesh: pole: 8 (over y), row: 16 (over z, core), col: 4 (over x).
Axes of the slice: x: 4, y: 8, z: 8, core: 2. Of those that a mesh axis runs over, the one named last changes fastest.
Arguments:
- front_h: bfloat16 [4096, 4096], P(('row', 'col')), may hold values from -6 to 6
- front_s: bfloat16 [4096, 4096], P(('row', 'col')), may hold values from -6 to 6
- panel_h: bfloat16 [4096, 256], P('row'), may hold values from -6 to 6
- panel_s: bfloat16 [4096, 256], P('row'), may hold values from -4 to 4
- pivot_h: bfloat16 [256, 256], replicated, may hold values from -1.7 to 8.5, as said below
- pivot_s: bfloat16 [256, 256], replicated, may hold values from -0.1 to 1.5, as said below
- pole_shift: float32 [8, 2], P('pole'), may hold values from -0.5 to 1.5, as said below
- pole_weight: float32 [8, 2], P('pole'), may hold values from -6 to 6
- pattern: int32 [16, 16], replicated, may hold values 0 or 1
- ancestor_inverse: bfloat16 [8, 2, 16, 4, 64, 4096], P('pole', None, None, 'col', None, 'row'), may hold values from -0.09375 to 0.09375
Outputs:
- schur: bfloat16 [8, 2, 16, 4, 64, 4096], P('pole', None, None, 'col', None, 'row')
- density_rows: float32 [4096, 256], P(('row', 'col'), 'pole')
- density_pivot: float32 [256, 256], P(None, 'pole')
Inputs may be any that keep to these rules, and one draw needn't show every extreme that they name: `pivot_h`: symmetric; each row's off-diagonal entries sum in magnitude to at most 6.6, the diagonal lies in 8 to 8.5. `pivot_s`: symmetric; each row's off-diagonal entries sum in magnitude to at most 0.33, the diagonal lies in 1 to 1.5. `pole_shift`: column 0 lies in -0.5 to 0.5, column 1 in 0.25 to 1.5.
All inputs are finite; a program needn't handle non-finite values.
Results may differ from a plain program's by a relative error of at most 0.0063.
Values may be sent and summed in bfloat16 or wider, within the bound.
No kernel may reach another device: no remote copies, remote signals or barrier semaphores. Data moves between devices by JAX's collectives and lax.ppermute only.
A program may use at most 64 MiB of HBM per device.

v0:
```python
import jax
import jax.numpy as jnp
from jax import lax
from jax.sharding import PartitionSpec as P

NEWTON = 4


highest = lax.Precision.HIGHEST


def complex_matmul(left_real, left_imag, right_real, right_imag):
    real = jnp.dot(
        left_real, right_real, precision=highest, preferred_element_type=jnp.float32
    ) - jnp.dot(left_imag, right_imag, precision=highest, preferred_element_type=jnp.float32)
    imag = jnp.dot(
        left_real, right_imag, precision=highest, preferred_element_type=jnp.float32
    ) + jnp.dot(left_imag, right_real, precision=highest, preferred_element_type=jnp.float32)
    return (real, imag)


def complex_einsum(form, left_real, left_imag, right_real, right_imag, accurate):
    if accurate:
        real = jnp.einsum(form, left_real, right_real, precision=highest) - jnp.einsum(
            form, left_imag, right_imag, precision=highest
        )
        imag = jnp.einsum(form, left_real, right_imag, precision=highest) + jnp.einsum(
            form, left_imag, right_real, precision=highest
        )
    else:
        real = jnp.einsum(
            form, left_real, right_real, preferred_element_type=jnp.float32
        ) - jnp.einsum(form, left_imag, right_imag, preferred_element_type=jnp.float32)
        imag = jnp.einsum(
            form, left_real, right_imag, preferred_element_type=jnp.float32
        ) + jnp.einsum(form, left_imag, right_real, preferred_element_type=jnp.float32)
    return (real, imag)


def invert_pivot(pivot_h, pivot_s, shift_real, shift_imag, sweeps):
    matrix_real = pivot_h.astype(jnp.float32) - shift_real * pivot_s.astype(jnp.float32)
    matrix_imag = -shift_imag * pivot_s.astype(jnp.float32)
    diag_real = jnp.diagonal(matrix_real)
    diag_imag = jnp.diagonal(matrix_imag)
    denom = diag_real * diag_real + diag_imag * diag_imag
    identity = jnp.eye(matrix_real.shape[0], dtype=jnp.float32)

    def advance(index, state):
        approx_real, approx_imag = state
        prod_real, prod_imag = complex_matmul(matrix_real, matrix_imag, approx_real, approx_imag)
        return complex_matmul(approx_real, approx_imag, 2.0 * identity - prod_real, -prod_imag)

    start = (jnp.diag(diag_real / denom), jnp.diag(-diag_imag / denom))
    return lax.fori_loop(0, sweeps, advance, start)


def solve_rows(rows_h, rows_s, shift_real, shift_imag, inv_real, inv_imag):
    coupled_real = (rows_h.astype(jnp.float32) - shift_real * rows_s.astype(jnp.float32)).astype(
        jnp.bfloat16
    )
    coupled_imag = (-shift_imag * rows_s.astype(jnp.float32)).astype(jnp.bfloat16)
    result_real, result_imag = complex_matmul(
        coupled_real.astype(jnp.float32), coupled_imag.astype(jnp.float32), inv_real, inv_imag
    )
    return (coupled_real, coupled_imag, jnp.stack([result_real, result_imag]).astype(jnp.bfloat16))


def shards(
    front_h,
    front_s,
    panel_h,
    panel_s,
    pivot_h,
    pivot_s,
    pole_shift,
    pole_weight,
    pattern,
    ancestor_inverse,
):
    row_count = lax.axis_size("row")
    col_count = lax.axis_size("col")
    pole_count = lax.axis_size("pole")
    row_index = lax.axis_index("row")
    col_index = lax.axis_index("col")
    shift_real = pole_shift[0, 0]
    shift_imag = pole_shift[0, 1]
    weight_real = pole_weight[0, 0]
    weight_imag = pole_weight[0, 1]
    supernode = pivot_h.shape[0]
    piece = supernode // pole_count
    hamil_cols, margin_cols = (
        lax.all_to_all(front_h, "row", split_axis=1, concat_axis=0, tiled=True),
        lax.all_to_all(front_s, "row", split_axis=1, concat_axis=0, tiled=True),
    )
    width = hamil_cols.shape[0] // row_count
    block_rows = hamil_cols.shape[1]
    local_cols = jnp.arange(row_count * width)
    global_cols = (local_cols // width * col_count + col_index) * width + local_cols % width
    global_rows = row_index * block_rows + jnp.arange(block_rows)
    tile_mask = jnp.take(
        jnp.take(pattern, global_cols // supernode, axis=0), global_rows // supernode, axis=1
    ).astype(jnp.float32)
    margin_f = margin_cols.astype(jnp.float32)
    front_real = tile_mask * (hamil_cols.astype(jnp.float32) - shift_real * margin_f)
    front_imag = tile_mask * (-shift_imag * margin_f)
    inv_real, inv_imag = invert_pivot(pivot_h, pivot_s, shift_real, shift_imag, NEWTON)
    coupling_real, coupling_imag, solved = solve_rows(
        panel_h, panel_s, shift_real, shift_imag, inv_real, inv_imag
    )
    solved_strip = lax.dynamic_slice_in_dim(solved, col_index * width, width, axis=1)
    far_solved = lax.all_gather(solved_strip, "row", axis=1, tiled=True)
    update_real, update_imag = complex_einsum(
        "gk,ik->gi", far_solved[0], far_solved[1], coupling_real, coupling_imag, False
    )
    schur = jnp.stack([front_real - update_real, front_imag - update_imag]).astype(jnp.bfloat16)
    schur = schur.reshape(1, 2, row_count, 1, width, block_rows)
    ancestor = ancestor_inverse.reshape(2, row_count * width, block_rows)
    part_real, part_imag = complex_einsum(
        "gi,gk->ik", ancestor[0], ancestor[1], far_solved[0], far_solved[1], False
    )
    column = lax.psum_scatter(
        jnp.stack([-part_real, -part_imag]), "col", scatter_dimension=1, tiled=True
    )
    strip_f = solved_strip.astype(jnp.float32)
    corr_real, corr_imag = complex_einsum(
        "sk,sl->kl", strip_f[0], strip_f[1], column[0], column[1], True
    )
    correction = lax.psum(jnp.stack([corr_real, corr_imag]), ("row", "col"))
    rows_ready = weight_real * column[1] + weight_imag * column[0]
    block_real = inv_real - correction[0]
    block_imag = inv_imag - correction[1]
    pivot_density = weight_real * block_imag + weight_imag * block_real
    pole_items = (rows_ready, pivot_density)
    start_col = lax.axis_index("pole") * piece
    summed = lax.psum((pole_items[0], pole_items[1]), "pole")
    shares = tuple(
        (lax.dynamic_slice_in_dim(member, start_col, piece, axis=1) for member in summed)
    )
    rows_out = shares[0]
    pivot_out = shares[1]
    return (schur, rows_out, pivot_out)


def solution(mesh):
    in_specs = (
        P(("row", "col"), None),
        P(("row", "col"), None),
        P("row", None),
        P("row", None),
        P(),
        P(),
        P("pole", None),
        P("pole", None),
        P(),
        P("pole", None, None, "col", None, "row"),
    )
    out_specs = (
        P("pole", None, None, "col", None, "row"),
        P(("row", "col"), "pole"),
        P(None, "pole"),
    )
    return jax.shard_map(shards, mesh=mesh, in_specs=in_specs, out_specs=out_specs, check_vma=False)
```

profile of v0, /device:TPU:1, one launch (start us, length us, event | category | flops | bytes accessed | tf_op | source)
XLA Modules:
  0.0 430.8 jit_solution(9885962896862770048)
XLA Ops:
  7.2 1.9 copy.63
  9.1 12.0 %all-to-all-start.1 = ((bf16[64,16,256]{2,0,1:T(8,128)(2,1)}), bf16[64,16,256]{2,0,1:T(8,128)(2,1)S(1)}, u32[]{:S(2)}, u32[]{:S(2)}) async-start(bf16[64,16,256]{2,0,1:T(8,128)(2,1)} %bitcast.131), calls=%async_computation.1 | async-start | bytes 1048576 | tf_op jit(solution)/shard_map/all_to_all | solution.py:93
  21.1 0.6 copy-done.11
  21.7 0.6 fusion.68
  23.0 0.7 convert_multiply_fusion.2
  23.7 2.3 gather_fusion.3
  26.1 2.3 gather_fusion.2
  28.5 16.5 %while.13 = (s32[]{:T(128)}, f32[256,256]{0,1:T(8,128)S(1)}, f32[256,256]{0,1:T(8,128)S(1)}, f32[256,256]{1,0:T(8,128)S(1)}, f32[256,256]{1,0:T(8,128)S(1)}, /*index=5*/s32[]{:T(128)}) while((s32[]{:T(128)}, f32[256,256]{0,1:T(8,128)S(1)}, f32[256,256]{0,1:T(8,128)S(1)}, f32[256,256]{1,0:T(8,128)S(1)}, f32[256,256]{1,0:T(8,128)S(1)}, ...), condition=%wide.region_1.2_spmd.clone, body=%wide.region_0.1_spmd.clone.sunk | while | flops 1611137024 | bytes 7864389 | solution.py:54
  29.0 0.4 fusion.147
  29.4 0.6 fusion.149
  30.0 0.4 fusion.143
  30.8 0.6 fusion.145
  31.4 0.6 fusion.148
  32.0 0.6 fusion.150
  33.1 0.4 fusion.147
  33.5 0.6 fusion.149
  34.5 0.4 fusion.144
  35.0 0.6 fusion.145
  35.6 0.6 fusion.148
  36.2 0.6 fusion.150
  37.2 0.4 fusion.147
  37.6 0.6 fusion.149
  38.7 0.4 fusion.144
  39.1 0.6 fusion.145
  39.7 0.6 fusion.148
  40.3 0.6 fusion.150
  41.8 0.6 fusion.149
  42.8 0.4 fusion.144
  43.2 0.6 fusion.145
  43.8 0.6 fusion.148
  44.4 0.6 fusion.150
  46.4 0.6 fusion.40
  47.1 0.9 copy.64
  48.0 7.2 %all-to-all-start = ((bf16[64,16,256]{2,0,1:T(8,128)(2,1)}), bf16[64,16,256]{2,0,1:T(8,128)(2,1)S(1)}, u32[]{:S(2)}, u32[]{:S(2)}) async-start(bf16[64,16,256]{2,0,1:T(8,128)(2,1)} %bitcast.132), calls=%async_computation | async-start | bytes 1048576 | tf_op jit(solution)/shard_map/all_to_all | solution.py:92
  55.3 0.8 copy.40
  56.1 0.9 copy.39
  57.0 2.8 gather_fusion
  60.2 1.1 gather_fusion.1
  61.3 1.3 copy.32
  62.6 1.3 dynamic-slice
  64.5 0.6 copy-done.12
  65.2 0.7 fusion.67
  65.8 2.3 fusion.66
  68.1 5.4 %all-to-all-done = bf16[64,16,256]{2,0,1:T(8,128)(2,1)S(1)} async-done(((bf16[64,16,256]{2,0,1:T(8,128)(2,1)}), bf16[64,16,256]{2,0,1:T(8,128)(2,1)S(1)}, u32[]{:S(2)}, u32[]{:S(2)}) %all-to-all-start) | async-done | bytes 524320 | tf_op jit(solution)/shard_map/all_to_all | solution.py:92
  73.5 0.9 fusion.20
  74.7 16.8 %all-gather.2.cloned.1.call-done = bf16[2,1024,256]{2,1,0:T(8,128)(2,1)} async-done(((bf16[2,64,256]{2,1,0:T(8,128)(2,1)}), bf16[2,1024,256]{2,1,0:T(8,128)(2,1)}) %all-gather.2.cloned.1.call-update) | async-done | bytes 1048592 | tf_op jit(solution)/shard_map/all_gather | solution.py:111
  91.6 1.6 fusion.24
  93.2 1.4 fusion.21
  95.3 0.8 pad_maximum_fusion.1
  96.2 2.1 copy.37
  98.6 1.1 fusion.9
  99.8 48.2 %all-reduce.8.cloned.1.call-done = f32[2,256,256]{2,0,1:T(2,128)} async-done(((f32[2,256,256]{2,0,1:T(2,128)}), f32[2,256,256]{2,0,1:T(2,128)}) %all-reduce.8.cloned.1.call-update) | async-done | bytes 524304
  147.9 1.1 constant_dynamic-slice_fusion.3
  150.3 0.9 pad_maximum_fusion.2
  151.6 1.9 fusion.44
  153.5 192.0 %all-reduce.6.cloned.1.call-done = f32[2,256,256]{2,1,0:T(8,128)} async-done(((f32[2,256,256]{2,1,0:T(8,128)}), f32[2,256,256]{2,1,0:T(8,128)}) %all-reduce.6.cloned.1.call-update) | async-done | bytes 524304 | tf_op jit(solution)/shard_map/psum | solution.py:128
  345.5 3.3 fusion.31
  349.2 0.7 copy-done.4
  349.8 1.1 pad_maximum_fusion
  350.9 70.1 %all-reduce.10.cloned.1.call-done = (f32[64,256]{1,0:T(8,128)}, f32[256,256]{1,0:T(8,128)}) async-done(((f32[64,256]{1,0:T(8,128)}, f32[256,256]{1,0:T(8,128)}), (f32[64,256]{1,0:T(8,128)}, f32[256,256]{1,0:T(8,128)})) %all-reduce.10.cloned.1.call-update) | async-done | bytes 327696 | tf_op jit(solution)/shard_map/psum | solution.py:135
  421.0 0.8 constant_dynamic-slice_fusion.1
  421.9 0.7 copy.41
  422.6 1.0 constant_dynamic-slice_fusion
  423.6 0.7 copy.42
  (71 shorter events, 9.0 us)
Async XLA Ops:
  7.2 49.8 %copy-start = (s32[16,16]{1,0:T(8,128)S(1)}, s32[16,16]{1,0:T(8,128)}, u32[]{:S(2)}) copy-start(s32[16,16]{1,0:T(8,128)} %param.20) | copy-start | bytes 3076
  9.1 13.9 %copy-start.3 = (bf16[256,256]{1,0:T(8,128)(2,1)S(1)}, bf16[256,256]{1,0:T(8,128)(2,1)}, u32[]{:S(2)}) copy-start(bf16[256,256]{1,0:T(8,128)(2,1)} %param.15) | copy-start | bytes 393220
  9.1 13.9 %copy-start.8 = (bf16[256,256]{1,0:T(8,128)(2,1)S(1)}, bf16[256,256]{1,0:T(8,128)(2,1)}, u32[]{:S(2)}) copy-start(bf16[256,256]{1,0:T(8,128)(2,1)} %param.17) | copy-start | bytes 393220
  9.1 13.9 %copy-start.9 = (bf16[256,256]{1,0:T(8,128)(2,1)S(1)}, bf16[256,256]{1,0:T(8,128)(2,1)}, u32[]{:S(2)}) copy-start(bf16[256,256]{1,0:T(8,128)(2,1)} %param.16) | copy-start | bytes 393220
  9.1 13.9 %copy-start.10 = (bf16[256,256]{1,0:T(8,128)(2,1)S(1)}, bf16[256,256]{1,0:T(8,128)(2,1)}, u32[]{:S(2)}) copy-start(bf16[256,256]{1,0:T(8,128)(2,1)} %param.14) | copy-start | bytes 393220
  9.1 38.9 %all-to-all-start.1 = ((bf16[64,16,256]{2,0,1:T(8,128)(2,1)}), bf16[64,16,256]{2,0,1:T(8,128)(2,1)S(1)}, u32[]{:S(2)}, u32[]{:S(2)}) async-start(bf16[64,16,256]{2,0,1:T(8,128)(2,1)} %bitcast.131), calls=%async_computation.1 | async-start | bytes 1048576 | tf_op jit(solution)/shard_map/all_to_all | solution.py:93
  21.1 0.7 copy-start.11
  21.1 70.5 %all-gather.2.cloned.1.call-start = ((), (), s32[]{:S(2)}) async-start(), calls=%async_computation.2 | async-start | bytes 1114112 | tf_op jit(solution)/shard_map/all_gather | solution.py:111
  46.1 1.0 copy-start.6
  48.0 25.5 %all-to-all-start = ((bf16[64,16,256]{2,0,1:T(8,128)(2,1)}), bf16[64,16,256]{2,0,1:T(8,128)(2,1)S(1)}, u32[]{:S(2)}, u32[]{:S(2)}) async-start(bf16[64,16,256]{2,0,1:T(8,128)(2,1)} %bitcast.132), calls=%async_computation | async-start | bytes 1048576 | tf_op jit(solution)/shard_map/all_to_all | solution.py:92
  55.2 92.7 %all-reduce.8.cloned.1.call-start = ((), (), s32[]{:S(2)}) async-start(), calls=%async_computation.4 | async-start | bytes 1048576
  64.5 0.7 copy-start.12
  68.1 6.3 %copy-start.2 = (s32[256,1024]{0,1:T(8,128)S(1)}, s32[256,1024]{0,1:T(8,128)}, u32[]{:S(2)}) copy-start(s32[256,1024]{0,1:T(8,128)} %copy.32) | copy-start | bytes 3145732
  91.5 1.6 copy-start.1
  93.2 1.5 copy-start.7
  98.3 247.2 %all-reduce.6.cloned.1.call-start = ((), (), s32[]{:S(2)}) async-start(), calls=%async_computation.3 | async-start | bytes 1048576 | tf_op jit(solution)/shard_map/psum | solution.py:128
  99.8 49.3 %copy-start.5 = (bf16[2,64,256]{2,1,0:T(8,128)(2,1)S(1)}, bf16[2,64,256]{2,1,0:T(8,128)(2,1)}, u32[]{:S(2)}) copy-start(bf16[2,64,256]{2,1,0:T(8,128)(2,1)} %fusion.40) | copy-start | bytes 196612
  151.2 269.9 %all-reduce.10.cloned.1.call-start = ((), (), s32[]{:S(2)}) async-start(), calls=%async_computation.5 | async-start | bytes 655360 | tf_op jit(solution)/shard_map/psum | solution.py:135
  348.8 1.0 copy-start.4
Sparse Core Ops, SparseCore 0:
  47.2 44.3 all-gather.1
  98.4 49.5 all-reduce.7
  151.4 194.0 all-reduce.5
  348.9 72.0 all-reduce.9
where the time goes:
time: 435 us; the launch traced here: 431 us
  waiting for transfers between devices  333 us (77%)
  local copies, waits for them, and re-layouts  27.7 us (6%)
  matrix products  24.5 us (6%)
  starting transfers between devices  19.4 us (4%)
  between operations  15.4 us (4%)
  other arithmetic  10.8 us (2%)
    psum x1, waiting for transfers between devices, shards(): correction = lax.psum(jnp.stack([corr_real, corr_imag]), ('row', 'col'))  192 us
    psum x1, waiting for transfers between devices, shards(): summed = lax.psum((pole_items[0], pole_items[1]), 'pole')  70.1 us
    unnamed x5, waiting for transfers between devices  48.2 us
    all_gather x1, waiting for transfers between devices, shards(): far_solved = lax.all_gather(solved_strip, 'row', axis=1, tiled=True)  16.8 us
    all_to_all x1, starting transfers between devices, shards(): lax.all_to_all(front_s, 'row', split_axis=1, concat_axis=0, tiled=True)  12 us
  transfers between devices with their start and end apart: 6, of which 5 were waited for; matrix products, arithmetic and copies ran while one was open for 10% of the time, Pallas kernels for 0%

commit v1 on v0

v1 whole, which is shorter than its diff:
```python
import jax
import jax.numpy as jnp
from jax import lax
from jax.sharding import PartitionSpec as P

bf16 = jnp.bfloat16
f32 = jnp.float32


def block(real, imag):
    return jnp.concatenate(
        [jnp.concatenate([real, imag], axis=1), jnp.concatenate([-imag, real], axis=1)], axis=0
    )


def halves(wide):
    size = wide.shape[1] // 2
    return wide[:, :size], wide[:, size:]


def product(left, right):
    return jnp.dot(left, right, precision=lax.Precision.HIGH, preferred_element_type=f32)


def invert_pivot(pivot_h, pivot_s, shift_real, shift_imag):
    size = pivot_h.shape[0]
    margin = pivot_s.astype(f32)
    real = pivot_h.astype(f32) - shift_real * margin
    imag = -shift_imag * margin
    on_diag = jnp.eye(size, dtype=bool)
    diag_real = jnp.sum(jnp.where(on_diag, real, 0.0), axis=0)
    diag_imag = jnp.sum(jnp.where(on_diag, imag, 0.0), axis=0)
    denom = diag_real * diag_real + diag_imag * diag_imag
    inv_real, inv_imag = diag_real / denom, -diag_imag / denom
    err_real = jnp.where(on_diag, 0.0, imag * inv_imag - real * inv_real)
    err_imag = jnp.where(on_diag, 0.0, -(real * inv_imag + imag * inv_real))
    one = jnp.concatenate([on_diag.astype(f32), jnp.zeros((size, size), f32)], axis=1)
    err = jnp.concatenate([err_real, err_imag], axis=1)
    err2 = product(err, block(err_real, err_imag))
    square = block(*halves(err2))
    err3 = product(err, square)
    err4 = product(err2, square)
    first = one + err + err2 + err3
    fourth = block(*halves(err4))
    second = first + product(first, fourth)
    err8 = product(err4, fourth)
    total = second + product(second, block(*halves(err8)))
    sum_real, sum_imag = halves(total)
    scale_real, scale_imag = inv_real[:, None], inv_imag[:, None]
    return (
        scale_real * sum_real - scale_imag * sum_imag,
        scale_real * sum_imag + scale_imag * sum_real,
    )


def couple(rows_h, rows_s, shift_real, shift_imag):
    margin = rows_s.astype(f32)
    real = (rows_h.astype(f32) - shift_real * margin).astype(bf16)
    imag = (-shift_imag * margin).astype(bf16)
    return real, imag


def dot(left, right):
    return jnp.dot(left, right, preferred_element_type=f32)


def contract(left, right):
    return lax.dot_general(left, right, (((0,), (0,)), ((), ())), preferred_element_type=f32)


def split(value):
    high = value.astype(bf16)
    return high, (value - high.astype(f32)).astype(bf16)


def pack(member, col_count, pole_count):
    size = member.shape[0]
    width, piece = size // col_count, size // pole_count
    fold = 128 // width
    member = member.reshape(pole_count, fold, piece // fold, col_count, width)
    return member.transpose(0, 3, 2, 1, 4).reshape(pole_count * col_count, piece // fold, 128)


def unpack(member, width, piece):
    fold = 128 // width
    member = member.reshape(-1, piece // fold, fold, width)
    return member.transpose(2, 1, 0, 3).reshape(piece, -1)


def shards(
    front_h,
    front_s,
    panel_h,
    panel_s,
    pivot_h,
    pivot_s,
    pole_shift,
    pole_weight,
    pattern,
    ancestor_inverse,
):
    row_count = lax.axis_size("row")
    col_count = lax.axis_size("col")
    pole_count = lax.axis_size("pole")
    row_index = lax.axis_index("row")
    col_index = lax.axis_index("col")
    shift_real = pole_shift[0, 0]
    shift_imag = pole_shift[0, 1]
    weight_real = pole_weight[0, 0]
    weight_imag = pole_weight[0, 1]
    size = pivot_h.shape[0]
    width = size // col_count
    piece = size // pole_count
    half = width // 2
    order = row_count * width
    core = row_index % 2

    strip = lax.dynamic_slice_in_dim(jnp.stack([panel_h, panel_s]), col_index * width, width, axis=1)
    strip = strip.reshape(2, 2, half, size).transpose(1, 0, 2, 3)
    sent = jnp.broadcast_to(strip[None], (row_count // 2, 2, 2, half, size))
    far = lax.all_to_all(
        sent.reshape(row_count, 2, half, size), "row", split_axis=0, concat_axis=0, tiled=True
    )

    fronts = jnp.stack([front_h, front_s]).reshape(2, width, row_count, size).transpose(2, 0, 1, 3)
    fronts, _ = lax.optimization_barrier((fronts, far))
    tiles = lax.all_to_all(fronts, "row", split_axis=0, concat_axis=0, tiled=True)

    inv_real, inv_imag = invert_pivot(pivot_h, pivot_s, shift_real, shift_imag)
    inv_high, inv_low = split(block(inv_real, inv_imag))

    def solve(real, imag):
        wide = jnp.concatenate([real, imag], axis=1)
        return (dot(wide, inv_high) + dot(wide, inv_low)).astype(bf16)

    coupling_real, coupling_imag = couple(panel_h, panel_s, shift_real, shift_imag)
    solved = solve(coupling_real, coupling_imag)

    far_half = solve(
        *couple(
            far[:, 0].reshape(row_count * half, size),
            far[:, 1].reshape(row_count * half, size),
            shift_real,
            shift_imag,
        )
    )
    other = lax.ppermute(far_half, "row", [(i, i ^ 1) for i in range(row_count)])
    mine = far_half.reshape(row_count, 1, half, 2 * size)
    other = other.reshape(row_count, 1, half, 2 * size)
    far_solved = jnp.where(
        core == 0,
        jnp.concatenate([mine, other], axis=1),
        jnp.concatenate([other, mine], axis=1),
    ).reshape(order, 2 * size)

    far_real, far_imag = halves(far_solved)
    ancestor = ancestor_inverse.reshape(2 * order, size)
    part = contract(
        jnp.concatenate([far_solved, jnp.concatenate([-far_imag, far_real], axis=1)], axis=0),
        ancestor,
    )
    part_real, part_imag = part[:size], part[size:]
    rows_part = -(weight_real * part_imag + weight_imag * part_real)
    twin_part = -(weight_real * part_real - weight_imag * part_imag)
    solved_real, solved_imag = halves(solved)
    right = jnp.concatenate([solved_real, solved_imag], axis=0)
    left_high, left_low = split(jnp.concatenate([rows_part, twin_part], axis=1))
    correction = dot(left_high, right) + dot(left_low, right)
    pivot_part = (
        jnp.where(
            (row_index == 0) & (col_index == 0),
            weight_real * inv_imag + weight_imag * inv_real,
            0.0,
        ).T
        - correction
    )

    both = jnp.stack(
        [pack(rows_part, col_count, pole_count), pack(pivot_part, col_count, pole_count)], axis=1
    )
    both = lax.all_to_all(both, ("pole", "col"), split_axis=0, concat_axis=0, tiled=True)
    both = jnp.sum(both, axis=0)
    rows_out = unpack(both[:1, :, :], width, piece).T

    spread = jnp.broadcast_to(both[1][None], (row_count * col_count,) + both.shape[1:])
    spread = lax.all_to_all(spread, ("row", "col"), split_axis=0, concat_axis=0, tiled=True)
    spread = jnp.sum(spread.reshape((row_count, col_count) + both.shape[1:]), axis=0)
    pivot_out = unpack(spread, width, piece).T

    update = dot(far_solved, block(coupling_real.T, coupling_imag.T))
    mask = lax.dynamic_slice_in_dim(pattern, row_index, 1, axis=1).astype(f32)[:, :, None]
    hamil = tiles[:, 0].astype(f32)
    margin = tiles[:, 1].astype(f32)
    front_real = (mask * (hamil - shift_real * margin)).reshape(order, size)
    front_imag = (mask * (-shift_imag * margin)).reshape(order, size)
    update_real, update_imag = halves(update)
    schur = jnp.stack([front_real - update_real, front_imag - update_imag]).astype(bf16)
    schur = schur.reshape(1, 2, row_count, 1, width, size)
    return (schur, rows_out, pivot_out)


def solution(mesh):
    in_specs = (
        P(("row", "col"), None),
        P(("row", "col"), None),
        P("row", None),
        P("row", None),
        P(),
        P(),
        P("pole", None),
        P("pole", None),
        P(),
        P("pole", None, None, "col", None, "row"),
    )
    out_specs = (
        P("pole", None, None, "col", None, "row"),
        P(("row", "col"), "pole"),
        P(None, "pole"),
    )
    return jax.shard_map(shards, mesh=mesh, in_specs=in_specs, out_specs=out_specs, check_vma=False)
```

time: 435 us -> 131 us (0.30)
  waiting for transfers between devices: 333 us -> 61.7 us
  local copies, waits for them, and re-layouts: 27.7 us -> 9.26 us
  starting transfers between devices: 19.4 us -> 35.2 us
  between operations: 15.4 us -> 1.83 us
  matrix products: 24.5 us -> 11.8 us
    psum x2 -> x0, waiting for transfers between devices: 262 us -> none  [the longest x1 192 us: shards(): correction = lax.psum(jnp.stack([corr_real, corr_imag]), ('row', 'col'))]
    all_to_all x2 -> x4, waiting for transfers between devices: 5.41 us -> 61.7 us  [the longest x1 27.6 us: shards(): lax.all_to_all(fronts, 'row', split_axis=0, concat_axis=0, tiled=True)]
    unnamed x5 -> x0, waiting for transfers between devices: 48.2 us -> none
    all_gather x1 -> x0, waiting for transfers between devices: 16.8 us -> none  [shards(): far_solved = lax.all_gather(solved_strip, 'row', axis=1, tiled=True)]
    all_to_all x2 -> x4, starting transfers between devices: 19.2 us -> 33.3 us  [the longest x1 11.8 us: shards(): lax.all_to_all(sent.reshape(row_count, 2, half, size), 'row', split_axis=...]
    dot_general x48 -> x14, matrix products: 24.5 us -> 11.8 us  [the longest x7 7.13 us: dot(): return jnp.dot(left, right, preferred_element_type=f32)]
    gather x5 -> x0, local copies, waits for them, and re-layouts: 9.87 us -> none  [the longest x1 2.81 us: shards(): jnp.take(pattern, global_cols // supernode, axis=0)]
    add x2 -> x0, other arithmetic: 5.21 us -> none  [the longest x1 3.27 us: shards(): pivot_density = weight_real * block_imag + weight_imag * block_real]
  transfers between devices with their start and end apart: 6 -> 5, of which waited for: 5 -> 4; matrix products, arithmetic and copies ran while one was open for 10% -> 14% of each run, Pallas kernels for 0% -> 0%
where the time goes in v1:
time: 131 us; the launch traced here: 130 us
  waiting for transfers between devices  61.7 us (47%)
  starting transfers between devices  35.2 us (27%)
  matrix products  11.8 us (9%)
  other arithmetic  10.6 us (8%)
  local copies, waits for them, and re-layouts  9.26 us (7%)
  between operations  1.83 us (1%)
    all_to_all x1, waiting for transfers between devices, shards(): lax.all_to_all(fronts, 'row', split_axis=0, concat_axis=0, tiled=True)  27.6 us
    all_to_all x1, waiting for transfers between devices, shards(): lax.all_to_all(both, ('pole', 'col'), split_axis=0, concat_axis=0, tiled=...  14.7 us
    all_to_all x1, starting transfers between devices, shards(): lax.all_to_all(sent.reshape(row_count, 2, half, size), 'row', split_axis=...  11.8 us
    all_to_all x1, waiting for transfers between devices, shards(): lax.all_to_all(spread, ('row', 'col'), split_axis=0, concat_axis=0, tiled...  11 us
    all_to_all x1, starting transfers between devices, shards(): lax.all_to_all(both, ('pole', 'col'), split_axis=0, concat_axis=0, tiled=...  9.67 us
    all_to_all x1, waiting for transfers between devices, shards(): lax.all_to_all(sent.reshape(row_count, 2, half, size), 'row', split_axis=...  8.35 us
    dot_general x7, matrix products, dot(): return jnp.dot(left, right, preferred_element_type=f32)  7.13 us
    all_to_all x1, starting transfers between devices, shards(): lax.all_to_all(spread, ('row', 'col'), split_axis=0, concat_axis=0, tiled...  6.04 us
  transfers between devices with their start and end apart: 5, of which 4 were waited for; matrix products, arithmetic and copies ran while one was open for 14% of the time, Pallas kernels for 0%

profile of v1, /device:TPU:1, one launch (start us, length us, event | category | flops | bytes accessed | tf_op | source)
XLA Modules:
  0.0 130.4 jit_solution(5384729531461941445)
XLA Ops:
  0.6 0.0 copy-start
  0.7 0.9 fusion.59
  1.6 0.9 broadcast_in_dim.15
  2.5 11.8 %all-to-all-start = ((bf16[16,2,32,256]{3,2,1,0:T(8,128)(2,1)}), bf16[16,2,32,256]{3,2,1,0:T(8,128)(2,1)S(1)}, u32[]{:S(2)}, u32[]{:S(2)}) async-start(bf16[16,2,32,256]{3,2,1,0:T(8,128)(2,1)} %bitcast.5), calls=%async_computation | async-start | bytes 1048576 | tf_op jit(solution)/shard_map/all_to_all | solution.py:121
  14.3 0.6 fusion.85
  15.6 0.7 fusion.56
  16.3 0.7 fusion.48
  17.1 0.8 fusion.81
  17.9 0.6 fusion.12
  18.6 0.7 fusion.26
  19.3 0.7 fusion.25
  20.0 0.7 convolution_add_fusion.3
  20.7 0.7 convolution_add_fusion.2
  21.3 0.7 convolution_add_fusion.1
  22.0 0.1 fusion.80
  22.1 1.1 fusion.58
  23.3 8.4 %all-to-all-done = bf16[16,2,32,256]{3,2,1,0:T(8,128)(2,1)S(1)} async-done(((bf16[16,2,32,256]{3,2,1,0:T(8,128)(2,1)}), bf16[16,2,32,256]{3,2,1,0:T(8,128)(2,1)S(1)}, u32[]{:S(2)}, u32[]{:S(2)}) %all-to-all-start) | async-done | bytes 524320 | tf_op jit(solution)/shard_map/all_to_all | solution.py:121
  31.6 0.8 fusion.29
  32.4 0.5 fusion.42
  32.8 0.0 copy-start.11
  32.9 0.5 fusion.6
  33.3 1.9 %collective-permute-start = (bf16[512,512]{1,0:T(8,128)(2,1)S(1)}, bf16[512,512]{1,0:T(8,128)(2,1)S(1)}, u32[]{:S(2)}, u32[]{:S(2)}) collective-permute-start(bf16[512,512]{1,0:T(8,128)(2,1)S(1)} %fusion.6), channel_id=1, source_target_pairs={{0,4},{4,0},{8,12},{12,8},{16,20},{20,16},{24,28},{28,24},{32,36},... | collective-permute-start | bytes 1572872 | tf_op jit(solution)/shard_map/ppermute | solution.py:147
  35.3 0.6 fusion.84
  35.9 1.3 %fusion.7 = bf16[256,512]{1,0:T(8,128)(2,1)S(1)} fusion(f32[256,512]{1,0:T(8,128)} %fusion.58, bf16[256,256]{1,0:T(8,128)(2,1)S(1)} %get-tuple-element.8, bf16[256,256]{1,0:T(8,128)(2,1)S(1)} %fusion.56, f32[256,256]{1,0:T(8,128)S(1)} %get-tuple-element.19, f32[256,256]{1,0:T(8,128)S(1)} %get-tuple-element.9, f32[256,256]{1,0:T(8,128)S(1)} %get-tuple-element.10), kind=kOutput, calls=%fused_computation.14 | convolution fusion | flops 136839168 | bytes 1835008 | tf_op jit(solution)/shard_map/dot_general | solution.py:64
  37.3 0.1 maximum_select_fusion
  37.4 0.1 slice_negate_fusion
  37.5 0.7 fusion
  38.2 0.1 copy-done.1
  38.3 1.3 %add_negate_fusion = (f32[256,256]{1,0:T(8,128)S(1)}, f32[256,256]{1,0:T(8,128)S(1)}) fusion(f32[512,256]{1,0:T(8,128)S(1)} %fusion, f32[]{:T(128)} %bitcast.27, f32[]{:T(128)} %bitcast.25), kind=kLoop, calls=%fused_computation.97 | loop fusion | flops 524288 | bytes 1048584 | tf_op jit(solution)/shard_map/neg | solution.py:163
  39.7 0.2 reshape.145
  39.9 0.3 fusion.46
  40.2 1.5 %fusion.8 = f32[256,256]{0,1:T(8,128)S(1)} fusion(f32[256,256]{0,1:T(8,128)S(1)} %fusion.46, f32[256,256]{1,0:T(8,128)S(1)} %get-tuple-element.21, f32[256,256]{1,0:T(8,128)S(1)} %get-tuple-element.20, f32[256,256]{1,0:T(8,128)S(1)} %get-tuple-element.19, f32[256,256]{1,0:T(8,128)S(1)} %get-tuple-element.10, bf16[256,256]{1,0:T(8,128)(2,1)S(1)} %get-tuple-element.32, ...), kind=kOutput, calls=%fused_computation.16 | convolution fusion | flops 68681728 | bytes 1835017 | tf_op jit(solution)/shard_map/dot_general | solution.py:64
  41.7 0.1 copy.103
  41.9 0.2 reshape.146
  42.1 0.4 copy.104
  42.5 0.3 stack_reshape.7
  42.8 0.4 copy.114
  43.2 0.0 copy-start.7
  43.2 0.3 stack_reshape.6
  43.6 0.9 copy.105
  44.5 9.7 %all-to-all-start.2 = ((f32[32,2,16,128]{3,2,1,0:T(8,128)}), f32[32,2,16,128]{3,2,1,0:T(8,128)S(1)}, u32[]{:S(2)}, u32[]{:S(2)}) async-start(f32[32,2,16,128]{3,2,1,0:T(8,128)} %copy.105), calls=%async_computation.2 | async-start | bytes 1048576 | tf_op jit(solution)/shard_map/all_to_all | solution.py:181
  54.2 0.1 copy.111
  54.3 0.1 copy.112
  54.4 0.1 maximum_bitcast_fusion
  54.5 0.0 copy-start.9
  54.5 1.3 %copy.91 = bf16[16,2,64,256]{3,2,1,0:T(8,128)(2,1)} copy(bf16[16,2,64,256]{3,0,2,1:T(8,128)(2,1)S(1)} %maximum_bitcast_fusion) | data formatting | bytes 2097152 | tf_op jit(solution)/shard_map/optimization_barrier | solution.py:126
  55.8 14.7 %all-to-all-done.2 = f32[32,2,16,128]{3,2,1,0:T(8,128)S(1)} async-done(((f32[32,2,16,128]{3,2,1,0:T(8,128)}), f32[32,2,16,128]{3,2,1,0:T(8,128)S(1)}, u32[]{:S(2)}, u32[]{:S(2)}) %all-to-all-start.2) | async-done | bytes 524320 | tf_op jit(solution)/shard_map/all_to_all | solution.py:181
  70.6 5.7 %all-to-all-start.1 = ((bf16[16,2,64,256]{3,2,1,0:T(8,128)(2,1)}), bf16[16,2,64,256]{3,2,1,0:T(8,128)(2,1)S(1)}, u32[]{:S(2)}, u32[]{:S(2)}) async-start(bf16[16,2,64,256]{3,2,1,0:T(8,128)(2,1)} %copy.91), calls=%async_computation.1 | async-start | bytes 2097152 | tf_op jit(solution)/shard_map/all_to_all | solution.py:127
  76.3 0.2 convert_reduce_fusion
  76.5 0.1 mul.196
  76.6 0.1 mul.197
  76.7 27.6 %all-to-all-done.1 = bf16[16,2,64,256]{3,2,1,0:T(8,128)(2,1)S(1)} async-done(((bf16[16,2,64,256]{3,2,1,0:T(8,128)(2,1)}), bf16[16,2,64,256]{3,2,1,0:T(8,128)(2,1)S(1)}, u32[]{:S(2)}, u32[]{:S(2)}) %all-to-all-start.1) | async-done | bytes 1048608 | tf_op jit(solution)/shard_map/all_to_all | solution.py:127
  104.3 0.9 broadcast_in_dim.19
  105.2 6.0 %all-to-all-start.3 = ((f32[64,16,128]{2,1,0:T(8,128)}), f32[64,16,128]{2,1,0:T(8,128)}, u32[]{:S(2)}, u32[]{:S(2)}) async-start(f32[64,16,128]{2,1,0:T(8,128)} %broadcast_in_dim.19), calls=%async_computation.3 | async-start | bytes 1048576 | tf_op jit(solution)/shard_map/all_to_all | solution.py:186
  111.2 2.0 %fusion.33 = f32[1024,512]{1,0:T(8,128)S(1)} fusion(bf16[1024,512]{1,0:T(8,128)(2,1)} %bitcast.71, bf16[256,256]{0,1:T(8,128)(2,1)S(1)} %bitcast.83, bf16[256,256]{0,1:T(8,128)(2,1)S(1)} %get-tuple-element.7, bf16[256,256]{0,1:T(8,128)(2,1)S(1)} %bitcast.82), kind=kOutput, calls=%fused_computation.57 | convolution fusion | flops 538968064 | bytes 3538944 | tf_op jit(solution)/shard_map/dot_general | solution.py:64
  113.2 0.1 reshape.147
  113.3 0.6 copy.106
  113.9 2.1 %fusion.9 = (f32[16,1,64,256]{3,2,1,0:T(8,128)S(1)}, f32[16,1,64,256]{3,2,1,0:T(8,128)S(1)}) fusion(bf16[16,2,64,256]{3,2,1,0:T(8,128)(2,1)} %copy-done.2, f32[]{:T(128)} %bitcast.6, f32[]{:T(128)} %bitcast.9), kind=kLoop, calls=%fused_computation.17 | loop fusion | flops 1310720 | bytes 3145736 | tf_op jit(solution)/shard_map/sub | solution.py:194
  116.0 0.3 fusion.11
  116.4 1.1 pad_maximum_fusion
  117.4 11.0 %all-to-all-done.3 = f32[64,16,128]{2,1,0:T(8,128)} async-done(((f32[64,16,128]{2,1,0:T(8,128)}), f32[64,16,128]{2,1,0:T(8,128)}, u32[]{:S(2)}, u32[]{:S(2)}) %all-to-all-start.3) | async-done | bytes 524320 | tf_op jit(solution)/shard_map/all_to_all | solution.py:186
  128.4 1.1 reduce_sum.39
  129.5 0.1 reshape.150
  129.6 0.7 reshape.151
  (32 shorter events, 0.4 us)
Async XLA Ops:
  0.6 36.8 %copy-start = (bf16[1,2,16,1,64,256]{5,4,3,2,1,0:T(8,128)(2,1)S(1)}, bf16[1,2,16,1,64,256]{5,4,3,2,1,0:T(8,128)(2,1)}, u32[]{:S(2)}) copy-start(bf16[1,2,16,1,64,256]{5,4,3,2,1,0:T(8,128)(2,1)} %param.19) | copy-start | bytes 3145732
  0.6 15.0 %copy-start.4 = (bf16[256,256]{1,0:T(8,128)(2,1)S(1)}, bf16[256,256]{1,0:T(8,128)(2,1)}, u32[]{:S(2)}) copy-start(bf16[256,256]{1,0:T(8,128)(2,1)} %param.12) | copy-start | bytes 393220
  0.7 14.9 %copy-start.3 = (bf16[256,256]{1,0:T(8,128)(2,1)S(1)}, bf16[256,256]{1,0:T(8,128)(2,1)}, u32[]{:S(2)}) copy-start(bf16[256,256]{1,0:T(8,128)(2,1)} %param.13) | copy-start | bytes 393220
  0.7 13.7 %copy-start.10 = (f32[1,2]{1,0:T(1,128)S(1)}, f32[1,2]{1,0:T(1,128)}, u32[]{:S(2)}) copy-start(f32[1,2]{1,0:T(1,128)} %param.16) | copy-start | bytes 28
  0.7 15.7 %copy-start.6 = (bf16[256,256]{1,0:T(8,128)(2,1)S(1)}, bf16[256,256]{1,0:T(8,128)(2,1)}, u32[]{:S(2)}) copy-start(bf16[256,256]{1,0:T(8,128)(2,1)} %param.14) | copy-start | bytes 393220
  0.7 15.7 %copy-start.5 = (bf16[256,256]{1,0:T(8,128)(2,1)S(1)}, bf16[256,256]{1,0:T(8,128)(2,1)}, u32[]{:S(2)}) copy-start(bf16[256,256]{1,0:T(8,128)(2,1)} %param.15) | copy-start | bytes 393220
  2.5 29.2 %all-to-all-start = ((bf16[16,2,32,256]{3,2,1,0:T(8,128)(2,1)}), bf16[16,2,32,256]{3,2,1,0:T(8,128)(2,1)S(1)}, u32[]{:S(2)}, u32[]{:S(2)}) async-start(bf16[16,2,32,256]{3,2,1,0:T(8,128)(2,1)} %bitcast.5), calls=%async_computation | async-start | bytes 1048576 | tf_op jit(solution)/shard_map/all_to_all | solution.py:121
  32.8 2.4 %copy-start.11 = (f32[1,2]{1,0:T(1,128)S(1)}, f32[1,2]{1,0:T(1,128)}, u32[]{:S(2)}) copy-start(f32[1,2]{1,0:T(1,128)} %param.17) | copy-start | bytes 28
  33.3 3.9 %collective-permute-start = (bf16[512,512]{1,0:T(8,128)(2,1)S(1)}, bf16[512,512]{1,0:T(8,128)(2,1)S(1)}, u32[]{:S(2)}, u32[]{:S(2)}) collective-permute-start(bf16[512,512]{1,0:T(8,128)(2,1)S(1)} %fusion.6), channel_id=1, source_target_pairs={{0,4},{4,0},{8,12},{12,8},{16,20},{20,16},{24,28},{28,24},{32,36},... | collective-permute-start | bytes 1572872 | tf_op jit(solution)/shard_map/ppermute | solution.py:147
  37.4 1.0 copy-start.1
  43.2 10.9 %copy-start.7 = (bf16[64,4096]{1,0:T(8,128)(2,1)S(1)}, bf16[64,4096]{1,0:T(8,128)(2,1)}, u32[]{:S(2)}) copy-start(bf16[64,4096]{1,0:T(8,128)(2,1)} %param.10) | copy-start | bytes 1572868
  43.6 10.7 %copy-start.8 = (bf16[64,4096]{1,0:T(8,128)(2,1)S(1)}, bf16[64,4096]{1,0:T(8,128)(2,1)}, u32[]{:S(2)}) copy-start(bf16[64,4096]{1,0:T(8,128)(2,1)} %param.11) | copy-start | bytes 1572868
  44.5 26.1 %all-to-all-start.2 = ((f32[32,2,16,128]{3,2,1,0:T(8,128)}), f32[32,2,16,128]{3,2,1,0:T(8,128)S(1)}, u32[]{:S(2)}, u32[]{:S(2)}) async-start(f32[32,2,16,128]{3,2,1,0:T(8,128)} %copy.105), calls=%async_computation.2 | async-start | bytes 1048576 | tf_op jit(solution)/shard_map/all_to_all | solution.py:181
  54.5 21.8 %copy-start.9 = (s32[16,16]{1,0:T(8,128)S(1)}, s32[16,16]{1,0:T(8,128)}, u32[]{:S(2)}) copy-start(s32[16,16]{1,0:T(8,128)} %param.18) | copy-start | bytes 3076
  70.6 33.7 %all-to-all-start.1 = ((bf16[16,2,64,256]{3,2,1,0:T(8,128)(2,1)}), bf16[16,2,64,256]{3,2,1,0:T(8,128)(2,1)S(1)}, u32[]{:S(2)}, u32[]{:S(2)}) async-start(bf16[16,2,64,256]{3,2,1,0:T(8,128)(2,1)} %copy.91), calls=%async_computation.1 | async-start | bytes 2097152 | tf_op jit(solution)/shard_map/all_to_all | solution.py:127
  104.3 6.9 %copy-start.2 = (bf16[16,2,64,256]{3,2,1,0:T(8,128)(2,1)}, bf16[16,2,64,256]{3,2,1,0:T(8,128)(2,1)S(1)}, u32[]{:S(2)}) copy-start(bf16[16,2,64,256]{3,2,1,0:T(8,128)(2,1)S(1)} %all-to-all-done.1) | copy-start | bytes 3145732
  105.2 23.2 %all-to-all-start.3 = ((f32[64,16,128]{2,1,0:T(8,128)}), f32[64,16,128]{2,1,0:T(8,128)}, u32[]{:S(2)}, u32[]{:S(2)}) async-start(f32[64,16,128]{2,1,0:T(8,128)} %broadcast_in_dim.19), calls=%async_computation.3 | async-start | bytes 1048576 | tf_op jit(solution)/shard_map/all_to_all | solution.py:186

commit v2 on v1

--- a/solution.py
+++ b/solution.py
@@ -69,8 +69,8 @@
 
 
 def split(value):
-    high = value.astype(bf16)
-    return high, (value - high.astype(f32)).astype(bf16)
+    high = lax.reduce_precision(value, 8, 7)
+    return high.astype(bf16), (value - high).astype(bf16)
 
 
 def pack(member, col_count, pole_count):
@@ -118,13 +118,18 @@
     strip = lax.dynamic_slice_in_dim(jnp.stack([panel_h, panel_s]), col_index * width, width, axis=1)
     strip = strip.reshape(2, 2, half, size).transpose(1, 0, 2, 3)
     sent = jnp.broadcast_to(strip[None], (row_count // 2, 2, 2, half, size))
-    far = lax.all_to_all(
-        sent.reshape(row_count, 2, half, size), "row", split_axis=0, concat_axis=0, tiled=True
-    )
-
-    fronts = jnp.stack([front_h, front_s]).reshape(2, width, row_count, size).transpose(2, 0, 1, 3)
-    fronts, _ = lax.optimization_barrier((fronts, far))
-    tiles = lax.all_to_all(fronts, "row", split_axis=0, concat_axis=0, tiled=True)
+    sent = sent.reshape(row_count, 2 * half, size)
+    share = width // pole_count
+    fronts = lax.dynamic_slice_in_dim(
+        jnp.stack([front_h, front_s]), lax.axis_index("pole") * share, share, axis=1
+    )
+    fronts = fronts.reshape(2, share, row_count, size).transpose(2, 0, 1, 3)
+    sent = jnp.concatenate([sent, fronts.reshape(row_count, 2 * share, size)], axis=1)
+    received = lax.all_to_all(sent, "row", split_axis=0, concat_axis=0, tiled=True)
+    far = received[:, : 2 * half].reshape(row_count, 2, half, size)
+    tiles = lax.all_gather(received[:, 2 * half :], "pole", axis=0, tiled=False)
+    tiles = tiles.reshape(pole_count, row_count, 2, share, size).transpose(1, 2, 0, 3, 4)
+    tiles = tiles.reshape(row_count, 2, width, size)
 
     inv_real, inv_imag = invert_pivot(pivot_h, pivot_s, shift_real, shift_imag)
     inv_high, inv_low = split(block(inv_real, inv_imag))

time: 131 us -> 123 us (0.939)
  waiting for transfers between devices: 61.7 us -> 43 us
  between operations: 1.83 us -> 15.3 us
  starting transfers between devices: 35.2 us -> 30.6 us
    all_to_all x2 -> x1, waiting for transfers between devices: 35.9 us -> 10.9 us  [shards(): lax.all_to_all(sent, 'row', split_axis=0, concat_axis=0, tiled=True)]
    all_to_all x1, waiting for transfers between devices: 14.7 us -> 21.3 us  [shards(): lax.all_to_all(both, ('pole', 'col'), split_axis=0, concat_axis=0, tiled=...]
    all_to_all x2 -> x1, starting transfers between devices: 17.6 us -> 11.8 us  [shards(): lax.all_to_all(sent, 'row', split_axis=0, concat_axis=0, tiled=True)]
    transpose x0 -> x2, local copies, waits for them, and re-layouts: none -> 1.38 us  [the longest x1 1.34 us: shards(): tiles.reshape(pole_count, row_count, 2, share, size)]
    optimization_barrier x1 -> x0, local copies, waits for them, and re-layouts: 1.34 us -> none  [shards(): fronts, _ = lax.optimization_barrier((fronts, far))]
  transfers between devices with their start and end apart: 5 -> 5, of which waited for: 4 -> 3; matrix products, arithmetic and copies ran while one was open for 14% -> 22% of each run, Pallas kernels for 0% -> 0%
where the time goes in v2:
time: 123 us; the launch traced here: 122 us
  waiting for transfers between devices  43 us (35%)
  starting transfers between devices  30.6 us (25%)
  between operations  15.3 us (12%)
  matrix products  12 us (10%)
  other arithmetic  11.2 us (9%)
  local copies, waits for them, and re-layouts  9.66 us (8%)
    all_to_all x1, waiting for transfers between devices, shards(): lax.all_to_all(both, ('pole', 'col'), split_axis=0, concat_axis=0, tiled=...  21.3 us
    all_to_all x1, starting transfers between devices, shards(): lax.all_to_all(sent, 'row', split_axis=0, concat_axis=0, tiled=True)  11.8 us
    all_to_all x1, waiting for transfers between devices, shards(): lax.all_to_all(sent, 'row', split_axis=0, concat_axis=0, tiled=True)  10.9 us
    all_to_all x1, waiting for transfers between devices, shards(): lax.all_to_all(spread, ('row', 'col'), split_axis=0, concat_axis=0, tiled...  10.8 us
    all_to_all x1, starting transfers between devices, shards(): lax.all_to_all(both, ('pole', 'col'), split_axis=0, concat_axis=0, tiled=...  9.67 us
    dot_general x7, matrix products, dot(): return jnp.dot(left, right, preferred_element_type=f32)  7.36 us
    all_to_all x1, starting transfers between devices, shards(): lax.all_to_all(spread, ('row', 'col'), split_axis=0, concat_axis=0, tiled...  7.14 us
    dot_general x6, matrix products, product(): jnp.dot(left, right, precision=lax.Precision.HIGH, preferred_element_type...  3.94 us
  transfers between devices with their start and end apart: 5, of which 3 were waited for; matrix products, arithmetic and copies ran while one was open for 22% of the time, Pallas kernels for 0%

profile of v2, /device:TPU:1, one launch (start us, length us, event | category | flops | bytes accessed | tf_op | source)
XLA Modules:
  0.0 121.8 jit_solution(17966940990702172021)
XLA Ops:
  7.2 0.0 copy-start
  7.2 0.9 fusion.60
  8.1 0.9 fusion.59
  9.0 0.0 copy-start.14
  9.1 0.0 copy-start.4
  9.1 0.1 broadcast_in_dim.15
  9.2 0.9 pad_maximum_fusion.1
  10.0 11.8 %all-to-all-start = ((bf16[16,80,256]{2,1,0:T(8,128)(2,1)}), bf16[16,80,256]{2,1,0:T(8,128)(2,1)S(1)}, u32[]{:S(2)}, u32[]{:S(2)}) async-start(bf16[16,80,256]{2,1,0:T(8,128)(2,1)} %pad_maximum_fusion.1), calls=%async_computation | async-start | bytes 1310720 | tf_op jit(solution)/shard_map/all_to_all | solution.py:128
  21.9 0.0 all-gather.3.cloned.1.call-start
  22.0 0.6 fusion.86
  23.3 0.7 fusion.54
  24.0 0.7 fusion.46
  24.8 0.8 fusion.82
  25.6 0.7 fusion.13
  26.3 0.7 fusion.27
  27.0 0.7 fusion.26
  27.7 0.6 convolution_add_fusion.3
  28.4 0.7 convolution_add_fusion.2
  29.1 0.7 convolution_add_fusion.1
  29.7 0.1 fusion.81
  29.9 1.1 fusion.58
  31.0 10.9 %all-to-all-done = bf16[16,80,256]{2,1,0:T(8,128)(2,1)S(1)} async-done(((bf16[16,80,256]{2,1,0:T(8,128)(2,1)}), bf16[16,80,256]{2,1,0:T(8,128)(2,1)S(1)}, u32[]{:S(2)}, u32[]{:S(2)}) %all-to-all-start) | async-done | bytes 655392 | tf_op jit(solution)/shard_map/all_to_all | solution.py:128
  42.0 0.8 fusion.29
  42.7 0.4 fusion.42
  43.2 0.5 fusion.6
  43.7 1.9 %collective-permute-start = (bf16[512,512]{1,0:T(8,128)(2,1)S(1)}, bf16[512,512]{1,0:T(8,128)(2,1)S(1)}, u32[]{:S(2)}, u32[]{:S(2)}) collective-permute-start(bf16[512,512]{1,0:T(8,128)(2,1)S(1)} %fusion.6), channel_id=1, source_target_pairs={{0,4},{4,0},{8,12},{12,8},{16,20},{20,16},{24,28},{28,24},{32,36},... | collective-permute-start | bytes 1572872 | tf_op jit(solution)/shard_map/ppermute | solution.py:152
  45.6 0.7 fusion.85
  46.3 1.5 %fusion.7 = bf16[256,512]{1,0:T(8,128)(2,1)S(1)} fusion(f32[256,512]{1,0:T(8,128)} %fusion.58, bf16[256,256]{1,0:T(8,128)(2,1)S(1)} %copy-done.7, bf16[256,256]{1,0:T(8,128)(2,1)} %copy-done.9, f32[256,256]{1,0:T(8,128)S(1)} %get-tuple-element.17, f32[256,256]{1,0:T(8,128)} %copy-done.12, f32[256,256]{1,0:T(8,128)S(1)} %get-tuple-element.8), kind=kOutput, calls=%fused_computation.16 | convolution fusion | flops 136577024 | bytes 1835008 | tf_op jit(solution)/shard_map/dot_general | solution.py:64
  47.8 0.7 fusion.84
  48.5 0.7 slice.115
  49.1 0.0 all-gather.3.cloned.1.call-update
  49.1 0.1 maximum_select_fusion
  49.3 0.1 slice_negate_fusion
  49.4 0.7 fusion
  50.1 0.1 copy-done.1
  50.2 1.4 %add_negate_fusion = (f32[256,256]{1,0:T(8,128)S(1)}, f32[256,256]{1,0:T(8,128)S(1)}) fusion(f32[512,256]{1,0:T(8,128)S(1)} %fusion, f32[]{:T(128)} %bitcast.34, f32[]{:T(128)} %bitcast.32), kind=kLoop, calls=%fused_computation.102 | loop fusion | flops 524288 | bytes 1048584 | tf_op jit(solution)/shard_map/neg | solution.py:168
  51.6 0.2 reshape.160
  51.9 0.3 fusion.57
  52.2 1.6 %fusion.8 = f32[256,256]{0,1:T(8,128)S(1)} fusion(f32[256,256]{0,1:T(8,128)S(1)} %fusion.57, f32[256,256]{1,0:T(8,128)S(1)} %get-tuple-element.19, f32[256,256]{1,0:T(8,128)S(1)} %get-tuple-element.18, f32[256,256]{1,0:T(8,128)S(1)} %get-tuple-element.17, f32[256,256]{1,0:T(8,128)S(1)} %get-tuple-element.8, bf16[256,256]{1,0:T(8,128)(2,1)S(1)} %copy-done.11, ...), kind=kOutput, calls=%fused_computation.18 | convolution fusion | flops 68550656 | bytes 1835017 | tf_op jit(solution)/shard_map/dot_general | solution.py:64
  53.8 0.1 copy.84
  53.9 0.2 reshape.161
  54.2 0.4 copy.85
  54.6 0.3 stack_reshape.7
  54.9 0.4 copy.98
  55.3 0.3 stack_reshape.6
  55.7 0.9 copy.86
  56.5 9.7 %all-to-all-start.1 = ((f32[32,2,16,128]{3,2,1,0:T(8,128)}), f32[32,2,16,128]{3,2,1,0:T(8,128)S(1)}, u32[]{:S(2)}, u32[]{:S(2)}) async-start(f32[32,2,16,128]{3,2,1,0:T(8,128)} %copy.86), calls=%async_computation.1 | async-start | bytes 1048576 | tf_op jit(solution)/shard_map/all_to_all | solution.py:186
  66.2 0.2 convert_reduce_fusion
  66.4 0.1 mul.199
  66.5 0.1 mul.200
  66.6 21.3 %all-to-all-done.1 = f32[32,2,16,128]{3,2,1,0:T(8,128)S(1)} async-done(((f32[32,2,16,128]{3,2,1,0:T(8,128)}), f32[32,2,16,128]{3,2,1,0:T(8,128)S(1)}, u32[]{:S(2)}, u32[]{:S(2)}) %all-to-all-start.1) | async-done | bytes 524320 | tf_op jit(solution)/shard_map/all_to_all | solution.py:186
  87.9 0.8 broadcast_in_dim.19
  88.7 7.1 %all-to-all-start.2 = ((f32[64,16,128]{2,1,0:T(8,128)}), f32[64,16,128]{2,1,0:T(8,128)}, u32[]{:S(2)}, u32[]{:S(2)}) async-start(f32[64,16,128]{2,1,0:T(8,128)} %broadcast_in_dim.19), calls=%async_computation.2 | async-start | bytes 1048576 | tf_op jit(solution)/shard_map/all_to_all | solution.py:191
  95.9 2.0 %fusion.34 = f32[1024,512]{1,0:T(8,128)S(1)} fusion(bf16[1024,512]{1,0:T(8,128)(2,1)} %bitcast.84, bf16[256,256]{0,1:T(8,128)(2,1)S(1)} %bitcast.98, bf16[256,256]{0,1:T(8,128)(2,1)S(1)} %get-tuple-element.5, bf16[256,256]{0,1:T(8,128)(2,1)S(1)} %bitcast.97), kind=kOutput, calls=%fused_computation.64 | convolution fusion | flops 538968064 | bytes 3538944 | tf_op jit(solution)/shard_map/dot_general | solution.py:64
  97.8 0.1 reshape.162
  97.9 0.6 copy.87
  98.5 1.3 %copy.97 = bf16[16,2,8,8,256]{4,3,2,1,0:T(8,128)(2,1)S(1)} copy(bf16[16,2,8,8,256]{4,3,1,0,2:T(8,128)(2,1)} %bitcast.93) | data formatting | bytes 2097152 | tf_op jit(solution)/shard_map/transpose | solution.py:131
  99.9 0.9 fusion.9
  100.8 0.3 fusion.12
  101.1 1.1 pad_maximum_fusion
  102.2 10.8 %all-to-all-done.2 = f32[64,16,128]{2,1,0:T(8,128)} async-done(((f32[64,16,128]{2,1,0:T(8,128)}), f32[64,16,128]{2,1,0:T(8,128)}, u32[]{:S(2)}, u32[]{:S(2)}) %all-to-all-start.2) | async-done | bytes 524320 | tf_op jit(solution)/shard_map/all_to_all | solution.py:191
  113.0 1.1 reduce_sum.39
  114.1 0.1 reshape.165
  114.3 0.7 reshape.166
  (44 shorter events, 0.5 us)
Async XLA Ops:
  7.2 42.2 %copy-start = (bf16[1,2,16,1,64,256]{5,4,3,2,1,0:T(8,128)(2,1)S(1)}, bf16[1,2,16,1,64,256]{5,4,3,2,1,0:T(8,128)(2,1)}, u32[]{:S(2)}) copy-start(bf16[1,2,16,1,64,256]{5,4,3,2,1,0:T(8,128)(2,1)} %param.19) | copy-start | bytes 3145732
  9.0 13.0 %copy-start.14 = (f32[1,2]{1,0:T(1,128)S(1)}, f32[1,2]{1,0:T(1,128)}, u32[]{:S(2)}) copy-start(f32[1,2]{1,0:T(1,128)} %param.16) | copy-start | bytes 28
  9.0 14.2 %copy-start.2 = (bf16[256,256]{1,0:T(8,128)(2,1)S(1)}, bf16[256,256]{1,0:T(8,128)(2,1)}, u32[]{:S(2)}) copy-start(bf16[256,256]{1,0:T(8,128)(2,1)} %param.13) | copy-start | bytes 393220
  9.0 14.3 %copy-start.3 = (bf16[256,256]{1,0:T(8,128)(2,1)S(1)}, bf16[256,256]{1,0:T(8,128)(2,1)}, u32[]{:S(2)}) copy-start(bf16[256,256]{1,0:T(8,128)(2,1)} %param.12) | copy-start | bytes 393220
  9.1 14.9 %copy-start.4 = (bf16[256,256]{1,0:T(8,128)(2,1)S(1)}, bf16[256,256]{1,0:T(8,128)(2,1)}, u32[]{:S(2)}) copy-start(bf16[256,256]{1,0:T(8,128)(2,1)} %param.15) | copy-start | bytes 393220
  9.1 14.9 %copy-start.5 = (bf16[256,256]{1,0:T(8,128)(2,1)S(1)}, bf16[256,256]{1,0:T(8,128)(2,1)}, u32[]{:S(2)}) copy-start(bf16[256,256]{1,0:T(8,128)(2,1)} %param.14) | copy-start | bytes 393220
  10.0 31.9 %all-to-all-start = ((bf16[16,80,256]{2,1,0:T(8,128)(2,1)}), bf16[16,80,256]{2,1,0:T(8,128)(2,1)S(1)}, u32[]{:S(2)}, u32[]{:S(2)}) async-start(bf16[16,80,256]{2,1,0:T(8,128)(2,1)} %pad_maximum_fusion.1), calls=%async_computation | async-start | bytes 1310720 | tf_op jit(solution)/shard_map/all_to_all | solution.py:128
  21.9 76.6 %all-gather.3.cloned.1.call-start = ((), (), s32[]{:S(2)}) async-start(), calls=%async_computation.3 | async-start | bytes 1179648 | tf_op jit(solution)/shard_map/all_gather | solution.py:130
  23.3 6.6 %copy-start.6 = (bf16[256,256]{1,0:T(8,128)(2,1)}, bf16[256,256]{1,0:T(8,128)(2,1)S(1)}, u32[]{:S(2)}) copy-start(bf16[256,256]{1,0:T(8,128)(2,1)S(1)} %get-tuple-element.6) | copy-start | bytes 393220
  24.0 5.8 %copy-start.9 = (bf16[256,256]{1,0:T(8,128)(2,1)}, bf16[256,256]{1,0:T(8,128)(2,1)S(1)}, u32[]{:S(2)}) copy-start(bf16[256,256]{1,0:T(8,128)(2,1)S(1)} %fusion.54) | copy-start | bytes 393220
  29.9 13.3 %copy-start.12 = (f32[256,256]{1,0:T(8,128)}, f32[256,256]{1,0:T(8,128)S(1)}, u32[]{:S(2)}) copy-start(f32[256,256]{1,0:T(8,128)S(1)} %get-tuple-element.7) | copy-start | bytes 786436
  43.2 2.4 %copy-start.15 = (f32[1,2]{1,0:T(1,128)S(1)}, f32[1,2]{1,0:T(1,128)}, u32[]{:S(2)}) copy-start(f32[1,2]{1,0:T(1,128)} %param.17) | copy-start | bytes 28
  43.2 3.1 %copy-start.7 = (bf16[256,256]{1,0:T(8,128)(2,1)S(1)}, bf16[256,256]{1,0:T(8,128)(2,1)}, u32[]{:S(2)}) copy-start(bf16[256,256]{1,0:T(8,128)(2,1)} %copy-done.6) | copy-start | bytes 393220
  43.7 5.5 %collective-permute-start = (bf16[512,512]{1,0:T(8,128)(2,1)S(1)}, bf16[512,512]{1,0:T(8,128)(2,1)S(1)}, u32[]{:S(2)}, u32[]{:S(2)}) collective-permute-start(bf16[512,512]{1,0:T(8,128)(2,1)S(1)} %fusion.6), channel_id=1, source_target_pairs={{0,4},{4,0},{8,12},{12,8},{16,20},{20,16},{24,28},{28,24},{32,36},... | collective-permute-start | bytes 1572872 | tf_op jit(solution)/shard_map/ppermute | solution.py:152
  49.2 1.0 copy-start.1
  49.4 2.5 %copy-start.11 = (bf16[256,256]{1,0:T(8,128)(2,1)S(1)}, bf16[256,256]{1,0:T(8,128)(2,1)}, u32[]{:S(2)}) copy-start(bf16[256,256]{1,0:T(8,128)(2,1)} %get-tuple-element.30) | copy-start | bytes 393220
  55.3 10.9 %copy-start.13 = (s32[16,16]{1,0:T(8,128)S(1)}, s32[16,16]{1,0:T(8,128)}, u32[]{:S(2)}) copy-start(s32[16,16]{1,0:T(8,128)} %param.18) | copy-start | bytes 3076
  55.7 40.2 %copy-start.8 = (bf16[256,256]{1,0:T(8,128)(2,1)S(1)}, bf16[256,256]{1,0:T(8,128)(2,1)}, u32[]{:S(2)}) copy-start(bf16[256,256]{1,0:T(8,128)(2,1)} %copy-done.6) | copy-start | bytes 393220
  55.7 40.2 %copy-start.10 = (bf16[256,256]{1,0:T(8,128)(2,1)S(1)}, bf16[256,256]{1,0:T(8,128)(2,1)}, u32[]{:S(2)}) copy-start(bf16[256,256]{1,0:T(8,128)(2,1)} %copy-done.9) | copy-start | bytes 393220
  56.5 31.3 %all-to-all-start.1 = ((f32[32,2,16,128]{3,2,1,0:T(8,128)}), f32[32,2,16,128]{3,2,1,0:T(8,128)S(1)}, u32[]{:S(2)}, u32[]{:S(2)}) async-start(f32[32,2,16,128]{3,2,1,0:T(8,128)} %copy.86), calls=%async_computation.1 | async-start | bytes 1048576 | tf_op jit(solution)/shard_map/all_to_all | solution.py:186
  88.7 24.3 %all-to-all-start.2 = ((f32[64,16,128]{2,1,0:T(8,128)}), f32[64,16,128]{2,1,0:T(8,128)}, u32[]{:S(2)}, u32[]{:S(2)}) async-start(f32[64,16,128]{2,1,0:T(8,128)} %broadcast_in_dim.19), calls=%async_computation.2 | async-start | bytes 1048576 | tf_op jit(solution)/shard_map/all_to_all | solution.py:191
Sparse Core Ops, SparseCore 0:
  49.3 38.8 all-gather.2

commit v3 on v0

v3 whole, which is shorter than its diff:
```python
import functools

import jax
import jax.numpy as jnp
from jax import lax
from jax.experimental import pallas as pl
from jax.experimental.pallas import tpu as pltpu
from jax.sharding import PartitionSpec as P

bf16 = jnp.bfloat16
f32 = jnp.float32
VMEM = pl.BlockSpec(memory_space=pltpu.VMEM)
SMEM = pl.BlockSpec(memory_space=pltpu.SMEM)


def call(body, outs, ins, flops, name):
    moved = sum(x.size * x.dtype.itemsize for x in list(ins) + list(outs))
    return pl.pallas_call(
        body,
        out_shape=outs,
        in_specs=[SMEM if x.size <= 256 else VMEM for x in ins],
        out_specs=[VMEM] * len(outs),
        compiler_params=pltpu.CompilerParams(vmem_limit_bytes=40 * 2**20),
        cost_estimate=pl.CostEstimate(flops=flops, bytes_accessed=moved, transcendentals=0),
        name=name,
    )(*ins)


def shape(*dims, dtype=bf16):
    return jax.ShapeDtypeStruct(dims, dtype)


def dot(left, right):
    return jnp.dot(left, right, preferred_element_type=f32)


def contract(left, right, axis_left, axis_right):
    dims = (((axis_left,), (axis_right,)), ((), ()))
    return lax.dot_general(left, right, dims, preferred_element_type=f32)


def split(value):
    high = value.astype(bf16)
    return high, (value - high.astype(f32)).astype(bf16)


def product(left, right):
    return dot(left[0], right[0]) + (dot(left[0], right[1]) + dot(left[1], right[0]))


def block(wide):
    size = wide.shape[1] // 2
    real, imag = wide[:, :size], wide[:, size:]
    return jnp.concatenate([wide, jnp.concatenate([-imag, real], axis=1)], axis=0)


def both_of(pair, form):
    return form(pair[0]), form(pair[1])


def couple(rows_h, rows_s, shift_real, shift_imag):
    margin = rows_s.astype(f32)
    real = (rows_h.astype(f32) - shift_real * margin).astype(bf16)
    imag = (-shift_imag * margin).astype(bf16)
    return real, imag


def invert_body(
    shift, weight, pivot_h, pivot_s, panel_h, panel_s, inverse, right, wide, base
):
    size = pivot_h.shape[0]
    shift_real, shift_imag = shift[0, 0], shift[0, 1]
    margin = pivot_s[...].astype(f32)
    real = pivot_h[...].astype(f32) - shift_real * margin
    imag = -shift_imag * margin
    on_diag = lax.broadcasted_iota(jnp.int32, (size, size), 0) == lax.broadcasted_iota(
        jnp.int32, (size, size), 1
    )

    def scales(axis):
        diag_real = jnp.sum(jnp.where(on_diag, real, 0.0), axis=axis, keepdims=True)
        diag_imag = jnp.sum(jnp.where(on_diag, imag, 0.0), axis=axis, keepdims=True)
        denom = diag_real * diag_real + diag_imag * diag_imag
        return diag_real / denom, -diag_imag / denom

    col_real, col_imag = scales(0)
    err_real = jnp.where(on_diag, 0.0, imag * col_imag - real * col_real)
    err_imag = jnp.where(on_diag, 0.0, -(real * col_imag + imag * col_real))
    one = jnp.concatenate([jnp.where(on_diag, 1.0, 0.0), jnp.zeros((size, size), f32)], axis=1)
    err = jnp.concatenate([err_real, err_imag], axis=1)
    err_pair = split(err)
    err2 = product(err_pair, both_of(err_pair, block))
    err2_pair = split(err2)
    square = both_of(err2_pair, block)
    err3 = product(err_pair, square)
    err4_pair = split(product(err2_pair, square))
    first = one + err + err2 + err3
    fourth = both_of(err4_pair, block)
    second = first + product(split(first), fourth)
    err8_pair = split(product(err4_pair, fourth))
    total = second + product(split(second), both_of(err8_pair, block))
    sum_real, sum_imag = total[:, :size], total[:, size:]
    row_real, row_imag = scales(1)
    inv_real = row_real * sum_real - row_imag * sum_imag
    inv_imag = row_real * sum_imag + row_imag * sum_real
    inv_pair = both_of(split(jnp.concatenate([inv_real, inv_imag], axis=1)), block)
    inverse[0] = inv_pair[0]
    inverse[1] = inv_pair[1]
    first_device = (lax.axis_index("row") == 0) & (lax.axis_index("col") == 0)
    density = weight[0, 0] * inv_imag + weight[0, 1] * inv_real
    base[...] = jnp.where(first_device, density.T, 0.0)
    coupling_real, coupling_imag = couple(panel_h[...], panel_s[...], shift_real, shift_imag)
    coupling = jnp.concatenate([coupling_real, coupling_imag], axis=1)
    solved = (dot(coupling, inv_pair[0]) + dot(coupling, inv_pair[1])).astype(bf16)
    right[:size] = solved[:, :size]
    right[size:] = solved[:, size:]
    wide[:size] = jnp.concatenate([coupling_real, -coupling_imag], axis=1)
    wide[size:] = jnp.concatenate([coupling_imag, coupling_real], axis=1)


def solve_body(shift, received, inverse, solved):
    strips, twice, size = received.shape
    half = twice // 2
    rows_h = received[:, :half].reshape(strips * half, size)
    rows_s = received[:, half:].reshape(strips * half, size)
    coupling = jnp.concatenate(couple(rows_h, rows_s, shift[0, 0], shift[0, 1]), axis=1)
    solved[...] = (dot(coupling, inverse[0]) + dot(coupling, inverse[1])).astype(bf16)


def ordered(mine, other):
    low = lax.rem(lax.axis_index("row"), 2) == 0
    return jnp.where(low, mine, other), jnp.where(low, other, mine)


def fold(member, out, at):
    pieces = out.shape[0]
    half = out.shape[1] // 2
    cols = 2 * member.shape[1] // 128
    low_lane = lax.broadcasted_iota(jnp.int32, (half, 128), 1) < 64
    for pole in range(pieces // cols):
        for pair in range(cols // 2):
            rows = pole * 2 * half
            top = member[rows : rows + half, pair * 128 : pair * 128 + 128]
            bottom = member[rows + half : rows + 2 * half, pair * 128 : pair * 128 + 128]
            even = jnp.where(low_lane, top, pltpu.roll(bottom, 64, 1))
            odd = jnp.where(low_lane, pltpu.roll(top, 64, 1), bottom)
            out[pole * cols + 2 * pair, at : at + half] = even
            out[pole * cols + 2 * pair + 1, at : at + half] = odd


def column_body(weight, mine, other, ancestor, right, base, out, far):
    strips, half = ancestor.shape[1], ancestor.shape[2] // 2
    size = ancestor.shape[3]
    wide = mine.shape[1]
    top, bottom = ordered(mine[...], other[...])
    far[:, :half] = top.reshape(strips, half, wide)
    far[:, half:] = bottom.reshape(strips, half, wide)
    rows = far[...].reshape(strips * 2 * half, wide)
    by_real = contract(rows, ancestor[0].reshape(strips * 2 * half, size), 0, 0)
    by_imag = contract(rows, ancestor[1].reshape(strips * 2 * half, size), 0, 0)
    part_real = by_real[:size] - by_imag[size:]
    part_imag = by_real[size:] + by_imag[:size]
    weight_real, weight_imag = weight[0, 0], weight[0, 1]
    density = -(weight_real * part_imag + weight_imag * part_real)
    twin = -(weight_real * part_real - weight_imag * part_imag)
    high, low = split(jnp.concatenate([density, twin], axis=1))
    pivot = base[...] - (dot(high, right[...]) + dot(low, right[...]))
    fold(density, out, 0)
    fold(pivot, out, out.shape[1] // 2)


def strips_body(front_h, front_s, kept, given):
    size = kept.shape[3]
    core = lax.rem(lax.axis_index("row"), 2)
    for chip in range(kept.shape[0]):
        own = pl.ds(pl.multiple_of((2 * chip + core) * size, size), size)
        far = pl.ds(pl.multiple_of((2 * chip + 1 - core) * size, size), size)
        kept[chip, 0] = front_h[:, own]
        kept[chip, 1] = front_s[:, own]
        given[chip, 0] = front_h[:, far]
        given[chip, 1] = front_s[:, far]


def blocks_body(kept, swapped, *outs):
    chips = kept.shape[0]
    chip = lax.rem(lax.axis_index("row"), 2 * chips) // 2
    for step, out in enumerate(outs):
        to = lax.rem(chip + step, chips)
        low, high = ordered(kept[to], swapped[to])
        out[0] = low
        out[1] = high


def schur_body(shift, pattern, mine, other, wide, *refs):
    blocks, out = refs[:-1], refs[-1]
    chips = len(blocks)
    half = blocks[0].shape[2] // 2
    size = blocks[0].shape[3]
    shift_real, shift_imag = shift[0, 0], shift[0, 1]
    row = lax.axis_index("row")
    for step, tiles in enumerate(blocks):
        chip = lax.rem(row // 2 + chips - step, chips)
        at = pl.ds(pl.multiple_of(chip * 2 * half, 2 * half), 2 * half)
        low, high = ordered(mine[at, :], other[at, :])
        solved = jnp.concatenate([low[:half], high[:half], low[half:], high[half:]], axis=0)
        update = contract(solved, wide[...], 1, 1)
        for core in range(2):
            strip = 2 * chip + core
            mask = pattern[strip, row].astype(f32)
            rows = slice(core * 2 * half, (core + 1) * 2 * half)
            margin = mask * tiles[core, 1].astype(f32)
            real = mask * tiles[core, 0].astype(f32) - shift_real * margin
            out[0, strip] = (real - update[rows, :size]).astype(bf16)
            out[1, strip] = (-shift_imag * margin - update[rows, size:]).astype(bf16)


def unfold(member, width, piece):
    times = 128 // width
    member = member.reshape(-1, piece // times, times, width)
    return member.transpose(2, 1, 0, 3).reshape(piece, -1)


def shards(
    front_h,
    front_s,
    panel_h,
    panel_s,
    pivot_h,
    pivot_s,
    pole_shift,
    pole_weight,
    pattern,
    ancestor_inverse,
):
    row_count = lax.axis_size("row")
    col_count = lax.axis_size("col")
    pole_count = lax.axis_size("pole")
    col_index = lax.axis_index("col")
    size = pivot_h.shape[0]
    width = size // col_count
    piece = size // pole_count
    half = width // 2
    chips = row_count // 2
    neighbour = [(i, i ^ 1) for i in range(row_count)]

    strip = lax.dynamic_slice_in_dim(jnp.stack([panel_h, panel_s]), col_index * width, width, axis=1)
    strip = strip.reshape(2, 2, half, size).transpose(1, 0, 2, 3)
    sent = jnp.broadcast_to(strip[None], (chips, 2, 2, half, size))
    sent = sent.reshape(row_count, 2 * half, size)
    received = lax.all_to_all(sent, "row", split_axis=0, concat_axis=0, tiled=True)

    kept, given = call(
        strips_body,
        [shape(chips, 2, width, size)] * 2,
        [front_h, front_s],
        0,
        "front_strips",
    )
    swapped = lax.ppermute(given, "row", neighbour)

    inverse, right, wide, base = call(
        invert_body,
        [
            shape(2, 2 * size, 2 * size),
            shape(2 * size, size),
            shape(2 * size, 2 * size),
            shape(size, size, dtype=f32),
        ],
        [pole_shift, pole_weight, pivot_h, pivot_s, panel_h, panel_s],
        6 * 4 * 3 * 2 * size**3,
        "pivot_inverse",
    )
    (mine,) = call(
        solve_body,
        [shape(row_count * half, 2 * size)],
        [pole_shift, received, inverse],
        2 * 8 * row_count * half * size * size,
        "solved_rows",
    )
    other = lax.ppermute(mine, "row", neighbour)

    ancestor = ancestor_inverse.reshape(2, row_count, width, size)
    (both,) = pl.pallas_call(
        column_body,
        out_shape=[shape(pole_count * col_count, piece, 128, dtype=f32)],
        in_specs=[SMEM] + [VMEM] * 5,
        out_specs=[VMEM],
        scratch_shapes=[pltpu.VMEM((row_count, width, 2 * size), bf16)],
        compiler_params=pltpu.CompilerParams(vmem_limit_bytes=40 * 2**20),
        cost_estimate=pl.CostEstimate(
            flops=8 * row_count * width * size * size, bytes_accessed=4 * 2**20, transcendentals=0
        ),
        name="column",
    )(pole_weight, mine, other, ancestor, right, base)

    kept, swapped, both = lax.optimization_barrier((kept, swapped, both))
    blocks = call(
        blocks_body,
        [shape(2, 2, width, size)] * chips,
        [kept, swapped],
        0,
        "front_blocks",
    )
    arrived = list(blocks[:1]) + [
        lax.ppermute(
            blocks[step], "row", [(i, (i + 2 * step) % row_count) for i in range(row_count)]
        )
        for step in range(1, chips)
    ]

    both = lax.all_to_all(both, ("pole", "col"), split_axis=0, concat_axis=0, tiled=True)
    both = jnp.sum(both, axis=0).reshape(2, piece // 2, 128)
    rows_out = unfold(both[:1], width, piece).T

    spread = jnp.broadcast_to(both[1][None], (row_count * col_count,) + both.shape[1:])
    spread = lax.all_to_all(spread, ("row", "col"), split_axis=0, concat_axis=0, tiled=True)
    spread = jnp.sum(spread.reshape((row_count, col_count) + both.shape[1:]), axis=0)
    pivot_out = unfold(spread, width, piece).T

    (schur,) = call(
        schur_body,
        [shape(2, row_count, width, size)],
        [pole_shift, pattern, mine, other, wide, *arrived],
        8 * row_count * width * size * size,
        "schur",
    )
    return (schur.reshape(1, 2, row_count, 1, width, size), rows_out, pivot_out)


def solution(mesh):
    in_specs = (
        P(("row", "col"), None),
        P(("row", "col"), None),
        P("row", None),
        P("row", None),
        P(),
        P(),
        P("pole", None),
        P("pole", None),
        P(),
        P("pole", None, None, "col", None, "row"),
    )
    out_specs = (
        P("pole", None, None, "col", None, "row"),
        P(("row", "col"), "pole"),
        P(None, "pole"),
    )
    return jax.shard_map(shards, mesh=mesh, in_specs=in_specs, out_specs=out_specs, check_vma=False)
```

time: 435 us -> 120 us (0.28)
  waiting for transfers between devices: 333 us -> 24.6 us
  starting transfers between devices: 19.4 us -> 51.7 us
  blocking collectives: 0 us -> 26.3 us
  matrix products: 24.5 us -> 0 us
  local copies, waits for them, and re-layouts: 27.7 us -> 3.28 us
  between operations: 15.4 us -> 0.92 us
  Pallas kernels: 0 us -> 10.7 us
  other arithmetic: 10.8 us -> 1.91 us
    psum x2 -> x0, waiting for transfers between devices: 262 us -> none  [the longest x1 192 us: shards(): correction = lax.psum(jnp.stack([corr_real, corr_imag]), ('row', 'col'))]
    unnamed x5 -> x0, waiting for transfers between devices: 48.2 us -> none
    ppermute x0 -> x9, starting transfers between devices: none -> 32.7 us  [the longest x7 28.3 us: shards(): lax.ppermute(blocks[step], 'row', [(i, (i + 2 * step) % row_count) for i...]
    all_to_all x0 -> x1, blocking collectives: none -> 26.3 us  [shards(): lax.all_to_all(both, ('pole', 'col'), split_axis=0, concat_axis=0, tiled=...]
    dot_general x48 -> x0, matrix products: 24.5 us -> none  [the longest x9 4.36 us: complex_matmul(): jnp.dot(left_imag, right_imag, precision=highest, preferred_element_type=...]
    all_gather x1 -> x0, waiting for transfers between devices: 16.8 us -> none  [shards(): far_solved = lax.all_gather(solved_strip, 'row', axis=1, tiled=True)]
    ppermute x0 -> x9, waiting for transfers between devices: none -> 11.6 us  [the longest x7 11.6 us: shards(): lax.ppermute(blocks[step], 'row', [(i, (i + 2 * step) % row_count) for i...]
    pallas_call x0 -> x6, Pallas kernels: none -> 10.7 us  [the longest x5 8.89 us: call(): pl.pallas_call(body, out_shape=outs, in_specs=[SMEM if x.size <= 256 else...]
  transfers between devices with their start and end apart: 6 -> 11, of which waited for: 5 -> 5; matrix products, arithmetic and copies ran while one was open for 10% -> 1% of each run, Pallas kernels for 0% -> 8%
where the time goes in v3:
time: 120 us; the launch traced here: 119 us
  starting transfers between devices  51.7 us (43%)
  blocking collectives  26.3 us (22%)
  waiting for transfers between devices  24.6 us (20%)
  Pallas kernels  10.7 us (9%)
  local copies, waits for them, and re-layouts  3.28 us (3%)
  other arithmetic  1.91 us (2%)
    ppermute x7, starting transfers between devices, shards(): lax.ppermute(blocks[step], 'row', [(i, (i + 2 * step) % row_count) for i...  28.3 us
    all_to_all x1, blocking collectives, shards(): lax.all_to_all(both, ('pole', 'col'), split_axis=0, concat_axis=0, tiled=...  26.3 us
    all_to_all x1, waiting for transfers between devices, shards(): lax.all_to_all(sent, 'row', split_axis=0, concat_axis=0, tiled=True)  13 us
    all_to_all x1, starting transfers between devices, shards(): lax.all_to_all(sent, 'row', split_axis=0, concat_axis=0, tiled=True)  12 us
    ppermute x7, waiting for transfers between devices, shards(): lax.ppermute(blocks[step], 'row', [(i, (i + 2 * step) % row_count) for i...  11.6 us
    pallas_call x5, Pallas kernels, call(): pl.pallas_call(body, out_shape=outs, in_specs=[SMEM if x.size <= 256 else...  8.89 us
    all_to_all x1, starting transfers between devices, shards(): lax.all_to_all(spread, ('row', 'col'), split_axis=0, concat_axis=0, tiled...  6.96 us
    ppermute x1, starting transfers between devices, shards(): swapped = lax.ppermute(given, 'row', neighbour)  2.41 us
  transfers between devices with their start and end apart: 11, of which 5 were waited for; matrix products, arithmetic and copies ran while one was open for 1% of the time, Pallas kernels for 8%

profile of v3, /device:TPU:1, one launch (start us, length us, event | category | flops | bytes accessed | tf_op | source)
XLA Modules:
  0.0 119.4 jit_solution(15755463197407504816)
XLA Ops:
  0.6 0.8 fusion
  1.4 0.9 broadcast_in_dim.4
  2.3 0.0 copy-start.3
  2.3 0.0 copy-start.4
  2.3 0.0 copy-start.6
  2.3 0.0 copy-start.7
  2.3 0.0 copy-start.8
  2.3 0.0 copy-start.9
  2.3 12.0 %all-to-all-start = ((bf16[16,64,256]{2,1,0:T(8,128)(2,1)}), bf16[16,64,256]{2,1,0:T(8,128)(2,1)S(1)}, u32[]{:S(2)}, u32[]{:S(2)}) async-start(bf16[16,64,256]{2,1,0:T(8,128)(2,1)} %bitcast.4), calls=%async_computation | async-start | bytes 1048576 | tf_op jit(solution)/shard_map/all_to_all | solution.py:250
  14.3 0.0 copy-done.3
  14.3 0.0 copy-done.4
  14.3 0.0 copy-done.6
  14.3 0.0 copy-done.7
  14.3 0.0 copy-done.8
  14.3 0.0 copy-done.9
  14.3 4.2 %pivot_inverse.1 = (bf16[2,512,512]{2,1,0:T(8,128)(2,1)S(1)}, bf16[512,256]{1,0:T(8,128)(2,1)S(1)}, bf16[512,512]{1,0:T(8,128)(2,1)S(1)}, f32[256,256]{1,0:T(8,128)S(1)}) custom-call(f32[1,2]{1,0:T(1,128)S(1)} %copy-done.6, f32[1,2]{1,0:T(1,128)S(1)} %copy-done.7, bf16[256,256]{1,0:T(8,128)(2,1)S(1)} %copy-done.8, bf16[256,256]{1,0:T(8,128)(2,1)S(1)} %copy-done.9, ...), custom_call_target="tpu_custom_call" | custom-call | flops 2415919104 | bytes 2621456 | tf_op jit(solution)/shard_map/pivot_inverse/pallas_call | solution.py:18
  18.6 13.0 %all-to-all-done.received = bf16[16,64,256]{2,1,0:T(8,128)(2,1)S(1)} async-done(((bf16[16,64,256]{2,1,0:T(8,128)(2,1)}), bf16[16,64,256]{2,1,0:T(8,128)(2,1)S(1)}, u32[]{:S(2)}, u32[]{:S(2)}) %all-to-all-start) | async-done | bytes 524320 | tf_op jit(solution)/shard_map/all_to_all | solution.py:250
  31.6 0.0 copy-start.1
  31.6 0.0 copy-start.2
  31.6 1.3 %solved_rows.1.mine = bf16[512,512]{1,0:T(8,128)(2,1)S(1)} custom-call(f32[1,2]{1,0:T(1,128)S(1)} %copy-done.6, bf16[16,64,256]{2,1,0:T(8,128)(2,1)S(1)} %all-to-all-done.received, bf16[2,512,512]{2,1,0:T(8,128)(2,1)S(1)} %get-tuple-element.20.inverse), custom_call_target="tpu_custom_call" | custom-call | flops 536870912 | bytes 2097160 | tf_op jit(solution)/shard_map/solved_rows/pallas_call | solution.py:18
  32.9 0.0 copy-start
  32.9 2.1 %collective-permute-start = (bf16[512,512]{1,0:T(8,128)(2,1)S(1)}, bf16[512,512]{1,0:T(8,128)(2,1)S(1)}, u32[]{:S(2)}, u32[]{:S(2)}) collective-permute-start(bf16[512,512]{1,0:T(8,128)(2,1)S(1)} %solved_rows.1.mine), channel_id=1, source_target_pairs={{0,4},{4,0},{8,12},{12,8},{16,20},{20,16},{24,28},{28,24},{32,36},... | collective-permute-start | bytes 1572872 | tf_op jit(solution)/shard_map/ppermute | solution.py:280
  34.9 0.0 copy-done.1
  35.0 0.0 copy-done.2
  35.0 0.2 front_strips.1
  35.1 2.4 %collective-permute-start.1 = (bf16[8,2,64,256]{3,2,1,0:T(8,128)(2,1)S(1)}, bf16[8,2,64,256]{3,2,1,0:T(8,128)(2,1)S(1)}, u32[]{:S(2)}, u32[]{:S(2)}) collective-permute-start(bf16[8,2,64,256]{3,2,1,0:T(8,128)(2,1)S(1)} %get-tuple-element.23), channel_id=1, source_target_pairs={{0,4},{4,0},{8,12},{12,8},{16,20},{20,16},{24,28},{28,24},{32,36},... | collective-permute-start | bytes 1572872 | tf_op jit(solution)/shard_map/ppermute | solution.py:259
  37.5 0.0 collective-permute-done.other
  37.5 0.0 copy-done
  37.6 1.8 %column.1 = f32[32,32,128]{2,1,0:T(8,128)S(1)} custom-call(f32[1,2]{1,0:T(1,128)S(1)} %copy-done.7, bf16[512,512]{1,0:T(8,128)(2,1)S(1)} %solved_rows.1.mine, bf16[512,512]{1,0:T(8,128)(2,1)S(1)} %collective-permute-done.other, bf16[2,16,64,256]{3,2,1,0:T(8,128)(2,1)S(1)} %bitcast.17, bf16[512,256]{1,0:T(8,128)(2,1)S(1)} %get-tuple-element.24.right, ...), custom_call_target="tpu_custom_call" | custom-call | flops 536870912 | bytes 4194304 | tf_op jit(solution)/shard_map/column/pallas_call | solution.py:283
  39.4 0.0 collective-permute-done.1.swapped
  39.4 26.3 %all_to_all.15 = f32[32,32,128]{2,1,0:T(8,128)S(1)} all-to-all(f32[32,32,128]{2,1,0:T(8,128)S(1)} %column.1), channel_id=1, replica_groups=mesh['pole'=8,'row'=16,'col'=4] {'pole','col'}, dimensions={0} | all-to-all | bytes 1048576 | tf_op jit(solution)/shard_map/all_to_all | solution.py:311
  65.8 0.8 broadcast_in_dim.5
  66.6 7.0 %all-to-all-start.2 = ((f32[64,16,128]{2,1,0:T(8,128)}), f32[64,16,128]{2,1,0:T(8,128)}, u32[]{:S(2)}, u32[]{:S(2)}) async-start(f32[64,16,128]{2,1,0:T(8,128)} %broadcast_in_dim.5), calls=%async_computation.2 | async-start | bytes 1048576 | tf_op jit(solution)/shard_map/all_to_all | solution.py:316
  73.5 0.1 front_blocks.1
  73.6 0.0 copy-start.5
  73.7 3.3 %collective-permute-start.2 = (bf16[2,2,64,256]{3,2,1,0:T(8,128)(2,1)S(1)}, bf16[2,2,64,256]{3,2,1,0:T(8,128)(2,1)S(1)}, u32[]{:S(2)}, u32[]{:S(2)}) collective-permute-start(bf16[2,2,64,256]{3,2,1,0:T(8,128)(2,1)S(1)} %get-tuple-element.29), channel_id=1, source_target_pairs={{0,8},{4,12},{8,16},{12,20},{16,24},{20,28},{24,32},{28,36},{32,40... | collective-permute-start | bytes 393224 | tf_op jit(solution)/shard_map/ppermute | solution.py:305
  77.0 4.0 %collective-permute-start.3 = (bf16[2,2,64,256]{3,2,1,0:T(8,128)(2,1)S(1)}, bf16[2,2,64,256]{3,2,1,0:T(8,128)(2,1)S(1)}, u32[]{:S(2)}, u32[]{:S(2)}) collective-permute-start(bf16[2,2,64,256]{3,2,1,0:T(8,128)(2,1)S(1)} %get-tuple-element.30), channel_id=1, source_target_pairs={{0,16},{4,20},{8,24},{12,28},{16,32},{20,36},{24,40},{28,44},{32,4... | collective-permute-start | bytes 393224 | tf_op jit(solution)/shard_map/ppermute | solution.py:305
  81.0 4.5 %collective-permute-start.4 = (bf16[2,2,64,256]{3,2,1,0:T(8,128)(2,1)S(1)}, bf16[2,2,64,256]{3,2,1,0:T(8,128)(2,1)S(1)}, u32[]{:S(2)}, u32[]{:S(2)}) collective-permute-start(bf16[2,2,64,256]{3,2,1,0:T(8,128)(2,1)S(1)} %get-tuple-element.31), channel_id=1, source_target_pairs={{0,24},{4,28},{8,32},{12,36},{16,40},{20,44},{24,48},{28,52},{32,5... | collective-permute-start | bytes 393224 | tf_op jit(solution)/shard_map/ppermute | solution.py:305
  85.5 3.8 %collective-permute-start.5 = (bf16[2,2,64,256]{3,2,1,0:T(8,128)(2,1)S(1)}, bf16[2,2,64,256]{3,2,1,0:T(8,128)(2,1)S(1)}, u32[]{:S(2)}, u32[]{:S(2)}) collective-permute-start(bf16[2,2,64,256]{3,2,1,0:T(8,128)(2,1)S(1)} %get-tuple-element.32), channel_id=1, source_target_pairs={{0,32},{4,36},{8,40},{12,44},{16,48},{20,52},{24,56},{28,60},{32,0... | collective-permute-start | bytes 393224 | tf_op jit(solution)/shard_map/ppermute | solution.py:305
  89.3 4.6 %collective-permute-start.6 = (bf16[2,2,64,256]{3,2,1,0:T(8,128)(2,1)S(1)}, bf16[2,2,64,256]{3,2,1,0:T(8,128)(2,1)S(1)}, u32[]{:S(2)}, u32[]{:S(2)}) collective-permute-start(bf16[2,2,64,256]{3,2,1,0:T(8,128)(2,1)S(1)} %get-tuple-element.33), channel_id=1, source_target_pairs={{0,40},{4,44},{8,48},{12,52},{16,56},{20,60},{24,0},{28,4},{32,8},... | collective-permute-start | bytes 393224 | tf_op jit(solution)/shard_map/ppermute | solution.py:305
  93.8 0.0 collective-permute-done.2.refs_1_
  93.9 5.1 %collective-permute-start.7 = (bf16[2,2,64,256]{3,2,1,0:T(8,128)(2,1)S(1)}, bf16[2,2,64,256]{3,2,1,0:T(8,128)(2,1)S(1)}, u32[]{:S(2)}, u32[]{:S(2)}) collective-permute-start(bf16[2,2,64,256]{3,2,1,0:T(8,128)(2,1)S(1)} %get-tuple-element.34), channel_id=1, source_target_pairs={{0,48},{4,52},{8,56},{12,60},{16,0},{20,4},{24,8},{28,12},{32,16},... | collective-permute-start | bytes 393224 | tf_op jit(solution)/shard_map/ppermute | solution.py:305
  98.9 0.0 collective-permute-done.3.refs_2_
  99.0 3.0 %collective-permute-start.8 = (bf16[2,2,64,256]{3,2,1,0:T(8,128)(2,1)S(1)}, bf16[2,2,64,256]{3,2,1,0:T(8,128)(2,1)S(1)}, u32[]{:S(2)}, u32[]{:S(2)}) collective-permute-start(bf16[2,2,64,256]{3,2,1,0:T(8,128)(2,1)S(1)} %get-tuple-element.35), channel_id=1, source_target_pairs={{0,56},{4,60},{8,0},{12,4},{16,8},{20,12},{24,16},{28,20},{32,24},... | collective-permute-start | bytes 393224 | tf_op jit(solution)/shard_map/ppermute | solution.py:305
  102.0 5.1 %collective-permute-done.4.refs_3_ = bf16[2,2,64,256]{3,2,1,0:T(8,128)(2,1)S(1)} collective-permute-done((bf16[2,2,64,256]{3,2,1,0:T(8,128)(2,1)S(1)}, bf16[2,2,64,256]{3,2,1,0:T(8,128)(2,1)S(1)}, u32[]{:S(2)}, u32[]{:S(2)}) %collective-permute-start.4) | collective-permute-done | bytes 131104 | tf_op jit(solution)/shard_map/ppermute | solution.py:305
  107.1 4.2 %collective-permute-done.5.refs_4_ = bf16[2,2,64,256]{3,2,1,0:T(8,128)(2,1)S(1)} collective-permute-done((bf16[2,2,64,256]{3,2,1,0:T(8,128)(2,1)S(1)}, bf16[2,2,64,256]{3,2,1,0:T(8,128)(2,1)S(1)}, u32[]{:S(2)}, u32[]{:S(2)}) %collective-permute-start.5) | collective-permute-done | bytes 131104 | tf_op jit(solution)/shard_map/ppermute | solution.py:305
  111.3 0.0 collective-permute-done.6.refs_5_
  111.3 1.9 %collective-permute-done.7.refs_6_ = bf16[2,2,64,256]{3,2,1,0:T(8,128)(2,1)S(1)} collective-permute-done((bf16[2,2,64,256]{3,2,1,0:T(8,128)(2,1)S(1)}, bf16[2,2,64,256]{3,2,1,0:T(8,128)(2,1)S(1)}, u32[]{:S(2)}, u32[]{:S(2)}) %collective-permute-start.7) | collective-permute-done | bytes 131104 | tf_op jit(solution)/shard_map/ppermute | solution.py:305
  113.2 0.4 collective-permute-done.8.refs_7_
  113.6 0.0 copy-done.5
  113.6 3.2 %schur.1 = bf16[2,16,64,256]{3,2,1,0:T(8,128)(2,1)} custom-call(f32[1,2]{1,0:T(1,128)S(1)} %copy-done.6, s32[16,16]{1,0:T(8,128)S(1)} %copy-done.5, bf16[512,512]{1,0:T(8,128)(2,1)S(1)} %solved_rows.1.mine, bf16[512,512]{1,0:T(8,128)(2,1)S(1)} %collective-permute-done.other, bf16[512,512]{1,0:T(8,128)(2,1)S(1)} %get-tuple-element.21.wide, ...), custom_call_target="tpu_custom_call" | custom-call | flops 536870912 | bytes 3671048 | tf_op jit(solution)/shard_map/schur/pallas_call | solution.py:18
  116.7 0.1 reshape.43
  116.8 0.6 copy.21
  117.4 0.0 all-to-all-done.2
  117.4 1.1 reduce_sum.19
  118.5 0.1 reshape.46
  118.6 0.7 reshape.47
  (4 shorter events, 0.1 us)
Async XLA Ops:
  2.3 12.0 %copy-start.3 = (bf16[256,256]{1,0:T(8,128)(2,1)S(1)}, bf16[256,256]{1,0:T(8,128)(2,1)}, u32[]{:S(2)}) copy-start(bf16[256,256]{1,0:T(8,128)(2,1)} %panel_h.1) | copy-start | bytes 393220
  2.3 12.0 %copy-start.4 = (bf16[256,256]{1,0:T(8,128)(2,1)S(1)}, bf16[256,256]{1,0:T(8,128)(2,1)}, u32[]{:S(2)}) copy-start(bf16[256,256]{1,0:T(8,128)(2,1)} %panel_s.1) | copy-start | bytes 393220
  2.3 12.0 %copy-start.6 = (f32[1,2]{1,0:T(1,128)S(1)}, f32[1,2]{1,0:T(1,128)}, u32[]{:S(2)}) copy-start(f32[1,2]{1,0:T(1,128)} %shift.5) | copy-start | bytes 28
  2.3 12.0 %copy-start.7 = (f32[1,2]{1,0:T(1,128)S(1)}, f32[1,2]{1,0:T(1,128)}, u32[]{:S(2)}) copy-start(f32[1,2]{1,0:T(1,128)} %weight.3) | copy-start | bytes 28
  2.3 12.0 %copy-start.8 = (bf16[256,256]{1,0:T(8,128)(2,1)S(1)}, bf16[256,256]{1,0:T(8,128)(2,1)}, u32[]{:S(2)}) copy-start(bf16[256,256]{1,0:T(8,128)(2,1)} %pivot_h.1) | copy-start | bytes 393220
  2.3 12.0 %copy-start.9 = (bf16[256,256]{1,0:T(8,128)(2,1)S(1)}, bf16[256,256]{1,0:T(8,128)(2,1)}, u32[]{:S(2)}) copy-start(bf16[256,256]{1,0:T(8,128)(2,1)} %pivot_s.1) | copy-start | bytes 393220
  2.3 29.3 %all-to-all-start = ((bf16[16,64,256]{2,1,0:T(8,128)(2,1)}), bf16[16,64,256]{2,1,0:T(8,128)(2,1)S(1)}, u32[]{:S(2)}, u32[]{:S(2)}) async-start(bf16[16,64,256]{2,1,0:T(8,128)(2,1)} %bitcast.4), calls=%async_computation | async-start | bytes 1048576 | tf_op jit(solution)/shard_map/all_to_all | solution.py:250
  31.6 3.3 %copy-start.1 = (bf16[64,4096]{1,0:T(8,128)(2,1)S(1)}, bf16[64,4096]{1,0:T(8,128)(2,1)}, u32[]{:S(2)}) copy-start(bf16[64,4096]{1,0:T(8,128)(2,1)} %front_h.1) | copy-start | bytes 1572868
  31.6 3.3 %copy-start.2 = (bf16[64,4096]{1,0:T(8,128)(2,1)S(1)}, bf16[64,4096]{1,0:T(8,128)(2,1)}, u32[]{:S(2)}) copy-start(bf16[64,4096]{1,0:T(8,128)(2,1)} %front_s.1) | copy-start | bytes 1572868
  32.9 4.7 %copy-start = (bf16[1,2,16,1,64,256]{5,4,3,2,1,0:T(8,128)(2,1)S(1)}, bf16[1,2,16,1,64,256]{5,4,3,2,1,0:T(8,128)(2,1)}, u32[]{:S(2)}) copy-start(bf16[1,2,16,1,64,256]{5,4,3,2,1,0:T(8,128)(2,1)} %param.19) | copy-start | bytes 3145732
  32.9 4.7 %collective-permute-start = (bf16[512,512]{1,0:T(8,128)(2,1)S(1)}, bf16[512,512]{1,0:T(8,128)(2,1)S(1)}, u32[]{:S(2)}, u32[]{:S(2)}) collective-permute-start(bf16[512,512]{1,0:T(8,128)(2,1)S(1)} %solved_rows.1.mine), channel_id=1, source_target_pairs={{0,4},{4,0},{8,12},{12,8},{16,20},{20,16},{24,28},{28,24},{32,36},... | collective-permute-start | bytes 1572872 | tf_op jit(solution)/shard_map/ppermute | solution.py:280
  35.1 4.3 %collective-permute-start.1 = (bf16[8,2,64,256]{3,2,1,0:T(8,128)(2,1)S(1)}, bf16[8,2,64,256]{3,2,1,0:T(8,128)(2,1)S(1)}, u32[]{:S(2)}, u32[]{:S(2)}) collective-permute-start(bf16[8,2,64,256]{3,2,1,0:T(8,128)(2,1)S(1)} %get-tuple-element.23), channel_id=1, source_target_pairs={{0,4},{4,0},{8,12},{12,8},{16,20},{20,16},{24,28},{28,24},{32,36},... | collective-permute-start | bytes 1572872 | tf_op jit(solution)/shard_map/ppermute | solution.py:259
  66.6 50.8 %all-to-all-start.2 = ((f32[64,16,128]{2,1,0:T(8,128)}), f32[64,16,128]{2,1,0:T(8,128)}, u32[]{:S(2)}, u32[]{:S(2)}) async-start(f32[64,16,128]{2,1,0:T(8,128)} %broadcast_in_dim.5), calls=%async_computation.2 | async-start | bytes 1048576 | tf_op jit(solution)/shard_map/all_to_all | solution.py:316
  73.6 39.9 %copy-start.5 = (s32[16,16]{1,0:T(8,128)S(1)}, s32[16,16]{1,0:T(8,128)}, u32[]{:S(2)}) copy-start(s32[16,16]{1,0:T(8,128)} %pattern.1) | copy-start | bytes 3076
  73.7 20.2 %collective-permute-start.2 = (bf16[2,2,64,256]{3,2,1,0:T(8,128)(2,1)S(1)}, bf16[2,2,64,256]{3,2,1,0:T(8,128)(2,1)S(1)}, u32[]{:S(2)}, u32[]{:S(2)}) collective-permute-start(bf16[2,2,64,256]{3,2,1,0:T(8,128)(2,1)S(1)} %get-tuple-element.29), channel_id=1, source_target_pairs={{0,8},{4,12},{8,16},{12,20},{16,24},{20,28},{24,32},{28,36},{32,40... | collective-permute-start | bytes 393224 | tf_op jit(solution)/shard_map/ppermute | solution.py:305
  77.0 22.0 %collective-permute-start.3 = (bf16[2,2,64,256]{3,2,1,0:T(8,128)(2,1)S(1)}, bf16[2,2,64,256]{3,2,1,0:T(8,128)(2,1)S(1)}, u32[]{:S(2)}, u32[]{:S(2)}) collective-permute-start(bf16[2,2,64,256]{3,2,1,0:T(8,128)(2,1)S(1)} %get-tuple-element.30), channel_id=1, source_target_pairs={{0,16},{4,20},{8,24},{12,28},{16,32},{20,36},{24,40},{28,44},{32,4... | collective-permute-start | bytes 393224 | tf_op jit(solution)/shard_map/ppermute | solution.py:305
  81.0 26.1 %collective-permute-start.4 = (bf16[2,2,64,256]{3,2,1,0:T(8,128)(2,1)S(1)}, bf16[2,2,64,256]{3,2,1,0:T(8,128)(2,1)S(1)}, u32[]{:S(2)}, u32[]{:S(2)}) collective-permute-start(bf16[2,2,64,256]{3,2,1,0:T(8,128)(2,1)S(1)} %get-tuple-element.31), channel_id=1, source_target_pairs={{0,24},{4,28},{8,32},{12,36},{16,40},{20,44},{24,48},{28,52},{32,5... | collective-permute-start | bytes 393224 | tf_op jit(solution)/shard_map/ppermute | solution.py:305
  85.5 25.8 %collective-permute-start.5 = (bf16[2,2,64,256]{3,2,1,0:T(8,128)(2,1)S(1)}, bf16[2,2,64,256]{3,2,1,0:T(8,128)(2,1)S(1)}, u32[]{:S(2)}, u32[]{:S(2)}) collective-permute-start(bf16[2,2,64,256]{3,2,1,0:T(8,128)(2,1)S(1)} %get-tuple-element.32), channel_id=1, source_target_pairs={{0,32},{4,36},{8,40},{12,44},{16,48},{20,52},{24,56},{28,60},{32,0... | collective-permute-start | bytes 393224 | tf_op jit(solution)/shard_map/ppermute | solution.py:305
  89.3 22.0 %collective-permute-start.6 = (bf16[2,2,64,256]{3,2,1,0:T(8,128)(2,1)S(1)}, bf16[2,2,64,256]{3,2,1,0:T(8,128)(2,1)S(1)}, u32[]{:S(2)}, u32[]{:S(2)}) collective-permute-start(bf16[2,2,64,256]{3,2,1,0:T(8,128)(2,1)S(1)} %get-tuple-element.33), channel_id=1, source_target_pairs={{0,40},{4,44},{8,48},{12,52},{16,56},{20,60},{24,0},{28,4},{32,8},... | collective-permute-start | bytes 393224 | tf_op jit(solution)/shard_map/ppermute | solution.py:305
  93.9 19.3 %collective-permute-start.7 = (bf16[2,2,64,256]{3,2,1,0:T(8,128)(2,1)S(1)}, bf16[2,2,64,256]{3,2,1,0:T(8,128)(2,1)S(1)}, u32[]{:S(2)}, u32[]{:S(2)}) collective-permute-start(bf16[2,2,64,256]{3,2,1,0:T(8,128)(2,1)S(1)} %get-tuple-element.34), channel_id=1, source_target_pairs={{0,48},{4,52},{8,56},{12,60},{16,0},{20,4},{24,8},{28,12},{32,16},... | collective-permute-start | bytes 393224 | tf_op jit(solution)/shard_map/ppermute | solution.py:305
  99.0 14.6 %collective-permute-start.8 = (bf16[2,2,64,256]{3,2,1,0:T(8,128)(2,1)S(1)}, bf16[2,2,64,256]{3,2,1,0:T(8,128)(2,1)S(1)}, u32[]{:S(2)}, u32[]{:S(2)}) collective-permute-start(bf16[2,2,64,256]{3,2,1,0:T(8,128)(2,1)S(1)} %get-tuple-element.35), channel_id=1, source_target_pairs={{0,56},{4,60},{8,0},{12,4},{16,8},{20,12},{24,16},{28,20},{32,24},... | collective-permute-start | bytes 393224 | tf_op jit(solution)/shard_map/ppermute | solution.py:305

commit v4 on v3

--- a/solution.py
+++ b/solution.py
@@ -118,13 +118,39 @@
     wide[size:] = jnp.concatenate([coupling_imag, coupling_real], axis=1)
 
 
-def solve_body(shift, received, inverse, solved):
-    strips, twice, size = received.shape
-    half = twice // 2
+def pack_body(panel_h, panel_s, front_h, front_s, out, panels, fronts, sems):
+    half = panels.shape[1] // 2
+    share, size = fronts.shape[0], out.shape[2]
+    pole = lax.axis_index("pole")
+    shares = panels.shape[1] // share
+    at = pl.ds(pl.multiple_of(lax.axis_index("col") * 2 * half, 2 * half), 2 * half)
+    of = pl.ds(pl.multiple_of(lax.rem(pole, shares) * share, share), share)
+    copy_h = pltpu.make_async_copy(panel_h.at[at], panels.at[0], sems.at[0])
+    copy_s = pltpu.make_async_copy(panel_s.at[at], panels.at[1], sems.at[1])
+    share_h = pltpu.make_async_copy(front_h.at[of], fronts, sems.at[2])
+    share_s = pltpu.make_async_copy(front_s.at[of], fronts, sems.at[2])
+    copy_h.start()
+    copy_s.start()
+    pl.when(pole < shares)(share_h.start)
+    pl.when(pole >= shares)(share_s.start)
+    copy_h.wait()
+    copy_s.wait()
+    share_h.wait()
+    for row in range(out.shape[0]):
+        core = row % 2
+        out[row, :half] = panels[0, core * half : (core + 1) * half]
+        out[row, half : 2 * half] = panels[1, core * half : (core + 1) * half]
+        out[row, 2 * half :] = fronts[:, row * size : (row + 1) * size]
+
+
+def solve_body(shift, received, inverse, solved, share):
+    strips, rows, size = received.shape
+    half = solved.shape[0] // strips
     rows_h = received[:, :half].reshape(strips * half, size)
-    rows_s = received[:, half:].reshape(strips * half, size)
+    rows_s = received[:, half : 2 * half].reshape(strips * half, size)
     coupling = jnp.concatenate(couple(rows_h, rows_s, shift[0, 0], shift[0, 1]), axis=1)
     solved[...] = (dot(coupling, inverse[0]) + dot(coupling, inverse[1])).astype(bf16)
+    share[...] = received[:, 2 * half :]
 
 
 def ordered(mine, other):
@@ -169,55 +195,46 @@
     fold(pivot, out, out.shape[1] // 2)
 
 
-def strips_body(front_h, front_s, kept, given):
-    size = kept.shape[3]
-    core = lax.rem(lax.axis_index("row"), 2)
-    for chip in range(kept.shape[0]):
-        own = pl.ds(pl.multiple_of((2 * chip + core) * size, size), size)
-        far = pl.ds(pl.multiple_of((2 * chip + 1 - core) * size, size), size)
-        kept[chip, 0] = front_h[:, own]
-        kept[chip, 1] = front_s[:, own]
-        given[chip, 0] = front_h[:, far]
-        given[chip, 1] = front_s[:, far]
-
-
-def blocks_body(kept, swapped, *outs):
-    chips = kept.shape[0]
-    chip = lax.rem(lax.axis_index("row"), 2 * chips) // 2
-    for step, out in enumerate(outs):
-        to = lax.rem(chip + step, chips)
-        low, high = ordered(kept[to], swapped[to])
-        out[0] = low
-        out[1] = high
+def sums_body(parts, spread, rows):
+    half, width = parts.shape[1] // 2, rows.shape[1]
+    total = jnp.sum(parts[...], axis=0)
+    rows[:half] = total[:half, :width]
+    rows[half:] = total[:half, width:]
+    spread[...] = jnp.broadcast_to(total[None, half:], spread.shape)
+
+
+def pivot_body(parts, out):
+    half = parts.shape[1]
+    width = 64
+    cols = out.shape[1] // width
+    total = jnp.sum(parts[...].reshape(-1, cols, half, 128), axis=0)
+    for index in range(128 // width):
+        lanes = slice(index * width, (index + 1) * width)
+        strips = [total[col][:, lanes] for col in range(cols)]
+        out[index * half : (index + 1) * half] = jnp.concatenate(strips, axis=1)
 
 
 def schur_body(shift, pattern, mine, other, wide, *refs):
-    blocks, out = refs[:-1], refs[-1]
-    chips = len(blocks)
-    half = blocks[0].shape[2] // 2
-    size = blocks[0].shape[3]
+    shares, out, front = refs[:-2], refs[-2], refs[-1]
+    poles, strips, share, size = front.shape
+    pole = lax.axis_index("pole")
+    row = lax.axis_index("row")
+    for step, member in enumerate(shares):
+        front[lax.rem(pole + poles - step, poles)] = member[...]
     shift_real, shift_imag = shift[0, 0], shift[0, 1]
-    row = lax.axis_index("row")
-    for step, tiles in enumerate(blocks):
-        chip = lax.rem(row // 2 + chips - step, chips)
-        at = pl.ds(pl.multiple_of(chip * 2 * half, 2 * half), 2 * half)
-        low, high = ordered(mine[at, :], other[at, :])
-        solved = jnp.concatenate([low[:half], high[:half], low[half:], high[half:]], axis=0)
+    half = mine.shape[0] // strips
+    top, bottom = ordered(mine[...], other[...])
+    for strip in range(strips):
+        rows = slice(strip * half, (strip + 1) * half)
+        solved = jnp.concatenate([top[rows], bottom[rows]], axis=0)
         update = contract(solved, wide[...], 1, 1)
-        for core in range(2):
-            strip = 2 * chip + core
-            mask = pattern[strip, row].astype(f32)
-            rows = slice(core * 2 * half, (core + 1) * 2 * half)
-            margin = mask * tiles[core, 1].astype(f32)
-            real = mask * tiles[core, 0].astype(f32) - shift_real * margin
-            out[0, strip] = (real - update[rows, :size]).astype(bf16)
-            out[1, strip] = (-shift_imag * margin - update[rows, size:]).astype(bf16)
-
-
-def unfold(member, width, piece):
-    times = 128 // width
-    member = member.reshape(-1, piece // times, times, width)
-    return member.transpose(2, 1, 0, 3).reshape(piece, -1)
+        mask = pattern[strip, row].astype(f32)
+        for part in range(poles // 2):
+            at = slice(part * share, (part + 1) * share)
+            margin = mask * front[poles // 2 + part, strip].astype(f32)
+            real = mask * front[part, strip].astype(f32) - shift_real * margin
+            out[0, strip, at] = (real - update[at, :size]).astype(bf16)
+            out[1, strip, at] = (-shift_imag * margin - update[at, size:]).astype(bf16)
 
 
 def shards(
@@ -240,23 +257,26 @@
     width = size // col_count
     piece = size // pole_count
     half = width // 2
-    chips = row_count // 2
     neighbour = [(i, i ^ 1) for i in range(row_count)]
 
-    strip = lax.dynamic_slice_in_dim(jnp.stack([panel_h, panel_s]), col_index * width, width, axis=1)
-    strip = strip.reshape(2, 2, half, size).transpose(1, 0, 2, 3)
-    sent = jnp.broadcast_to(strip[None], (chips, 2, 2, half, size))
-    sent = sent.reshape(row_count, 2 * half, size)
+    share = 2 * width // pole_count
+    params = pltpu.CompilerParams(vmem_limit_bytes=40 * 2**20)
+
+    (sent,) = pl.pallas_call(
+        pack_body,
+        out_shape=[shape(row_count, width + share, size)],
+        in_specs=[pl.BlockSpec(memory_space=pl.ANY)] * 4,
+        out_specs=[VMEM],
+        scratch_shapes=[
+            pltpu.VMEM((2, width, size), bf16),
+            pltpu.VMEM((share, row_count * size), bf16),
+            pltpu.SemaphoreType.DMA((3,)),
+        ],
+        compiler_params=params,
+        cost_estimate=pl.CostEstimate(flops=0, bytes_accessed=2**20, transcendentals=0),
+        name="pack",
+    )(panel_h, panel_s, front_h, front_s)
     received = lax.all_to_all(sent, "row", split_axis=0, concat_axis=0, tiled=True)
-
-    kept, given = call(
-        strips_body,
-        [shape(chips, 2, width, size)] * 2,
-        [front_h, front_s],
-        0,
-        "front_strips",
-    )
-    swapped = lax.ppermute(given, "row", neighbour)
 
     inverse, right, wide, base = call(
         invert_body,
@@ -270,9 +290,9 @@
         6 * 4 * 3 * 2 * size**3,
         "pivot_inverse",
     )
-    (mine,) = call(
+    mine, shared = call(
         solve_body,
-        [shape(row_count * half, 2 * size)],
+        [shape(row_count * half, 2 * size), shape(row_count, share, size)],
         [pole_shift, received, inverse],
         2 * 8 * row_count * half * size * size,
         "solved_rows",
@@ -293,38 +313,50 @@
         name="column",
     )(pole_weight, mine, other, ancestor, right, base)
 
-    kept, swapped, both = lax.optimization_barrier((kept, swapped, both))
-    blocks = call(
-        blocks_body,
-        [shape(2, 2, width, size)] * chips,
-        [kept, swapped],
+    shared, both = lax.optimization_barrier((shared, both))
+    onward = [(i, (i + 1) % pole_count) for i in range(pole_count)]
+    back = [(i, (i - 1) % pole_count) for i in range(pole_count)]
+    shares = {0: shared}
+
+    def go_round(steps):
+        for step in steps:
+            shares[step + 1] = lax.ppermute(shares[step], "pole", onward)
+            if step + 1 < pole_count // 2:
+                before = shares[(pole_count - step) % pole_count]
+                shares[pole_count - step - 1] = lax.ppermute(before, "pole", back)
+
+    go_round(range(2))
+    both = lax.all_to_all(both, ("pole", "col"), split_axis=0, concat_axis=0, tiled=True)
+    spread, rows_out = call(
+        sums_body,
+        [
+            shape(row_count * col_count, piece // 2, 128, dtype=f32),
+            shape(piece, width, dtype=f32),
+        ],
+        [both],
         0,
-        "front_blocks",
-    )
-    arrived = list(blocks[:1]) + [
-        lax.ppermute(
-            blocks[step], "row", [(i, (i + 2 * step) % row_count) for i in range(row_count)]
-        )
-        for step in range(1, chips)
-    ]
-
-    both = lax.all_to_all(both, ("pole", "col"), split_axis=0, concat_axis=0, tiled=True)
-    both = jnp.sum(both, axis=0).reshape(2, piece // 2, 128)
-    rows_out = unfold(both[:1], width, piece).T
-
-    spread = jnp.broadcast_to(both[1][None], (row_count * col_count,) + both.shape[1:])
+        "sums",
+    )
+    spread, shares[2], shares[pole_count - 2] = lax.optimization_barrier(
+        (spread, shares[2], shares[pole_count - 2])
+    )
+    go_round(range(2, pole_count // 2))
     spread = lax.all_to_all(spread, ("row", "col"), split_axis=0, concat_axis=0, tiled=True)
-    spread = jnp.sum(spread.reshape((row_count, col_count) + both.shape[1:]), axis=0)
-    pivot_out = unfold(spread, width, piece).T
-
-    (schur,) = call(
+    (pivot_out,) = call(pivot_body, [shape(piece, size, dtype=f32)], [spread], 0, "pivot")
+
+    (schur,) = pl.pallas_call(
         schur_body,
-        [shape(2, row_count, width, size)],
-        [pole_shift, pattern, mine, other, wide, *arrived],
-        8 * row_count * width * size * size,
-        "schur",
-    )
-    return (schur.reshape(1, 2, row_count, 1, width, size), rows_out, pivot_out)
+        out_shape=[shape(2, row_count, width, size)],
+        in_specs=[SMEM] * 2 + [VMEM] * (3 + pole_count),
+        out_specs=[VMEM],
+        scratch_shapes=[pltpu.VMEM((pole_count, row_count, share, size), bf16)],
+        compiler_params=params,
+        cost_estimate=pl.CostEstimate(
+            flops=8 * row_count * width * size * size, bytes_accessed=4 * 2**20, transcendentals=0
+        ),
+        name="schur",
+    )(pole_shift, pattern, mine, other, wide, *[shares[step] for step in range(pole_count)])
+    return (schur.reshape(1, 2, row_count, 1, width, size), rows_out.T, pivot_out.T)
 
 
 def solution(mesh):

time: 120 us -> 112 us (0.933)
  blocking collectives: 26.3 us -> 0 us
  waiting for transfers between devices: 24.6 us -> 35.8 us
  Pallas kernels: 10.7 us -> 15.2 us
  local copies, waits for them, and re-layouts: 3.28 us -> 6.93 us
  other arithmetic: 1.91 us -> 0 us
    all_to_all x1 -> x0, blocking collectives: 26.3 us -> none  [shards(): lax.all_to_all(both, ('pole', 'col'), split_axis=0, concat_axis=0, tiled=...]
    ppermute x8 -> x7, starting transfers between devices: 30.7 us -> 20.1 us  [the longest x3 12.4 us: go_round(): shares[pole_count - step - 1] = lax.ppermute(before, 'pole', back)]
    all_to_all x0 -> x1, starting transfers between devices: none -> 9.67 us  [shards(): lax.all_to_all(both, ('pole', 'col'), split_axis=0, concat_axis=0, tiled=...]
    ppermute x8 -> x7, waiting for transfers between devices: 11.6 us -> 20 us  [the longest x4 10.6 us: go_round(): shares[step + 1] = lax.ppermute(shares[step], 'pole', onward)]
    unnamed x20 -> x32, local copies, waits for them, and re-layouts: 0.05 us -> 6.93 us
    pallas_call x0 -> x2, Pallas kernels: none -> 5.43 us  [the longest x1 4.28 us: shards(): pl.pallas_call(schur_body, out_shape=[shape(2, row_count, width, size)],...]
    ppermute x1, waiting for transfers between devices: 0.01 us -> 1.88 us  [shards(): other = lax.ppermute(mine, 'row', neighbour)]
    pallas_call x5 -> x4, Pallas kernels: 8.89 us -> 7.11 us  [call(): pl.pallas_call(body, out_shape=outs, in_specs=[SMEM if x.size <= 256 else...]
  transfers between devices with their start and end apart: 11 -> 11, of which waited for: 5 -> 6; matrix products, arithmetic and copies ran while one was open for 1% -> 0% of each run, Pallas kernels for 8% -> 9%
where the time goes in v4:
time: 112 us; the launch traced here: 111 us
  starting transfers between devices  52 us (46%)
  waiting for transfers between devices  35.8 us (32%)
  Pallas kernels  15.2 us (14%)
  local copies, waits for them, and re-layouts  6.93 us (6%)
    all_to_all x1, waiting for transfers between devices, shards(): lax.all_to_all(sent, 'row', split_axis=0, concat_axis=0, tiled=True)  13.9 us
    ppermute x3, starting transfers between devices, go_round(): shares[pole_count - step - 1] = lax.ppermute(before, 'pole', back)  12.4 us
    all_to_all x1, starting transfers between devices, shards(): lax.all_to_all(sent, 'row', split_axis=0, concat_axis=0, tiled=True)  12 us
    ppermute x4, waiting for transfers between devices, go_round(): shares[step + 1] = lax.ppermute(shares[step], 'pole', onward)  10.6 us
    all_to_all x1, starting transfers between devices, shards(): lax.all_to_all(both, ('pole', 'col'), split_axis=0, concat_axis=0, tiled=...  9.67 us
    ppermute x3, waiting for transfers between devices, go_round(): shares[pole_count - step - 1] = lax.ppermute(before, 'pole', back)  9.38 us
    all_to_all x1, starting transfers between devices, shards(): lax.all_to_all(spread, ('row', 'col'), split_axis=0, concat_axis=0, tiled...  8.34 us
    ppermute x4, starting transfers between devices, go_round(): shares[step + 1] = lax.ppermute(shares[step], 'pole', onward)  7.67 us
  transfers between devices with their start and end apart: 11, of which 6 were waited for; matrix products, arithmetic and copies ran while one was open for 0% of the time, Pallas kernels for 9%

profile of v4, /device:TPU:1, one launch (start us, length us, event | category | flops | bytes accessed | tf_op | source)
XLA Modules:
  0.0 110.8 jit_solution(12955806552383025535)
XLA Ops:
  0.6 0.0 copy-start.1
  0.6 1.0 copy-done.1
  1.7 0.0 copy-start.2
  1.7 1.0 copy-done.2
  2.7 0.0 copy-start.5
  2.7 0.9 copy-done.5
  3.6 0.0 copy-start.7
  3.6 0.9 copy-done.7
  4.5 1.1 %pack.1 = bf16[16,80,256]{2,1,0:T(8,128)(2,1)} custom-call(bf16[256,256]{1,0:T(8,128)(2,1)S(1)} %copy-done.5, bf16[256,256]{1,0:T(8,128)(2,1)S(1)} %copy-done.7, bf16[64,4096]{1,0:T(8,128)(2,1)S(1)} %copy-done.1, bf16[64,4096]{1,0:T(8,128)(2,1)S(1)} %copy-done.2), custom_call_target="tpu_custom_call" | custom-call | bytes 1048576 | tf_op jit(solution)/shard_map/pack/pallas_call | solution.py:265
  5.7 0.0 copy-start.6
  5.7 0.0 copy-start.8
  5.7 0.0 copy-start.10
  5.7 0.0 copy-start.11
  5.7 0.0 copy-start.12
  5.7 0.0 copy-start.13
  5.8 12.0 %all-to-all-start = ((bf16[16,80,256]{2,1,0:T(8,128)(2,1)}), bf16[16,80,256]{2,1,0:T(8,128)(2,1)S(1)}, u32[]{:S(2)}, u32[]{:S(2)}) async-start(bf16[16,80,256]{2,1,0:T(8,128)(2,1)} %pack.1), calls=%async_computation | async-start | bytes 1310720 | tf_op jit(solution)/shard_map/all_to_all | solution.py:279
  17.7 0.0 copy-done.6
  17.7 0.0 copy-done.8
  17.7 0.0 copy-done.10
  17.8 0.0 copy-done.11
  17.8 0.0 copy-done.12
  17.8 0.0 copy-done.13
  17.8 4.3 %pivot_inverse.1 = (bf16[2,512,512]{2,1,0:T(8,128)(2,1)S(1)}, bf16[512,256]{1,0:T(8,128)(2,1)S(1)}, bf16[512,512]{1,0:T(8,128)(2,1)S(1)}, f32[256,256]{1,0:T(8,128)S(1)}) custom-call(f32[1,2]{1,0:T(1,128)S(1)} %copy-done.11, f32[1,2]{1,0:T(1,128)S(1)} %copy-done.10, bf16[256,256]{1,0:T(8,128)(2,1)S(1)} %copy-done.12, bf16[256,256]{1,0:T(8,128)(2,1)S(1)} %copy-done.13, ...), custom_call_target="tpu_custom_call" | custom-call | flops 2415919104 | bytes 2621456 | tf_op jit(solution)/shard_map/pivot_inverse/pallas_call | solution.py:18
  22.0 0.0 copy-start.3
  22.1 0.8 copy-done.3
  22.9 0.0 copy-start.14
  22.9 1.0 copy-done.14
  23.8 0.0 copy-start
  23.8 13.9 %all-to-all-done.received = bf16[16,80,256]{2,1,0:T(8,128)(2,1)S(1)} async-done(((bf16[16,80,256]{2,1,0:T(8,128)(2,1)}), bf16[16,80,256]{2,1,0:T(8,128)(2,1)S(1)}, u32[]{:S(2)}, u32[]{:S(2)}) %all-to-all-start) | async-done | bytes 655392 | tf_op jit(solution)/shard_map/all_to_all | solution.py:279
  37.8 0.0 copy-start.15
  37.8 1.2 %copy-done.15 = bf16[2,512,512]{2,1,0:T(8,128)(2,1)S(1)} copy-done((bf16[2,512,512]{2,1,0:T(8,128)(2,1)S(1)}, bf16[2,512,512]{2,1,0:T(8,128)(2,1)}, u32[]{:S(2)}) %copy-start.15) | copy-done | bytes 1048600
  39.0 1.3 %solved_rows.1 = (bf16[512,512]{1,0:T(8,128)(2,1)S(1)}, bf16[16,16,256]{2,1,0:T(8,128)(2,1)S(1)}) custom-call(f32[1,2]{1,0:T(1,128)S(1)} %copy-done.11, bf16[16,80,256]{2,1,0:T(8,128)(2,1)S(1)} %all-to-all-done.received, bf16[2,512,512]{2,1,0:T(8,128)(2,1)S(1)} %copy-done.15), custom_call_target="tpu_custom_call" | custom-call | flops 536870912 | bytes 2359304 | tf_op jit(solution)/shard_map/solved_rows/pallas_call | solution.py:18
  40.2 1.9 %collective-permute-start = (bf16[512,512]{1,0:T(8,128)(2,1)S(1)}, bf16[512,512]{1,0:T(8,128)(2,1)S(1)}, u32[]{:S(2)}, u32[]{:S(2)}) collective-permute-start(bf16[512,512]{1,0:T(8,128)(2,1)S(1)} %get-tuple-element.17.mine), channel_id=1, source_target_pairs={{0,4},{4,0},{8,12},{12,8},{16,20},{20,16},{24,28},{28,24},{32,36},... | collective-permute-start | bytes 1572872 | tf_op jit(solution)/shard_map/ppermute | solution.py:300
  42.2 1.9 %collective-permute-done.other = bf16[512,512]{1,0:T(8,128)(2,1)S(1)} collective-permute-done((bf16[512,512]{1,0:T(8,128)(2,1)S(1)}, bf16[512,512]{1,0:T(8,128)(2,1)S(1)}, u32[]{:S(2)}, u32[]{:S(2)}) %collective-permute-start) | collective-permute-done | bytes 524320 | tf_op jit(solution)/shard_map/ppermute | solution.py:300
  44.0 0.0 copy-done
  44.0 2.6 %column.1 = f32[32,32,128]{2,1,0:T(8,128)} custom-call(f32[1,2]{1,0:T(1,128)S(1)} %copy-done.10, bf16[512,512]{1,0:T(8,128)(2,1)S(1)} %get-tuple-element.17.mine, bf16[512,512]{1,0:T(8,128)(2,1)S(1)} %collective-permute-done.other, bf16[2,16,64,256]{3,2,1,0:T(8,128)(2,1)S(1)} %bitcast.6, bf16[512,256]{1,0:T(8,128)(2,1)S(1)} %get-tuple-element.20.right, ...), custom_call_target="tpu_custom_call" | custom-call | flops 536870912 | bytes 4194304 | tf_op jit(solution)/shard_map/column/pallas_call | solution.py:303
  46.7 9.7 %all-to-all-start.1 = ((f32[32,32,128]{2,1,0:T(8,128)}), f32[32,32,128]{2,1,0:T(8,128)S(1)}, u32[]{:S(2)}, u32[]{:S(2)}) async-start(f32[32,32,128]{2,1,0:T(8,128)} %column.1), calls=%async_computation.1 | async-start | bytes 1048576 | tf_op jit(solution)/shard_map/all_to_all | solution.py:329
  56.4 4.4 %collective-permute-start.3 = (bf16[16,16,256]{2,1,0:T(8,128)(2,1)S(1)}, bf16[16,16,256]{2,1,0:T(8,128)(2,1)S(1)}, u32[]{:S(2)}, u32[]{:S(2)}) collective-permute-start(bf16[16,16,256]{2,1,0:T(8,128)(2,1)S(1)} %get-tuple-element.22.refs_0_), channel_id=1, source_target_pairs={{0,448},{64,0},{128,64},{192,128},{256,192},{320,256},{384,320},{4... | collective-permute-start | bytes 393224 | tf_op jit(solution)/shard_map/ppermute | solution.py:326
  60.8 1.9 %collective-permute-start.1 = (bf16[16,16,256]{2,1,0:T(8,128)(2,1)S(1)}, bf16[16,16,256]{2,1,0:T(8,128)(2,1)S(1)}, u32[]{:S(2)}, u32[]{:S(2)}) collective-permute-start(bf16[16,16,256]{2,1,0:T(8,128)(2,1)S(1)} %get-tuple-element.22.refs_0_), channel_id=1, source_target_pairs={{0,64},{64,128},{128,192},{192,256},{256,320},{320,384},{384,448},... | collective-permute-start | bytes 393224 | tf_op jit(solution)/shard_map/ppermute | solution.py:323
  62.7 9.4 %collective-permute-done.3.refs_7_ = bf16[16,16,256]{2,1,0:T(8,128)(2,1)S(1)} collective-permute-done((bf16[16,16,256]{2,1,0:T(8,128)(2,1)S(1)}, bf16[16,16,256]{2,1,0:T(8,128)(2,1)S(1)}, u32[]{:S(2)}, u32[]{:S(2)}) %collective-permute-start.3) | collective-permute-done | bytes 131104 | tf_op jit(solution)/shard_map/ppermute | solution.py:326
  72.1 3.4 %collective-permute-start.4 = (bf16[16,16,256]{2,1,0:T(8,128)(2,1)S(1)}, bf16[16,16,256]{2,1,0:T(8,128)(2,1)S(1)}, u32[]{:S(2)}, u32[]{:S(2)}) collective-permute-start(bf16[16,16,256]{2,1,0:T(8,128)(2,1)S(1)} %collective-permute-done.3.refs_7_), channel_id=1, source_target_pairs={{0,448},{64,0},{128,64},{192,128},{256,192},{320,256},{384,320},{4... | collective-permute-start | bytes 393224 | tf_op jit(solution)/shard_map/ppermute | solution.py:326
  75.5 0.0 collective-permute-done.1.refs_1_
  75.5 1.9 %collective-permute-start.2 = (bf16[16,16,256]{2,1,0:T(8,128)(2,1)S(1)}, bf16[16,16,256]{2,1,0:T(8,128)(2,1)S(1)}, u32[]{:S(2)}, u32[]{:S(2)}) collective-permute-start(bf16[16,16,256]{2,1,0:T(8,128)(2,1)S(1)} %collective-permute-done.1.refs_1_), channel_id=1, source_target_pairs={{0,64},{64,128},{128,192},{192,256},{256,320},{320,384},{384,448},... | collective-permute-start | bytes 393224 | tf_op jit(solution)/shard_map/ppermute | solution.py:323
  77.5 0.0 all-to-all-done.1.parts
  77.5 0.9 sums.1
  78.4 0.0 collective-permute-done.4.refs_6_
  78.4 4.1 %collective-permute-done.2.refs_2_ = bf16[16,16,256]{2,1,0:T(8,128)(2,1)S(1)} collective-permute-done((bf16[16,16,256]{2,1,0:T(8,128)(2,1)S(1)}, bf16[16,16,256]{2,1,0:T(8,128)(2,1)S(1)}, u32[]{:S(2)}, u32[]{:S(2)}) %collective-permute-start.2) | collective-permute-done | bytes 131104 | tf_op jit(solution)/shard_map/ppermute | solution.py:323
  82.5 0.0 copy-start.4
  82.5 0.0 copy-start.9
  82.5 8.3 %all-to-all-start.2 = ((f32[64,16,128]{2,1,0:T(8,128)}), f32[64,16,128]{2,1,0:T(8,128)S(1)}, u32[]{:S(2)}, u32[]{:S(2)}) async-start(f32[64,16,128]{2,1,0:T(8,128)} %get-tuple-element.28), calls=%async_computation.2 | async-start | bytes 1048576 | tf_op jit(solution)/shard_map/all_to_all | solution.py:344
  90.8 1.9 %collective-permute-start.5 = (bf16[16,16,256]{2,1,0:T(8,128)(2,1)S(1)}, bf16[16,16,256]{2,1,0:T(8,128)(2,1)S(1)}, u32[]{:S(2)}, u32[]{:S(2)}) collective-permute-start(bf16[16,16,256]{2,1,0:T(8,128)(2,1)S(1)} %collective-permute-done.2.refs_2_), channel_id=1, source_target_pairs={{0,64},{64,128},{128,192},{192,256},{256,320},{320,384},{384,448},... | collective-permute-start | bytes 393224 | tf_op jit(solution)/shard_map/ppermute | solution.py:323
  92.8 4.6 %collective-permute-start.7 = (bf16[16,16,256]{2,1,0:T(8,128)(2,1)S(1)}, bf16[16,16,256]{2,1,0:T(8,128)(2,1)S(1)}, u32[]{:S(2)}, u32[]{:S(2)}) collective-permute-start(bf16[16,16,256]{2,1,0:T(8,128)(2,1)S(1)} %collective-permute-done.4.refs_6_), channel_id=1, source_target_pairs={{0,448},{64,0},{128,64},{192,128},{256,192},{320,256},{384,320},{4... | collective-permute-start | bytes 393224 | tf_op jit(solution)/shard_map/ppermute | solution.py:326
  97.3 1.2 %collective-permute-done.5.refs_3_ = bf16[16,16,256]{2,1,0:T(8,128)(2,1)S(1)} collective-permute-done((bf16[16,16,256]{2,1,0:T(8,128)(2,1)S(1)}, bf16[16,16,256]{2,1,0:T(8,128)(2,1)S(1)}, u32[]{:S(2)}, u32[]{:S(2)}) %collective-permute-start.5) | collective-permute-done | bytes 131104 | tf_op jit(solution)/shard_map/ppermute | solution.py:323
  98.5 1.9 %collective-permute-start.6 = (bf16[16,16,256]{2,1,0:T(8,128)(2,1)S(1)}, bf16[16,16,256]{2,1,0:T(8,128)(2,1)S(1)}, u32[]{:S(2)}, u32[]{:S(2)}) collective-permute-start(bf16[16,16,256]{2,1,0:T(8,128)(2,1)S(1)} %collective-permute-done.5.refs_3_), channel_id=1, source_target_pairs={{0,64},{64,128},{128,192},{192,256},{256,320},{320,384},{384,448},... | collective-permute-start | bytes 393224 | tf_op jit(solution)/shard_map/ppermute | solution.py:323
  100.5 0.0 collective-permute-done.7.refs_5_
  100.5 5.3 %collective-permute-done.6.refs_4_ = bf16[16,16,256]{2,1,0:T(8,128)(2,1)S(1)} collective-permute-done((bf16[16,16,256]{2,1,0:T(8,128)(2,1)S(1)}, bf16[16,16,256]{2,1,0:T(8,128)(2,1)S(1)}, u32[]{:S(2)}, u32[]{:S(2)}) %collective-permute-start.6) | collective-permute-done | bytes 131104 | tf_op jit(solution)/shard_map/ppermute | solution.py:323
  105.8 0.0 copy-done.4
  105.8 0.0 copy-done.9
  105.8 4.3 %schur.1 = bf16[2,16,64,256]{3,2,1,0:T(8,128)(2,1)} custom-call(f32[1,2]{1,0:T(1,128)S(1)} %copy-done.11, s32[16,16]{1,0:T(8,128)S(1)} %copy-done.9, bf16[512,512]{1,0:T(8,128)(2,1)S(1)} %get-tuple-element.17.mine, bf16[512,512]{1,0:T(8,128)(2,1)S(1)} %collective-permute-done.other, bf16[512,512]{1,0:T(8,128)(2,1)S(1)} %copy-done.4, ...), custom_call_target="tpu_custom_call" | custom-call | flops 536870912 | bytes 4194304 | tf_op jit(solution)/shard_map/schur/pallas_call | solution.py:347
  110.0 0.0 all-to-all-done.2.parts
  110.0 0.7 pivot.1
Async XLA Ops:
  0.6 1.0 copy-start.1
  1.7 1.0 copy-start.2
  2.7 0.9 copy-start.5
  3.6 0.9 copy-start.7
  5.7 12.1 %copy-start.6 = (bf16[256,256]{1,0:T(8,128)(2,1)S(1)}, bf16[256,256]{1,0:T(8,128)(2,1)}, u32[]{:S(2)}) copy-start(bf16[256,256]{1,0:T(8,128)(2,1)} %panel_h.3) | copy-start | bytes 393220
  5.7 12.0 %copy-start.8 = (bf16[256,256]{1,0:T(8,128)(2,1)S(1)}, bf16[256,256]{1,0:T(8,128)(2,1)}, u32[]{:S(2)}) copy-start(bf16[256,256]{1,0:T(8,128)(2,1)} %panel_s.3) | copy-start | bytes 393220
  5.7 12.0 %copy-start.10 = (f32[1,2]{1,0:T(1,128)S(1)}, f32[1,2]{1,0:T(1,128)}, u32[]{:S(2)}) copy-start(f32[1,2]{1,0:T(1,128)} %weight.3) | copy-start | bytes 28
  5.7 12.0 %copy-start.11 = (f32[1,2]{1,0:T(1,128)S(1)}, f32[1,2]{1,0:T(1,128)}, u32[]{:S(2)}) copy-start(f32[1,2]{1,0:T(1,128)} %shift.5) | copy-start | bytes 28
  5.7 12.0 %copy-start.12 = (bf16[256,256]{1,0:T(8,128)(2,1)S(1)}, bf16[256,256]{1,0:T(8,128)(2,1)}, u32[]{:S(2)}) copy-start(bf16[256,256]{1,0:T(8,128)(2,1)} %pivot_h.1) | copy-start | bytes 393220
  5.7 12.0 %copy-start.13 = (bf16[256,256]{1,0:T(8,128)(2,1)S(1)}, bf16[256,256]{1,0:T(8,128)(2,1)}, u32[]{:S(2)}) copy-start(bf16[256,256]{1,0:T(8,128)(2,1)} %pivot_s.1) | copy-start | bytes 393220
  5.8 32.0 %all-to-all-start = ((bf16[16,80,256]{2,1,0:T(8,128)(2,1)}), bf16[16,80,256]{2,1,0:T(8,128)(2,1)S(1)}, u32[]{:S(2)}, u32[]{:S(2)}) async-start(bf16[16,80,256]{2,1,0:T(8,128)(2,1)} %pack.1), calls=%async_computation | async-start | bytes 1310720 | tf_op jit(solution)/shard_map/all_to_all | solution.py:279
  22.0 0.8 copy-start.3
  22.9 1.0 copy-start.14
  23.8 20.2 %copy-start = (bf16[1,2,16,1,64,256]{5,4,3,2,1,0:T(8,128)(2,1)S(1)}, bf16[1,2,16,1,64,256]{5,4,3,2,1,0:T(8,128)(2,1)}, u32[]{:S(2)}) copy-start(bf16[1,2,16,1,64,256]{5,4,3,2,1,0:T(8,128)(2,1)} %param.19) | copy-start | bytes 3145732
  37.8 1.2 %copy-start.15 = (bf16[2,512,512]{2,1,0:T(8,128)(2,1)S(1)}, bf16[2,512,512]{2,1,0:T(8,128)(2,1)}, u32[]{:S(2)}) copy-start(bf16[2,512,512]{2,1,0:T(8,128)(2,1)} %copy-done.14) | copy-start | bytes 3145732
  40.2 3.8 %collective-permute-start = (bf16[512,512]{1,0:T(8,128)(2,1)S(1)}, bf16[512,512]{1,0:T(8,128)(2,1)S(1)}, u32[]{:S(2)}, u32[]{:S(2)}) collective-permute-start(bf16[512,512]{1,0:T(8,128)(2,1)S(1)} %get-tuple-element.17.mine), channel_id=1, source_target_pairs={{0,4},{4,0},{8,12},{12,8},{16,20},{20,16},{24,28},{28,24},{32,36},... | collective-permute-start | bytes 1572872 | tf_op jit(solution)/shard_map/ppermute | solution.py:300
  46.7 30.8 %all-to-all-start.1 = ((f32[32,32,128]{2,1,0:T(8,128)}), f32[32,32,128]{2,1,0:T(8,128)S(1)}, u32[]{:S(2)}, u32[]{:S(2)}) async-start(f32[32,32,128]{2,1,0:T(8,128)} %column.1), calls=%async_computation.1 | async-start | bytes 1048576 | tf_op jit(solution)/shard_map/all_to_all | solution.py:329
  56.4 15.7 %collective-permute-start.3 = (bf16[16,16,256]{2,1,0:T(8,128)(2,1)S(1)}, bf16[16,16,256]{2,1,0:T(8,128)(2,1)S(1)}, u32[]{:S(2)}, u32[]{:S(2)}) collective-permute-start(bf16[16,16,256]{2,1,0:T(8,128)(2,1)S(1)} %get-tuple-element.22.refs_0_), channel_id=1, source_target_pairs={{0,448},{64,0},{128,64},{192,128},{256,192},{320,256},{384,320},{4... | collective-permute-start | bytes 393224 | tf_op jit(solution)/shard_map/ppermute | solution.py:326
  60.8 14.8 %collective-permute-start.1 = (bf16[16,16,256]{2,1,0:T(8,128)(2,1)S(1)}, bf16[16,16,256]{2,1,0:T(8,128)(2,1)S(1)}, u32[]{:S(2)}, u32[]{:S(2)}) collective-permute-start(bf16[16,16,256]{2,1,0:T(8,128)(2,1)S(1)} %get-tuple-element.22.refs_0_), channel_id=1, source_target_pairs={{0,64},{64,128},{128,192},{192,256},{256,320},{320,384},{384,448},... | collective-permute-start | bytes 393224 | tf_op jit(solution)/shard_map/ppermute | solution.py:323
  72.1 6.3 %collective-permute-start.4 = (bf16[16,16,256]{2,1,0:T(8,128)(2,1)S(1)}, bf16[16,16,256]{2,1,0:T(8,128)(2,1)S(1)}, u32[]{:S(2)}, u32[]{:S(2)}) collective-permute-start(bf16[16,16,256]{2,1,0:T(8,128)(2,1)S(1)} %collective-permute-done.3.refs_7_), channel_id=1, source_target_pairs={{0,448},{64,0},{128,64},{192,128},{256,192},{320,256},{384,320},{4... | collective-permute-start | bytes 393224 | tf_op jit(solution)/shard_map/ppermute | solution.py:326
  75.5 6.9 %collective-permute-start.2 = (bf16[16,16,256]{2,1,0:T(8,128)(2,1)S(1)}, bf16[16,16,256]{2,1,0:T(8,128)(2,1)S(1)}, u32[]{:S(2)}, u32[]{:S(2)}) collective-permute-start(bf16[16,16,256]{2,1,0:T(8,128)(2,1)S(1)} %collective-permute-done.1.refs_1_), channel_id=1, source_target_pairs={{0,64},{64,128},{128,192},{192,256},{256,320},{320,384},{384,448},... | collective-permute-start | bytes 393224 | tf_op jit(solution)/shard_map/ppermute | solution.py:323
  82.5 23.3 %copy-start.4 = (bf16[512,512]{1,0:T(8,128)(2,1)S(1)}, bf16[512,512]{1,0:T(8,128)(2,1)}, u32[]{:S(2)}) copy-start(bf16[512,512]{1,0:T(8,128)(2,1)} %copy-done.3) | copy-start | bytes 1572868
  82.5 23.3 %copy-start.9 = (s32[16,16]{1,0:T(8,128)S(1)}, s32[16,16]{1,0:T(8,128)}, u32[]{:S(2)}) copy-start(s32[16,16]{1,0:T(8,128)} %pattern.1) | copy-start | bytes 3076
  82.5 27.6 %all-to-all-start.2 = ((f32[64,16,128]{2,1,0:T(8,128)}), f32[64,16,128]{2,1,0:T(8,128)S(1)}, u32[]{:S(2)}, u32[]{:S(2)}) async-start(f32[64,16,128]{2,1,0:T(8,128)} %get-tuple-element.28), calls=%async_computation.2 | async-start | bytes 1048576 | tf_op jit(solution)/shard_map/all_to_all | solution.py:344
  90.8 7.7 %collective-permute-start.5 = (bf16[16,16,256]{2,1,0:T(8,128)(2,1)S(1)}, bf16[16,16,256]{2,1,0:T(8,128)(2,1)S(1)}, u32[]{:S(2)}, u32[]{:S(2)}) collective-permute-start(bf16[16,16,256]{2,1,0:T(8,128)(2,1)S(1)} %collective-permute-done.2.refs_2_), channel_id=1, source_target_pairs={{0,64},{64,128},{128,192},{192,256},{256,320},{320,384},{384,448},... | collective-permute-start | bytes 393224 | tf_op jit(solution)/shard_map/ppermute | solution.py:323
  92.8 7.7 %collective-permute-start.7 = (bf16[16,16,256]{2,1,0:T(8,128)(2,1)S(1)}, bf16[16,16,256]{2,1,0:T(8,128)(2,1)S(1)}, u32[]{:S(2)}, u32[]{:S(2)}) collective-permute-start(bf16[16,16,256]{2,1,0:T(8,128)(2,1)S(1)} %collective-permute-done.4.refs_6_), channel_id=1, source_target_pairs={{0,448},{64,0},{128,64},{192,128},{256,192},{320,256},{384,320},{4... | collective-permute-start | bytes 393224 | tf_op jit(solution)/shard_map/ppermute | solution.py:326
  98.5 7.2 %collective-permute-start.6 = (bf16[16,16,256]{2,1,0:T(8,128)(2,1)S(1)}, bf16[16,16,256]{2,1,0:T(8,128)(2,1)S(1)}, u32[]{:S(2)}, u32[]{:S(2)}) collective-permute-start(bf16[16,16,256]{2,1,0:T(8,128)(2,1)S(1)} %collective-permute-done.5.refs_3_), channel_id=1, source_target_pairs={{0,64},{64,128},{128,192},{192,256},{256,320},{320,384},{384,448},... | collective-permute-start | bytes 393224 | tf_op jit(solution)/shard_map/ppermute | solution.py:323

commit v5 on v4

--- a/solution.py
+++ b/solution.py
@@ -13,14 +13,14 @@
 SMEM = pl.BlockSpec(memory_space=pltpu.SMEM)
 
 
-def call(body, outs, ins, flops, name):
+def call(body, outs, ins, flops, name, grant=16):
     moved = sum(x.size * x.dtype.itemsize for x in list(ins) + list(outs))
     return pl.pallas_call(
         body,
         out_shape=outs,
         in_specs=[SMEM if x.size <= 256 else VMEM for x in ins],
         out_specs=[VMEM] * len(outs),
-        compiler_params=pltpu.CompilerParams(vmem_limit_bytes=40 * 2**20),
+        compiler_params=pltpu.CompilerParams(vmem_limit_bytes=grant * 2**20),
         cost_estimate=pl.CostEstimate(flops=flops, bytes_accessed=moved, transcendentals=0),
         name=name,
     )(*ins)
@@ -65,9 +65,7 @@
     return real, imag
 
 
-def invert_body(
-    shift, weight, pivot_h, pivot_s, panel_h, panel_s, inverse, right, wide, base
-):
+def invert_body(shift, pivot_h, pivot_s, inverse):
     size = pivot_h.shape[0]
     shift_real, shift_imag = shift[0, 0], shift[0, 1]
     margin = pivot_s[...].astype(f32)
@@ -103,44 +101,48 @@
     row_real, row_imag = scales(1)
     inv_real = row_real * sum_real - row_imag * sum_imag
     inv_imag = row_real * sum_imag + row_imag * sum_real
-    inv_pair = both_of(split(jnp.concatenate([inv_real, inv_imag], axis=1)), block)
-    inverse[0] = inv_pair[0]
-    inverse[1] = inv_pair[1]
-    first_device = (lax.axis_index("row") == 0) & (lax.axis_index("col") == 0)
-    density = weight[0, 0] * inv_imag + weight[0, 1] * inv_real
-    base[...] = jnp.where(first_device, density.T, 0.0)
-    coupling_real, coupling_imag = couple(panel_h[...], panel_s[...], shift_real, shift_imag)
-    coupling = jnp.concatenate([coupling_real, coupling_imag], axis=1)
-    solved = (dot(coupling, inv_pair[0]) + dot(coupling, inv_pair[1])).astype(bf16)
+    inverse[0], inverse[1] = split(jnp.concatenate([inv_real, inv_imag], axis=1))
+
+
+def solve(rows_h, rows_s, shift, inverse):
+    coupling = jnp.concatenate(couple(rows_h, rows_s, shift[0, 0], shift[0, 1]), axis=1)
+    return (dot(coupling, block(inverse[0])) + dot(coupling, block(inverse[1]))).astype(bf16)
+
+
+def local_body(shift, weight, panel_h, panel_s, inverse, right, base):
+    size = panel_h.shape[1]
+    solved = solve(panel_h[...], panel_s[...], shift, inverse)
     right[:size] = solved[:, :size]
     right[size:] = solved[:, size:]
-    wide[:size] = jnp.concatenate([coupling_real, -coupling_imag], axis=1)
-    wide[size:] = jnp.concatenate([coupling_imag, coupling_real], axis=1)
+    whole = inverse[0].astype(f32) + inverse[1].astype(f32)
+    density = weight[0, 0] * whole[:, size:] + weight[0, 1] * whole[:, :size]
+    first_device = (lax.axis_index("row") == 0) & (lax.axis_index("col") == 0)
+    base[...] = jnp.where(first_device, density.T, 0.0)
 
 
 def pack_body(panel_h, panel_s, front_h, front_s, out, panels, fronts, sems):
     half = panels.shape[1] // 2
-    share, size = fronts.shape[0], out.shape[2]
-    pole = lax.axis_index("pole")
+    share, size = fronts.shape[1], out.shape[2]
     shares = panels.shape[1] // share
     at = pl.ds(pl.multiple_of(lax.axis_index("col") * 2 * half, 2 * half), 2 * half)
-    of = pl.ds(pl.multiple_of(lax.rem(pole, shares) * share, share), share)
-    copy_h = pltpu.make_async_copy(panel_h.at[at], panels.at[0], sems.at[0])
-    copy_s = pltpu.make_async_copy(panel_s.at[at], panels.at[1], sems.at[1])
-    share_h = pltpu.make_async_copy(front_h.at[of], fronts, sems.at[2])
-    share_s = pltpu.make_async_copy(front_s.at[of], fronts, sems.at[2])
-    copy_h.start()
-    copy_s.start()
-    pl.when(pole < shares)(share_h.start)
-    pl.when(pole >= shares)(share_s.start)
-    copy_h.wait()
-    copy_s.wait()
-    share_h.wait()
+    of = pl.ds(pl.multiple_of(lax.rem(lax.axis_index("pole"), shares) * share, share), share)
+    copies = [
+        pltpu.make_async_copy(panel_h.at[at], panels.at[0], sems.at[0]),
+        pltpu.make_async_copy(panel_s.at[at], panels.at[1], sems.at[1]),
+        pltpu.make_async_copy(front_h.at[of], fronts.at[0], sems.at[2]),
+        pltpu.make_async_copy(front_s.at[of], fronts.at[1], sems.at[3]),
+    ]
+    for copy in copies:
+        copy.start()
+    for copy in copies:
+        copy.wait()
     for row in range(out.shape[0]):
         core = row % 2
-        out[row, :half] = panels[0, core * half : (core + 1) * half]
-        out[row, half : 2 * half] = panels[1, core * half : (core + 1) * half]
-        out[row, 2 * half :] = fronts[:, row * size : (row + 1) * size]
+        for part in range(2):
+            low = part * half
+            out[row, low : low + half] = panels[part, core * half : (core + 1) * half]
+            low = 2 * half + part * share
+            out[row, low : low + share] = fronts[part, :, row * size : (row + 1) * size]
 
 
 def solve_body(shift, received, inverse, solved, share):
@@ -148,8 +150,7 @@
     half = solved.shape[0] // strips
     rows_h = received[:, :half].reshape(strips * half, size)
     rows_s = received[:, half : 2 * half].reshape(strips * half, size)
-    coupling = jnp.concatenate(couple(rows_h, rows_s, shift[0, 0], shift[0, 1]), axis=1)
-    solved[...] = (dot(coupling, inverse[0]) + dot(coupling, inverse[1])).astype(bf16)
+    solved[...] = solve(rows_h, rows_s, shift, inverse)
     share[...] = received[:, 2 * half :]
 
 
@@ -214,27 +215,42 @@
         out[index * half : (index + 1) * half] = jnp.concatenate(strips, axis=1)
 
 
-def schur_body(shift, pattern, mine, other, wide, *refs):
-    shares, out, front = refs[:-2], refs[-2], refs[-1]
-    poles, strips, share, size = front.shape
+def update_body(shift, panel_h, panel_s, mine, other, out):
+    strips, rows = out.shape[0], out.shape[1] * out.shape[2]
+    half = mine.shape[0] // strips
+    group = 4
+    top, bottom = ordered(mine[...], other[...])
+    real, imag = couple(panel_h[...], panel_s[...], shift[0, 0], shift[0, 1])
+    wide = jnp.concatenate(
+        [jnp.concatenate([real, -imag], axis=1), jnp.concatenate([imag, real], axis=1)], axis=0
+    )
+    for first in range(0, strips, group):
+        solved = jnp.concatenate(
+            [
+                member[strip * half : (strip + 1) * half]
+                for strip in range(first, first + group)
+                for member in (top, bottom)
+            ],
+            axis=0,
+        )
+        update = contract(solved, wide, 1, 1)
+        out[first : first + group] = update.reshape((group,) + out.shape[1:])
+
+
+def schur_body(shift, pattern, update, *refs):
+    shares, out = refs[:-1], refs[-1]
+    strips, count, share, size = out.shape[1:]
     pole = lax.axis_index("pole")
     row = lax.axis_index("row")
+    shift_real, shift_imag = shift[0, 0], shift[0, 1]
     for step, member in enumerate(shares):
-        front[lax.rem(pole + poles - step, poles)] = member[...]
-    shift_real, shift_imag = shift[0, 0], shift[0, 1]
-    half = mine.shape[0] // strips
-    top, bottom = ordered(mine[...], other[...])
-    for strip in range(strips):
-        rows = slice(strip * half, (strip + 1) * half)
-        solved = jnp.concatenate([top[rows], bottom[rows]], axis=0)
-        update = contract(solved, wide[...], 1, 1)
-        mask = pattern[strip, row].astype(f32)
-        for part in range(poles // 2):
-            at = slice(part * share, (part + 1) * share)
-            margin = mask * front[poles // 2 + part, strip].astype(f32)
-            real = mask * front[part, strip].astype(f32) - shift_real * margin
-            out[0, strip, at] = (real - update[at, :size]).astype(bf16)
-            out[1, strip, at] = (-shift_imag * margin - update[at, size:]).astype(bf16)
+        at = lax.rem(pole + count - step, count)
+        for strip in range(strips):
+            mask = pattern[strip, row].astype(f32)
+            margin = mask * member[strip, share:].astype(f32)
+            real = mask * member[strip, :share].astype(f32) - shift_real * margin
+            out[0, strip, at] = (real - update[strip, at, :, :size]).astype(bf16)
+            out[1, strip, at] = (-shift_imag * margin - update[strip, at, :, size:]).astype(bf16)
 
 
 def shards(
@@ -259,45 +275,46 @@
     half = width // 2
     neighbour = [(i, i ^ 1) for i in range(row_count)]
 
-    share = 2 * width // pole_count
-    params = pltpu.CompilerParams(vmem_limit_bytes=40 * 2**20)
+    quarters = 4
+    share = width // quarters
 
     (sent,) = pl.pallas_call(
         pack_body,
-        out_shape=[shape(row_count, width + share, size)],
+        out_shape=[shape(row_count, width + 2 * share, size)],
         in_specs=[pl.BlockSpec(memory_space=pl.ANY)] * 4,
         out_specs=[VMEM],
         scratch_shapes=[
             pltpu.VMEM((2, width, size), bf16),
-            pltpu.VMEM((share, row_count * size), bf16),
-            pltpu.SemaphoreType.DMA((3,)),
+            pltpu.VMEM((2, share, row_count * size), bf16),
+            pltpu.SemaphoreType.DMA((4,)),
         ],
-        compiler_params=params,
         cost_estimate=pl.CostEstimate(flops=0, bytes_accessed=2**20, transcendentals=0),
         name="pack",
     )(panel_h, panel_s, front_h, front_s)
     received = lax.all_to_all(sent, "row", split_axis=0, concat_axis=0, tiled=True)
 
-    inverse, right, wide, base = call(
+    (inverse,) = call(
         invert_body,
-        [
-            shape(2, 2 * size, 2 * size),
-            shape(2 * size, size),
-            shape(2 * size, 2 * size),
-            shape(size, size, dtype=f32),
-        ],
-        [pole_shift, pole_weight, pivot_h, pivot_s, panel_h, panel_s],
+        [shape(2, size, 2 * size)],
+        [pole_shift, pivot_h, pivot_s],
         6 * 4 * 3 * 2 * size**3,
         "pivot_inverse",
     )
     mine, shared = call(
         solve_body,
-        [shape(row_count * half, 2 * size), shape(row_count, share, size)],
+        [shape(row_count * half, 2 * size), shape(row_count, 2 * share, size)],
         [pole_shift, received, inverse],
         2 * 8 * row_count * half * size * size,
         "solved_rows",
     )
     other = lax.ppermute(mine, "row", neighbour)
+    right, base = call(
+        local_body,
+        [shape(2 * size, size), shape(size, size, dtype=f32)],
+        [pole_shift, pole_weight, panel_h, panel_s, inverse],
+        2 * 8 * size**3,
+        "local_rows",
+    )
 
     ancestor = ancestor_inverse.reshape(2, row_count, width, size)
     (both,) = pl.pallas_call(
@@ -306,26 +323,13 @@
         in_specs=[SMEM] + [VMEM] * 5,
         out_specs=[VMEM],
         scratch_shapes=[pltpu.VMEM((row_count, width, 2 * size), bf16)],
-        compiler_params=pltpu.CompilerParams(vmem_limit_bytes=40 * 2**20),
+        compiler_params=pltpu.CompilerParams(vmem_limit_bytes=16 * 2**20),
         cost_estimate=pl.CostEstimate(
             flops=8 * row_count * width * size * size, bytes_accessed=4 * 2**20, transcendentals=0
         ),
         name="column",
     )(pole_weight, mine, other, ancestor, right, base)
 
-    shared, both = lax.optimization_barrier((shared, both))
-    onward = [(i, (i + 1) % pole_count) for i in range(pole_count)]
-    back = [(i, (i - 1) % pole_count) for i in range(pole_count)]
-    shares = {0: shared}
-
-    def go_round(steps):
-        for step in steps:
-            shares[step + 1] = lax.ppermute(shares[step], "pole", onward)
-            if step + 1 < pole_count // 2:
-                before = shares[(pole_count - step) % pole_count]
-                shares[pole_count - step - 1] = lax.ppermute(before, "pole", back)
-
-    go_round(range(2))
     both = lax.all_to_all(both, ("pole", "col"), split_axis=0, concat_axis=0, tiled=True)
     spread, rows_out = call(
         sums_body,
@@ -337,25 +341,30 @@
         0,
         "sums",
     )
-    spread, shares[2], shares[pole_count - 2] = lax.optimization_barrier(
-        (spread, shares[2], shares[pole_count - 2])
-    )
-    go_round(range(2, pole_count // 2))
+    shared, spread = lax.optimization_barrier((shared, spread))
     spread = lax.all_to_all(spread, ("row", "col"), split_axis=0, concat_axis=0, tiled=True)
     (pivot_out,) = call(pivot_body, [shape(piece, size, dtype=f32)], [spread], 0, "pivot")
 
-    (schur,) = pl.pallas_call(
+    onward = [(i, (i + 1) % pole_count) for i in range(pole_count)]
+    back = [(i, (i - 1) % pole_count) for i in range(pole_count)]
+    before = lax.ppermute(shared, "pole", onward)
+    after = lax.ppermute(shared, "pole", back)
+    second = lax.ppermute(before, "pole", onward)
+
+    (update,) = call(
+        update_body,
+        [shape(row_count, quarters, share, 2 * size, dtype=f32)],
+        [pole_shift, panel_h, panel_s, mine, other],
+        8 * row_count * width * size * size,
+        "update",
+    )
+    (schur,) = call(
         schur_body,
-        out_shape=[shape(2, row_count, width, size)],
-        in_specs=[SMEM] * 2 + [VMEM] * (3 + pole_count),
-        out_specs=[VMEM],
-        scratch_shapes=[pltpu.VMEM((pole_count, row_count, share, size), bf16)],
-        compiler_params=params,
-        cost_estimate=pl.CostEstimate(
-            flops=8 * row_count * width * size * size, bytes_accessed=4 * 2**20, transcendentals=0
-        ),
-        name="schur",
-    )(pole_shift, pattern, mine, other, wide, *[shares[step] for step in range(pole_count)])
+        [shape(2, row_count, quarters, share, size)],
+        [pole_shift, pattern, update, shared, before, second, after],
+        0,
+        "schur",
+    )
     return (schur.reshape(1, 2, row_count, 1, width, size), rows_out.T, pivot_out.T)
 
 

time: 112 us -> 104 us (0.929)
  blocking collectives: 0 us -> 26 us
  starting transfers between devices: 52 us -> 30.1 us
  waiting for transfers between devices: 35.8 us -> 29.4 us
  local copies, waits for them, and re-layouts: 6.93 us -> 1.1 us
    all_to_all x0 -> x1, blocking collectives: none -> 26 us  [shards(): lax.all_to_all(both, ('pole', 'col'), split_axis=0, concat_axis=0, tiled=...]
    ppermute x7 -> x3, starting transfers between devices: 20.1 us -> 8.4 us  [the longest x1 4.28 us: shards(): after = lax.ppermute(shared, 'pole', back)]
    all_to_all x1 -> x0, starting transfers between devices: 9.67 us -> none  [shards(): lax.all_to_all(both, ('pole', 'col'), split_axis=0, concat_axis=0, tiled=...]
    ppermute x7 -> x3, waiting for transfers between devices: 20 us -> 10.6 us  [the longest x1 6.36 us: shards(): second = lax.ppermute(before, 'pole', onward)]
    unnamed x32 -> x26, local copies, waits for them, and re-layouts: 6.93 us -> 1.1 us
    all_to_all x1, waiting for transfers between devices: 13.9 us -> 18.8 us  [shards(): lax.all_to_all(sent, 'row', split_axis=0, concat_axis=0, tiled=True)]
    pallas_call x4 -> x7, Pallas kernels: 7.11 us -> 10.9 us  [call(): pl.pallas_call(body, out_shape=outs, in_specs=[SMEM if x.size <= 256 else...]
    pallas_call x2 -> x1, Pallas kernels: 5.43 us -> 2.03 us  [shards(): pl.pallas_call(pack_body, out_shape=[shape(row_count, width + 2 * share,...]
  transfers between devices with their start and end apart: 11 -> 6, of which waited for: 6 -> 3; matrix products, arithmetic and copies ran while one was open for 0% -> 0% of each run, Pallas kernels for 9% -> 8%
where the time goes in v5:
time: 104 us; the launch traced here: 102 us
  starting transfers between devices  30.1 us (29%)
  waiting for transfers between devices  29.4 us (28%)
  blocking collectives  26 us (25%)
  Pallas kernels  14.8 us (14%)
  local copies, waits for them, and re-layouts  1.1 us (1%)
    all_to_all x1, blocking collectives, shards(): lax.all_to_all(both, ('pole', 'col'), split_axis=0, concat_axis=0, tiled=...  26 us
    all_to_all x1, waiting for transfers between devices, shards(): lax.all_to_all(sent, 'row', split_axis=0, concat_axis=0, tiled=True)  18.8 us
    all_to_all x1, starting transfers between devices, shards(): lax.all_to_all(sent, 'row', split_axis=0, concat_axis=0, tiled=True)  11.8 us
    pallas_call x7, Pallas kernels, call(): pl.pallas_call(body, out_shape=outs, in_specs=[SMEM if x.size <= 256 else...  10.9 us
    all_to_all x1, starting transfers between devices, shards(): lax.all_to_all(spread, ('row', 'col'), split_axis=0, concat_axis=0, tiled...  7.92 us
    ppermute x1, waiting for transfers between devices, shards(): second = lax.ppermute(before, 'pole', onward)  6.36 us
    ppermute x1, starting transfers between devices, shards(): after = lax.ppermute(shared, 'pole', back)  4.28 us
    ppermute x1, waiting for transfers between devices, shards(): before = lax.ppermute(shared, 'pole', onward)  4.23 us
  transfers between devices with their start and end apart: 6, of which 3 were waited for; matrix products, arithmetic and copies ran while one was open for 0% of the time, Pallas kernels for 8%

profile of v5, /device:TPU:1, one launch (start us, length us, event | category | flops | bytes accessed | tf_op | source)
XLA Modules:
  0.0 102.3 jit_solution(5063825780202362944)
XLA Ops:
  0.6 0.0 copy-start.7
  0.6 0.0 copy-start.10
  0.7 0.0 copy-start.9
  0.7 2.0 %pack.1 = bf16[16,96,256]{2,1,0:T(8,128)(2,1)} custom-call(bf16[256,256]{1,0:T(8,128)(2,1)} %panel_h.5, bf16[256,256]{1,0:T(8,128)(2,1)} %panel_s.5, bf16[64,4096]{1,0:T(8,128)(2,1)} %front_h.1, bf16[64,4096]{1,0:T(8,128)(2,1)} %front_s.1), custom_call_target="tpu_custom_call" | custom-call | bytes 1048576 | tf_op jit(solution)/shard_map/pack/pallas_call | solution.py:281
  2.7 11.8 %all-to-all-start = ((bf16[16,96,256]{2,1,0:T(8,128)(2,1)}), bf16[16,96,256]{2,1,0:T(8,128)(2,1)S(1)}, u32[]{:S(2)}, u32[]{:S(2)}) async-start(bf16[16,96,256]{2,1,0:T(8,128)(2,1)} %pack.1), calls=%async_computation | async-start | bytes 1572864 | tf_op jit(solution)/shard_map/all_to_all | solution.py:294
  14.5 0.0 copy-done.7
  14.5 0.0 copy-done.10
  14.6 0.0 copy-done.9
  14.6 0.0 copy-start.1
  14.6 0.0 copy-start.2
  14.6 0.0 copy-start.8
  14.6 3.8 %pivot_inverse.1.inverse = bf16[2,256,512]{2,1,0:T(8,128)(2,1)S(1)} custom-call(f32[1,2]{1,0:T(1,128)S(1)} %copy-done.7, bf16[256,256]{1,0:T(8,128)(2,1)S(1)} %copy-done.9, bf16[256,256]{1,0:T(8,128)(2,1)S(1)} %copy-done.10), custom_call_target="tpu_custom_call" | custom-call | flops 2415919104 | bytes 786440 | tf_op jit(solution)/shard_map/pivot_inverse/pallas_call | solution.py:18
  18.4 0.0 copy-start.11
  18.4 0.0 copy-start
  18.4 18.8 %all-to-all-done.received = bf16[16,96,256]{2,1,0:T(8,128)(2,1)S(1)} async-done(((bf16[16,96,256]{2,1,0:T(8,128)(2,1)}), bf16[16,96,256]{2,1,0:T(8,128)(2,1)S(1)}, u32[]{:S(2)}, u32[]{:S(2)}) %all-to-all-start) | async-done | bytes 786464 | tf_op jit(solution)/shard_map/all_to_all | solution.py:294
  37.2 1.3 %solved_rows.1 = (bf16[512,512]{1,0:T(8,128)(2,1)S(1)}, bf16[16,32,256]{2,1,0:T(8,128)(2,1)S(1)}) custom-call(f32[1,2]{1,0:T(1,128)S(1)} %copy-done.7, bf16[16,96,256]{2,1,0:T(8,128)(2,1)S(1)} %all-to-all-done.received, bf16[2,256,512]{2,1,0:T(8,128)(2,1)S(1)} %pivot_inverse.1.inverse), custom_call_target="tpu_custom_call" | custom-call | flops 536870912 | bytes 2097160 | tf_op jit(solution)/shard_map/solved_rows/pallas_call | solution.py:18
  38.5 0.0 copy-done.11
  38.5 0.0 copy-start.4
  38.5 1.9 %collective-permute-start = (bf16[512,512]{1,0:T(8,128)(2,1)S(1)}, bf16[512,512]{1,0:T(8,128)(2,1)S(1)}, u32[]{:S(2)}, u32[]{:S(2)}) collective-permute-start(bf16[512,512]{1,0:T(8,128)(2,1)S(1)} %get-tuple-element.11.mine), channel_id=1, source_target_pairs={{0,4},{4,0},{8,12},{12,8},{16,20},{20,16},{24,28},{28,24},{32,36},... | collective-permute-start | bytes 1572872 | tf_op jit(solution)/shard_map/ppermute | solution.py:310
  40.4 0.0 copy-done.1
  40.4 0.0 copy-done.2
  40.4 0.0 copy-done.8
  40.4 0.0 copy-start.12
  40.5 1.0 %copy-done.12 = bf16[2,256,512]{2,1,0:T(8,128)(2,1)S(1)} copy-done((bf16[2,256,512]{2,1,0:T(8,128)(2,1)S(1)}, bf16[2,256,512]{2,1,0:T(8,128)(2,1)}, u32[]{:S(2)}) %copy-start.12) | copy-done | bytes 524312
  41.5 1.0 local_rows.1
  42.5 0.0 collective-permute-done.other
  42.5 0.0 copy-done
  42.5 1.9 %column.1 = f32[32,32,128]{2,1,0:T(8,128)S(1)} custom-call(f32[1,2]{1,0:T(1,128)S(1)} %copy-done.8, bf16[512,512]{1,0:T(8,128)(2,1)S(1)} %get-tuple-element.11.mine, bf16[512,512]{1,0:T(8,128)(2,1)S(1)} %collective-permute-done.other, bf16[2,16,64,256]{3,2,1,0:T(8,128)(2,1)S(1)} %bitcast.6, bf16[512,256]{1,0:T(8,128)(2,1)S(1)} %get-tuple-element.13.right, ...), custom_call_target="tpu_custom_call" | custom-call | flops 536870912 | bytes 4194304 | tf_op jit(solution)/shard_map/column/pallas_call | solution.py:320
  44.4 0.0 copy-start.3
  44.4 26.0 %all_to_all.15.parts = f32[32,32,128]{2,1,0:T(8,128)S(1)} all-to-all(f32[32,32,128]{2,1,0:T(8,128)S(1)} %column.1), channel_id=1, replica_groups=mesh['pole'=8,'row'=16,'col'=4] {'pole','col'}, dimensions={0} | all-to-all | bytes 1048576 | tf_op jit(solution)/shard_map/all_to_all | solution.py:333
  70.4 0.0 copy-done.4
  70.4 0.9 sums.1
  71.3 0.0 copy-start.5
  71.3 0.0 copy-start.6
  71.3 7.9 %all-to-all-start.2 = ((f32[64,16,128]{2,1,0:T(8,128)}), f32[64,16,128]{2,1,0:T(8,128)S(1)}, u32[]{:S(2)}, u32[]{:S(2)}) async-start(f32[64,16,128]{2,1,0:T(8,128)} %get-tuple-element.18), calls=%async_computation.2 | async-start | bytes 1048576 | tf_op jit(solution)/shard_map/all_to_all | solution.py:345
  79.2 2.2 %collective-permute-start.1 = (bf16[16,32,256]{2,1,0:T(8,128)(2,1)}, bf16[16,32,256]{2,1,0:T(8,128)(2,1)S(1)}, u32[]{:S(2)}, u32[]{:S(2)}) collective-permute-start(bf16[16,32,256]{2,1,0:T(8,128)(2,1)} %copy-done.4), channel_id=1, source_target_pairs={{0,64},{64,128},{128,192},{192,256},{256,320},{320,384},{384,448},... | collective-permute-start | bytes 786440 | tf_op jit(solution)/shard_map/ppermute | solution.py:350
  81.5 4.3 %collective-permute-start.3 = (bf16[16,32,256]{2,1,0:T(8,128)(2,1)}, bf16[16,32,256]{2,1,0:T(8,128)(2,1)S(1)}, u32[]{:S(2)}, u32[]{:S(2)}) collective-permute-start(bf16[16,32,256]{2,1,0:T(8,128)(2,1)} %copy-done.4), channel_id=1, source_target_pairs={{0,448},{64,0},{128,64},{192,128},{256,192},{320,256},{384,320},{4... | collective-permute-start | bytes 786440 | tf_op jit(solution)/shard_map/ppermute | solution.py:351
  85.8 4.2 %collective-permute-done.1.refs_1_ = bf16[16,32,256]{2,1,0:T(8,128)(2,1)S(1)} collective-permute-done((bf16[16,32,256]{2,1,0:T(8,128)(2,1)}, bf16[16,32,256]{2,1,0:T(8,128)(2,1)S(1)}, u32[]{:S(2)}, u32[]{:S(2)}) %collective-permute-start.1) | collective-permute-done | bytes 262176 | tf_op jit(solution)/shard_map/ppermute | solution.py:350
  90.0 1.9 %collective-permute-start.2 = (bf16[16,32,256]{2,1,0:T(8,128)(2,1)S(1)}, bf16[16,32,256]{2,1,0:T(8,128)(2,1)S(1)}, u32[]{:S(2)}, u32[]{:S(2)}) collective-permute-start(bf16[16,32,256]{2,1,0:T(8,128)(2,1)S(1)} %collective-permute-done.1.refs_1_), channel_id=1, source_target_pairs={{0,64},{64,128},{128,192},{192,256},{256,320},{320,384},{384,448},... | collective-permute-start | bytes 786440 | tf_op jit(solution)/shard_map/ppermute | solution.py:352
  91.9 0.0 copy-done.3
  91.9 1.3 %update.1 = f32[16,4,16,512]{3,2,1,0:T(8,128)S(1)} custom-call(f32[1,2]{1,0:T(1,128)S(1)} %copy-done.7, bf16[256,256]{1,0:T(8,128)(2,1)S(1)} %copy-done.1, bf16[256,256]{1,0:T(8,128)(2,1)S(1)} %copy-done.3, bf16[512,512]{1,0:T(8,128)(2,1)S(1)} %get-tuple-element.11.mine, bf16[512,512]{1,0:T(8,128)(2,1)S(1)} %collective-permute-done.other), custom_call_target="tpu_custom_call" | custom-call | flops 536870912 | bytes 3407880 | tf_op jit(solution)/shard_map/update/pallas_call | solution.py:18
  93.2 0.0 collective-permute-done.3.refs_3_
  93.2 6.4 %collective-permute-done.2.refs_2_ = bf16[16,32,256]{2,1,0:T(8,128)(2,1)S(1)} collective-permute-done((bf16[16,32,256]{2,1,0:T(8,128)(2,1)S(1)}, bf16[16,32,256]{2,1,0:T(8,128)(2,1)S(1)}, u32[]{:S(2)}, u32[]{:S(2)}) %collective-permute-start.2) | collective-permute-done | bytes 262176 | tf_op jit(solution)/shard_map/ppermute | solution.py:352
  99.6 0.0 copy-done.5
  99.6 0.0 copy-done.6
  99.6 2.0 %schur.1 = bf16[2,16,4,16,256]{4,3,2,1,0:T(8,128)(2,1)} custom-call(f32[1,2]{1,0:T(1,128)S(1)} %copy-done.7, s32[16,16]{1,0:T(8,128)S(1)} %copy-done.6, f32[16,4,16,512]{3,2,1,0:T(8,128)S(1)} %update.1, bf16[16,32,256]{2,1,0:T(8,128)(2,1)S(1)} %copy-done.5, bf16[16,32,256]{2,1,0:T(8,128)(2,1)S(1)} %collective-permute-done.1.refs_1_, ...), custom_call_target="tpu_custom_call" | custom-call | bytes 4195336 | tf_op jit(solution)/shard_map/schur/pallas_call | solution.py:18
  101.6 0.0 all-to-all-done.2.parts
  101.6 0.7 pivot.1
Async XLA Ops:
  0.6 13.9 %copy-start.7 = (f32[1,2]{1,0:T(1,128)S(1)}, f32[1,2]{1,0:T(1,128)}, u32[]{:S(2)}) copy-start(f32[1,2]{1,0:T(1,128)} %shift.9) | copy-start | bytes 28
  0.6 13.9 %copy-start.10 = (bf16[256,256]{1,0:T(8,128)(2,1)S(1)}, bf16[256,256]{1,0:T(8,128)(2,1)}, u32[]{:S(2)}) copy-start(bf16[256,256]{1,0:T(8,128)(2,1)} %pivot_s.1) | copy-start | bytes 393220
  0.7 13.9 %copy-start.9 = (bf16[256,256]{1,0:T(8,128)(2,1)S(1)}, bf16[256,256]{1,0:T(8,128)(2,1)}, u32[]{:S(2)}) copy-start(bf16[256,256]{1,0:T(8,128)(2,1)} %pivot_h.1) | copy-start | bytes 393220
  2.7 34.5 %all-to-all-start = ((bf16[16,96,256]{2,1,0:T(8,128)(2,1)}), bf16[16,96,256]{2,1,0:T(8,128)(2,1)S(1)}, u32[]{:S(2)}, u32[]{:S(2)}) async-start(bf16[16,96,256]{2,1,0:T(8,128)(2,1)} %pack.1), calls=%async_computation | async-start | bytes 1572864 | tf_op jit(solution)/shard_map/all_to_all | solution.py:294
  14.6 25.8 %copy-start.1 = (bf16[256,256]{1,0:T(8,128)(2,1)S(1)}, bf16[256,256]{1,0:T(8,128)(2,1)}, u32[]{:S(2)}) copy-start(bf16[256,256]{1,0:T(8,128)(2,1)} %panel_h.5) | copy-start | bytes 393220
  14.6 25.8 %copy-start.2 = (bf16[256,256]{1,0:T(8,128)(2,1)S(1)}, bf16[256,256]{1,0:T(8,128)(2,1)}, u32[]{:S(2)}) copy-start(bf16[256,256]{1,0:T(8,128)(2,1)} %panel_s.5) | copy-start | bytes 393220
  14.6 25.8 %copy-start.8 = (f32[1,2]{1,0:T(1,128)S(1)}, f32[1,2]{1,0:T(1,128)}, u32[]{:S(2)}) copy-start(f32[1,2]{1,0:T(1,128)} %weight.3) | copy-start | bytes 28
  18.4 20.1 %copy-start.11 = (bf16[2,256,512]{2,1,0:T(8,128)(2,1)}, bf16[2,256,512]{2,1,0:T(8,128)(2,1)S(1)}, u32[]{:S(2)}) copy-start(bf16[2,256,512]{2,1,0:T(8,128)(2,1)S(1)} %pivot_inverse.1.inverse) | copy-start | bytes 1572868
  18.4 24.1 %copy-start = (bf16[1,2,16,1,64,256]{5,4,3,2,1,0:T(8,128)(2,1)S(1)}, bf16[1,2,16,1,64,256]{5,4,3,2,1,0:T(8,128)(2,1)}, u32[]{:S(2)}) copy-start(bf16[1,2,16,1,64,256]{5,4,3,2,1,0:T(8,128)(2,1)} %param.19) | copy-start | bytes 3145732
  38.5 32.0 %copy-start.4 = (bf16[16,32,256]{2,1,0:T(8,128)(2,1)}, bf16[16,32,256]{2,1,0:T(8,128)(2,1)S(1)}, u32[]{:S(2)}) copy-start(bf16[16,32,256]{2,1,0:T(8,128)(2,1)S(1)} %get-tuple-element.16.refs_0_) | copy-start | bytes 786436
  38.5 4.0 %collective-permute-start = (bf16[512,512]{1,0:T(8,128)(2,1)S(1)}, bf16[512,512]{1,0:T(8,128)(2,1)S(1)}, u32[]{:S(2)}, u32[]{:S(2)}) collective-permute-start(bf16[512,512]{1,0:T(8,128)(2,1)S(1)} %get-tuple-element.11.mine), channel_id=1, source_target_pairs={{0,4},{4,0},{8,12},{12,8},{16,20},{20,16},{24,28},{28,24},{32,36},... | collective-permute-start | bytes 1572872 | tf_op jit(solution)/shard_map/ppermute | solution.py:310
  40.4 1.0 %copy-start.12 = (bf16[2,256,512]{2,1,0:T(8,128)(2,1)S(1)}, bf16[2,256,512]{2,1,0:T(8,128)(2,1)}, u32[]{:S(2)}) copy-start(bf16[2,256,512]{2,1,0:T(8,128)(2,1)} %copy-done.11) | copy-start | bytes 1572868
  44.4 47.5 %copy-start.3 = (bf16[256,256]{1,0:T(8,128)(2,1)S(1)}, bf16[256,256]{1,0:T(8,128)(2,1)}, u32[]{:S(2)}) copy-start(bf16[256,256]{1,0:T(8,128)(2,1)} %panel_s.5) | copy-start | bytes 393220
  71.3 28.3 %copy-start.5 = (bf16[16,32,256]{2,1,0:T(8,128)(2,1)S(1)}, bf16[16,32,256]{2,1,0:T(8,128)(2,1)}, u32[]{:S(2)}) copy-start(bf16[16,32,256]{2,1,0:T(8,128)(2,1)} %copy-done.4) | copy-start | bytes 786436
  71.3 28.3 %copy-start.6 = (s32[16,16]{1,0:T(8,128)S(1)}, s32[16,16]{1,0:T(8,128)}, u32[]{:S(2)}) copy-start(s32[16,16]{1,0:T(8,128)} %pattern.1) | copy-start | bytes 3076
  71.3 30.3 %all-to-all-start.2 = ((f32[64,16,128]{2,1,0:T(8,128)}), f32[64,16,128]{2,1,0:T(8,128)S(1)}, u32[]{:S(2)}, u32[]{:S(2)}) async-start(f32[64,16,128]{2,1,0:T(8,128)} %get-tuple-element.18), calls=%async_computation.2 | async-start | bytes 1048576 | tf_op jit(solution)/shard_map/all_to_all | solution.py:345
  79.2 10.7 %collective-permute-start.1 = (bf16[16,32,256]{2,1,0:T(8,128)(2,1)}, bf16[16,32,256]{2,1,0:T(8,128)(2,1)S(1)}, u32[]{:S(2)}, u32[]{:S(2)}) collective-permute-start(bf16[16,32,256]{2,1,0:T(8,128)(2,1)} %copy-done.4), channel_id=1, source_target_pairs={{0,64},{64,128},{128,192},{192,256},{256,320},{320,384},{384,448},... | collective-permute-start | bytes 786440 | tf_op jit(solution)/shard_map/ppermute | solution.py:350
  81.5 11.7 %collective-permute-start.3 = (bf16[16,32,256]{2,1,0:T(8,128)(2,1)}, bf16[16,32,256]{2,1,0:T(8,128)(2,1)S(1)}, u32[]{:S(2)}, u32[]{:S(2)}) collective-permute-start(bf16[16,32,256]{2,1,0:T(8,128)(2,1)} %copy-done.4), channel_id=1, source_target_pairs={{0,448},{64,0},{128,64},{192,128},{256,192},{320,256},{384,320},{4... | collective-permute-start | bytes 786440 | tf_op jit(solution)/shard_map/ppermute | solution.py:351
  90.0 9.6 %collective-permute-start.2 = (bf16[16,32,256]{2,1,0:T(8,128)(2,1)S(1)}, bf16[16,32,256]{2,1,0:T(8,128)(2,1)S(1)}, u32[]{:S(2)}, u32[]{:S(2)}) collective-permute-start(bf16[16,32,256]{2,1,0:T(8,128)(2,1)S(1)} %collective-permute-done.1.refs_1_), channel_id=1, source_target_pairs={{0,64},{64,128},{128,192},{192,256},{256,320},{320,384},{384,448},... | collective-permute-start | bytes 786440 | tf_op jit(solution)/shard_map/ppermute | solution.py:352

commit v6 on v5

--- a/solution.py
+++ b/solution.py
@@ -330,6 +330,12 @@
         name="column",
     )(pole_weight, mine, other, ancestor, right, base)
 
+    onward = [(i, (i + 1) % pole_count) for i in range(pole_count)]
+    back = [(i, (i - 1) % pole_count) for i in range(pole_count)]
+    shared, both = lax.optimization_barrier((shared, both))
+    before = lax.ppermute(shared, "pole", onward)
+    after = lax.ppermute(shared, "pole", back)
+
     both = lax.all_to_all(both, ("pole", "col"), split_axis=0, concat_axis=0, tiled=True)
     spread, rows_out = call(
         sums_body,
@@ -341,15 +347,10 @@
         0,
         "sums",
     )
-    shared, spread = lax.optimization_barrier((shared, spread))
+    before, after, spread = lax.optimization_barrier((before, after, spread))
+    second = lax.ppermute(before, "pole", onward)
     spread = lax.all_to_all(spread, ("row", "col"), split_axis=0, concat_axis=0, tiled=True)
     (pivot_out,) = call(pivot_body, [shape(piece, size, dtype=f32)], [spread], 0, "pivot")
-
-    onward = [(i, (i + 1) % pole_count) for i in range(pole_count)]
-    back = [(i, (i - 1) % pole_count) for i in range(pole_count)]
-    before = lax.ppermute(shared, "pole", onward)
-    after = lax.ppermute(shared, "pole", back)
-    second = lax.ppermute(before, "pole", onward)
 
     (update,) = call(
         update_body,

time: 104 us -> 101 us (0.971)
  blocking collectives: 26 us -> 0 us
  waiting for transfers between devices: 29.4 us -> 43.3 us
  starting transfers between devices: 30.1 us -> 39.5 us
    all_to_all x1 -> x0, blocking collectives: 26 us -> none  [shards(): lax.all_to_all(both, ('pole', 'col'), split_axis=0, concat_axis=0, tiled=...]
    all_to_all x0 -> x1, waiting for transfers between devices: none -> 10.4 us  [shards(): lax.all_to_all(both, ('pole', 'col'), split_axis=0, concat_axis=0, tiled=...]
    all_to_all x0 -> x1, starting transfers between devices: none -> 9.8 us  [shards(): lax.all_to_all(both, ('pole', 'col'), split_axis=0, concat_axis=0, tiled=...]
    all_to_all x1, waiting for transfers between devices: 0.01 us -> 4.69 us  [shards(): lax.all_to_all(spread, ('row', 'col'), split_axis=0, concat_axis=0, tiled...]
    ppermute x1, waiting for transfers between devices: 4.23 us -> 1.51 us  [shards(): before = lax.ppermute(shared, 'pole', onward)]
  transfers between devices with their start and end apart: 6 -> 7, of which waited for: 3 -> 6; matrix products, arithmetic and copies ran while one was open for 0% -> 0% of each run, Pallas kernels for 8% -> 9%
where the time goes in v6:
time: 101 us; the launch traced here: 100 us
  waiting for transfers between devices  43.3 us (43%)
  starting transfers between devices  39.5 us (39%)
  Pallas kernels  15.6 us (15%)
  local copies, waits for them, and re-layouts  1.09 us (1%)
    all_to_all x1, waiting for transfers between devices, shards(): lax.all_to_all(sent, 'row', split_axis=0, concat_axis=0, tiled=True)  18.8 us
    all_to_all x1, starting transfers between devices, shards(): lax.all_to_all(sent, 'row', split_axis=0, concat_axis=0, tiled=True)  11.8 us
    pallas_call x7, Pallas kernels, call(): pl.pallas_call(body, out_shape=outs, in_specs=[SMEM if x.size <= 256 else...  10.9 us
    all_to_all x1, waiting for transfers between devices, shards(): lax.all_to_all(both, ('pole', 'col'), split_axis=0, concat_axis=0, tiled=...  10.4 us
    all_to_all x1, starting transfers between devices, shards(): lax.all_to_all(both, ('pole', 'col'), split_axis=0, concat_axis=0, tiled=...  9.8 us
    all_to_all x1, starting transfers between devices, shards(): lax.all_to_all(spread, ('row', 'col'), split_axis=0, concat_axis=0, tiled...  7.64 us
    ppermute x1, waiting for transfers between devices, shards(): second = lax.ppermute(before, 'pole', onward)  7.3 us
    all_to_all x1, waiting for transfers between devices, shards(): lax.all_to_all(spread, ('row', 'col'), split_axis=0, concat_axis=0, tiled...  4.69 us
  transfers between devices with their start and end apart: 7, of which 6 were waited for; matrix products, arithmetic and copies ran while one was open for 0% of the time, Pallas kernels for 9%

profile of v6, /device:TPU:1, one launch (start us, length us, event | category | flops | bytes accessed | tf_op | source)
XLA Modules:
  0.0 100.3 jit_solution(12996463338770246210)
XLA Ops:
  0.6 0.0 copy-start.7
  0.6 0.0 copy-start.10
  0.7 0.0 copy-start.9
  0.7 2.0 %pack.1 = bf16[16,96,256]{2,1,0:T(8,128)(2,1)} custom-call(bf16[256,256]{1,0:T(8,128)(2,1)} %panel_h.5, bf16[256,256]{1,0:T(8,128)(2,1)} %panel_s.5, bf16[64,4096]{1,0:T(8,128)(2,1)} %front_h.1, bf16[64,4096]{1,0:T(8,128)(2,1)} %front_s.1), custom_call_target="tpu_custom_call" | custom-call | bytes 1048576 | tf_op jit(solution)/shard_map/pack/pallas_call | solution.py:281
  2.7 11.8 %all-to-all-start = ((bf16[16,96,256]{2,1,0:T(8,128)(2,1)}), bf16[16,96,256]{2,1,0:T(8,128)(2,1)S(1)}, u32[]{:S(2)}, u32[]{:S(2)}) async-start(bf16[16,96,256]{2,1,0:T(8,128)(2,1)} %pack.1), calls=%async_computation | async-start | bytes 1572864 | tf_op jit(solution)/shard_map/all_to_all | solution.py:294
  14.5 0.0 copy-done.7
  14.5 0.0 copy-done.10
  14.6 0.0 copy-done.9
  14.6 0.0 copy-start.1
  14.6 0.0 copy-start.2
  14.6 0.0 copy-start.8
  14.6 3.8 %pivot_inverse.1.inverse = bf16[2,256,512]{2,1,0:T(8,128)(2,1)S(1)} custom-call(f32[1,2]{1,0:T(1,128)S(1)} %copy-done.7, bf16[256,256]{1,0:T(8,128)(2,1)S(1)} %copy-done.9, bf16[256,256]{1,0:T(8,128)(2,1)S(1)} %copy-done.10), custom_call_target="tpu_custom_call" | custom-call | flops 2415919104 | bytes 786440 | tf_op jit(solution)/shard_map/pivot_inverse/pallas_call | solution.py:18
  18.4 0.0 copy-start.11
  18.4 0.0 copy-start
  18.4 18.8 %all-to-all-done.received = bf16[16,96,256]{2,1,0:T(8,128)(2,1)S(1)} async-done(((bf16[16,96,256]{2,1,0:T(8,128)(2,1)}), bf16[16,96,256]{2,1,0:T(8,128)(2,1)S(1)}, u32[]{:S(2)}, u32[]{:S(2)}) %all-to-all-start) | async-done | bytes 786464 | tf_op jit(solution)/shard_map/all_to_all | solution.py:294
  37.2 1.3 %solved_rows.1 = (bf16[512,512]{1,0:T(8,128)(2,1)S(1)}, bf16[16,32,256]{2,1,0:T(8,128)(2,1)S(1)}) custom-call(f32[1,2]{1,0:T(1,128)S(1)} %copy-done.7, bf16[16,96,256]{2,1,0:T(8,128)(2,1)S(1)} %all-to-all-done.received, bf16[2,256,512]{2,1,0:T(8,128)(2,1)S(1)} %pivot_inverse.1.inverse), custom_call_target="tpu_custom_call" | custom-call | flops 536870912 | bytes 2097160 | tf_op jit(solution)/shard_map/solved_rows/pallas_call | solution.py:18
  38.5 0.0 copy-done.11
  38.5 0.0 copy-start.4
  38.5 1.9 %collective-permute-start = (bf16[512,512]{1,0:T(8,128)(2,1)S(1)}, bf16[512,512]{1,0:T(8,128)(2,1)S(1)}, u32[]{:S(2)}, u32[]{:S(2)}) collective-permute-start(bf16[512,512]{1,0:T(8,128)(2,1)S(1)} %get-tuple-element.14.mine), channel_id=1, source_target_pairs={{0,4},{4,0},{8,12},{12,8},{16,20},{20,16},{24,28},{28,24},{32,36},... | collective-permute-start | bytes 1572872 | tf_op jit(solution)/shard_map/ppermute | solution.py:310
  40.4 0.0 copy-done.1
  40.4 0.0 copy-done.2
  40.4 0.0 copy-done.8
  40.4 0.0 copy-start.12
  40.5 1.0 %copy-done.12 = bf16[2,256,512]{2,1,0:T(8,128)(2,1)S(1)} copy-done((bf16[2,256,512]{2,1,0:T(8,128)(2,1)S(1)}, bf16[2,256,512]{2,1,0:T(8,128)(2,1)}, u32[]{:S(2)}) %copy-start.12) | copy-done | bytes 524312
  41.5 1.0 local_rows.1
  42.5 0.0 collective-permute-done.other
  42.5 0.0 copy-done
  42.5 2.6 %column.1 = f32[32,32,128]{2,1,0:T(8,128)} custom-call(f32[1,2]{1,0:T(1,128)S(1)} %copy-done.8, bf16[512,512]{1,0:T(8,128)(2,1)S(1)} %get-tuple-element.14.mine, bf16[512,512]{1,0:T(8,128)(2,1)S(1)} %collective-permute-done.other, bf16[2,16,64,256]{3,2,1,0:T(8,128)(2,1)S(1)} %bitcast.6, bf16[512,256]{1,0:T(8,128)(2,1)S(1)} %get-tuple-element.16.right, ...), custom_call_target="tpu_custom_call" | custom-call | flops 536870912 | bytes 4194304 | tf_op jit(solution)/shard_map/column/pallas_call | solution.py:320
  45.2 0.0 copy-start.3
  45.2 0.0 copy-done.4
  45.2 9.8 %all-to-all-start.1 = ((f32[32,32,128]{2,1,0:T(8,128)}), f32[32,32,128]{2,1,0:T(8,128)S(1)}, u32[]{:S(2)}, u32[]{:S(2)}) async-start(f32[32,32,128]{2,1,0:T(8,128)} %column.1), calls=%async_computation.1 | async-start | bytes 1048576 | tf_op jit(solution)/shard_map/all_to_all | solution.py:339
  55.0 4.4 %collective-permute-start.2 = (bf16[16,32,256]{2,1,0:T(8,128)(2,1)}, bf16[16,32,256]{2,1,0:T(8,128)(2,1)S(1)}, u32[]{:S(2)}, u32[]{:S(2)}) collective-permute-start(bf16[16,32,256]{2,1,0:T(8,128)(2,1)} %copy-done.4), channel_id=1, source_target_pairs={{0,448},{64,0},{128,64},{192,128},{256,192},{320,256},{384,320},{4... | collective-permute-start | bytes 786440 | tf_op jit(solution)/shard_map/ppermute | solution.py:337
  59.4 1.9 %collective-permute-start.1 = (bf16[16,32,256]{2,1,0:T(8,128)(2,1)}, bf16[16,32,256]{2,1,0:T(8,128)(2,1)S(1)}, u32[]{:S(2)}, u32[]{:S(2)}) collective-permute-start(bf16[16,32,256]{2,1,0:T(8,128)(2,1)} %copy-done.4), channel_id=1, source_target_pairs={{0,64},{64,128},{128,192},{192,256},{256,320},{320,384},{384,448},... | collective-permute-start | bytes 786440 | tf_op jit(solution)/shard_map/ppermute | solution.py:336
  61.3 10.4 %all-to-all-done.1.parts = f32[32,32,128]{2,1,0:T(8,128)S(1)} async-done(((f32[32,32,128]{2,1,0:T(8,128)}), f32[32,32,128]{2,1,0:T(8,128)S(1)}, u32[]{:S(2)}, u32[]{:S(2)}) %all-to-all-start.1) | async-done | bytes 524320 | tf_op jit(solution)/shard_map/all_to_all | solution.py:339
  71.8 0.9 sums.1
  72.7 0.5 collective-permute-done.2.refs_3_
  73.2 1.5 %collective-permute-done.1.refs_1_ = bf16[16,32,256]{2,1,0:T(8,128)(2,1)S(1)} collective-permute-done((bf16[16,32,256]{2,1,0:T(8,128)(2,1)}, bf16[16,32,256]{2,1,0:T(8,128)(2,1)S(1)}, u32[]{:S(2)}, u32[]{:S(2)}) %collective-permute-start.1) | collective-permute-done | bytes 262176 | tf_op jit(solution)/shard_map/ppermute | solution.py:336
  74.7 0.0 copy-start.5
  74.7 0.0 copy-start.6
  74.7 7.6 %all-to-all-start.2 = ((f32[64,16,128]{2,1,0:T(8,128)}), f32[64,16,128]{2,1,0:T(8,128)S(1)}, u32[]{:S(2)}, u32[]{:S(2)}) async-start(f32[64,16,128]{2,1,0:T(8,128)} %get-tuple-element.24), calls=%async_computation.2 | async-start | bytes 1048576 | tf_op jit(solution)/shard_map/all_to_all | solution.py:352
  82.3 1.9 %collective-permute-start.3 = (bf16[16,32,256]{2,1,0:T(8,128)(2,1)S(1)}, bf16[16,32,256]{2,1,0:T(8,128)(2,1)S(1)}, u32[]{:S(2)}, u32[]{:S(2)}) collective-permute-start(bf16[16,32,256]{2,1,0:T(8,128)(2,1)S(1)} %collective-permute-done.1.refs_1_), channel_id=1, source_target_pairs={{0,64},{64,128},{128,192},{192,256},{256,320},{320,384},{384,448},... | collective-permute-start | bytes 786440 | tf_op jit(solution)/shard_map/ppermute | solution.py:351
  84.3 0.0 copy-done.3
  84.3 1.3 %update.1 = f32[16,4,16,512]{3,2,1,0:T(8,128)S(1)} custom-call(f32[1,2]{1,0:T(1,128)S(1)} %copy-done.7, bf16[256,256]{1,0:T(8,128)(2,1)S(1)} %copy-done.1, bf16[256,256]{1,0:T(8,128)(2,1)S(1)} %copy-done.3, bf16[512,512]{1,0:T(8,128)(2,1)S(1)} %get-tuple-element.14.mine, bf16[512,512]{1,0:T(8,128)(2,1)S(1)} %collective-permute-done.other), custom_call_target="tpu_custom_call" | custom-call | flops 536870912 | bytes 3407880 | tf_op jit(solution)/shard_map/update/pallas_call | solution.py:18
  85.6 7.3 %collective-permute-done.3.refs_2_ = bf16[16,32,256]{2,1,0:T(8,128)(2,1)S(1)} collective-permute-done((bf16[16,32,256]{2,1,0:T(8,128)(2,1)S(1)}, bf16[16,32,256]{2,1,0:T(8,128)(2,1)S(1)}, u32[]{:S(2)}, u32[]{:S(2)}) %collective-permute-start.3) | collective-permute-done | bytes 262176 | tf_op jit(solution)/shard_map/ppermute | solution.py:351
  92.9 0.0 copy-done.5
  92.9 0.0 copy-done.6
  92.9 2.0 %schur.1 = bf16[2,16,4,16,256]{4,3,2,1,0:T(8,128)(2,1)} custom-call(f32[1,2]{1,0:T(1,128)S(1)} %copy-done.7, s32[16,16]{1,0:T(8,128)S(1)} %copy-done.6, f32[16,4,16,512]{3,2,1,0:T(8,128)S(1)} %update.1, bf16[16,32,256]{2,1,0:T(8,128)(2,1)S(1)} %copy-done.5, bf16[16,32,256]{2,1,0:T(8,128)(2,1)S(1)} %collective-permute-done.1.refs_1_, ...), custom_call_target="tpu_custom_call" | custom-call | bytes 4195336 | tf_op jit(solution)/shard_map/schur/pallas_call | solution.py:18
  94.9 4.7 %all-to-all-done.2.parts = f32[64,16,128]{2,1,0:T(8,128)S(1)} async-done(((f32[64,16,128]{2,1,0:T(8,128)}), f32[64,16,128]{2,1,0:T(8,128)S(1)}, u32[]{:S(2)}, u32[]{:S(2)}) %all-to-all-start.2) | async-done | bytes 524320 | tf_op jit(solution)/shard_map/all_to_all | solution.py:352
  99.6 0.7 pivot.1
Async XLA Ops:
  0.6 13.9 %copy-start.7 = (f32[1,2]{1,0:T(1,128)S(1)}, f32[1,2]{1,0:T(1,128)}, u32[]{:S(2)}) copy-start(f32[1,2]{1,0:T(1,128)} %shift.9) | copy-start | bytes 28
  0.6 13.9 %copy-start.10 = (bf16[256,256]{1,0:T(8,128)(2,1)S(1)}, bf16[256,256]{1,0:T(8,128)(2,1)}, u32[]{:S(2)}) copy-start(bf16[256,256]{1,0:T(8,128)(2,1)} %pivot_s.1) | copy-start | bytes 393220
  0.7 13.9 %copy-start.9 = (bf16[256,256]{1,0:T(8,128)(2,1)S(1)}, bf16[256,256]{1,0:T(8,128)(2,1)}, u32[]{:S(2)}) copy-start(bf16[256,256]{1,0:T(8,128)(2,1)} %pivot_h.1) | copy-start | bytes 393220
  2.7 34.5 %all-to-all-start = ((bf16[16,96,256]{2,1,0:T(8,128)(2,1)}), bf16[16,96,256]{2,1,0:T(8,128)(2,1)S(1)}, u32[]{:S(2)}, u32[]{:S(2)}) async-start(bf16[16,96,256]{2,1,0:T(8,128)(2,1)} %pack.1), calls=%async_computation | async-start | bytes 1572864 | tf_op jit(solution)/shard_map/all_to_all | solution.py:294
  14.6 25.8 %copy-start.1 = (bf16[256,256]{1,0:T(8,128)(2,1)S(1)}, bf16[256,256]{1,0:T(8,128)(2,1)}, u32[]{:S(2)}) copy-start(bf16[256,256]{1,0:T(8,128)(2,1)} %panel_h.5) | copy-start | bytes 393220
  14.6 25.8 %copy-start.2 = (bf16[256,256]{1,0:T(8,128)(2,1)S(1)}, bf16[256,256]{1,0:T(8,128)(2,1)}, u32[]{:S(2)}) copy-start(bf16[256,256]{1,0:T(8,128)(2,1)} %panel_s.5) | copy-start | bytes 393220
  14.6 25.8 %copy-start.8 = (f32[1,2]{1,0:T(1,128)S(1)}, f32[1,2]{1,0:T(1,128)}, u32[]{:S(2)}) copy-start(f32[1,2]{1,0:T(1,128)} %weight.3) | copy-start | bytes 28
  18.4 20.1 %copy-start.11 = (bf16[2,256,512]{2,1,0:T(8,128)(2,1)}, bf16[2,256,512]{2,1,0:T(8,128)(2,1)S(1)}, u32[]{:S(2)}) copy-start(bf16[2,256,512]{2,1,0:T(8,128)(2,1)S(1)} %pivot_inverse.1.inverse) | copy-start | bytes 1572868
  18.4 24.1 %copy-start = (bf16[1,2,16,1,64,256]{5,4,3,2,1,0:T(8,128)(2,1)S(1)}, bf16[1,2,16,1,64,256]{5,4,3,2,1,0:T(8,128)(2,1)}, u32[]{:S(2)}) copy-start(bf16[1,2,16,1,64,256]{5,4,3,2,1,0:T(8,128)(2,1)} %param.19) | copy-start | bytes 3145732
  38.5 6.7 %copy-start.4 = (bf16[16,32,256]{2,1,0:T(8,128)(2,1)}, bf16[16,32,256]{2,1,0:T(8,128)(2,1)S(1)}, u32[]{:S(2)}) copy-start(bf16[16,32,256]{2,1,0:T(8,128)(2,1)S(1)} %get-tuple-element.18.refs_0_) | copy-start | bytes 786436
  38.5 4.0 %collective-permute-start = (bf16[512,512]{1,0:T(8,128)(2,1)S(1)}, bf16[512,512]{1,0:T(8,128)(2,1)S(1)}, u32[]{:S(2)}, u32[]{:S(2)}) collective-permute-start(bf16[512,512]{1,0:T(8,128)(2,1)S(1)} %get-tuple-element.14.mine), channel_id=1, source_target_pairs={{0,4},{4,0},{8,12},{12,8},{16,20},{20,16},{24,28},{28,24},{32,36},... | collective-permute-start | bytes 1572872 | tf_op jit(solution)/shard_map/ppermute | solution.py:310
  40.4 1.0 %copy-start.12 = (bf16[2,256,512]{2,1,0:T(8,128)(2,1)S(1)}, bf16[2,256,512]{2,1,0:T(8,128)(2,1)}, u32[]{:S(2)}) copy-start(bf16[2,256,512]{2,1,0:T(8,128)(2,1)} %copy-done.11) | copy-start | bytes 1572868
  45.2 39.1 %copy-start.3 = (bf16[256,256]{1,0:T(8,128)(2,1)S(1)}, bf16[256,256]{1,0:T(8,128)(2,1)}, u32[]{:S(2)}) copy-start(bf16[256,256]{1,0:T(8,128)(2,1)} %panel_s.5) | copy-start | bytes 393220
  45.2 26.6 %all-to-all-start.1 = ((f32[32,32,128]{2,1,0:T(8,128)}), f32[32,32,128]{2,1,0:T(8,128)S(1)}, u32[]{:S(2)}, u32[]{:S(2)}) async-start(f32[32,32,128]{2,1,0:T(8,128)} %column.1), calls=%async_computation.1 | async-start | bytes 1048576 | tf_op jit(solution)/shard_map/all_to_all | solution.py:339
  55.0 18.2 %collective-permute-start.2 = (bf16[16,32,256]{2,1,0:T(8,128)(2,1)}, bf16[16,32,256]{2,1,0:T(8,128)(2,1)S(1)}, u32[]{:S(2)}, u32[]{:S(2)}) collective-permute-start(bf16[16,32,256]{2,1,0:T(8,128)(2,1)} %copy-done.4), channel_id=1, source_target_pairs={{0,448},{64,0},{128,64},{192,128},{256,192},{320,256},{384,320},{4... | collective-permute-start | bytes 786440 | tf_op jit(solution)/shard_map/ppermute | solution.py:337
  59.4 15.3 %collective-permute-start.1 = (bf16[16,32,256]{2,1,0:T(8,128)(2,1)}, bf16[16,32,256]{2,1,0:T(8,128)(2,1)S(1)}, u32[]{:S(2)}, u32[]{:S(2)}) collective-permute-start(bf16[16,32,256]{2,1,0:T(8,128)(2,1)} %copy-done.4), channel_id=1, source_target_pairs={{0,64},{64,128},{128,192},{192,256},{256,320},{320,384},{384,448},... | collective-permute-start | bytes 786440 | tf_op jit(solution)/shard_map/ppermute | solution.py:336
  74.7 18.2 %copy-start.5 = (bf16[16,32,256]{2,1,0:T(8,128)(2,1)S(1)}, bf16[16,32,256]{2,1,0:T(8,128)(2,1)}, u32[]{:S(2)}) copy-start(bf16[16,32,256]{2,1,0:T(8,128)(2,1)} %copy-done.4) | copy-start | bytes 786436
  74.7 18.2 %copy-start.6 = (s32[16,16]{1,0:T(8,128)S(1)}, s32[16,16]{1,0:T(8,128)}, u32[]{:S(2)}) copy-start(s32[16,16]{1,0:T(8,128)} %pattern.1) | copy-start | bytes 3076
  74.7 24.9 %all-to-all-start.2 = ((f32[64,16,128]{2,1,0:T(8,128)}), f32[64,16,128]{2,1,0:T(8,128)S(1)}, u32[]{:S(2)}, u32[]{:S(2)}) async-start(f32[64,16,128]{2,1,0:T(8,128)} %get-tuple-element.24), calls=%async_computation.2 | async-start | bytes 1048576 | tf_op jit(solution)/shard_map/all_to_all | solution.py:352
  82.3 10.5 %collective-permute-start.3 = (bf16[16,32,256]{2,1,0:T(8,128)(2,1)S(1)}, bf16[16,32,256]{2,1,0:T(8,128)(2,1)S(1)}, u32[]{:S(2)}, u32[]{:S(2)}) collective-permute-start(bf16[16,32,256]{2,1,0:T(8,128)(2,1)S(1)} %collective-permute-done.1.refs_1_), channel_id=1, source_target_pairs={{0,64},{64,128},{128,192},{192,256},{256,320},{320,384},{384,448},... | collective-permute-start | bytes 786440 | tf_op jit(solution)/shard_map/ppermute | solution.py:351

commit v7 on v6

--- a/solution.py
+++ b/solution.py
@@ -120,29 +120,24 @@
     base[...] = jnp.where(first_device, density.T, 0.0)
 
 
-def pack_body(panel_h, panel_s, front_h, front_s, out, panels, fronts, sems):
-    half = panels.shape[1] // 2
-    share, size = fronts.shape[1], out.shape[2]
-    shares = panels.shape[1] // share
-    at = pl.ds(pl.multiple_of(lax.axis_index("col") * 2 * half, 2 * half), 2 * half)
+def pack_body(panel_h, panel_s, front_h, front_s, out, sem):
+    rows, height, size = out.shape
+    shares = 4
+    width = front_h.shape[0]
+    half, share = width // 2, width // shares
+    strip = lax.axis_index("col") * width
     of = pl.ds(pl.multiple_of(lax.rem(lax.axis_index("pole"), shares) * share, share), share)
-    copies = [
-        pltpu.make_async_copy(panel_h.at[at], panels.at[0], sems.at[0]),
-        pltpu.make_async_copy(panel_s.at[at], panels.at[1], sems.at[1]),
-        pltpu.make_async_copy(front_h.at[of], fronts.at[0], sems.at[2]),
-        pltpu.make_async_copy(front_s.at[of], fronts.at[1], sems.at[3]),
-    ]
-    for copy in copies:
-        copy.start()
-    for copy in copies:
-        copy.wait()
-    for row in range(out.shape[0]):
-        core = row % 2
-        for part in range(2):
+    for row in range(rows):
+        at = pl.ds(pl.multiple_of(strip + (row % 2) * half, half), half)
+        columns = pl.ds(row * size, size)
+        for part, (panel, front) in enumerate(((panel_h, front_h), (panel_s, front_s))):
             low = part * half
-            out[row, low : low + half] = panels[part, core * half : (core + 1) * half]
+            pltpu.make_async_copy(panel.at[at], out.at[row, pl.ds(low, half)], sem).start()
             low = 2 * half + part * share
-            out[row, low : low + share] = fronts[part, :, row * size : (row + 1) * size]
+            pltpu.make_async_copy(
+                front.at[of, columns], out.at[row, pl.ds(low, share)], sem
+            ).start()
+    pltpu.make_async_copy(out, out, sem).wait()
 
 
 def solve_body(shift, received, inverse, solved, share):
@@ -171,8 +166,8 @@
             bottom = member[rows + half : rows + 2 * half, pair * 128 : pair * 128 + 128]
             even = jnp.where(low_lane, top, pltpu.roll(bottom, 64, 1))
             odd = jnp.where(low_lane, pltpu.roll(top, 64, 1), bottom)
-            out[pole * cols + 2 * pair, at : at + half] = even
-            out[pole * cols + 2 * pair + 1, at : at + half] = odd
+            out[pole * cols + 2 * pair, at : at + half] = even.astype(out.dtype)
+            out[pole * cols + 2 * pair + 1, at : at + half] = odd.astype(out.dtype)
 
 
 def column_body(weight, mine, other, ancestor, right, base, out, far):
@@ -198,17 +193,17 @@
 
 def sums_body(parts, spread, rows):
     half, width = parts.shape[1] // 2, rows.shape[1]
-    total = jnp.sum(parts[...], axis=0)
+    total = jnp.sum(parts[...].astype(f32), axis=0)
     rows[:half] = total[:half, :width]
     rows[half:] = total[:half, width:]
-    spread[...] = jnp.broadcast_to(total[None, half:], spread.shape)
+    spread[...] = jnp.broadcast_to(total[None, half:].astype(spread.dtype), spread.shape)
 
 
 def pivot_body(parts, out):
     half = parts.shape[1]
     width = 64
     cols = out.shape[1] // width
-    total = jnp.sum(parts[...].reshape(-1, cols, half, 128), axis=0)
+    total = jnp.sum(parts[...].astype(f32).reshape(-1, cols, half, 128), axis=0)
     for index in range(128 // width):
         lanes = slice(index * width, (index + 1) * width)
         strips = [total[col][:, lanes] for col in range(cols)]
@@ -282,12 +277,8 @@
         pack_body,
         out_shape=[shape(row_count, width + 2 * share, size)],
         in_specs=[pl.BlockSpec(memory_space=pl.ANY)] * 4,
-        out_specs=[VMEM],
-        scratch_shapes=[
-            pltpu.VMEM((2, width, size), bf16),
-            pltpu.VMEM((2, share, row_count * size), bf16),
-            pltpu.SemaphoreType.DMA((4,)),
-        ],
+        out_specs=[pl.BlockSpec(memory_space=pl.ANY)],
+        scratch_shapes=[pltpu.SemaphoreType.DMA],
         cost_estimate=pl.CostEstimate(flops=0, bytes_accessed=2**20, transcendentals=0),
         name="pack",
     )(panel_h, panel_s, front_h, front_s)
@@ -319,7 +310,7 @@
     ancestor = ancestor_inverse.reshape(2, row_count, width, size)
     (both,) = pl.pallas_call(
         column_body,
-        out_shape=[shape(pole_count * col_count, piece, 128, dtype=f32)],
+        out_shape=[shape(pole_count * col_count, piece, 128)],
         in_specs=[SMEM] + [VMEM] * 5,
         out_specs=[VMEM],
         scratch_shapes=[pltpu.VMEM((row_count, width, 2 * size), bf16)],
@@ -340,14 +331,14 @@
     spread, rows_out = call(
         sums_body,
         [
-            shape(row_count * col_count, piece // 2, 128, dtype=f32),
+            shape(row_count * col_count, piece // 2, 128),
             shape(piece, width, dtype=f32),
         ],
         [both],
         0,
         "sums",
     )
-    before, after, spread = lax.optimization_barrier((before, after, spread))
+    before, spread = lax.optimization_barrier((before, spread))
     second = lax.ppermute(before, "pole", onward)
     spread = lax.all_to_all(spread, ("row", "col"), split_axis=0, concat_axis=0, tiled=True)
     (pivot_out,) = call(pivot_body, [shape(piece, size, dtype=f32)], [spread], 0, "pivot")

time: 101 us -> 116 us (1.15)
  Pallas kernels: 15.6 us -> 38.3 us
  waiting for transfers between devices: 43.3 us -> 35.8 us
    pallas_call x1, Pallas kernels: 2.03 us -> 25 us  [shards(): pl.pallas_call(pack_body, out_shape=[shape(row_count, width + 2 * share,...]
    all_to_all x1, waiting for transfers between devices: 4.69 us -> 0.01 us  [shards(): lax.all_to_all(spread, ('row', 'col'), split_axis=0, concat_axis=0, tiled...]
    ppermute x1, waiting for transfers between devices: 7.3 us -> 3.96 us  [shards(): second = lax.ppermute(before, 'pole', onward)]
    ppermute x1, waiting for transfers between devices: 0.53 us -> 2.73 us  [shards(): after = lax.ppermute(shared, 'pole', back)]
    all_to_all x1, waiting for transfers between devices: 10.4 us -> 8.31 us  [shards(): lax.all_to_all(both, ('pole', 'col'), split_axis=0, concat_axis=0, tiled=...]
    ppermute x1, starting transfers between devices: 4.42 us -> 3.06 us  [shards(): after = lax.ppermute(shared, 'pole', back)]
    ppermute x1, starting transfers between devices: 1.92 us -> 3.14 us  [shards(): before = lax.ppermute(shared, 'pole', onward)]
  transfers between devices with their start and end apart: 7 -> 7, of which waited for: 6 -> 5; matrix products, arithmetic and copies ran while one was open for 0% -> 0% of each run, Pallas kernels for 9% -> 8%
where the time goes in v7:
time: 116 us; the launch traced here: 115 us
  starting transfers between devices  39.3 us (34%)
  Pallas kernels  38.3 us (33%)
  waiting for transfers between devices  35.8 us (31%)
    pallas_call x1, Pallas kernels, shards(): pl.pallas_call(pack_body, out_shape=[shape(row_count, width + 2 * share,...  25 us
    all_to_all x1, waiting for transfers between devices, shards(): lax.all_to_all(sent, 'row', split_axis=0, concat_axis=0, tiled=True)  18.8 us
    all_to_all x1, starting transfers between devices, shards(): lax.all_to_all(sent, 'row', split_axis=0, concat_axis=0, tiled=True)  11.8 us
    pallas_call x7, Pallas kernels, call(): pl.pallas_call(body, out_shape=outs, in_specs=[SMEM if x.size <= 256 else...  10.8 us
    all_to_all x1, starting transfers between devices, shards(): lax.all_to_all(both, ('pole', 'col'), split_axis=0, concat_axis=0, tiled=...  9.67 us
    all_to_all x1, waiting for transfers between devices, shards(): lax.all_to_all(both, ('pole', 'col'), split_axis=0, concat_axis=0, tiled=...  8.31 us
    all_to_all x1, starting transfers between devices, shards(): lax.all_to_all(spread, ('row', 'col'), split_axis=0, concat_axis=0, tiled...  7.4 us
    ppermute x1, waiting for transfers between devices, shards(): second = lax.ppermute(before, 'pole', onward)  3.96 us
  transfers between devices with their start and end apart: 7, of which 5 were waited for; matrix products, arithmetic and copies ran while one was open for 0% of the time, Pallas kernels for 8%

profile of v7, /device:TPU:1, one launch (start us, length us, event | category | flops | bytes accessed | tf_op | source)
XLA Modules:
  0.0 115.3 jit_solution(11002565586863312305)
XLA Ops:
  0.6 0.0 copy-start.4
  0.6 0.0 copy-start.7
  0.7 0.0 copy-start.6
  0.7 25.0 %pack.1 = bf16[16,96,256]{2,1,0:T(8,128)(2,1)} custom-call(bf16[256,256]{1,0:T(8,128)(2,1)} %panel_h.5, bf16[256,256]{1,0:T(8,128)(2,1)} %panel_s.5, bf16[64,4096]{1,0:T(8,128)(2,1)} %front_h.1, bf16[64,4096]{1,0:T(8,128)(2,1)} %front_s.1), custom_call_target="tpu_custom_call" | custom-call | bytes 1048576 | tf_op jit(solution)/shard_map/pack/pallas_call | solution.py:276
  25.6 11.8 %all-to-all-start = ((bf16[16,96,256]{2,1,0:T(8,128)(2,1)}), bf16[16,96,256]{2,1,0:T(8,128)(2,1)S(1)}, u32[]{:S(2)}, u32[]{:S(2)}) async-start(bf16[16,96,256]{2,1,0:T(8,128)(2,1)} %pack.1), calls=%async_computation | async-start | bytes 1572864 | tf_op jit(solution)/shard_map/all_to_all | solution.py:285
  37.5 0.0 copy-done.4
  37.5 0.0 copy-done.7
  37.5 0.0 copy-done.6
  37.5 0.0 copy-start.1
  37.5 0.0 copy-start.2
  37.5 0.0 copy-start.5
  37.5 3.8 %pivot_inverse.1.inverse = bf16[2,256,512]{2,1,0:T(8,128)(2,1)S(1)} custom-call(f32[1,2]{1,0:T(1,128)S(1)} %copy-done.4, bf16[256,256]{1,0:T(8,128)(2,1)S(1)} %copy-done.6, bf16[256,256]{1,0:T(8,128)(2,1)S(1)} %copy-done.7), custom_call_target="tpu_custom_call" | custom-call | flops 2415919104 | bytes 786440 | tf_op jit(solution)/shard_map/pivot_inverse/pallas_call | solution.py:18
  41.3 0.0 copy-start.8
  41.3 0.0 copy-start
  41.3 18.8 %all-to-all-done.received = bf16[16,96,256]{2,1,0:T(8,128)(2,1)S(1)} async-done(((bf16[16,96,256]{2,1,0:T(8,128)(2,1)}), bf16[16,96,256]{2,1,0:T(8,128)(2,1)S(1)}, u32[]{:S(2)}, u32[]{:S(2)}) %all-to-all-start) | async-done | bytes 786464 | tf_op jit(solution)/shard_map/all_to_all | solution.py:285
  60.1 1.3 %solved_rows.1 = (bf16[512,512]{1,0:T(8,128)(2,1)S(1)}, bf16[16,32,256]{2,1,0:T(8,128)(2,1)S(1)}) custom-call(f32[1,2]{1,0:T(1,128)S(1)} %copy-done.4, bf16[16,96,256]{2,1,0:T(8,128)(2,1)S(1)} %all-to-all-done.received, bf16[2,256,512]{2,1,0:T(8,128)(2,1)S(1)} %pivot_inverse.1.inverse), custom_call_target="tpu_custom_call" | custom-call | flops 536870912 | bytes 2097160 | tf_op jit(solution)/shard_map/solved_rows/pallas_call | solution.py:18
  61.4 0.0 copy-done.8
  61.4 1.9 %collective-permute-start = (bf16[512,512]{1,0:T(8,128)(2,1)S(1)}, bf16[512,512]{1,0:T(8,128)(2,1)S(1)}, u32[]{:S(2)}, u32[]{:S(2)}) collective-permute-start(bf16[512,512]{1,0:T(8,128)(2,1)S(1)} %get-tuple-element.13.mine), channel_id=1, source_target_pairs={{0,4},{4,0},{8,12},{12,8},{16,20},{20,16},{24,28},{28,24},{32,36},... | collective-permute-start | bytes 1572872 | tf_op jit(solution)/shard_map/ppermute | solution.py:301
  63.3 0.0 copy-done.1
  63.3 0.0 copy-done.2
  63.3 0.0 copy-done.5
  63.4 0.0 copy-start.9
  63.4 1.0 copy-done.9
  64.4 1.0 local_rows.1
  65.4 0.0 collective-permute-done.other
  65.4 0.0 copy-done
  65.4 2.6 %column.1 = bf16[32,32,128]{2,1,0:T(8,128)(2,1)} custom-call(f32[1,2]{1,0:T(1,128)S(1)} %copy-done.5, bf16[512,512]{1,0:T(8,128)(2,1)S(1)} %get-tuple-element.13.mine, bf16[512,512]{1,0:T(8,128)(2,1)S(1)} %collective-permute-done.other, bf16[2,16,64,256]{3,2,1,0:T(8,128)(2,1)S(1)} %bitcast.6, bf16[512,256]{1,0:T(8,128)(2,1)S(1)} %get-tuple-element.15.right, ...), custom_call_target="tpu_custom_call" | custom-call | flops 536870912 | bytes 4194304 | tf_op jit(solution)/shard_map/column/pallas_call | solution.py:311
  68.0 9.7 %all-to-all-start.1 = ((bf16[32,32,128]{2,1,0:T(8,128)(2,1)}), bf16[32,32,128]{2,1,0:T(8,128)(2,1)S(1)}, u32[]{:S(2)}, u32[]{:S(2)}) async-start(bf16[32,32,128]{2,1,0:T(8,128)(2,1)} %column.1), calls=%async_computation.1 | async-start | bytes 524288 | tf_op jit(solution)/shard_map/all_to_all | solution.py:330
  77.7 0.0 copy-start.3
  77.7 3.1 %collective-permute-start.1 = (bf16[16,32,256]{2,1,0:T(8,128)(2,1)S(1)}, bf16[16,32,256]{2,1,0:T(8,128)(2,1)S(1)}, u32[]{:S(2)}, u32[]{:S(2)}) collective-permute-start(bf16[16,32,256]{2,1,0:T(8,128)(2,1)S(1)} %get-tuple-element.17.refs_0_), channel_id=1, source_target_pairs={{0,64},{64,128},{128,192},{192,256},{256,320},{320,384},{384,448},... | collective-permute-start | bytes 786440 | tf_op jit(solution)/shard_map/ppermute | solution.py:327
  80.8 8.3 %all-to-all-done.1.parts = bf16[32,32,128]{2,1,0:T(8,128)(2,1)S(1)} async-done(((bf16[32,32,128]{2,1,0:T(8,128)(2,1)}), bf16[32,32,128]{2,1,0:T(8,128)(2,1)S(1)}, u32[]{:S(2)}, u32[]{:S(2)}) %all-to-all-start.1) | async-done | bytes 262176 | tf_op jit(solution)/shard_map/all_to_all | solution.py:330
  89.1 0.8 sums.1
  89.9 2.0 %collective-permute-done.1.refs_1_ = bf16[16,32,256]{2,1,0:T(8,128)(2,1)S(1)} collective-permute-done((bf16[16,32,256]{2,1,0:T(8,128)(2,1)S(1)}, bf16[16,32,256]{2,1,0:T(8,128)(2,1)S(1)}, u32[]{:S(2)}, u32[]{:S(2)}) %collective-permute-start.1) | collective-permute-done | bytes 262176 | tf_op jit(solution)/shard_map/ppermute | solution.py:327
  91.9 7.4 %all-to-all-start.2 = ((bf16[64,16,128]{2,1,0:T(8,128)(2,1)}), bf16[64,16,128]{2,1,0:T(8,128)(2,1)S(1)}, u32[]{:S(2)}, u32[]{:S(2)}) async-start(bf16[64,16,128]{2,1,0:T(8,128)(2,1)} %get-tuple-element.22), calls=%async_computation.2 | async-start | bytes 524288 | tf_op jit(solution)/shard_map/all_to_all | solution.py:343
  99.3 3.1 %collective-permute-start.3 = (bf16[16,32,256]{2,1,0:T(8,128)(2,1)S(1)}, bf16[16,32,256]{2,1,0:T(8,128)(2,1)S(1)}, u32[]{:S(2)}, u32[]{:S(2)}) collective-permute-start(bf16[16,32,256]{2,1,0:T(8,128)(2,1)S(1)} %get-tuple-element.17.refs_0_), channel_id=1, source_target_pairs={{0,448},{64,0},{128,64},{192,128},{256,192},{320,256},{384,320},{4... | collective-permute-start | bytes 786440 | tf_op jit(solution)/shard_map/ppermute | solution.py:328
  102.4 2.2 %collective-permute-start.2 = (bf16[16,32,256]{2,1,0:T(8,128)(2,1)S(1)}, bf16[16,32,256]{2,1,0:T(8,128)(2,1)S(1)}, u32[]{:S(2)}, u32[]{:S(2)}) collective-permute-start(bf16[16,32,256]{2,1,0:T(8,128)(2,1)S(1)} %collective-permute-done.1.refs_1_), channel_id=1, source_target_pairs={{0,64},{64,128},{128,192},{192,256},{256,320},{320,384},{384,448},... | collective-permute-start | bytes 786440 | tf_op jit(solution)/shard_map/ppermute | solution.py:342
  104.6 1.3 %update.1 = f32[16,4,16,512]{3,2,1,0:T(8,128)S(1)} custom-call(f32[1,2]{1,0:T(1,128)S(1)} %copy-done.4, bf16[256,256]{1,0:T(8,128)(2,1)S(1)} %copy-done.1, bf16[256,256]{1,0:T(8,128)(2,1)S(1)} %copy-done.2, bf16[512,512]{1,0:T(8,128)(2,1)S(1)} %get-tuple-element.13.mine, bf16[512,512]{1,0:T(8,128)(2,1)S(1)} %collective-permute-done.other), custom_call_target="tpu_custom_call" | custom-call | flops 536870912 | bytes 3407880 | tf_op jit(solution)/shard_map/update/pallas_call | solution.py:18
  105.9 2.7 %collective-permute-done.3.refs_3_ = bf16[16,32,256]{2,1,0:T(8,128)(2,1)S(1)} collective-permute-done((bf16[16,32,256]{2,1,0:T(8,128)(2,1)S(1)}, bf16[16,32,256]{2,1,0:T(8,128)(2,1)S(1)}, u32[]{:S(2)}, u32[]{:S(2)}) %collective-permute-start.3) | collective-permute-done | bytes 262176 | tf_op jit(solution)/shard_map/ppermute | solution.py:328
  108.6 4.0 %collective-permute-done.2.refs_2_ = bf16[16,32,256]{2,1,0:T(8,128)(2,1)S(1)} collective-permute-done((bf16[16,32,256]{2,1,0:T(8,128)(2,1)S(1)}, bf16[16,32,256]{2,1,0:T(8,128)(2,1)S(1)}, u32[]{:S(2)}, u32[]{:S(2)}) %collective-permute-start.2) | collective-permute-done | bytes 262176 | tf_op jit(solution)/shard_map/ppermute | solution.py:342
  112.6 0.0 copy-done.3
  112.6 2.0 %schur.1 = bf16[2,16,4,16,256]{4,3,2,1,0:T(8,128)(2,1)} custom-call(f32[1,2]{1,0:T(1,128)S(1)} %copy-done.4, s32[16,16]{1,0:T(8,128)S(1)} %copy-done.3, f32[16,4,16,512]{3,2,1,0:T(8,128)S(1)} %update.1, bf16[16,32,256]{2,1,0:T(8,128)(2,1)S(1)} %get-tuple-element.17.refs_0_, bf16[16,32,256]{2,1,0:T(8,128)(2,1)S(1)} %collective-permute-done.1.refs_1_, ...), custom_call_target="tpu_custom_call" | custom-call | bytes 4195336 | tf_op jit(solution)/shard_map/schur/pallas_call | solution.py:18
  114.6 0.0 all-to-all-done.2.parts
  114.6 0.7 pivot.1
Async XLA Ops:
  0.6 36.8 %copy-start.4 = (f32[1,2]{1,0:T(1,128)S(1)}, f32[1,2]{1,0:T(1,128)}, u32[]{:S(2)}) copy-start(f32[1,2]{1,0:T(1,128)} %shift.9) | copy-start | bytes 28
  0.6 36.8 %copy-start.7 = (bf16[256,256]{1,0:T(8,128)(2,1)S(1)}, bf16[256,256]{1,0:T(8,128)(2,1)}, u32[]{:S(2)}) copy-start(bf16[256,256]{1,0:T(8,128)(2,1)} %pivot_s.1) | copy-start | bytes 393220
  0.7 36.8 %copy-start.6 = (bf16[256,256]{1,0:T(8,128)(2,1)S(1)}, bf16[256,256]{1,0:T(8,128)(2,1)}, u32[]{:S(2)}) copy-start(bf16[256,256]{1,0:T(8,128)(2,1)} %pivot_h.1) | copy-start | bytes 393220
  25.6 34.5 %all-to-all-start = ((bf16[16,96,256]{2,1,0:T(8,128)(2,1)}), bf16[16,96,256]{2,1,0:T(8,128)(2,1)S(1)}, u32[]{:S(2)}, u32[]{:S(2)}) async-start(bf16[16,96,256]{2,1,0:T(8,128)(2,1)} %pack.1), calls=%async_computation | async-start | bytes 1572864 | tf_op jit(solution)/shard_map/all_to_all | solution.py:285
  37.5 25.8 %copy-start.1 = (bf16[256,256]{1,0:T(8,128)(2,1)S(1)}, bf16[256,256]{1,0:T(8,128)(2,1)}, u32[]{:S(2)}) copy-start(bf16[256,256]{1,0:T(8,128)(2,1)} %panel_h.5) | copy-start | bytes 393220
  37.5 25.8 %copy-start.2 = (bf16[256,256]{1,0:T(8,128)(2,1)S(1)}, bf16[256,256]{1,0:T(8,128)(2,1)}, u32[]{:S(2)}) copy-start(bf16[256,256]{1,0:T(8,128)(2,1)} %panel_s.5) | copy-start | bytes 393220
  37.5 25.8 %copy-start.5 = (f32[1,2]{1,0:T(1,128)S(1)}, f32[1,2]{1,0:T(1,128)}, u32[]{:S(2)}) copy-start(f32[1,2]{1,0:T(1,128)} %weight.3) | copy-start | bytes 28
  41.3 20.1 %copy-start.8 = (bf16[2,256,512]{2,1,0:T(8,128)(2,1)}, bf16[2,256,512]{2,1,0:T(8,128)(2,1)S(1)}, u32[]{:S(2)}) copy-start(bf16[2,256,512]{2,1,0:T(8,128)(2,1)S(1)} %pivot_inverse.1.inverse) | copy-start | bytes 1572868
  41.3 24.1 %copy-start = (bf16[1,2,16,1,64,256]{5,4,3,2,1,0:T(8,128)(2,1)S(1)}, bf16[1,2,16,1,64,256]{5,4,3,2,1,0:T(8,128)(2,1)}, u32[]{:S(2)}) copy-start(bf16[1,2,16,1,64,256]{5,4,3,2,1,0:T(8,128)(2,1)} %param.19) | copy-start | bytes 3145732
  61.4 4.0 %collective-permute-start = (bf16[512,512]{1,0:T(8,128)(2,1)S(1)}, bf16[512,512]{1,0:T(8,128)(2,1)S(1)}, u32[]{:S(2)}, u32[]{:S(2)}) collective-permute-start(bf16[512,512]{1,0:T(8,128)(2,1)S(1)} %get-tuple-element.13.mine), channel_id=1, source_target_pairs={{0,4},{4,0},{8,12},{12,8},{16,20},{20,16},{24,28},{28,24},{32,36},... | collective-permute-start | bytes 1572872 | tf_op jit(solution)/shard_map/ppermute | solution.py:301
  63.4 1.0 copy-start.9
  68.0 21.1 %all-to-all-start.1 = ((bf16[32,32,128]{2,1,0:T(8,128)(2,1)}), bf16[32,32,128]{2,1,0:T(8,128)(2,1)S(1)}, u32[]{:S(2)}, u32[]{:S(2)}) async-start(bf16[32,32,128]{2,1,0:T(8,128)(2,1)} %column.1), calls=%async_computation.1 | async-start | bytes 524288 | tf_op jit(solution)/shard_map/all_to_all | solution.py:330
  77.7 34.9 %copy-start.3 = (s32[16,16]{1,0:T(8,128)S(1)}, s32[16,16]{1,0:T(8,128)}, u32[]{:S(2)}) copy-start(s32[16,16]{1,0:T(8,128)} %pattern.1) | copy-start | bytes 3076
  77.7 14.2 %collective-permute-start.1 = (bf16[16,32,256]{2,1,0:T(8,128)(2,1)S(1)}, bf16[16,32,256]{2,1,0:T(8,128)(2,1)S(1)}, u32[]{:S(2)}, u32[]{:S(2)}) collective-permute-start(bf16[16,32,256]{2,1,0:T(8,128)(2,1)S(1)} %get-tuple-element.17.refs_0_), channel_id=1, source_target_pairs={{0,64},{64,128},{128,192},{192,256},{256,320},{320,384},{384,448},... | collective-permute-start | bytes 786440 | tf_op jit(solution)/shard_map/ppermute | solution.py:327
  91.9 22.7 %all-to-all-start.2 = ((bf16[64,16,128]{2,1,0:T(8,128)(2,1)}), bf16[64,16,128]{2,1,0:T(8,128)(2,1)S(1)}, u32[]{:S(2)}, u32[]{:S(2)}) async-start(bf16[64,16,128]{2,1,0:T(8,128)(2,1)} %get-tuple-element.22), calls=%async_computation.2 | async-start | bytes 524288 | tf_op jit(solution)/shard_map/all_to_all | solution.py:343
  99.3 9.3 %collective-permute-start.3 = (bf16[16,32,256]{2,1,0:T(8,128)(2,1)S(1)}, bf16[16,32,256]{2,1,0:T(8,128)(2,1)S(1)}, u32[]{:S(2)}, u32[]{:S(2)}) collective-permute-start(bf16[16,32,256]{2,1,0:T(8,128)(2,1)S(1)} %get-tuple-element.17.refs_0_), channel_id=1, source_target_pairs={{0,448},{64,0},{128,64},{192,128},{256,192},{320,256},{384,320},{4... | collective-permute-start | bytes 786440 | tf_op jit(solution)/shard_map/ppermute | solution.py:328
  102.4 10.2 %collective-permute-start.2 = (bf16[16,32,256]{2,1,0:T(8,128)(2,1)S(1)}, bf16[16,32,256]{2,1,0:T(8,128)(2,1)S(1)}, u32[]{:S(2)}, u32[]{:S(2)}) collective-permute-start(bf16[16,32,256]{2,1,0:T(8,128)(2,1)S(1)} %collective-permute-done.1.refs_1_), channel_id=1, source_target_pairs={{0,64},{64,128},{128,192},{192,256},{256,320},{320,384},{384,448},... | collective-permute-start | bytes 786440 | tf_op jit(solution)/shard_map/ppermute | solution.py:342

commit v8 on v6

--- a/solution.py
+++ b/solution.py
@@ -171,8 +171,8 @@
             bottom = member[rows + half : rows + 2 * half, pair * 128 : pair * 128 + 128]
             even = jnp.where(low_lane, top, pltpu.roll(bottom, 64, 1))
             odd = jnp.where(low_lane, pltpu.roll(top, 64, 1), bottom)
-            out[pole * cols + 2 * pair, at : at + half] = even
-            out[pole * cols + 2 * pair + 1, at : at + half] = odd
+            out[pole * cols + 2 * pair, at : at + half] = even.astype(out.dtype)
+            out[pole * cols + 2 * pair + 1, at : at + half] = odd.astype(out.dtype)
 
 
 def column_body(weight, mine, other, ancestor, right, base, out, far):
@@ -198,17 +198,17 @@
 
 def sums_body(parts, spread, rows):
     half, width = parts.shape[1] // 2, rows.shape[1]
-    total = jnp.sum(parts[...], axis=0)
+    total = jnp.sum(parts[...].astype(f32), axis=0)
     rows[:half] = total[:half, :width]
     rows[half:] = total[:half, width:]
-    spread[...] = jnp.broadcast_to(total[None, half:], spread.shape)
+    spread[...] = jnp.broadcast_to(total[None, half:].astype(spread.dtype), spread.shape)
 
 
 def pivot_body(parts, out):
     half = parts.shape[1]
     width = 64
     cols = out.shape[1] // width
-    total = jnp.sum(parts[...].reshape(-1, cols, half, 128), axis=0)
+    total = jnp.sum(parts[...].astype(f32).reshape(-1, cols, half, 128), axis=0)
     for index in range(128 // width):
         lanes = slice(index * width, (index + 1) * width)
         strips = [total[col][:, lanes] for col in range(cols)]
@@ -319,7 +319,7 @@
     ancestor = ancestor_inverse.reshape(2, row_count, width, size)
     (both,) = pl.pallas_call(
         column_body,
-        out_shape=[shape(pole_count * col_count, piece, 128, dtype=f32)],
+        out_shape=[shape(pole_count * col_count, piece, 128)],
         in_specs=[SMEM] + [VMEM] * 5,
         out_specs=[VMEM],
         scratch_shapes=[pltpu.VMEM((row_count, width, 2 * size), bf16)],
@@ -340,14 +340,14 @@
     spread, rows_out = call(
         sums_body,
         [
-            shape(row_count * col_count, piece // 2, 128, dtype=f32),
+            shape(row_count * col_count, piece // 2, 128),
             shape(piece, width, dtype=f32),
         ],
         [both],
         0,
         "sums",
     )
-    before, after, spread = lax.optimization_barrier((before, after, spread))
+    before, spread = lax.optimization_barrier((before, spread))
     second = lax.ppermute(before, "pole", onward)
     spread = lax.all_to_all(spread, ("row", "col"), split_axis=0, concat_axis=0, tiled=True)
     (pivot_out,) = call(pivot_body, [shape(piece, size, dtype=f32)], [spread], 0, "pivot")

time: 101 us -> 93.3 us (0.924)
  waiting for transfers between devices: 43.3 us -> 35.8 us
    all_to_all x1, waiting for transfers between devices: 4.69 us -> 0.01 us  [shards(): lax.all_to_all(spread, ('row', 'col'), split_axis=0, concat_axis=0, tiled...]
    ppermute x1, waiting for transfers between devices: 7.3 us -> 3.96 us  [shards(): second = lax.ppermute(before, 'pole', onward)]
    ppermute x1, waiting for transfers between devices: 0.53 us -> 2.73 us  [shards(): after = lax.ppermute(shared, 'pole', back)]
    all_to_all x1, waiting for transfers between devices: 10.4 us -> 8.31 us  [shards(): lax.all_to_all(both, ('pole', 'col'), split_axis=0, concat_axis=0, tiled=...]
    ppermute x1, starting transfers between devices: 4.42 us -> 3.06 us  [shards(): after = lax.ppermute(shared, 'pole', back)]
    ppermute x1, starting transfers between devices: 1.92 us -> 3.14 us  [shards(): before = lax.ppermute(shared, 'pole', onward)]
  transfers between devices with their start and end apart: 7 -> 7, of which waited for: 6 -> 5; matrix products, arithmetic and copies ran while one was open for 0% -> 0% of each run, Pallas kernels for 9% -> 10%
where the time goes in v8:
time: 93.3 us; the launch traced here: 92.4 us
  starting transfers between devices  39.3 us (42%)
  waiting for transfers between devices  35.8 us (38%)
  Pallas kernels  15.4 us (17%)
  local copies, waits for them, and re-layouts  1.08 us (1%)
    all_to_all x1, waiting for transfers between devices, shards(): lax.all_to_all(sent, 'row', split_axis=0, concat_axis=0, tiled=True)  18.8 us
    all_to_all x1, starting transfers between devices, shards(): lax.all_to_all(sent, 'row', split_axis=0, concat_axis=0, tiled=True)  11.8 us
    pallas_call x7, Pallas kernels, call(): pl.pallas_call(body, out_shape=outs, in_specs=[SMEM if x.size <= 256 else...  10.8 us
    all_to_all x1, starting transfers between devices, shards(): lax.all_to_all(both, ('pole', 'col'), split_axis=0, concat_axis=0, tiled=...  9.66 us
    all_to_all x1, waiting for transfers between devices, shards(): lax.all_to_all(both, ('pole', 'col'), split_axis=0, concat_axis=0, tiled=...  8.31 us
    all_to_all x1, starting transfers between devices, shards(): lax.all_to_all(spread, ('row', 'col'), split_axis=0, concat_axis=0, tiled...  7.44 us
    ppermute x1, waiting for transfers between devices, shards(): second = lax.ppermute(before, 'pole', onward)  3.96 us
    ppermute x1, starting transfers between devices, shards(): before = lax.ppermute(shared, 'pole', onward)  3.14 us
  transfers between devices with their start and end apart: 7, of which 5 were waited for; matrix products, arithmetic and copies ran while one was open for 0% of the time, Pallas kernels for 10%

profile of v8, /device:TPU:1, one launch (start us, length us, event | category | flops | bytes accessed | tf_op | source)
XLA Modules:
  0.0 92.4 jit_solution(11199854343143983845)
XLA Ops:
  0.6 0.0 copy-start.4
  0.6 0.0 copy-start.7
  0.7 0.0 copy-start.6
  0.7 2.0 %pack.1 = bf16[16,96,256]{2,1,0:T(8,128)(2,1)} custom-call(bf16[256,256]{1,0:T(8,128)(2,1)} %panel_h.5, bf16[256,256]{1,0:T(8,128)(2,1)} %panel_s.5, bf16[64,4096]{1,0:T(8,128)(2,1)} %front_h.1, bf16[64,4096]{1,0:T(8,128)(2,1)} %front_s.1), custom_call_target="tpu_custom_call" | custom-call | bytes 1048576 | tf_op jit(solution)/shard_map/pack/pallas_call | solution.py:281
  2.7 11.8 %all-to-all-start = ((bf16[16,96,256]{2,1,0:T(8,128)(2,1)}), bf16[16,96,256]{2,1,0:T(8,128)(2,1)S(1)}, u32[]{:S(2)}, u32[]{:S(2)}) async-start(bf16[16,96,256]{2,1,0:T(8,128)(2,1)} %pack.1), calls=%async_computation | async-start | bytes 1572864 | tf_op jit(solution)/shard_map/all_to_all | solution.py:294
  14.5 0.0 copy-done.4
  14.5 0.0 copy-done.7
  14.6 0.0 copy-done.6
  14.6 0.0 copy-start.1
  14.6 0.0 copy-start.2
  14.6 0.0 copy-start.5
  14.6 3.8 %pivot_inverse.1.inverse = bf16[2,256,512]{2,1,0:T(8,128)(2,1)S(1)} custom-call(f32[1,2]{1,0:T(1,128)S(1)} %copy-done.4, bf16[256,256]{1,0:T(8,128)(2,1)S(1)} %copy-done.6, bf16[256,256]{1,0:T(8,128)(2,1)S(1)} %copy-done.7), custom_call_target="tpu_custom_call" | custom-call | flops 2415919104 | bytes 786440 | tf_op jit(solution)/shard_map/pivot_inverse/pallas_call | solution.py:18
  18.4 0.0 copy-start.8
  18.4 0.0 copy-start
  18.4 18.8 %all-to-all-done.received = bf16[16,96,256]{2,1,0:T(8,128)(2,1)S(1)} async-done(((bf16[16,96,256]{2,1,0:T(8,128)(2,1)}), bf16[16,96,256]{2,1,0:T(8,128)(2,1)S(1)}, u32[]{:S(2)}, u32[]{:S(2)}) %all-to-all-start) | async-done | bytes 786464 | tf_op jit(solution)/shard_map/all_to_all | solution.py:294
  37.2 1.3 %solved_rows.1 = (bf16[512,512]{1,0:T(8,128)(2,1)S(1)}, bf16[16,32,256]{2,1,0:T(8,128)(2,1)S(1)}) custom-call(f32[1,2]{1,0:T(1,128)S(1)} %copy-done.4, bf16[16,96,256]{2,1,0:T(8,128)(2,1)S(1)} %all-to-all-done.received, bf16[2,256,512]{2,1,0:T(8,128)(2,1)S(1)} %pivot_inverse.1.inverse), custom_call_target="tpu_custom_call" | custom-call | flops 536870912 | bytes 2097160 | tf_op jit(solution)/shard_map/solved_rows/pallas_call | solution.py:18
  38.5 0.0 copy-done.8
  38.5 1.9 %collective-permute-start = (bf16[512,512]{1,0:T(8,128)(2,1)S(1)}, bf16[512,512]{1,0:T(8,128)(2,1)S(1)}, u32[]{:S(2)}, u32[]{:S(2)}) collective-permute-start(bf16[512,512]{1,0:T(8,128)(2,1)S(1)} %get-tuple-element.13.mine), channel_id=1, source_target_pairs={{0,4},{4,0},{8,12},{12,8},{16,20},{20,16},{24,28},{28,24},{32,36},... | collective-permute-start | bytes 1572872 | tf_op jit(solution)/shard_map/ppermute | solution.py:310
  40.4 0.0 copy-done.1
  40.4 0.0 copy-done.2
  40.4 0.0 copy-done.5
  40.4 0.0 copy-start.9
  40.4 1.0 %copy-done.9 = bf16[2,256,512]{2,1,0:T(8,128)(2,1)S(1)} copy-done((bf16[2,256,512]{2,1,0:T(8,128)(2,1)S(1)}, bf16[2,256,512]{2,1,0:T(8,128)(2,1)}, u32[]{:S(2)}) %copy-start.9) | copy-done | bytes 524312
  41.5 1.0 %local_rows.1 = (bf16[512,256]{1,0:T(8,128)(2,1)S(1)}, f32[256,256]{1,0:T(8,128)S(1)}) custom-call(f32[1,2]{1,0:T(1,128)S(1)} %copy-done.4, f32[1,2]{1,0:T(1,128)S(1)} %copy-done.5, bf16[256,256]{1,0:T(8,128)(2,1)S(1)} %copy-done.1, bf16[256,256]{1,0:T(8,128)(2,1)S(1)} %copy-done.2, bf16[2,256,512]{2,1,0:T(8,128)(2,1)S(1)} %copy-done.9), custom_call_target="tpu_custom_call" | custom-call | flops 268435456 | bytes 1310736 | tf_op jit(solution)/shard_map/local_rows/pallas_call | solution.py:18
  42.5 0.0 collective-permute-done.other
  42.5 0.0 copy-done
  42.5 2.6 %column.1 = bf16[32,32,128]{2,1,0:T(8,128)(2,1)} custom-call(f32[1,2]{1,0:T(1,128)S(1)} %copy-done.5, bf16[512,512]{1,0:T(8,128)(2,1)S(1)} %get-tuple-element.13.mine, bf16[512,512]{1,0:T(8,128)(2,1)S(1)} %collective-permute-done.other, bf16[2,16,64,256]{3,2,1,0:T(8,128)(2,1)S(1)} %bitcast.6, bf16[512,256]{1,0:T(8,128)(2,1)S(1)} %get-tuple-element.15.right, ...), custom_call_target="tpu_custom_call" | custom-call | flops 536870912 | bytes 4194304 | tf_op jit(solution)/shard_map/column/pallas_call | solution.py:320
  45.1 9.7 %all-to-all-start.1 = ((bf16[32,32,128]{2,1,0:T(8,128)(2,1)}), bf16[32,32,128]{2,1,0:T(8,128)(2,1)S(1)}, u32[]{:S(2)}, u32[]{:S(2)}) async-start(bf16[32,32,128]{2,1,0:T(8,128)(2,1)} %column.1), calls=%async_computation.1 | async-start | bytes 524288 | tf_op jit(solution)/shard_map/all_to_all | solution.py:339
  54.7 0.0 copy-start.3
  54.7 3.1 %collective-permute-start.1 = (bf16[16,32,256]{2,1,0:T(8,128)(2,1)S(1)}, bf16[16,32,256]{2,1,0:T(8,128)(2,1)S(1)}, u32[]{:S(2)}, u32[]{:S(2)}) collective-permute-start(bf16[16,32,256]{2,1,0:T(8,128)(2,1)S(1)} %get-tuple-element.17.refs_0_), channel_id=1, source_target_pairs={{0,64},{64,128},{128,192},{192,256},{256,320},{320,384},{384,448},... | collective-permute-start | bytes 786440 | tf_op jit(solution)/shard_map/ppermute | solution.py:336
  57.9 8.3 %all-to-all-done.1.parts = bf16[32,32,128]{2,1,0:T(8,128)(2,1)S(1)} async-done(((bf16[32,32,128]{2,1,0:T(8,128)(2,1)}), bf16[32,32,128]{2,1,0:T(8,128)(2,1)S(1)}, u32[]{:S(2)}, u32[]{:S(2)}) %all-to-all-start.1) | async-done | bytes 262176 | tf_op jit(solution)/shard_map/all_to_all | solution.py:339
  66.2 0.8 sums.1
  67.0 2.0 %collective-permute-done.1.refs_1_ = bf16[16,32,256]{2,1,0:T(8,128)(2,1)S(1)} collective-permute-done((bf16[16,32,256]{2,1,0:T(8,128)(2,1)S(1)}, bf16[16,32,256]{2,1,0:T(8,128)(2,1)S(1)}, u32[]{:S(2)}, u32[]{:S(2)}) %collective-permute-start.1) | collective-permute-done | bytes 262176 | tf_op jit(solution)/shard_map/ppermute | solution.py:336
  68.9 7.4 %all-to-all-start.2 = ((bf16[64,16,128]{2,1,0:T(8,128)(2,1)}), bf16[64,16,128]{2,1,0:T(8,128)(2,1)S(1)}, u32[]{:S(2)}, u32[]{:S(2)}) async-start(bf16[64,16,128]{2,1,0:T(8,128)(2,1)} %get-tuple-element.22), calls=%async_computation.2 | async-start | bytes 524288 | tf_op jit(solution)/shard_map/all_to_all | solution.py:352
  76.4 3.1 %collective-permute-start.3 = (bf16[16,32,256]{2,1,0:T(8,128)(2,1)S(1)}, bf16[16,32,256]{2,1,0:T(8,128)(2,1)S(1)}, u32[]{:S(2)}, u32[]{:S(2)}) collective-permute-start(bf16[16,32,256]{2,1,0:T(8,128)(2,1)S(1)} %get-tuple-element.17.refs_0_), channel_id=1, source_target_pairs={{0,448},{64,0},{128,64},{192,128},{256,192},{320,256},{384,320},{4... | collective-permute-start | bytes 786440 | tf_op jit(solution)/shard_map/ppermute | solution.py:337
  79.5 2.2 %collective-permute-start.2 = (bf16[16,32,256]{2,1,0:T(8,128)(2,1)S(1)}, bf16[16,32,256]{2,1,0:T(8,128)(2,1)S(1)}, u32[]{:S(2)}, u32[]{:S(2)}) collective-permute-start(bf16[16,32,256]{2,1,0:T(8,128)(2,1)S(1)} %collective-permute-done.1.refs_1_), channel_id=1, source_target_pairs={{0,64},{64,128},{128,192},{192,256},{256,320},{320,384},{384,448},... | collective-permute-start | bytes 786440 | tf_op jit(solution)/shard_map/ppermute | solution.py:351
  81.7 1.3 %update.1 = f32[16,4,16,512]{3,2,1,0:T(8,128)S(1)} custom-call(f32[1,2]{1,0:T(1,128)S(1)} %copy-done.4, bf16[256,256]{1,0:T(8,128)(2,1)S(1)} %copy-done.1, bf16[256,256]{1,0:T(8,128)(2,1)S(1)} %copy-done.2, bf16[512,512]{1,0:T(8,128)(2,1)S(1)} %get-tuple-element.13.mine, bf16[512,512]{1,0:T(8,128)(2,1)S(1)} %collective-permute-done.other), custom_call_target="tpu_custom_call" | custom-call | flops 536870912 | bytes 3407880 | tf_op jit(solution)/shard_map/update/pallas_call | solution.py:18
  83.0 2.7 %collective-permute-done.3.refs_3_ = bf16[16,32,256]{2,1,0:T(8,128)(2,1)S(1)} collective-permute-done((bf16[16,32,256]{2,1,0:T(8,128)(2,1)S(1)}, bf16[16,32,256]{2,1,0:T(8,128)(2,1)S(1)}, u32[]{:S(2)}, u32[]{:S(2)}) %collective-permute-start.3) | collective-permute-done | bytes 262176 | tf_op jit(solution)/shard_map/ppermute | solution.py:337
  85.7 4.0 %collective-permute-done.2.refs_2_ = bf16[16,32,256]{2,1,0:T(8,128)(2,1)S(1)} collective-permute-done((bf16[16,32,256]{2,1,0:T(8,128)(2,1)S(1)}, bf16[16,32,256]{2,1,0:T(8,128)(2,1)S(1)}, u32[]{:S(2)}, u32[]{:S(2)}) %collective-permute-start.2) | collective-permute-done | bytes 262176 | tf_op jit(solution)/shard_map/ppermute | solution.py:351
  89.7 0.0 copy-done.3
  89.7 2.0 %schur.1 = bf16[2,16,4,16,256]{4,3,2,1,0:T(8,128)(2,1)} custom-call(f32[1,2]{1,0:T(1,128)S(1)} %copy-done.4, s32[16,16]{1,0:T(8,128)S(1)} %copy-done.3, f32[16,4,16,512]{3,2,1,0:T(8,128)S(1)} %update.1, bf16[16,32,256]{2,1,0:T(8,128)(2,1)S(1)} %get-tuple-element.17.refs_0_, bf16[16,32,256]{2,1,0:T(8,128)(2,1)S(1)} %collective-permute-done.1.refs_1_, ...), custom_call_target="tpu_custom_call" | custom-call | bytes 4195336 | tf_op jit(solution)/shard_map/schur/pallas_call | solution.py:18
  91.7 0.0 all-to-all-done.2.parts
  91.7 0.7 pivot.1
Async XLA Ops:
  0.6 13.9 %copy-start.4 = (f32[1,2]{1,0:T(1,128)S(1)}, f32[1,2]{1,0:T(1,128)}, u32[]{:S(2)}) copy-start(f32[1,2]{1,0:T(1,128)} %shift.9) | copy-start | bytes 28
  0.6 13.9 %copy-start.7 = (bf16[256,256]{1,0:T(8,128)(2,1)S(1)}, bf16[256,256]{1,0:T(8,128)(2,1)}, u32[]{:S(2)}) copy-start(bf16[256,256]{1,0:T(8,128)(2,1)} %pivot_s.1) | copy-start | bytes 393220
  0.7 13.9 %copy-start.6 = (bf16[256,256]{1,0:T(8,128)(2,1)S(1)}, bf16[256,256]{1,0:T(8,128)(2,1)}, u32[]{:S(2)}) copy-start(bf16[256,256]{1,0:T(8,128)(2,1)} %pivot_h.1) | copy-start | bytes 393220
  2.7 34.5 %all-to-all-start = ((bf16[16,96,256]{2,1,0:T(8,128)(2,1)}), bf16[16,96,256]{2,1,0:T(8,128)(2,1)S(1)}, u32[]{:S(2)}, u32[]{:S(2)}) async-start(bf16[16,96,256]{2,1,0:T(8,128)(2,1)} %pack.1), calls=%async_computation | async-start | bytes 1572864 | tf_op jit(solution)/shard_map/all_to_all | solution.py:294
  14.6 25.8 %copy-start.1 = (bf16[256,256]{1,0:T(8,128)(2,1)S(1)}, bf16[256,256]{1,0:T(8,128)(2,1)}, u32[]{:S(2)}) copy-start(bf16[256,256]{1,0:T(8,128)(2,1)} %panel_h.5) | copy-start | bytes 393220
  14.6 25.8 %copy-start.2 = (bf16[256,256]{1,0:T(8,128)(2,1)S(1)}, bf16[256,256]{1,0:T(8,128)(2,1)}, u32[]{:S(2)}) copy-start(bf16[256,256]{1,0:T(8,128)(2,1)} %panel_s.5) | copy-start | bytes 393220
  14.6 25.8 %copy-start.5 = (f32[1,2]{1,0:T(1,128)S(1)}, f32[1,2]{1,0:T(1,128)}, u32[]{:S(2)}) copy-start(f32[1,2]{1,0:T(1,128)} %weight.3) | copy-start | bytes 28
  18.4 20.1 %copy-start.8 = (bf16[2,256,512]{2,1,0:T(8,128)(2,1)}, bf16[2,256,512]{2,1,0:T(8,128)(2,1)S(1)}, u32[]{:S(2)}) copy-start(bf16[2,256,512]{2,1,0:T(8,128)(2,1)S(1)} %pivot_inverse.1.inverse) | copy-start | bytes 1572868
  18.4 24.1 %copy-start = (bf16[1,2,16,1,64,256]{5,4,3,2,1,0:T(8,128)(2,1)S(1)}, bf16[1,2,16,1,64,256]{5,4,3,2,1,0:T(8,128)(2,1)}, u32[]{:S(2)}) copy-start(bf16[1,2,16,1,64,256]{5,4,3,2,1,0:T(8,128)(2,1)} %param.19) | copy-start | bytes 3145732
  38.5 4.0 %collective-permute-start = (bf16[512,512]{1,0:T(8,128)(2,1)S(1)}, bf16[512,512]{1,0:T(8,128)(2,1)S(1)}, u32[]{:S(2)}, u32[]{:S(2)}) collective-permute-start(bf16[512,512]{1,0:T(8,128)(2,1)S(1)} %get-tuple-element.13.mine), channel_id=1, source_target_pairs={{0,4},{4,0},{8,12},{12,8},{16,20},{20,16},{24,28},{28,24},{32,36},... | collective-permute-start | bytes 1572872 | tf_op jit(solution)/shard_map/ppermute | solution.py:310
  40.4 1.0 %copy-start.9 = (bf16[2,256,512]{2,1,0:T(8,128)(2,1)S(1)}, bf16[2,256,512]{2,1,0:T(8,128)(2,1)}, u32[]{:S(2)}) copy-start(bf16[2,256,512]{2,1,0:T(8,128)(2,1)} %copy-done.8) | copy-start | bytes 1572868
  45.1 21.1 %all-to-all-start.1 = ((bf16[32,32,128]{2,1,0:T(8,128)(2,1)}), bf16[32,32,128]{2,1,0:T(8,128)(2,1)S(1)}, u32[]{:S(2)}, u32[]{:S(2)}) async-start(bf16[32,32,128]{2,1,0:T(8,128)(2,1)} %column.1), calls=%async_computation.1 | async-start | bytes 524288 | tf_op jit(solution)/shard_map/all_to_all | solution.py:339
  54.7 34.9 %copy-start.3 = (s32[16,16]{1,0:T(8,128)S(1)}, s32[16,16]{1,0:T(8,128)}, u32[]{:S(2)}) copy-start(s32[16,16]{1,0:T(8,128)} %pattern.1) | copy-start | bytes 3076
  54.7 14.2 %collective-permute-start.1 = (bf16[16,32,256]{2,1,0:T(8,128)(2,1)S(1)}, bf16[16,32,256]{2,1,0:T(8,128)(2,1)S(1)}, u32[]{:S(2)}, u32[]{:S(2)}) collective-permute-start(bf16[16,32,256]{2,1,0:T(8,128)(2,1)S(1)} %get-tuple-element.17.refs_0_), channel_id=1, source_target_pairs={{0,64},{64,128},{128,192},{192,256},{256,320},{320,384},{384,448},... | collective-permute-start | bytes 786440 | tf_op jit(solution)/shard_map/ppermute | solution.py:336
  68.9 22.8 %all-to-all-start.2 = ((bf16[64,16,128]{2,1,0:T(8,128)(2,1)}), bf16[64,16,128]{2,1,0:T(8,128)(2,1)S(1)}, u32[]{:S(2)}, u32[]{:S(2)}) async-start(bf16[64,16,128]{2,1,0:T(8,128)(2,1)} %get-tuple-element.22), calls=%async_computation.2 | async-start | bytes 524288 | tf_op jit(solution)/shard_map/all_to_all | solution.py:352
  76.4 9.3 %collective-permute-start.3 = (bf16[16,32,256]{2,1,0:T(8,128)(2,1)S(1)}, bf16[16,32,256]{2,1,0:T(8,128)(2,1)S(1)}, u32[]{:S(2)}, u32[]{:S(2)}) collective-permute-start(bf16[16,32,256]{2,1,0:T(8,128)(2,1)S(1)} %get-tuple-element.17.refs_0_), channel_id=1, source_target_pairs={{0,448},{64,0},{128,64},{192,128},{256,192},{320,256},{384,320},{4... | collective-permute-start | bytes 786440 | tf_op jit(solution)/shard_map/ppermute | solution.py:337
  79.5 10.2 %collective-permute-start.2 = (bf16[16,32,256]{2,1,0:T(8,128)(2,1)S(1)}, bf16[16,32,256]{2,1,0:T(8,128)(2,1)S(1)}, u32[]{:S(2)}, u32[]{:S(2)}) collective-permute-start(bf16[16,32,256]{2,1,0:T(8,128)(2,1)S(1)} %collective-permute-done.1.refs_1_), channel_id=1, source_target_pairs={{0,64},{64,128},{128,192},{192,256},{256,320},{320,384},{384,448},... | collective-permute-start | bytes 786440 | tf_op jit(solution)/shard_map/ppermute | solution.py:351

commit v9 on v8

--- a/solution.py
+++ b/solution.py
@@ -145,13 +145,14 @@
             out[row, low : low + share] = fronts[part, :, row * size : (row + 1) * size]
 
 
-def solve_body(shift, received, inverse, solved, share):
+def solve_body(shift, received, inverse, solved, low, high):
     strips, rows, size = received.shape
     half = solved.shape[0] // strips
     rows_h = received[:, :half].reshape(strips * half, size)
     rows_s = received[:, half : 2 * half].reshape(strips * half, size)
     solved[...] = solve(rows_h, rows_s, shift, inverse)
-    share[...] = received[:, 2 * half :]
+    low[...] = received[: strips // 2, 2 * half :]
+    high[...] = received[strips // 2 :, 2 * half :]
 
 
 def ordered(mine, other):
@@ -238,17 +239,29 @@
 
 
 def schur_body(shift, pattern, update, *refs):
-    shares, out = refs[:-1], refs[-1]
+    low, high, from_below, from_above, below, above, out = refs
     strips, count, share, size = out.shape[1:]
+    half = strips // 2
     pole = lax.axis_index("pole")
     row = lax.axis_index("row")
     shift_real, shift_imag = shift[0, 0], shift[0, 1]
-    for step, member in enumerate(shares):
-        at = lax.rem(pole + count - step, count)
-        for strip in range(strips):
+    members = (
+        (low, 0, 0, 0),
+        (high, 0, 0, half),
+        (from_below, 0, -1, 0),
+        (below, 0, -1, half),
+        (below, half, -2, 0),
+        (above, 0, 1, 0),
+        (from_above, 0, 1, half),
+        (above, half, 2, half),
+    )
+    for member, start, step, first in members:
+        at = lax.rem(pole + count + step, count)
+        for index in range(half):
+            strip = first + index
             mask = pattern[strip, row].astype(f32)
-            margin = mask * member[strip, share:].astype(f32)
-            real = mask * member[strip, :share].astype(f32) - shift_real * margin
+            margin = mask * member[start + index, share:].astype(f32)
+            real = mask * member[start + index, :share].astype(f32) - shift_real * margin
             out[0, strip, at] = (real - update[strip, at, :, :size]).astype(bf16)
             out[1, strip, at] = (-shift_imag * margin - update[strip, at, :, size:]).astype(bf16)
 
@@ -300,9 +313,9 @@
         6 * 4 * 3 * 2 * size**3,
         "pivot_inverse",
     )
-    mine, shared = call(
+    mine, low, high = call(
         solve_body,
-        [shape(row_count * half, 2 * size), shape(row_count, 2 * share, size)],
+        [shape(row_count * half, 2 * size)] + [shape(row_count // 2, 2 * share, size)] * 2,
         [pole_shift, received, inverse],
         2 * 8 * row_count * half * size * size,
         "solved_rows",
@@ -332,9 +345,9 @@
 
     onward = [(i, (i + 1) % pole_count) for i in range(pole_count)]
     back = [(i, (i - 1) % pole_count) for i in range(pole_count)]
-    shared, both = lax.optimization_barrier((shared, both))
-    before = lax.ppermute(shared, "pole", onward)
-    after = lax.ppermute(shared, "pole", back)
+    low, high, both = lax.optimization_barrier((low, high, both))
+    from_below = lax.ppermute(low, "pole", onward)
+    from_above = lax.ppermute(high, "pole", back)
 
     both = lax.all_to_all(both, ("pole", "col"), split_axis=0, concat_axis=0, tiled=True)
     spread, rows_out = call(
@@ -347,8 +360,9 @@
         0,
         "sums",
     )
-    before, spread = lax.optimization_barrier((before, spread))
-    second = lax.ppermute(before, "pole", onward)
+    from_below, from_above, spread = lax.optimization_barrier((from_below, from_above, spread))
+    below = lax.ppermute(jnp.concatenate([high, from_below]), "pole", onward)
+    above = lax.ppermute(jnp.concatenate([low, from_above]), "pole", back)
     spread = lax.all_to_all(spread, ("row", "col"), split_axis=0, concat_axis=0, tiled=True)
     (pivot_out,) = call(pivot_body, [shape(piece, size, dtype=f32)], [spread], 0, "pivot")
 
@@ -362,7 +376,7 @@
     (schur,) = call(
         schur_body,
         [shape(2, row_count, quarters, share, size)],
-        [pole_shift, pattern, update, shared, before, second, after],
+        [pole_shift, pattern, update, low, high, from_below, from_above, below, above],
         0,
         "schur",
     )

time: 93.3 us -> 90.6 us (0.971)
  waiting for transfers between devices: 35.8 us -> 29.5 us
  starting transfers between devices: 39.3 us -> 42.7 us
    ppermute x3 -> x4, starting transfers between devices: 8.42 us -> 11.8 us  [the longest x1 3.35 us: shards(): from_above = lax.ppermute(high, 'pole', back)]
    all_to_all x1, waiting for transfers between devices: 8.31 us -> 4.96 us  [shards(): lax.all_to_all(both, ('pole', 'col'), split_axis=0, concat_axis=0, tiled=...]
    ppermute x3 -> x4, waiting for transfers between devices: 8.66 us -> 5.76 us  [the longest x1 3.03 us: shards(): below = lax.ppermute(jnp.concatenate([high, from_below]), 'pole', onward)]
  transfers between devices with their start and end apart: 7 -> 8, of which waited for: 5 -> 4; matrix products, arithmetic and copies ran while one was open for 0% -> 0% of each run, Pallas kernels for 10% -> 10%
where the time goes in v9:
time: 90.6 us; the launch traced here: 89.7 us
  starting transfers between devices  42.7 us (47%)
  waiting for transfers between devices  29.5 us (33%)
  Pallas kernels  15.4 us (17%)
  local copies, waits for them, and re-layouts  1.08 us (1%)
    all_to_all x1, waiting for transfers between devices, shards(): lax.all_to_all(sent, 'row', split_axis=0, concat_axis=0, tiled=True)  18.8 us
    all_to_all x1, starting transfers between devices, shards(): lax.all_to_all(sent, 'row', split_axis=0, concat_axis=0, tiled=True)  11.8 us
    pallas_call x7, Pallas kernels, call(): pl.pallas_call(body, out_shape=outs, in_specs=[SMEM if x.size <= 256 else...  10.8 us
    all_to_all x1, starting transfers between devices, shards(): lax.all_to_all(both, ('pole', 'col'), split_axis=0, concat_axis=0, tiled=...  9.66 us
    all_to_all x1, starting transfers between devices, shards(): lax.all_to_all(spread, ('row', 'col'), split_axis=0, concat_axis=0, tiled...  7.53 us
    all_to_all x1, waiting for transfers between devices, shards(): lax.all_to_all(both, ('pole', 'col'), split_axis=0, concat_axis=0, tiled=...  4.96 us
    ppermute x1, starting transfers between devices, shards(): from_above = lax.ppermute(high, 'pole', back)  3.35 us
    ppermute x1, starting transfers between devices, shards(): below = lax.ppermute(jnp.concatenate([high, from_below]), 'pole', onward)  3.15 us
  transfers between devices with their start and end apart: 8, of which 4 were waited for; matrix products, arithmetic and copies ran while one was open for 0% of the time, Pallas kernels for 10%

profile of v9, /device:TPU:1, one launch (start us, length us, event | category | flops | bytes accessed | tf_op | source)
XLA Modules:
  0.0 89.7 jit_solution(3211625155901390270)
XLA Ops:
  0.6 0.0 copy-start.4
  0.6 0.0 copy-start.7
  0.7 0.0 copy-start.6
  0.7 2.0 %pack.1 = bf16[16,96,256]{2,1,0:T(8,128)(2,1)} custom-call(bf16[256,256]{1,0:T(8,128)(2,1)} %panel_h.5, bf16[256,256]{1,0:T(8,128)(2,1)} %panel_s.5, bf16[64,4096]{1,0:T(8,128)(2,1)} %front_h.1, bf16[64,4096]{1,0:T(8,128)(2,1)} %front_s.1), custom_call_target="tpu_custom_call" | custom-call | bytes 1048576 | tf_op jit(solution)/shard_map/pack/pallas_call | solution.py:294
  2.7 11.8 %all-to-all-start = ((bf16[16,96,256]{2,1,0:T(8,128)(2,1)}), bf16[16,96,256]{2,1,0:T(8,128)(2,1)S(1)}, u32[]{:S(2)}, u32[]{:S(2)}) async-start(bf16[16,96,256]{2,1,0:T(8,128)(2,1)} %pack.1), calls=%async_computation | async-start | bytes 1572864 | tf_op jit(solution)/shard_map/all_to_all | solution.py:307
  14.5 0.0 copy-done.4
  14.5 0.0 copy-done.7
  14.6 0.0 copy-done.6
  14.6 0.0 copy-start.1
  14.6 0.0 copy-start.2
  14.6 0.0 copy-start.5
  14.6 3.8 %pivot_inverse.1.inverse = bf16[2,256,512]{2,1,0:T(8,128)(2,1)S(1)} custom-call(f32[1,2]{1,0:T(1,128)S(1)} %copy-done.4, bf16[256,256]{1,0:T(8,128)(2,1)S(1)} %copy-done.6, bf16[256,256]{1,0:T(8,128)(2,1)S(1)} %copy-done.7), custom_call_target="tpu_custom_call" | custom-call | flops 2415919104 | bytes 786440 | tf_op jit(solution)/shard_map/pivot_inverse/pallas_call | solution.py:18
  18.4 0.0 copy-start.8
  18.4 0.0 copy-start
  18.4 18.8 %all-to-all-done.received = bf16[16,96,256]{2,1,0:T(8,128)(2,1)S(1)} async-done(((bf16[16,96,256]{2,1,0:T(8,128)(2,1)}), bf16[16,96,256]{2,1,0:T(8,128)(2,1)S(1)}, u32[]{:S(2)}, u32[]{:S(2)}) %all-to-all-start) | async-done | bytes 786464 | tf_op jit(solution)/shard_map/all_to_all | solution.py:307
  37.2 1.3 %solved_rows.1 = (bf16[512,512]{1,0:T(8,128)(2,1)S(1)}, bf16[8,32,256]{2,1,0:T(8,128)(2,1)S(1)}, bf16[8,32,256]{2,1,0:T(8,128)(2,1)S(1)}) custom-call(f32[1,2]{1,0:T(1,128)S(1)} %copy-done.4, bf16[16,96,256]{2,1,0:T(8,128)(2,1)S(1)} %all-to-all-done.received, bf16[2,256,512]{2,1,0:T(8,128)(2,1)S(1)} %pivot_inverse.1.inverse), custom_call_target="tpu_custom_call" | custom-call | flops 536870912 | bytes 2097160 | tf_op jit(solution)/shard_map/solved_rows/pallas_call | solution.py:18
  38.5 0.0 copy-done.8
  38.5 1.9 %collective-permute-start = (bf16[512,512]{1,0:T(8,128)(2,1)S(1)}, bf16[512,512]{1,0:T(8,128)(2,1)S(1)}, u32[]{:S(2)}, u32[]{:S(2)}) collective-permute-start(bf16[512,512]{1,0:T(8,128)(2,1)S(1)} %get-tuple-element.16.mine), channel_id=1, source_target_pairs={{0,4},{4,0},{8,12},{12,8},{16,20},{20,16},{24,28},{28,24},{32,36},... | collective-permute-start | bytes 1572872 | tf_op jit(solution)/shard_map/ppermute | solution.py:323
  40.4 0.0 copy-done.1
  40.4 0.0 copy-done.2
  40.4 0.0 copy-done.5
  40.4 0.0 copy-start.9
  40.4 1.0 %copy-done.9 = bf16[2,256,512]{2,1,0:T(8,128)(2,1)S(1)} copy-done((bf16[2,256,512]{2,1,0:T(8,128)(2,1)S(1)}, bf16[2,256,512]{2,1,0:T(8,128)(2,1)}, u32[]{:S(2)}) %copy-start.9) | copy-done | bytes 524312
  41.5 1.0 %local_rows.1 = (bf16[512,256]{1,0:T(8,128)(2,1)S(1)}, f32[256,256]{1,0:T(8,128)S(1)}) custom-call(f32[1,2]{1,0:T(1,128)S(1)} %copy-done.4, f32[1,2]{1,0:T(1,128)S(1)} %copy-done.5, bf16[256,256]{1,0:T(8,128)(2,1)S(1)} %copy-done.1, bf16[256,256]{1,0:T(8,128)(2,1)S(1)} %copy-done.2, bf16[2,256,512]{2,1,0:T(8,128)(2,1)S(1)} %copy-done.9), custom_call_target="tpu_custom_call" | custom-call | flops 268435456 | bytes 1310736 | tf_op jit(solution)/shard_map/local_rows/pallas_call | solution.py:18
  42.5 0.0 collective-permute-done.other
  42.5 0.0 copy-done
  42.5 2.6 %column.1 = bf16[32,32,128]{2,1,0:T(8,128)(2,1)} custom-call(f32[1,2]{1,0:T(1,128)S(1)} %copy-done.5, bf16[512,512]{1,0:T(8,128)(2,1)S(1)} %get-tuple-element.16.mine, bf16[512,512]{1,0:T(8,128)(2,1)S(1)} %collective-permute-done.other, bf16[2,16,64,256]{3,2,1,0:T(8,128)(2,1)S(1)} %bitcast.6, bf16[512,256]{1,0:T(8,128)(2,1)S(1)} %get-tuple-element.19.right, ...), custom_call_target="tpu_custom_call" | custom-call | flops 536870912 | bytes 4194304 | tf_op jit(solution)/shard_map/column/pallas_call | solution.py:333
  45.1 9.7 %all-to-all-start.1 = ((bf16[32,32,128]{2,1,0:T(8,128)(2,1)}), bf16[32,32,128]{2,1,0:T(8,128)(2,1)S(1)}, u32[]{:S(2)}, u32[]{:S(2)}) async-start(bf16[32,32,128]{2,1,0:T(8,128)(2,1)} %column.1), calls=%async_computation.1 | async-start | bytes 524288 | tf_op jit(solution)/shard_map/all_to_all | solution.py:352
  54.7 3.1 %collective-permute-start.1 = (bf16[8,32,256]{2,1,0:T(8,128)(2,1)S(1)}, bf16[8,32,256]{2,1,0:T(8,128)(2,1)S(1)}, u32[]{:S(2)}, u32[]{:S(2)}) collective-permute-start(bf16[8,32,256]{2,1,0:T(8,128)(2,1)S(1)} %get-tuple-element.21.refs_0_), channel_id=1, source_target_pairs={{0,64},{64,128},{128,192},{192,256},{256,320},{320,384},{384,448},... | collective-permute-start | bytes 393224 | tf_op jit(solution)/shard_map/ppermute | solution.py:349
  57.9 3.4 %collective-permute-start.2 = (bf16[8,32,256]{2,1,0:T(8,128)(2,1)S(1)}, bf16[8,32,256]{2,1,0:T(8,128)(2,1)S(1)}, u32[]{:S(2)}, u32[]{:S(2)}) collective-permute-start(bf16[8,32,256]{2,1,0:T(8,128)(2,1)S(1)} %get-tuple-element.22.refs_1_), channel_id=1, source_target_pairs={{0,448},{64,0},{128,64},{192,128},{256,192},{320,256},{384,320},{4... | collective-permute-start | bytes 393224 | tf_op jit(solution)/shard_map/ppermute | solution.py:350
  61.2 5.0 %all-to-all-done.1.parts = bf16[32,32,128]{2,1,0:T(8,128)(2,1)S(1)} async-done(((bf16[32,32,128]{2,1,0:T(8,128)(2,1)}), bf16[32,32,128]{2,1,0:T(8,128)(2,1)S(1)}, u32[]{:S(2)}, u32[]{:S(2)}) %all-to-all-start.1) | async-done | bytes 262176 | tf_op jit(solution)/shard_map/all_to_all | solution.py:352
  66.2 0.8 sums.1
  67.0 0.0 collective-permute-done.1.refs_2_
  67.0 0.0 collective-permute-done.2.refs_3_
  67.0 7.5 %all-to-all-start.2 = ((bf16[64,16,128]{2,1,0:T(8,128)(2,1)}), bf16[64,16,128]{2,1,0:T(8,128)(2,1)S(1)}, u32[]{:S(2)}, u32[]{:S(2)}) async-start(bf16[64,16,128]{2,1,0:T(8,128)(2,1)} %get-tuple-element.28), calls=%async_computation.2 | async-start | bytes 524288 | tf_op jit(solution)/shard_map/all_to_all | solution.py:366
  74.5 0.0 copy-start.3
  74.6 2.1 %collective-permute-start.4 = (bf16[16,32,256]{2,1,0:T(8,128)(2,1)S(1)}, bf16[16,32,256]{2,1,0:T(8,128)(2,1)S(1)}, u32[]{:S(2)}, u32[]{:S(2)}) collective-permute-start(bf16[16,32,256]{2,1,0:T(8,128)(2,1)S(1)} %pad_maximum_fusion.1), channel_id=1, source_target_pairs={{0,448},{64,0},{128,64},{192,128},{256,192},{320,256},{384,320},{4... | collective-permute-start | bytes 786440 | tf_op jit(solution)/shard_map/ppermute | solution.py:365
  76.7 3.2 %collective-permute-start.3 = (bf16[16,32,256]{2,1,0:T(8,128)(2,1)S(1)}, bf16[16,32,256]{2,1,0:T(8,128)(2,1)S(1)}, u32[]{:S(2)}, u32[]{:S(2)}) collective-permute-start(bf16[16,32,256]{2,1,0:T(8,128)(2,1)S(1)} %pad_maximum_fusion), channel_id=1, source_target_pairs={{0,64},{64,128},{128,192},{192,256},{256,320},{320,384},{384,448},... | collective-permute-start | bytes 786440 | tf_op jit(solution)/shard_map/ppermute | solution.py:364
  79.9 1.3 %update.1 = f32[16,4,16,512]{3,2,1,0:T(8,128)S(1)} custom-call(f32[1,2]{1,0:T(1,128)S(1)} %copy-done.4, bf16[256,256]{1,0:T(8,128)(2,1)S(1)} %copy-done.1, bf16[256,256]{1,0:T(8,128)(2,1)S(1)} %copy-done.2, bf16[512,512]{1,0:T(8,128)(2,1)S(1)} %get-tuple-element.16.mine, bf16[512,512]{1,0:T(8,128)(2,1)S(1)} %collective-permute-done.other), custom_call_target="tpu_custom_call" | custom-call | flops 536870912 | bytes 3407880 | tf_op jit(solution)/shard_map/update/pallas_call | solution.py:18
  81.2 2.7 %collective-permute-done.4.refs_5_ = bf16[16,32,256]{2,1,0:T(8,128)(2,1)S(1)} collective-permute-done((bf16[16,32,256]{2,1,0:T(8,128)(2,1)S(1)}, bf16[16,32,256]{2,1,0:T(8,128)(2,1)S(1)}, u32[]{:S(2)}, u32[]{:S(2)}) %collective-permute-start.4) | collective-permute-done | bytes 262176 | tf_op jit(solution)/shard_map/ppermute | solution.py:365
  83.9 3.0 %collective-permute-done.3.refs_4_ = bf16[16,32,256]{2,1,0:T(8,128)(2,1)S(1)} collective-permute-done((bf16[16,32,256]{2,1,0:T(8,128)(2,1)S(1)}, bf16[16,32,256]{2,1,0:T(8,128)(2,1)S(1)}, u32[]{:S(2)}, u32[]{:S(2)}) %collective-permute-start.3) | collective-permute-done | bytes 262176 | tf_op jit(solution)/shard_map/ppermute | solution.py:364
  86.9 0.0 copy-done.3
  86.9 2.0 %schur.1 = bf16[2,16,4,16,256]{4,3,2,1,0:T(8,128)(2,1)} custom-call(f32[1,2]{1,0:T(1,128)S(1)} %copy-done.4, s32[16,16]{1,0:T(8,128)S(1)} %copy-done.3, f32[16,4,16,512]{3,2,1,0:T(8,128)S(1)} %update.1, bf16[8,32,256]{2,1,0:T(8,128)(2,1)S(1)} %get-tuple-element.21.refs_0_, bf16[8,32,256]{2,1,0:T(8,128)(2,1)S(1)} %get-tuple-element.22.refs_1_, ...), custom_call_target="tpu_custom_call" | custom-call | bytes 4195336 | tf_op jit(solution)/shard_map/schur/pallas_call | solution.py:18
  89.0 0.0 all-to-all-done.2.parts
  89.0 0.7 pivot.1
  (2 shorter events, 0.1 us)
Async XLA Ops:
  0.6 13.9 %copy-start.4 = (f32[1,2]{1,0:T(1,128)S(1)}, f32[1,2]{1,0:T(1,128)}, u32[]{:S(2)}) copy-start(f32[1,2]{1,0:T(1,128)} %shift.9) | copy-start | bytes 28
  0.6 13.9 %copy-start.7 = (bf16[256,256]{1,0:T(8,128)(2,1)S(1)}, bf16[256,256]{1,0:T(8,128)(2,1)}, u32[]{:S(2)}) copy-start(bf16[256,256]{1,0:T(8,128)(2,1)} %pivot_s.1) | copy-start | bytes 393220
  0.7 13.9 %copy-start.6 = (bf16[256,256]{1,0:T(8,128)(2,1)S(1)}, bf16[256,256]{1,0:T(8,128)(2,1)}, u32[]{:S(2)}) copy-start(bf16[256,256]{1,0:T(8,128)(2,1)} %pivot_h.1) | copy-start | bytes 393220
  2.7 34.5 %all-to-all-start = ((bf16[16,96,256]{2,1,0:T(8,128)(2,1)}), bf16[16,96,256]{2,1,0:T(8,128)(2,1)S(1)}, u32[]{:S(2)}, u32[]{:S(2)}) async-start(bf16[16,96,256]{2,1,0:T(8,128)(2,1)} %pack.1), calls=%async_computation | async-start | bytes 1572864 | tf_op jit(solution)/shard_map/all_to_all | solution.py:307
  14.6 25.8 %copy-start.1 = (bf16[256,256]{1,0:T(8,128)(2,1)S(1)}, bf16[256,256]{1,0:T(8,128)(2,1)}, u32[]{:S(2)}) copy-start(bf16[256,256]{1,0:T(8,128)(2,1)} %panel_h.5) | copy-start | bytes 393220
  14.6 25.8 %copy-start.2 = (bf16[256,256]{1,0:T(8,128)(2,1)S(1)}, bf16[256,256]{1,0:T(8,128)(2,1)}, u32[]{:S(2)}) copy-start(bf16[256,256]{1,0:T(8,128)(2,1)} %panel_s.5) | copy-start | bytes 393220
  14.6 25.8 %copy-start.5 = (f32[1,2]{1,0:T(1,128)S(1)}, f32[1,2]{1,0:T(1,128)}, u32[]{:S(2)}) copy-start(f32[1,2]{1,0:T(1,128)} %weight.3) | copy-start | bytes 28
  18.4 20.1 %copy-start.8 = (bf16[2,256,512]{2,1,0:T(8,128)(2,1)}, bf16[2,256,512]{2,1,0:T(8,128)(2,1)S(1)}, u32[]{:S(2)}) copy-start(bf16[2,256,512]{2,1,0:T(8,128)(2,1)S(1)} %pivot_inverse.1.inverse) | copy-start | bytes 1572868
  18.4 24.1 %copy-start = (bf16[1,2,16,1,64,256]{5,4,3,2,1,0:T(8,128)(2,1)S(1)}, bf16[1,2,16,1,64,256]{5,4,3,2,1,0:T(8,128)(2,1)}, u32[]{:S(2)}) copy-start(bf16[1,2,16,1,64,256]{5,4,3,2,1,0:T(8,128)(2,1)} %param.19) | copy-start | bytes 3145732
  38.5 4.0 %collective-permute-start = (bf16[512,512]{1,0:T(8,128)(2,1)S(1)}, bf16[512,512]{1,0:T(8,128)(2,1)S(1)}, u32[]{:S(2)}, u32[]{:S(2)}) collective-permute-start(bf16[512,512]{1,0:T(8,128)(2,1)S(1)} %get-tuple-element.16.mine), channel_id=1, source_target_pairs={{0,4},{4,0},{8,12},{12,8},{16,20},{20,16},{24,28},{28,24},{32,36},... | collective-permute-start | bytes 1572872 | tf_op jit(solution)/shard_map/ppermute | solution.py:323
  40.4 1.0 %copy-start.9 = (bf16[2,256,512]{2,1,0:T(8,128)(2,1)S(1)}, bf16[2,256,512]{2,1,0:T(8,128)(2,1)}, u32[]{:S(2)}) copy-start(bf16[2,256,512]{2,1,0:T(8,128)(2,1)} %copy-done.8) | copy-start | bytes 1572868
  45.1 21.1 %all-to-all-start.1 = ((bf16[32,32,128]{2,1,0:T(8,128)(2,1)}), bf16[32,32,128]{2,1,0:T(8,128)(2,1)S(1)}, u32[]{:S(2)}, u32[]{:S(2)}) async-start(bf16[32,32,128]{2,1,0:T(8,128)(2,1)} %column.1), calls=%async_computation.1 | async-start | bytes 524288 | tf_op jit(solution)/shard_map/all_to_all | solution.py:352
  54.7 12.2 %collective-permute-start.1 = (bf16[8,32,256]{2,1,0:T(8,128)(2,1)S(1)}, bf16[8,32,256]{2,1,0:T(8,128)(2,1)S(1)}, u32[]{:S(2)}, u32[]{:S(2)}) collective-permute-start(bf16[8,32,256]{2,1,0:T(8,128)(2,1)S(1)} %get-tuple-element.21.refs_0_), channel_id=1, source_target_pairs={{0,64},{64,128},{128,192},{192,256},{256,320},{320,384},{384,448},... | collective-permute-start | bytes 393224 | tf_op jit(solution)/shard_map/ppermute | solution.py:349
  57.9 9.1 %collective-permute-start.2 = (bf16[8,32,256]{2,1,0:T(8,128)(2,1)S(1)}, bf16[8,32,256]{2,1,0:T(8,128)(2,1)S(1)}, u32[]{:S(2)}, u32[]{:S(2)}) collective-permute-start(bf16[8,32,256]{2,1,0:T(8,128)(2,1)S(1)} %get-tuple-element.22.refs_1_), channel_id=1, source_target_pairs={{0,448},{64,0},{128,64},{192,128},{256,192},{320,256},{384,320},{4... | collective-permute-start | bytes 393224 | tf_op jit(solution)/shard_map/ppermute | solution.py:350
  67.0 22.0 %all-to-all-start.2 = ((bf16[64,16,128]{2,1,0:T(8,128)(2,1)}), bf16[64,16,128]{2,1,0:T(8,128)(2,1)S(1)}, u32[]{:S(2)}, u32[]{:S(2)}) async-start(bf16[64,16,128]{2,1,0:T(8,128)(2,1)} %get-tuple-element.28), calls=%async_computation.2 | async-start | bytes 524288 | tf_op jit(solution)/shard_map/all_to_all | solution.py:366
  74.5 12.4 %copy-start.3 = (s32[16,16]{1,0:T(8,128)S(1)}, s32[16,16]{1,0:T(8,128)}, u32[]{:S(2)}) copy-start(s32[16,16]{1,0:T(8,128)} %pattern.1) | copy-start | bytes 3076
  74.6 9.3 %collective-permute-start.4 = (bf16[16,32,256]{2,1,0:T(8,128)(2,1)S(1)}, bf16[16,32,256]{2,1,0:T(8,128)(2,1)S(1)}, u32[]{:S(2)}, u32[]{:S(2)}) collective-permute-start(bf16[16,32,256]{2,1,0:T(8,128)(2,1)S(1)} %pad_maximum_fusion.1), channel_id=1, source_target_pairs={{0,448},{64,0},{128,64},{192,128},{256,192},{320,256},{384,320},{4... | collective-permute-start | bytes 786440 | tf_op jit(solution)/shard_map/ppermute | solution.py:365
  76.7 10.2 %collective-permute-start.3 = (bf16[16,32,256]{2,1,0:T(8,128)(2,1)S(1)}, bf16[16,32,256]{2,1,0:T(8,128)(2,1)S(1)}, u32[]{:S(2)}, u32[]{:S(2)}) collective-permute-start(bf16[16,32,256]{2,1,0:T(8,128)(2,1)S(1)} %pad_maximum_fusion), channel_id=1, source_target_pairs={{0,64},{64,128},{128,192},{192,256},{256,320},{320,384},{384,448},... | collective-permute-start | bytes 786440 | tf_op jit(solution)/shard_map/ppermute | solution.py:364

commit v10 on v8

--- a/solution.py
+++ b/solution.py
@@ -145,13 +145,14 @@
             out[row, low : low + share] = fronts[part, :, row * size : (row + 1) * size]
 
 
-def solve_body(shift, received, inverse, solved, share):
+def solve_body(shift, received, inverse, solved, up, down):
     strips, rows, size = received.shape
     half = solved.shape[0] // strips
     rows_h = received[:, :half].reshape(strips * half, size)
     rows_s = received[:, half : 2 * half].reshape(strips * half, size)
     solved[...] = solve(rows_h, rows_s, shift, inverse)
-    share[...] = received[:, 2 * half :]
+    up[...] = received[: up.shape[0], 2 * half :]
+    down[...] = received[strips - down.shape[0] :, 2 * half :]
 
 
 def ordered(mine, other):
@@ -171,8 +172,9 @@
             bottom = member[rows + half : rows + 2 * half, pair * 128 : pair * 128 + 128]
             even = jnp.where(low_lane, top, pltpu.roll(bottom, 64, 1))
             odd = jnp.where(low_lane, pltpu.roll(top, 64, 1), bottom)
-            out[pole * cols + 2 * pair, at : at + half] = even.astype(out.dtype)
-            out[pole * cols + 2 * pair + 1, at : at + half] = odd.astype(out.dtype)
+            poles = pieces // cols
+            out[2 * pair * poles + pole, at : at + half] = even.astype(out.dtype)
+            out[(2 * pair + 1) * poles + pole, at : at + half] = odd.astype(out.dtype)
 
 
 def column_body(weight, mine, other, ancestor, right, base, out, far):
@@ -237,20 +239,60 @@
         out[first : first + group] = update.reshape((group,) + out.shape[1:])
 
 
-def schur_body(shift, pattern, update, *refs):
-    shares, out = refs[:-1], refs[-1]
+def relay_body(up, down, from_below, from_above, below, above):
+    more = up.shape[0]
+    less = more // 3
+    half = more - less
+    below[:less] = down[half:]
+    below[less:] = from_below[:half]
+    above[:less] = up[:less]
+    above[less:] = from_above[less:]
+
+
+def schur_tiles(shift, pattern, update, members, buffer, out, sems):
     strips, count, share, size = out.shape[1:]
     pole = lax.axis_index("pole")
     row = lax.axis_index("row")
     shift_real, shift_imag = shift[0, 0], shift[0, 1]
-    for step, member in enumerate(shares):
-        at = lax.rem(pole + count - step, count)
-        for strip in range(strips):
+    copies = []
+    for member, start, length, step, first in members:
+        at = lax.rem(pole + count + step, count)
+        for index in range(length):
+            strip = first + index
             mask = pattern[strip, row].astype(f32)
-            margin = mask * member[strip, share:].astype(f32)
-            real = mask * member[strip, :share].astype(f32) - shift_real * margin
-            out[0, strip, at] = (real - update[strip, at, :, :size]).astype(bf16)
-            out[1, strip, at] = (-shift_imag * margin - update[strip, at, :, size:]).astype(bf16)
+            margin = mask * member[start + index, share:].astype(f32)
+            real = mask * member[start + index, :share].astype(f32) - shift_real * margin
+            buffer[0, strip, at] = (real - update[strip, at, :, :size]).astype(bf16)
+            buffer[1, strip, at] = (-shift_imag * margin - update[strip, at, :, size:]).astype(bf16)
+        where = (slice(None), pl.ds(first, length), at)
+        copies.append(pltpu.make_async_copy(buffer.at[where], out.at[where], sems.at[len(copies)]))
+        copies[-1].start()
+    for copy in copies:
+        copy.wait()
+
+
+def schur_first_body(shift, pattern, update, up, down, from_below, from_above, out, buffer, sems):
+    more, less = up.shape[0], out.shape[1] - up.shape[0]
+    members = (
+        (up, 0, more, 0, 0),
+        (down, more - less, less, 0, more),
+        (from_below, 0, more, -1, 0),
+        (from_above, 0, more, 1, less),
+    )
+    schur_tiles(shift, pattern, update, members, buffer, out, sems)
+
+
+def schur_last_body(shift, pattern, update, below, above, begun, out, buffer, sems):
+    del begun
+    half = out.shape[1] // 2
+    less = below.shape[0] - half
+    members = (
+        (below, 0, less, -1, 2 * half - less),
+        (below, less, half, -2, 0),
+        (above, 0, less, 1, 0),
+        (above, less, half, 2, half),
+    )
+    schur_tiles(shift, pattern, update, members, buffer, out, sems)
 
 
 def shards(
@@ -300,9 +342,11 @@
         6 * 4 * 3 * 2 * size**3,
         "pivot_inverse",
     )
-    mine, shared = call(
+    less = row_count // 4
+    more = row_count - less
+    mine, up, down = call(
         solve_body,
-        [shape(row_count * half, 2 * size), shape(row_count, 2 * share, size)],
+        [shape(row_count * half, 2 * size)] + [shape(more, 2 * share, size)] * 2,
         [pole_shift, received, inverse],
         2 * 8 * row_count * half * size * size,
         "solved_rows",
@@ -332,11 +376,11 @@
 
     onward = [(i, (i + 1) % pole_count) for i in range(pole_count)]
     back = [(i, (i - 1) % pole_count) for i in range(pole_count)]
-    shared, both = lax.optimization_barrier((shared, both))
-    before = lax.ppermute(shared, "pole", onward)
-    after = lax.ppermute(shared, "pole", back)
-
-    both = lax.all_to_all(both, ("pole", "col"), split_axis=0, concat_axis=0, tiled=True)
+    up, down, both = lax.optimization_barrier((up, down, both))
+    from_below = lax.ppermute(up, "pole", onward)
+    from_above = lax.ppermute(down, "pole", back)
+
+    both = lax.all_to_all(both, ("col", "pole"), split_axis=0, concat_axis=0, tiled=True)
     spread, rows_out = call(
         sums_body,
         [
@@ -347,8 +391,16 @@
         0,
         "sums",
     )
-    before, spread = lax.optimization_barrier((before, spread))
-    second = lax.ppermute(before, "pole", onward)
+    from_below, from_above, spread = lax.optimization_barrier((from_below, from_above, spread))
+    below, above = call(
+        relay_body,
+        [shape(more, 2 * share, size)] * 2,
+        [up, down, from_below, from_above],
+        0,
+        "relay",
+    )
+    below = lax.ppermute(below, "pole", onward)
+    above = lax.ppermute(above, "pole", back)
     spread = lax.all_to_all(spread, ("row", "col"), split_axis=0, concat_axis=0, tiled=True)
     (pivot_out,) = call(pivot_body, [shape(piece, size, dtype=f32)], [spread], 0, "pivot")
 
@@ -359,13 +411,24 @@
         8 * row_count * width * size * size,
         "update",
     )
-    (schur,) = call(
-        schur_body,
-        [shape(2, row_count, quarters, share, size)],
-        [pole_shift, pattern, update, shared, before, second, after],
-        0,
-        "schur",
-    )
+
+    def tiles(body, ins, name, begun=()):
+        tile = shape(2, row_count, quarters, share, size)
+        return pl.pallas_call(
+            body,
+            out_shape=tile,
+            in_specs=[SMEM] * 2 + [VMEM] * (len(ins) - 2) + [pl.BlockSpec(memory_space=pl.ANY)] * len(begun),
+            out_specs=pl.BlockSpec(memory_space=pl.ANY),
+            input_output_aliases={len(ins): 0} if begun else {},
+            scratch_shapes=[pltpu.VMEM(tile.shape, bf16), pltpu.SemaphoreType.DMA((4,))],
+            compiler_params=pltpu.CompilerParams(vmem_limit_bytes=16 * 2**20),
+            cost_estimate=pl.CostEstimate(flops=0, bytes_accessed=3 * 2**20, transcendentals=0),
+            name=name,
+        )(*ins, *begun)
+
+    fixed = [pole_shift, pattern, update]
+    schur = tiles(schur_first_body, fixed + [up, down, from_below, from_above], "schur_first")
+    schur = tiles(schur_last_body, fixed + [below, above], "schur_last", (schur,))
     return (schur.reshape(1, 2, row_count, 1, width, size), rows_out.T, pivot_out.T)
 
 

time: 93.3 us -> 89.4 us (0.958)
  waiting for transfers between devices: 35.8 us -> 25.7 us
  starting transfers between devices: 39.3 us -> 43.9 us
  Pallas kernels: 15.4 us -> 16.6 us
    all_to_all x1, waiting for transfers between devices: 8.31 us -> 3.17 us  [shards(): lax.all_to_all(both, ('col', 'pole'), split_axis=0, concat_axis=0, tiled=...]
    ppermute x3 -> x4, waiting for transfers between devices: 8.66 us -> 3.73 us  [the longest x1 2.3 us: shards(): from_below = lax.ppermute(up, 'pole', onward)]
    ppermute x3 -> x4, starting transfers between devices: 8.42 us -> 13 us  [the longest x1 4.21 us: shards(): above = lax.ppermute(above, 'pole', back)]
    pallas_call x0 -> x2, Pallas kernels: none -> 3.17 us  [tiles(): pl.pallas_call(body, out_shape=tile, in_specs=[SMEM] * 2 + [VMEM] * (len(...]
    pallas_call x7, Pallas kernels: 10.8 us -> 8.83 us  [call(): pl.pallas_call(body, out_shape=outs, in_specs=[SMEM if x.size <= 256 else...]
  transfers between devices with their start and end apart: 7 -> 8, of which waited for: 5 -> 4; matrix products, arithmetic and copies ran while one was open for 0% -> 0% of each run, Pallas kernels for 10% -> 11%
where the time goes in v10:
time: 89.4 us; the launch traced here: 88.2 us
  starting transfers between devices  43.9 us (49%)
  waiting for transfers between devices  25.7 us (29%)
  Pallas kernels  16.6 us (19%)
  local copies, waits for them, and re-layouts  1.08 us (1%)
  between operations  0.92 us (1%)
    all_to_all x1, waiting for transfers between devices, shards(): lax.all_to_all(sent, 'row', split_axis=0, concat_axis=0, tiled=True)  18.8 us
    all_to_all x1, starting transfers between devices, shards(): lax.all_to_all(sent, 'row', split_axis=0, concat_axis=0, tiled=True)  11.8 us
    all_to_all x1, starting transfers between devices, shards(): lax.all_to_all(both, ('col', 'pole'), split_axis=0, concat_axis=0, tiled=...  9.66 us
    pallas_call x7, Pallas kernels, call(): pl.pallas_call(body, out_shape=outs, in_specs=[SMEM if x.size <= 256 else...  8.83 us
    all_to_all x1, starting transfers between devices, shards(): lax.all_to_all(spread, ('row', 'col'), split_axis=0, concat_axis=0, tiled...  7.44 us
    ppermute x1, starting transfers between devices, shards(): above = lax.ppermute(above, 'pole', back)  4.21 us
    ppermute x1, starting transfers between devices, shards(): from_above = lax.ppermute(down, 'pole', back)  3.36 us
    all_to_all x1, waiting for transfers between devices, shards(): lax.all_to_all(both, ('col', 'pole'), split_axis=0, concat_axis=0, tiled=...  3.17 us
  transfers between devices with their start and end apart: 8, of which 4 were waited for; matrix products, arithmetic and copies ran while one was open for 0% of the time, Pallas kernels for 11%

profile of v10, /device:TPU:1, one launch (start us, length us, event | category | flops | bytes accessed | tf_op | source)
XLA Modules:
  0.0 88.2 jit_solution(3075805688289856286)
XLA Ops:
  0.6 0.0 copy-start.4
  0.6 0.0 copy-start.7
  0.7 0.0 copy-start.6
  0.7 2.0 %pack.1 = bf16[16,96,256]{2,1,0:T(8,128)(2,1)} custom-call(bf16[256,256]{1,0:T(8,128)(2,1)} %panel_h.5, bf16[256,256]{1,0:T(8,128)(2,1)} %panel_s.5, bf16[64,4096]{1,0:T(8,128)(2,1)} %front_h.1, bf16[64,4096]{1,0:T(8,128)(2,1)} %front_s.1), custom_call_target="tpu_custom_call" | custom-call | bytes 1048576 | tf_op jit(solution)/shard_map/pack/pallas_call | solution.py:323
  2.7 11.8 %all-to-all-start = ((bf16[16,96,256]{2,1,0:T(8,128)(2,1)}), bf16[16,96,256]{2,1,0:T(8,128)(2,1)S(1)}, u32[]{:S(2)}, u32[]{:S(2)}) async-start(bf16[16,96,256]{2,1,0:T(8,128)(2,1)} %pack.1), calls=%async_computation | async-start | bytes 1572864 | tf_op jit(solution)/shard_map/all_to_all | solution.py:336
  14.5 0.0 copy-done.4
  14.5 0.0 copy-done.7
  14.6 0.0 copy-done.6
  14.6 0.0 copy-start.1
  14.6 0.0 copy-start.2
  14.6 0.0 copy-start.5
  14.6 3.8 %pivot_inverse.1.inverse = bf16[2,256,512]{2,1,0:T(8,128)(2,1)S(1)} custom-call(f32[1,2]{1,0:T(1,128)S(1)} %copy-done.4, bf16[256,256]{1,0:T(8,128)(2,1)S(1)} %copy-done.6, bf16[256,256]{1,0:T(8,128)(2,1)S(1)} %copy-done.7), custom_call_target="tpu_custom_call" | custom-call | flops 2415919104 | bytes 786440 | tf_op jit(solution)/shard_map/pivot_inverse/pallas_call | solution.py:18
  18.4 0.0 copy-start.8
  18.4 0.0 copy-start
  18.4 18.8 %all-to-all-done.received = bf16[16,96,256]{2,1,0:T(8,128)(2,1)S(1)} async-done(((bf16[16,96,256]{2,1,0:T(8,128)(2,1)}), bf16[16,96,256]{2,1,0:T(8,128)(2,1)S(1)}, u32[]{:S(2)}, u32[]{:S(2)}) %all-to-all-start) | async-done | bytes 786464 | tf_op jit(solution)/shard_map/all_to_all | solution.py:336
  37.2 1.3 %solved_rows.1 = (bf16[512,512]{1,0:T(8,128)(2,1)S(1)}, bf16[12,32,256]{2,1,0:T(8,128)(2,1)S(1)}, bf16[12,32,256]{2,1,0:T(8,128)(2,1)S(1)}) custom-call(f32[1,2]{1,0:T(1,128)S(1)} %copy-done.4, bf16[16,96,256]{2,1,0:T(8,128)(2,1)S(1)} %all-to-all-done.received, bf16[2,256,512]{2,1,0:T(8,128)(2,1)S(1)} %pivot_inverse.1.inverse), custom_call_target="tpu_custom_call" | custom-call | flops 536870912 | bytes 2228232 | tf_op jit(solution)/shard_map/solved_rows/pallas_call | solution.py:18
  38.5 0.0 copy-done.8
  38.5 1.9 %collective-permute-start = (bf16[512,512]{1,0:T(8,128)(2,1)S(1)}, bf16[512,512]{1,0:T(8,128)(2,1)S(1)}, u32[]{:S(2)}, u32[]{:S(2)}) collective-permute-start(bf16[512,512]{1,0:T(8,128)(2,1)S(1)} %get-tuple-element.18.mine), channel_id=1, source_target_pairs={{0,4},{4,0},{8,12},{12,8},{16,20},{20,16},{24,28},{28,24},{32,36},... | collective-permute-start | bytes 1572872 | tf_op jit(solution)/shard_map/ppermute | solution.py:354
  40.4 0.0 copy-done.1
  40.4 0.0 copy-done.2
  40.4 0.0 copy-done.5
  40.4 0.0 copy-start.9
  40.4 1.0 %copy-done.9 = bf16[2,256,512]{2,1,0:T(8,128)(2,1)S(1)} copy-done((bf16[2,256,512]{2,1,0:T(8,128)(2,1)S(1)}, bf16[2,256,512]{2,1,0:T(8,128)(2,1)}, u32[]{:S(2)}) %copy-start.9) | copy-done | bytes 524312
  41.5 1.0 %local_rows.1 = (bf16[512,256]{1,0:T(8,128)(2,1)S(1)}, f32[256,256]{1,0:T(8,128)S(1)}) custom-call(f32[1,2]{1,0:T(1,128)S(1)} %copy-done.4, f32[1,2]{1,0:T(1,128)S(1)} %copy-done.5, bf16[256,256]{1,0:T(8,128)(2,1)S(1)} %copy-done.1, bf16[256,256]{1,0:T(8,128)(2,1)S(1)} %copy-done.2, bf16[2,256,512]{2,1,0:T(8,128)(2,1)S(1)} %copy-done.9), custom_call_target="tpu_custom_call" | custom-call | flops 268435456 | bytes 1310736 | tf_op jit(solution)/shard_map/local_rows/pallas_call | solution.py:18
  42.5 0.0 collective-permute-done.other
  42.5 0.0 copy-done
  42.5 2.6 %column.1 = bf16[32,32,128]{2,1,0:T(8,128)(2,1)} custom-call(f32[1,2]{1,0:T(1,128)S(1)} %copy-done.5, bf16[512,512]{1,0:T(8,128)(2,1)S(1)} %get-tuple-element.18.mine, bf16[512,512]{1,0:T(8,128)(2,1)S(1)} %collective-permute-done.other, bf16[2,16,64,256]{3,2,1,0:T(8,128)(2,1)S(1)} %bitcast.6, bf16[512,256]{1,0:T(8,128)(2,1)S(1)} %get-tuple-element.21.right, ...), custom_call_target="tpu_custom_call" | custom-call | flops 536870912 | bytes 4194304 | tf_op jit(solution)/shard_map/column/pallas_call | solution.py:364
  45.1 9.7 %all-to-all-start.1 = ((bf16[32,32,128]{2,1,0:T(8,128)(2,1)}), bf16[32,32,128]{2,1,0:T(8,128)(2,1)S(1)}, u32[]{:S(2)}, u32[]{:S(2)}) async-start(bf16[32,32,128]{2,1,0:T(8,128)(2,1)} %column.1), calls=%async_computation.1 | async-start | bytes 524288 | tf_op jit(solution)/shard_map/all_to_all | solution.py:383
  54.7 3.1 %collective-permute-start.1 = (bf16[12,32,256]{2,1,0:T(8,128)(2,1)S(1)}, bf16[12,32,256]{2,1,0:T(8,128)(2,1)S(1)}, u32[]{:S(2)}, u32[]{:S(2)}) collective-permute-start(bf16[12,32,256]{2,1,0:T(8,128)(2,1)S(1)} %get-tuple-element.23.up), channel_id=1, source_target_pairs={{0,64},{64,128},{128,192},{192,256},{256,320},{320,384},{384,448},... | collective-permute-start | bytes 589832 | tf_op jit(solution)/shard_map/ppermute | solution.py:380
  57.9 3.4 %collective-permute-start.2 = (bf16[12,32,256]{2,1,0:T(8,128)(2,1)S(1)}, bf16[12,32,256]{2,1,0:T(8,128)(2,1)S(1)}, u32[]{:S(2)}, u32[]{:S(2)}) collective-permute-start(bf16[12,32,256]{2,1,0:T(8,128)(2,1)S(1)} %get-tuple-element.24.down), channel_id=1, source_target_pairs={{0,448},{64,0},{128,64},{192,128},{256,192},{320,256},{384,320},{4... | collective-permute-start | bytes 589832 | tf_op jit(solution)/shard_map/ppermute | solution.py:381
  61.2 3.2 %all-to-all-done.1.parts = bf16[32,32,128]{2,1,0:T(8,128)(2,1)S(1)} async-done(((bf16[32,32,128]{2,1,0:T(8,128)(2,1)}), bf16[32,32,128]{2,1,0:T(8,128)(2,1)S(1)}, u32[]{:S(2)}, u32[]{:S(2)}) %all-to-all-start.1) | async-done | bytes 262176 | tf_op jit(solution)/shard_map/all_to_all | solution.py:383
  64.4 0.8 sums.1
  65.2 2.3 %collective-permute-done.1.from_below = bf16[12,32,256]{2,1,0:T(8,128)(2,1)S(1)} collective-permute-done((bf16[12,32,256]{2,1,0:T(8,128)(2,1)S(1)}, bf16[12,32,256]{2,1,0:T(8,128)(2,1)S(1)}, u32[]{:S(2)}, u32[]{:S(2)}) %collective-permute-start.1) | collective-permute-done | bytes 196640 | tf_op jit(solution)/shard_map/ppermute | solution.py:380
  67.5 0.0 collective-permute-done.2.from_above
  67.5 7.4 %all-to-all-start.2 = ((bf16[64,16,128]{2,1,0:T(8,128)(2,1)}), bf16[64,16,128]{2,1,0:T(8,128)(2,1)S(1)}, u32[]{:S(2)}, u32[]{:S(2)}) async-start(bf16[64,16,128]{2,1,0:T(8,128)(2,1)} %get-tuple-element.32), calls=%async_computation.2 | async-start | bytes 524288 | tf_op jit(solution)/shard_map/all_to_all | solution.py:404
  74.9 0.0 copy-start.3
  75.0 2.3 %collective-permute-start.3 = (bf16[12,32,256]{2,1,0:T(8,128)(2,1)S(1)}, bf16[12,32,256]{2,1,0:T(8,128)(2,1)S(1)}, u32[]{:S(2)}, u32[]{:S(2)}) collective-permute-start(bf16[12,32,256]{2,1,0:T(8,128)(2,1)S(1)} %get-tuple-element.29), channel_id=1, source_target_pairs={{0,64},{64,128},{128,192},{192,256},{256,320},{320,384},{384,448},... | collective-permute-start | bytes 589832 | tf_op jit(solution)/shard_map/ppermute | solution.py:402
  77.3 4.2 %collective-permute-start.4 = (bf16[12,32,256]{2,1,0:T(8,128)(2,1)S(1)}, bf16[12,32,256]{2,1,0:T(8,128)(2,1)S(1)}, u32[]{:S(2)}, u32[]{:S(2)}) collective-permute-start(bf16[12,32,256]{2,1,0:T(8,128)(2,1)S(1)} %get-tuple-element.30), channel_id=1, source_target_pairs={{0,448},{64,0},{128,64},{192,128},{256,192},{320,256},{384,320},{4... | collective-permute-start | bytes 589832 | tf_op jit(solution)/shard_map/ppermute | solution.py:403
  81.5 1.3 %update.1 = f32[16,4,16,512]{3,2,1,0:T(8,128)S(1)} custom-call(f32[1,2]{1,0:T(1,128)S(1)} %copy-done.4, bf16[256,256]{1,0:T(8,128)(2,1)S(1)} %copy-done.1, bf16[256,256]{1,0:T(8,128)(2,1)S(1)} %copy-done.2, bf16[512,512]{1,0:T(8,128)(2,1)S(1)} %get-tuple-element.18.mine, bf16[512,512]{1,0:T(8,128)(2,1)S(1)} %collective-permute-done.other), custom_call_target="tpu_custom_call" | custom-call | flops 536870912 | bytes 3407880 | tf_op jit(solution)/shard_map/update/pallas_call | solution.py:18
  82.8 0.0 copy-done.3
  82.8 1.6 %schur_first.1.begun = bf16[2,16,4,16,256]{4,3,2,1,0:T(8,128)(2,1)} custom-call(f32[1,2]{1,0:T(1,128)S(1)} %copy-done.4, s32[16,16]{1,0:T(8,128)S(1)} %copy-done.3, f32[16,4,16,512]{3,2,1,0:T(8,128)S(1)} %update.1, bf16[12,32,256]{2,1,0:T(8,128)(2,1)S(1)} %get-tuple-element.23.up, bf16[12,32,256]{2,1,0:T(8,128)(2,1)S(1)} %get-tuple-element.24.down, ...), custom_call_target="tpu_custom_call" | custom-call | bytes 3145728 | tf_op jit(solution)/shard_map/schur_first/pallas_call | solution.py:417
  84.5 0.0 collective-permute-done.3.below
  84.5 1.4 %collective-permute-done.4.above = bf16[12,32,256]{2,1,0:T(8,128)(2,1)S(1)} collective-permute-done((bf16[12,32,256]{2,1,0:T(8,128)(2,1)S(1)}, bf16[12,32,256]{2,1,0:T(8,128)(2,1)S(1)}, u32[]{:S(2)}, u32[]{:S(2)}) %collective-permute-start.4) | collective-permute-done | bytes 196640 | tf_op jit(solution)/shard_map/ppermute | solution.py:403
  85.9 1.5 %schur_last.1 = bf16[2,16,4,16,256]{4,3,2,1,0:T(8,128)(2,1)} custom-call(f32[1,2]{1,0:T(1,128)S(1)} %copy-done.4, s32[16,16]{1,0:T(8,128)S(1)} %copy-done.3, f32[16,4,16,512]{3,2,1,0:T(8,128)S(1)} %update.1, bf16[12,32,256]{2,1,0:T(8,128)(2,1)S(1)} %collective-permute-done.3.below, ...), custom_call_target="tpu_custom_call", output_to_operand_aliasing={{}: (5, {})} | custom-call | bytes 3145728 | tf_op jit(solution)/shard_map/schur_last/pallas_call | solution.py:417
  87.4 0.0 all-to-all-done.2.parts
  87.4 0.7 pivot.1
  (1 shorter events, 0.0 us)
Async XLA Ops:
  0.6 13.9 %copy-start.4 = (f32[1,2]{1,0:T(1,128)S(1)}, f32[1,2]{1,0:T(1,128)}, u32[]{:S(2)}) copy-start(f32[1,2]{1,0:T(1,128)} %shift.11) | copy-start | bytes 28
  0.6 13.9 %copy-start.7 = (bf16[256,256]{1,0:T(8,128)(2,1)S(1)}, bf16[256,256]{1,0:T(8,128)(2,1)}, u32[]{:S(2)}) copy-start(bf16[256,256]{1,0:T(8,128)(2,1)} %pivot_s.1) | copy-start | bytes 393220
  0.7 13.9 %copy-start.6 = (bf16[256,256]{1,0:T(8,128)(2,1)S(1)}, bf16[256,256]{1,0:T(8,128)(2,1)}, u32[]{:S(2)}) copy-start(bf16[256,256]{1,0:T(8,128)(2,1)} %pivot_h.1) | copy-start | bytes 393220
  2.7 34.5 %all-to-all-start = ((bf16[16,96,256]{2,1,0:T(8,128)(2,1)}), bf16[16,96,256]{2,1,0:T(8,128)(2,1)S(1)}, u32[]{:S(2)}, u32[]{:S(2)}) async-start(bf16[16,96,256]{2,1,0:T(8,128)(2,1)} %pack.1), calls=%async_computation | async-start | bytes 1572864 | tf_op jit(solution)/shard_map/all_to_all | solution.py:336
  14.6 25.8 %copy-start.1 = (bf16[256,256]{1,0:T(8,128)(2,1)S(1)}, bf16[256,256]{1,0:T(8,128)(2,1)}, u32[]{:S(2)}) copy-start(bf16[256,256]{1,0:T(8,128)(2,1)} %panel_h.5) | copy-start | bytes 393220
  14.6 25.8 %copy-start.2 = (bf16[256,256]{1,0:T(8,128)(2,1)S(1)}, bf16[256,256]{1,0:T(8,128)(2,1)}, u32[]{:S(2)}) copy-start(bf16[256,256]{1,0:T(8,128)(2,1)} %panel_s.5) | copy-start | bytes 393220
  14.6 25.8 %copy-start.5 = (f32[1,2]{1,0:T(1,128)S(1)}, f32[1,2]{1,0:T(1,128)}, u32[]{:S(2)}) copy-start(f32[1,2]{1,0:T(1,128)} %weight.3) | copy-start | bytes 28
  18.4 20.1 %copy-start.8 = (bf16[2,256,512]{2,1,0:T(8,128)(2,1)}, bf16[2,256,512]{2,1,0:T(8,128)(2,1)S(1)}, u32[]{:S(2)}) copy-start(bf16[2,256,512]{2,1,0:T(8,128)(2,1)S(1)} %pivot_inverse.1.inverse) | copy-start | bytes 1572868
  18.4 24.1 %copy-start = (bf16[1,2,16,1,64,256]{5,4,3,2,1,0:T(8,128)(2,1)S(1)}, bf16[1,2,16,1,64,256]{5,4,3,2,1,0:T(8,128)(2,1)}, u32[]{:S(2)}) copy-start(bf16[1,2,16,1,64,256]{5,4,3,2,1,0:T(8,128)(2,1)} %param.19) | copy-start | bytes 3145732
  38.5 4.0 %collective-permute-start = (bf16[512,512]{1,0:T(8,128)(2,1)S(1)}, bf16[512,512]{1,0:T(8,128)(2,1)S(1)}, u32[]{:S(2)}, u32[]{:S(2)}) collective-permute-start(bf16[512,512]{1,0:T(8,128)(2,1)S(1)} %get-tuple-element.18.mine), channel_id=1, source_target_pairs={{0,4},{4,0},{8,12},{12,8},{16,20},{20,16},{24,28},{28,24},{32,36},... | collective-permute-start | bytes 1572872 | tf_op jit(solution)/shard_map/ppermute | solution.py:354
  40.4 1.0 %copy-start.9 = (bf16[2,256,512]{2,1,0:T(8,128)(2,1)S(1)}, bf16[2,256,512]{2,1,0:T(8,128)(2,1)}, u32[]{:S(2)}) copy-start(bf16[2,256,512]{2,1,0:T(8,128)(2,1)} %copy-done.8) | copy-start | bytes 1572868
  45.1 19.3 %all-to-all-start.1 = ((bf16[32,32,128]{2,1,0:T(8,128)(2,1)}), bf16[32,32,128]{2,1,0:T(8,128)(2,1)S(1)}, u32[]{:S(2)}, u32[]{:S(2)}) async-start(bf16[32,32,128]{2,1,0:T(8,128)(2,1)} %column.1), calls=%async_computation.1 | async-start | bytes 524288 | tf_op jit(solution)/shard_map/all_to_all | solution.py:383
  54.7 12.8 %collective-permute-start.1 = (bf16[12,32,256]{2,1,0:T(8,128)(2,1)S(1)}, bf16[12,32,256]{2,1,0:T(8,128)(2,1)S(1)}, u32[]{:S(2)}, u32[]{:S(2)}) collective-permute-start(bf16[12,32,256]{2,1,0:T(8,128)(2,1)S(1)} %get-tuple-element.23.up), channel_id=1, source_target_pairs={{0,64},{64,128},{128,192},{192,256},{256,320},{320,384},{384,448},... | collective-permute-start | bytes 589832 | tf_op jit(solution)/shard_map/ppermute | solution.py:380
  57.9 9.6 %collective-permute-start.2 = (bf16[12,32,256]{2,1,0:T(8,128)(2,1)S(1)}, bf16[12,32,256]{2,1,0:T(8,128)(2,1)S(1)}, u32[]{:S(2)}, u32[]{:S(2)}) collective-permute-start(bf16[12,32,256]{2,1,0:T(8,128)(2,1)S(1)} %get-tuple-element.24.down), channel_id=1, source_target_pairs={{0,448},{64,0},{128,64},{192,128},{256,192},{320,256},{384,320},{4... | collective-permute-start | bytes 589832 | tf_op jit(solution)/shard_map/ppermute | solution.py:381
  67.5 19.9 %all-to-all-start.2 = ((bf16[64,16,128]{2,1,0:T(8,128)(2,1)}), bf16[64,16,128]{2,1,0:T(8,128)(2,1)S(1)}, u32[]{:S(2)}, u32[]{:S(2)}) async-start(bf16[64,16,128]{2,1,0:T(8,128)(2,1)} %get-tuple-element.32), calls=%async_computation.2 | async-start | bytes 524288 | tf_op jit(solution)/shard_map/all_to_all | solution.py:404
  74.9 7.9 %copy-start.3 = (s32[16,16]{1,0:T(8,128)S(1)}, s32[16,16]{1,0:T(8,128)}, u32[]{:S(2)}) copy-start(s32[16,16]{1,0:T(8,128)} %pattern.3) | copy-start | bytes 3076
  75.0 9.5 %collective-permute-start.3 = (bf16[12,32,256]{2,1,0:T(8,128)(2,1)S(1)}, bf16[12,32,256]{2,1,0:T(8,128)(2,1)S(1)}, u32[]{:S(2)}, u32[]{:S(2)}) collective-permute-start(bf16[12,32,256]{2,1,0:T(8,128)(2,1)S(1)} %get-tuple-element.29), channel_id=1, source_target_pairs={{0,64},{64,128},{128,192},{192,256},{256,320},{320,384},{384,448},... | collective-permute-start | bytes 589832 | tf_op jit(solution)/shard_map/ppermute | solution.py:402
  77.3 8.6 %collective-permute-start.4 = (bf16[12,32,256]{2,1,0:T(8,128)(2,1)S(1)}, bf16[12,32,256]{2,1,0:T(8,128)(2,1)S(1)}, u32[]{:S(2)}, u32[]{:S(2)}) collective-permute-start(bf16[12,32,256]{2,1,0:T(8,128)(2,1)S(1)} %get-tuple-element.30), channel_id=1, source_target_pairs={{0,448},{64,0},{128,64},{192,128},{256,192},{320,256},{384,320},{4... | collective-permute-start | bytes 589832 | tf_op jit(solution)/shard_map/ppermute | solution.py:403

commit v11 on v10

--- a/solution.py
+++ b/solution.py
@@ -120,29 +120,42 @@
     base[...] = jnp.where(first_device, density.T, 0.0)
 
 
-def pack_body(panel_h, panel_s, front_h, front_s, out, panels, fronts, sems):
+def pack_body(panel_h, panel_s, front_h, front_s, out, panels, fronts, buffer, sems):
     half = panels.shape[1] // 2
     share, size = fronts.shape[1], out.shape[2]
     shares = panels.shape[1] // share
     at = pl.ds(pl.multiple_of(lax.axis_index("col") * 2 * half, 2 * half), 2 * half)
     of = pl.ds(pl.multiple_of(lax.rem(lax.axis_index("pole"), shares) * share, share), share)
-    copies = [
+    loads = [
         pltpu.make_async_copy(panel_h.at[at], panels.at[0], sems.at[0]),
         pltpu.make_async_copy(panel_s.at[at], panels.at[1], sems.at[1]),
         pltpu.make_async_copy(front_h.at[of], fronts.at[0], sems.at[2]),
         pltpu.make_async_copy(front_s.at[of], fronts.at[1], sems.at[3]),
     ]
-    for copy in copies:
-        copy.start()
-    for copy in copies:
-        copy.wait()
+    panel_rows, front_rows = pl.ds(0, 2 * half), pl.ds(2 * half, 2 * share)
+    stores = [
+        pltpu.make_async_copy(buffer.at[:, rows], out.at[:, rows], sems.at[4 + index])
+        for index, rows in enumerate((panel_rows, front_rows))
+    ]
+    for load in loads:
+        load.start()
+    loads[0].wait()
+    loads[1].wait()
     for row in range(out.shape[0]):
         core = row % 2
         for part in range(2):
             low = part * half
-            out[row, low : low + half] = panels[part, core * half : (core + 1) * half]
+            buffer[row, low : low + half] = panels[part, core * half : (core + 1) * half]
+    stores[0].start()
+    loads[2].wait()
+    loads[3].wait()
+    for row in range(out.shape[0]):
+        for part in range(2):
             low = 2 * half + part * share
-            out[row, low : low + share] = fronts[part, :, row * size : (row + 1) * size]
+            buffer[row, low : low + share] = fronts[part, :, row * size : (row + 1) * size]
+    stores[1].start()
+    for store in stores:
+        store.wait()
 
 
 def solve_body(shift, received, inverse, solved, up, down):
@@ -177,25 +190,41 @@
             out[(2 * pair + 1) * poles + pole, at : at + half] = odd.astype(out.dtype)
 
 
-def column_body(weight, mine, other, ancestor, right, base, out, far):
-    strips, half = ancestor.shape[1], ancestor.shape[2] // 2
-    size = ancestor.shape[3]
-    wide = mine.shape[1]
-    top, bottom = ordered(mine[...], other[...])
-    far[:, :half] = top.reshape(strips, half, wide)
-    far[:, half:] = bottom.reshape(strips, half, wide)
-    rows = far[...].reshape(strips * 2 * half, wide)
-    by_real = contract(rows, ancestor[0].reshape(strips * 2 * half, size), 0, 0)
-    by_imag = contract(rows, ancestor[1].reshape(strips * 2 * half, size), 0, 0)
-    part_real = by_real[:size] - by_imag[size:]
-    part_imag = by_real[size:] + by_imag[:size]
+def half_column(solved, ancestor, core):
+    strips, half, size = ancestor.shape[1], ancestor.shape[2] // 2, ancestor.shape[3]
+    at = pl.ds(pl.multiple_of(core * half, half), half)
+    rows = solved[...]
+    by_real = contract(rows, ancestor[0, :, at, :].reshape(strips * half, size), 0, 0)
+    by_imag = contract(rows, ancestor[1, :, at, :].reshape(strips * half, size), 0, 0)
+    return by_real[:size] - by_imag[size:], by_real[size:] + by_imag[:size]
+
+
+def own_column_body(mine, ancestor, part):
+    size = part.shape[1]
+    part[:size], part[size:] = half_column(mine, ancestor, lax.rem(lax.axis_index("row"), 2))
+
+
+def column_body(weight, other, ancestor, part, right, base, out, buffer, sems):
+    size = part.shape[1]
+    half = out.shape[1] // 2
+    part_real, part_imag = half_column(other, ancestor, 1 - lax.rem(lax.axis_index("row"), 2))
+    part_real += part[:size]
+    part_imag += part[size:]
+    stores = [
+        pltpu.make_async_copy(buffer.at[:, rows], out.at[:, rows], sems.at[index])
+        for index, rows in enumerate((pl.ds(0, half), pl.ds(half, half)))
+    ]
     weight_real, weight_imag = weight[0, 0], weight[0, 1]
     density = -(weight_real * part_imag + weight_imag * part_real)
+    fold(density, buffer, 0)
+    stores[0].start()
     twin = -(weight_real * part_real - weight_imag * part_imag)
     high, low = split(jnp.concatenate([density, twin], axis=1))
     pivot = base[...] - (dot(high, right[...]) + dot(low, right[...]))
-    fold(density, out, 0)
-    fold(pivot, out, out.shape[1] // 2)
+    fold(pivot, buffer, half)
+    stores[1].start()
+    for store in stores:
+        store.wait()
 
 
 def sums_body(parts, spread, rows):
@@ -324,11 +353,12 @@
         pack_body,
         out_shape=[shape(row_count, width + 2 * share, size)],
         in_specs=[pl.BlockSpec(memory_space=pl.ANY)] * 4,
-        out_specs=[VMEM],
+        out_specs=[pl.BlockSpec(memory_space=pl.ANY)],
         scratch_shapes=[
             pltpu.VMEM((2, width, size), bf16),
             pltpu.VMEM((2, share, row_count * size), bf16),
-            pltpu.SemaphoreType.DMA((4,)),
+            pltpu.VMEM((row_count, width + 2 * share, size), bf16),
+            pltpu.SemaphoreType.DMA((6,)),
         ],
         cost_estimate=pl.CostEstimate(flops=0, bytes_accessed=2**20, transcendentals=0),
         name="pack",
@@ -342,6 +372,14 @@
         6 * 4 * 3 * 2 * size**3,
         "pivot_inverse",
     )
+    right, base = call(
+        local_body,
+        [shape(2 * size, size), shape(size, size, dtype=f32)],
+        [pole_shift, pole_weight, panel_h, panel_s, inverse],
+        2 * 8 * size**3,
+        "local_rows",
+    )
+    inverse, right, base = lax.optimization_barrier((inverse, right, base))
     less = row_count // 4
     more = row_count - less
     mine, up, down = call(
@@ -352,27 +390,27 @@
         "solved_rows",
     )
     other = lax.ppermute(mine, "row", neighbour)
-    right, base = call(
-        local_body,
-        [shape(2 * size, size), shape(size, size, dtype=f32)],
-        [pole_shift, pole_weight, panel_h, panel_s, inverse],
-        2 * 8 * size**3,
-        "local_rows",
-    )
-
     ancestor = ancestor_inverse.reshape(2, row_count, width, size)
+    (part,) = call(
+        own_column_body,
+        [shape(2 * size, size, dtype=f32)],
+        [mine, ancestor],
+        4 * row_count * width * size * size,
+        "own_column",
+    )
+    folded = (col_count * pole_count, piece, 128)
     (both,) = pl.pallas_call(
         column_body,
-        out_shape=[shape(pole_count * col_count, piece, 128)],
+        out_shape=[shape(*folded)],
         in_specs=[SMEM] + [VMEM] * 5,
-        out_specs=[VMEM],
-        scratch_shapes=[pltpu.VMEM((row_count, width, 2 * size), bf16)],
+        out_specs=[pl.BlockSpec(memory_space=pl.ANY)],
+        scratch_shapes=[pltpu.VMEM(folded, bf16), pltpu.SemaphoreType.DMA((2,))],
         compiler_params=pltpu.CompilerParams(vmem_limit_bytes=16 * 2**20),
         cost_estimate=pl.CostEstimate(
-            flops=8 * row_count * width * size * size, bytes_accessed=4 * 2**20, transcendentals=0
+            flops=4 * row_count * width * size * size, bytes_accessed=2 * 2**20, transcendentals=0
         ),
         name="column",
-    )(pole_weight, mine, other, ancestor, right, base)
+    )(pole_weight, other, ancestor, part, right, base)
 
     onward = [(i, (i + 1) % pole_count) for i in range(pole_count)]
     back = [(i, (i - 1) % pole_count) for i in range(pole_count)]

time: 89.4 us -> 88.3 us (0.988)
  waiting for transfers between devices: 25.7 us -> 24.7 us
    all_to_all x1, waiting for transfers between devices: 18.8 us -> 16.4 us  [shards(): lax.all_to_all(sent, 'row', split_axis=0, concat_axis=0, tiled=True)]
    ppermute x1, waiting for transfers between devices: 0.01 us -> 1.39 us  [shards(): other = lax.ppermute(mine, 'row', neighbour)]
    pallas_call x7 -> x8, Pallas kernels: 8.83 us -> 9.29 us  [call(): pl.pallas_call(body, out_shape=outs, in_specs=[SMEM if x.size <= 256 else...]
  transfers between devices with their start and end apart: 8 -> 8, of which waited for: 4 -> 5; matrix products, arithmetic and copies ran while one was open for 0% -> 0% of each run, Pallas kernels for 11% -> 12%
where the time goes in v11:
time: 88.3 us; the launch traced here: 87.1 us
  starting transfers between devices  43.5 us (49%)
  waiting for transfers between devices  24.7 us (28%)
  Pallas kernels  16.5 us (19%)
  local copies, waits for them, and re-layouts  1.44 us (2%)
  between operations  0.92 us (1%)
    all_to_all x1, waiting for transfers between devices, shards(): lax.all_to_all(sent, 'row', split_axis=0, concat_axis=0, tiled=True)  16.4 us
    all_to_all x1, starting transfers between devices, shards(): lax.all_to_all(sent, 'row', split_axis=0, concat_axis=0, tiled=True)  11.8 us
    all_to_all x1, starting transfers between devices, shards(): lax.all_to_all(both, ('col', 'pole'), split_axis=0, concat_axis=0, tiled=...  9.69 us
    pallas_call x8, Pallas kernels, call(): pl.pallas_call(body, out_shape=outs, in_specs=[SMEM if x.size <= 256 else...  9.29 us
    all_to_all x1, starting transfers between devices, shards(): lax.all_to_all(spread, ('row', 'col'), split_axis=0, concat_axis=0, tiled...  7.04 us
    ppermute x1, starting transfers between devices, shards(): above = lax.ppermute(above, 'pole', back)  4.19 us
    all_to_all x1, waiting for transfers between devices, shards(): lax.all_to_all(both, ('col', 'pole'), split_axis=0, concat_axis=0, tiled=...  3.6 us
    ppermute x1, starting transfers between devices, shards(): from_above = lax.ppermute(down, 'pole', back)  3.36 us
  transfers between devices with their start and end apart: 8, of which 5 were waited for; matrix products, arithmetic and copies ran while one was open for 0% of the time, Pallas kernels for 12%

profile of v11, /device:TPU:1, one launch (start us, length us, event | category | flops | bytes accessed | tf_op | source)
XLA Modules:
  0.0 87.1 jit_solution(8412121192276446862)
XLA Ops:
  0.6 0.0 copy-start.8
  0.6 0.0 copy-start.11
  0.7 0.0 copy-start.10
  0.7 1.8 %pack.1 = bf16[16,96,256]{2,1,0:T(8,128)(2,1)} custom-call(bf16[256,256]{1,0:T(8,128)(2,1)} %panel_h.5, bf16[256,256]{1,0:T(8,128)(2,1)} %panel_s.5, bf16[64,4096]{1,0:T(8,128)(2,1)} %front_h.1, bf16[64,4096]{1,0:T(8,128)(2,1)} %front_s.1), custom_call_target="tpu_custom_call" | custom-call | bytes 1048576 | tf_op jit(solution)/shard_map/pack/pallas_call | solution.py:352
  2.5 11.8 %all-to-all-start = ((bf16[16,96,256]{2,1,0:T(8,128)(2,1)}), bf16[16,96,256]{2,1,0:T(8,128)(2,1)S(1)}, u32[]{:S(2)}, u32[]{:S(2)}) async-start(bf16[16,96,256]{2,1,0:T(8,128)(2,1)} %pack.1), calls=%async_computation | async-start | bytes 1572864 | tf_op jit(solution)/shard_map/all_to_all | solution.py:366
  14.3 0.0 copy-done.8
  14.4 0.0 copy-done.11
  14.4 0.0 copy-done.10
  14.4 0.0 copy-start.1
  14.4 0.0 copy-start.2
  14.4 0.0 copy-start.9
  14.4 3.8 %pivot_inverse.1.inverse = bf16[2,256,512]{2,1,0:T(8,128)(2,1)S(1)} custom-call(f32[1,2]{1,0:T(1,128)S(1)} %copy-done.8, bf16[256,256]{1,0:T(8,128)(2,1)S(1)} %copy-done.10, bf16[256,256]{1,0:T(8,128)(2,1)S(1)} %copy-done.11), custom_call_target="tpu_custom_call" | custom-call | flops 2415919104 | bytes 786440 | tf_op jit(solution)/shard_map/pivot_inverse/pallas_call | solution.py:18
  18.2 0.0 copy-done.1
  18.2 0.0 copy-done.2
  18.2 0.0 copy-done.9
  18.2 0.0 copy-start
  18.2 1.0 %local_rows.1 = (bf16[512,256]{1,0:T(8,128)(2,1)S(1)}, f32[256,256]{1,0:T(8,128)S(1)}) custom-call(f32[1,2]{1,0:T(1,128)S(1)} %copy-done.8, f32[1,2]{1,0:T(1,128)S(1)} %copy-done.9, bf16[256,256]{1,0:T(8,128)(2,1)S(1)} %copy-done.1, bf16[256,256]{1,0:T(8,128)(2,1)S(1)} %copy-done.2, bf16[2,256,512]{2,1,0:T(8,128)(2,1)S(1)} %pivot_inverse.1.inverse), custom_call_target="tpu_custom_call" | custom-call | flops 268435456 | bytes 1310736 | tf_op jit(solution)/shard_map/local_rows/pallas_call | solution.py:18
  19.2 0.0 copy-start.3
  19.2 0.7 copy-done.3
  19.9 0.0 copy-start.5
  19.9 0.7 copy-done.5
  20.6 16.4 %all-to-all-done.received = bf16[16,96,256]{2,1,0:T(8,128)(2,1)S(1)} async-done(((bf16[16,96,256]{2,1,0:T(8,128)(2,1)}), bf16[16,96,256]{2,1,0:T(8,128)(2,1)S(1)}, u32[]{:S(2)}, u32[]{:S(2)}) %all-to-all-start) | async-done | bytes 786464 | tf_op jit(solution)/shard_map/all_to_all | solution.py:366
  37.0 0.0 copy-start.4
  37.0 0.0 copy-start.6
  37.0 1.2 %solved_rows.1 = (bf16[512,512]{1,0:T(8,128)(2,1)S(1)}, bf16[12,32,256]{2,1,0:T(8,128)(2,1)S(1)}, bf16[12,32,256]{2,1,0:T(8,128)(2,1)S(1)}) custom-call(f32[1,2]{1,0:T(1,128)S(1)} %copy-done.8, bf16[16,96,256]{2,1,0:T(8,128)(2,1)S(1)} %all-to-all-done.received, bf16[2,256,512]{2,1,0:T(8,128)(2,1)S(1)} %pivot_inverse.1.inverse), custom_call_target="tpu_custom_call" | custom-call | flops 536870912 | bytes 2228232 | tf_op jit(solution)/shard_map/solved_rows/pallas_call | solution.py:18
  38.3 1.9 %collective-permute-start = (bf16[512,512]{1,0:T(8,128)(2,1)S(1)}, bf16[512,512]{1,0:T(8,128)(2,1)S(1)}, u32[]{:S(2)}, u32[]{:S(2)}) collective-permute-start(bf16[512,512]{1,0:T(8,128)(2,1)S(1)} %get-tuple-element.24.mine), channel_id=1, source_target_pairs={{0,4},{4,0},{8,12},{12,8},{16,20},{20,16},{24,28},{28,24},{32,36},... | collective-permute-start | bytes 1572872 | tf_op jit(solution)/shard_map/ppermute | solution.py:392
  40.2 0.0 copy-done
  40.2 0.5 own_column.1.part
  40.7 1.4 %collective-permute-done.other = bf16[512,512]{1,0:T(8,128)(2,1)S(1)} collective-permute-done((bf16[512,512]{1,0:T(8,128)(2,1)S(1)}, bf16[512,512]{1,0:T(8,128)(2,1)S(1)}, u32[]{:S(2)}, u32[]{:S(2)}) %collective-permute-start) | collective-permute-done | bytes 524320 | tf_op jit(solution)/shard_map/ppermute | solution.py:392
  42.1 0.0 copy-done.4
  42.1 0.0 copy-done.6
  42.1 2.3 %column.1 = bf16[32,32,128]{2,1,0:T(8,128)(2,1)} custom-call(f32[1,2]{1,0:T(1,128)S(1)} %copy-done.9, bf16[512,512]{1,0:T(8,128)(2,1)S(1)} %collective-permute-done.other, bf16[2,16,64,256]{3,2,1,0:T(8,128)(2,1)S(1)} %bitcast.7, f32[512,256]{1,0:T(8,128)S(1)} %own_column.1.part, bf16[512,256]{1,0:T(8,128)(2,1)S(1)} %copy-done.4, f32[256,256]{1,0:T(8,128)S(1)} %copy-done.6), custom_call_target="tpu_custom_call" | custom-call | flops 268435456 | bytes 2097152 | tf_op jit(solution)/shard_map/column/pallas_call | solution.py:402
  44.3 9.7 %all-to-all-start.1 = ((bf16[32,32,128]{2,1,0:T(8,128)(2,1)}), bf16[32,32,128]{2,1,0:T(8,128)(2,1)S(1)}, u32[]{:S(2)}, u32[]{:S(2)}) async-start(bf16[32,32,128]{2,1,0:T(8,128)(2,1)} %column.1), calls=%async_computation.1 | async-start | bytes 524288 | tf_op jit(solution)/shard_map/all_to_all | solution.py:421
  54.0 3.1 %collective-permute-start.1 = (bf16[12,32,256]{2,1,0:T(8,128)(2,1)S(1)}, bf16[12,32,256]{2,1,0:T(8,128)(2,1)S(1)}, u32[]{:S(2)}, u32[]{:S(2)}) collective-permute-start(bf16[12,32,256]{2,1,0:T(8,128)(2,1)S(1)} %get-tuple-element.29.up), channel_id=1, source_target_pairs={{0,64},{64,128},{128,192},{192,256},{256,320},{320,384},{384,448},... | collective-permute-start | bytes 589832 | tf_op jit(solution)/shard_map/ppermute | solution.py:418
  57.2 3.4 %collective-permute-start.2 = (bf16[12,32,256]{2,1,0:T(8,128)(2,1)S(1)}, bf16[12,32,256]{2,1,0:T(8,128)(2,1)S(1)}, u32[]{:S(2)}, u32[]{:S(2)}) collective-permute-start(bf16[12,32,256]{2,1,0:T(8,128)(2,1)S(1)} %get-tuple-element.30.down), channel_id=1, source_target_pairs={{0,448},{64,0},{128,64},{192,128},{256,192},{320,256},{384,320},{4... | collective-permute-start | bytes 589832 | tf_op jit(solution)/shard_map/ppermute | solution.py:419
  60.5 3.6 %all-to-all-done.1.parts = bf16[32,32,128]{2,1,0:T(8,128)(2,1)S(1)} async-done(((bf16[32,32,128]{2,1,0:T(8,128)(2,1)}), bf16[32,32,128]{2,1,0:T(8,128)(2,1)S(1)}, u32[]{:S(2)}, u32[]{:S(2)}) %all-to-all-start.1) | async-done | bytes 262176 | tf_op jit(solution)/shard_map/all_to_all | solution.py:421
  64.1 0.8 sums.1
  64.9 1.9 %collective-permute-done.1.from_below = bf16[12,32,256]{2,1,0:T(8,128)(2,1)S(1)} collective-permute-done((bf16[12,32,256]{2,1,0:T(8,128)(2,1)S(1)}, bf16[12,32,256]{2,1,0:T(8,128)(2,1)S(1)}, u32[]{:S(2)}, u32[]{:S(2)}) %collective-permute-start.1) | collective-permute-done | bytes 196640 | tf_op jit(solution)/shard_map/ppermute | solution.py:418
  66.8 0.0 collective-permute-done.2.from_above
  66.8 7.0 %all-to-all-start.2 = ((bf16[64,16,128]{2,1,0:T(8,128)(2,1)}), bf16[64,16,128]{2,1,0:T(8,128)(2,1)S(1)}, u32[]{:S(2)}, u32[]{:S(2)}) async-start(bf16[64,16,128]{2,1,0:T(8,128)(2,1)} %get-tuple-element.38), calls=%async_computation.2 | async-start | bytes 524288 | tf_op jit(solution)/shard_map/all_to_all | solution.py:442
  73.8 0.0 copy-start.7
  73.9 2.3 %collective-permute-start.3 = (bf16[12,32,256]{2,1,0:T(8,128)(2,1)S(1)}, bf16[12,32,256]{2,1,0:T(8,128)(2,1)S(1)}, u32[]{:S(2)}, u32[]{:S(2)}) collective-permute-start(bf16[12,32,256]{2,1,0:T(8,128)(2,1)S(1)} %get-tuple-element.35), channel_id=1, source_target_pairs={{0,64},{64,128},{128,192},{192,256},{256,320},{320,384},{384,448},... | collective-permute-start | bytes 589832 | tf_op jit(solution)/shard_map/ppermute | solution.py:440
  76.2 4.2 %collective-permute-start.4 = (bf16[12,32,256]{2,1,0:T(8,128)(2,1)S(1)}, bf16[12,32,256]{2,1,0:T(8,128)(2,1)S(1)}, u32[]{:S(2)}, u32[]{:S(2)}) collective-permute-start(bf16[12,32,256]{2,1,0:T(8,128)(2,1)S(1)} %get-tuple-element.36), channel_id=1, source_target_pairs={{0,448},{64,0},{128,64},{192,128},{256,192},{320,256},{384,320},{4... | collective-permute-start | bytes 589832 | tf_op jit(solution)/shard_map/ppermute | solution.py:441
  80.4 1.3 %update.1 = f32[16,4,16,512]{3,2,1,0:T(8,128)S(1)} custom-call(f32[1,2]{1,0:T(1,128)S(1)} %copy-done.8, bf16[256,256]{1,0:T(8,128)(2,1)S(1)} %copy-done.1, bf16[256,256]{1,0:T(8,128)(2,1)S(1)} %copy-done.2, bf16[512,512]{1,0:T(8,128)(2,1)S(1)} %get-tuple-element.24.mine, bf16[512,512]{1,0:T(8,128)(2,1)S(1)} %collective-permute-done.other), custom_call_target="tpu_custom_call" | custom-call | flops 536870912 | bytes 3407880 | tf_op jit(solution)/shard_map/update/pallas_call | solution.py:18
  81.7 0.0 copy-done.7
  81.7 1.6 %schur_first.1.begun = bf16[2,16,4,16,256]{4,3,2,1,0:T(8,128)(2,1)} custom-call(f32[1,2]{1,0:T(1,128)S(1)} %copy-done.8, s32[16,16]{1,0:T(8,128)S(1)} %copy-done.7, f32[16,4,16,512]{3,2,1,0:T(8,128)S(1)} %update.1, bf16[12,32,256]{2,1,0:T(8,128)(2,1)S(1)} %get-tuple-element.29.up, bf16[12,32,256]{2,1,0:T(8,128)(2,1)S(1)} %get-tuple-element.30.down, ...), custom_call_target="tpu_custom_call" | custom-call | bytes 3145728 | tf_op jit(solution)/shard_map/schur_first/pallas_call | solution.py:455
  83.4 0.0 collective-permute-done.3.below
  83.4 1.4 %collective-permute-done.4.above = bf16[12,32,256]{2,1,0:T(8,128)(2,1)S(1)} collective-permute-done((bf16[12,32,256]{2,1,0:T(8,128)(2,1)S(1)}, bf16[12,32,256]{2,1,0:T(8,128)(2,1)S(1)}, u32[]{:S(2)}, u32[]{:S(2)}) %collective-permute-start.4) | collective-permute-done | bytes 196640 | tf_op jit(solution)/shard_map/ppermute | solution.py:441
  84.8 1.5 %schur_last.1 = bf16[2,16,4,16,256]{4,3,2,1,0:T(8,128)(2,1)} custom-call(f32[1,2]{1,0:T(1,128)S(1)} %copy-done.8, s32[16,16]{1,0:T(8,128)S(1)} %copy-done.7, f32[16,4,16,512]{3,2,1,0:T(8,128)S(1)} %update.1, bf16[12,32,256]{2,1,0:T(8,128)(2,1)S(1)} %collective-permute-done.3.below, ...), custom_call_target="tpu_custom_call", output_to_operand_aliasing={{}: (5, {})} | custom-call | bytes 3145728 | tf_op jit(solution)/shard_map/schur_last/pallas_call | solution.py:455
  86.3 0.0 all-to-all-done.2.parts
  86.3 0.7 pivot.1
  (1 shorter events, 0.0 us)
Async XLA Ops:
  0.6 13.7 %copy-start.8 = (f32[1,2]{1,0:T(1,128)S(1)}, f32[1,2]{1,0:T(1,128)}, u32[]{:S(2)}) copy-start(f32[1,2]{1,0:T(1,128)} %shift.11) | copy-start | bytes 28
  0.6 13.7 %copy-start.11 = (bf16[256,256]{1,0:T(8,128)(2,1)S(1)}, bf16[256,256]{1,0:T(8,128)(2,1)}, u32[]{:S(2)}) copy-start(bf16[256,256]{1,0:T(8,128)(2,1)} %pivot_s.1) | copy-start | bytes 393220
  0.7 13.7 %copy-start.10 = (bf16[256,256]{1,0:T(8,128)(2,1)S(1)}, bf16[256,256]{1,0:T(8,128)(2,1)}, u32[]{:S(2)}) copy-start(bf16[256,256]{1,0:T(8,128)(2,1)} %pivot_h.1) | copy-start | bytes 393220
  2.5 34.5 %all-to-all-start = ((bf16[16,96,256]{2,1,0:T(8,128)(2,1)}), bf16[16,96,256]{2,1,0:T(8,128)(2,1)S(1)}, u32[]{:S(2)}, u32[]{:S(2)}) async-start(bf16[16,96,256]{2,1,0:T(8,128)(2,1)} %pack.1), calls=%async_computation | async-start | bytes 1572864 | tf_op jit(solution)/shard_map/all_to_all | solution.py:366
  14.4 3.8 %copy-start.1 = (bf16[256,256]{1,0:T(8,128)(2,1)S(1)}, bf16[256,256]{1,0:T(8,128)(2,1)}, u32[]{:S(2)}) copy-start(bf16[256,256]{1,0:T(8,128)(2,1)} %panel_h.5) | copy-start | bytes 393220
  14.4 3.8 %copy-start.2 = (bf16[256,256]{1,0:T(8,128)(2,1)S(1)}, bf16[256,256]{1,0:T(8,128)(2,1)}, u32[]{:S(2)}) copy-start(bf16[256,256]{1,0:T(8,128)(2,1)} %panel_s.5) | copy-start | bytes 393220
  14.4 3.8 %copy-start.9 = (f32[1,2]{1,0:T(1,128)S(1)}, f32[1,2]{1,0:T(1,128)}, u32[]{:S(2)}) copy-start(f32[1,2]{1,0:T(1,128)} %weight.3) | copy-start | bytes 28
  18.2 22.0 %copy-start = (bf16[1,2,16,1,64,256]{5,4,3,2,1,0:T(8,128)(2,1)S(1)}, bf16[1,2,16,1,64,256]{5,4,3,2,1,0:T(8,128)(2,1)}, u32[]{:S(2)}) copy-start(bf16[1,2,16,1,64,256]{5,4,3,2,1,0:T(8,128)(2,1)} %param.19) | copy-start | bytes 3145732
  19.2 0.7 copy-start.3
  19.9 0.7 copy-start.5
  37.0 5.1 %copy-start.4 = (bf16[512,256]{1,0:T(8,128)(2,1)S(1)}, bf16[512,256]{1,0:T(8,128)(2,1)}, u32[]{:S(2)}) copy-start(bf16[512,256]{1,0:T(8,128)(2,1)} %copy-done.3) | copy-start | bytes 786436
  37.0 5.1 %copy-start.6 = (f32[256,256]{1,0:T(8,128)S(1)}, f32[256,256]{1,0:T(8,128)}, u32[]{:S(2)}) copy-start(f32[256,256]{1,0:T(8,128)} %copy-done.5) | copy-start | bytes 786436
  38.3 3.8 %collective-permute-start = (bf16[512,512]{1,0:T(8,128)(2,1)S(1)}, bf16[512,512]{1,0:T(8,128)(2,1)S(1)}, u32[]{:S(2)}, u32[]{:S(2)}) collective-permute-start(bf16[512,512]{1,0:T(8,128)(2,1)S(1)} %get-tuple-element.24.mine), channel_id=1, source_target_pairs={{0,4},{4,0},{8,12},{12,8},{16,20},{20,16},{24,28},{28,24},{32,36},... | collective-permute-start | bytes 1572872 | tf_op jit(solution)/shard_map/ppermute | solution.py:392
  44.3 19.8 %all-to-all-start.1 = ((bf16[32,32,128]{2,1,0:T(8,128)(2,1)}), bf16[32,32,128]{2,1,0:T(8,128)(2,1)S(1)}, u32[]{:S(2)}, u32[]{:S(2)}) async-start(bf16[32,32,128]{2,1,0:T(8,128)(2,1)} %column.1), calls=%async_computation.1 | async-start | bytes 524288 | tf_op jit(solution)/shard_map/all_to_all | solution.py:421
  54.0 12.8 %collective-permute-start.1 = (bf16[12,32,256]{2,1,0:T(8,128)(2,1)S(1)}, bf16[12,32,256]{2,1,0:T(8,128)(2,1)S(1)}, u32[]{:S(2)}, u32[]{:S(2)}) collective-permute-start(bf16[12,32,256]{2,1,0:T(8,128)(2,1)S(1)} %get-tuple-element.29.up), channel_id=1, source_target_pairs={{0,64},{64,128},{128,192},{192,256},{256,320},{320,384},{384,448},... | collective-permute-start | bytes 589832 | tf_op jit(solution)/shard_map/ppermute | solution.py:418
  57.2 9.6 %collective-permute-start.2 = (bf16[12,32,256]{2,1,0:T(8,128)(2,1)S(1)}, bf16[12,32,256]{2,1,0:T(8,128)(2,1)S(1)}, u32[]{:S(2)}, u32[]{:S(2)}) collective-permute-start(bf16[12,32,256]{2,1,0:T(8,128)(2,1)S(1)} %get-tuple-element.30.down), channel_id=1, source_target_pairs={{0,448},{64,0},{128,64},{192,128},{256,192},{320,256},{384,320},{4... | collective-permute-start | bytes 589832 | tf_op jit(solution)/shard_map/ppermute | solution.py:419
  66.8 19.5 %all-to-all-start.2 = ((bf16[64,16,128]{2,1,0:T(8,128)(2,1)}), bf16[64,16,128]{2,1,0:T(8,128)(2,1)S(1)}, u32[]{:S(2)}, u32[]{:S(2)}) async-start(bf16[64,16,128]{2,1,0:T(8,128)(2,1)} %get-tuple-element.38), calls=%async_computation.2 | async-start | bytes 524288 | tf_op jit(solution)/shard_map/all_to_all | solution.py:442
  73.8 7.9 %copy-start.7 = (s32[16,16]{1,0:T(8,128)S(1)}, s32[16,16]{1,0:T(8,128)}, u32[]{:S(2)}) copy-start(s32[16,16]{1,0:T(8,128)} %pattern.3) | copy-start | bytes 3076
  73.9 9.5 %collective-permute-start.3 = (bf16[12,32,256]{2,1,0:T(8,128)(2,1)S(1)}, bf16[12,32,256]{2,1,0:T(8,128)(2,1)S(1)}, u32[]{:S(2)}, u32[]{:S(2)}) collective-permute-start(bf16[12,32,256]{2,1,0:T(8,128)(2,1)S(1)} %get-tuple-element.35), channel_id=1, source_target_pairs={{0,64},{64,128},{128,192},{192,256},{256,320},{320,384},{384,448},... | collective-permute-start | bytes 589832 | tf_op jit(solution)/shard_map/ppermute | solution.py:440
  76.2 8.6 %collective-permute-start.4 = (bf16[12,32,256]{2,1,0:T(8,128)(2,1)S(1)}, bf16[12,32,256]{2,1,0:T(8,128)(2,1)S(1)}, u32[]{:S(2)}, u32[]{:S(2)}) collective-permute-start(bf16[12,32,256]{2,1,0:T(8,128)(2,1)S(1)} %get-tuple-element.36), channel_id=1, source_target_pairs={{0,448},{64,0},{128,64},{192,128},{256,192},{320,256},{384,320},{4... | collective-permute-start | bytes 589832 | tf_op jit(solution)/shard_map/ppermute | solution.py:441

commit v12 on v11

--- a/solution.py
+++ b/solution.py
@@ -311,16 +311,19 @@
     schur_tiles(shift, pattern, update, members, buffer, out, sems)
 
 
-def schur_last_body(shift, pattern, update, below, above, begun, out, buffer, sems):
+def schur_below_body(shift, pattern, update, below, begun, out, buffer, sems):
     del begun
     half = out.shape[1] // 2
     less = below.shape[0] - half
-    members = (
-        (below, 0, less, -1, 2 * half - less),
-        (below, less, half, -2, 0),
-        (above, 0, less, 1, 0),
-        (above, less, half, 2, half),
-    )
+    members = ((below, 0, less, -1, 2 * half - less), (below, less, half, -2, 0))
+    schur_tiles(shift, pattern, update, members, buffer, out, sems)
+
+
+def schur_above_body(shift, pattern, update, above, begun, out, buffer, sems):
+    del begun
+    half = out.shape[1] // 2
+    less = above.shape[0] - half
+    members = ((above, 0, less, 1, 0), (above, less, half, 2, half))
     schur_tiles(shift, pattern, update, members, buffer, out, sems)
 
 
@@ -429,12 +432,11 @@
         0,
         "sums",
     )
-    from_below, from_above, spread = lax.optimization_barrier((from_below, from_above, spread))
     below, above = call(
         relay_body,
         [shape(more, 2 * share, size)] * 2,
         [up, down, from_below, from_above],
-        0,
+        10**11,
         "relay",
     )
     below = lax.ppermute(below, "pole", onward)
@@ -466,7 +468,8 @@
 
     fixed = [pole_shift, pattern, update]
     schur = tiles(schur_first_body, fixed + [up, down, from_below, from_above], "schur_first")
-    schur = tiles(schur_last_body, fixed + [below, above], "schur_last", (schur,))
+    schur = tiles(schur_below_body, fixed + [below], "schur_below", (schur,))
+    schur = tiles(schur_above_body, fixed + [above], "schur_above", (schur,))
     return (schur.reshape(1, 2, row_count, 1, width, size), rows_out.T, pivot_out.T)
 
 

time: 88.3 us -> 87.7 us (level)
  waiting for transfers between devices: 24.7 us -> 22.8 us
  Pallas kernels: 16.5 us -> 17.9 us
  starting transfers between devices: 43.5 us -> 44.5 us
    ppermute x1, waiting for transfers between devices: 1.88 us -> 0.01 us  [shards(): from_below = lax.ppermute(up, 'pole', onward)]
    ppermute x1, waiting for transfers between devices: 1.41 us -> 0.01 us  [shards(): above = lax.ppermute(above, 'pole', back)]
    all_to_all x1, waiting for transfers between devices: 16.4 us -> 17.8 us  [shards(): lax.all_to_all(sent, 'row', split_axis=0, concat_axis=0, tiled=True)]
    pallas_call x2 -> x3, Pallas kernels: 3.17 us -> 4.55 us  [tiles(): pl.pallas_call(body, out_shape=tile, in_specs=[SMEM] * 2 + [VMEM] * (len(...]
    all_to_all x1, starting transfers between devices: 7.04 us -> 8.02 us  [shards(): lax.all_to_all(spread, ('row', 'col'), split_axis=0, concat_axis=0, tiled...]
  transfers between devices with their start and end apart: 8 -> 8, of which waited for: 5 -> 3; matrix products, arithmetic and copies ran while one was open for 0% -> 0% of each run, Pallas kernels for 12% -> 14%
where the time goes in v12:
time: 87.7 us; the launch traced here: 87.2 us
  starting transfers between devices  44.5 us (51%)
  waiting for transfers between devices  22.8 us (26%)
  Pallas kernels  17.9 us (20%)
  local copies, waits for them, and re-layouts  1.09 us (1%)
  between operations  0.95 us (1%)
    all_to_all x1, waiting for transfers between devices, shards(): lax.all_to_all(sent, 'row', split_axis=0, concat_axis=0, tiled=True)  17.8 us
    all_to_all x1, starting transfers between devices, shards(): lax.all_to_all(sent, 'row', split_axis=0, concat_axis=0, tiled=True)  11.8 us
    all_to_all x1, starting transfers between devices, shards(): lax.all_to_all(both, ('col', 'pole'), split_axis=0, concat_axis=0, tiled=...  9.68 us
    pallas_call x8, Pallas kernels, call(): pl.pallas_call(body, out_shape=outs, in_specs=[SMEM if x.size <= 256 else...  9.29 us
    all_to_all x1, starting transfers between devices, shards(): lax.all_to_all(spread, ('row', 'col'), split_axis=0, concat_axis=0, tiled...  8.02 us
    pallas_call x3, Pallas kernels, tiles(): pl.pallas_call(body, out_shape=tile, in_specs=[SMEM] * 2 + [VMEM] * (len(...  4.55 us
    ppermute x1, starting transfers between devices, shards(): above = lax.ppermute(above, 'pole', back)  3.84 us
    all_to_all x1, waiting for transfers between devices, shards(): lax.all_to_all(both, ('col', 'pole'), split_axis=0, concat_axis=0, tiled=...  3.6 us
  transfers between devices with their start and end apart: 8, of which 3 were waited for; matrix products, arithmetic and copies ran while one was open for 0% of the time, Pallas kernels for 14%

profile of v12, /device:TPU:1, one launch (start us, length us, event | category | flops | bytes accessed | tf_op | source)
XLA Modules:
  0.0 87.2 jit_solution(1582842083684190638)
XLA Ops:
  0.6 0.0 copy-start.4
  0.6 0.0 copy-start.7
  0.7 0.0 copy-start.6
  0.7 1.8 %pack.1 = bf16[16,96,256]{2,1,0:T(8,128)(2,1)} custom-call(bf16[256,256]{1,0:T(8,128)(2,1)} %panel_h.5, bf16[256,256]{1,0:T(8,128)(2,1)} %panel_s.5, bf16[64,4096]{1,0:T(8,128)(2,1)} %front_h.1, bf16[64,4096]{1,0:T(8,128)(2,1)} %front_s.1), custom_call_target="tpu_custom_call" | custom-call | bytes 1048576 | tf_op jit(solution)/shard_map/pack/pallas_call | solution.py:355
  2.5 11.8 %all-to-all-start = ((bf16[16,96,256]{2,1,0:T(8,128)(2,1)}), bf16[16,96,256]{2,1,0:T(8,128)(2,1)S(1)}, u32[]{:S(2)}, u32[]{:S(2)}) async-start(bf16[16,96,256]{2,1,0:T(8,128)(2,1)} %pack.1), calls=%async_computation | async-start | bytes 1572864 | tf_op jit(solution)/shard_map/all_to_all | solution.py:369
  14.3 0.0 copy-done.4
  14.4 0.0 copy-done.7
  14.4 0.0 copy-done.6
  14.4 0.0 copy-start.1
  14.4 0.0 copy-start.2
  14.4 0.0 copy-start.5
  14.4 3.8 %pivot_inverse.1.inverse = bf16[2,256,512]{2,1,0:T(8,128)(2,1)S(1)} custom-call(f32[1,2]{1,0:T(1,128)S(1)} %copy-done.4, bf16[256,256]{1,0:T(8,128)(2,1)S(1)} %copy-done.6, bf16[256,256]{1,0:T(8,128)(2,1)S(1)} %copy-done.7), custom_call_target="tpu_custom_call" | custom-call | flops 2415919104 | bytes 786440 | tf_op jit(solution)/shard_map/pivot_inverse/pallas_call | solution.py:18
  18.2 0.0 copy-done.1
  18.2 0.0 copy-done.2
  18.2 0.0 copy-done.5
  18.2 0.0 copy-start.8
  18.2 0.0 copy-start
  18.2 1.0 %local_rows.1 = (bf16[512,256]{1,0:T(8,128)(2,1)S(1)}, f32[256,256]{1,0:T(8,128)S(1)}) custom-call(f32[1,2]{1,0:T(1,128)S(1)} %copy-done.4, f32[1,2]{1,0:T(1,128)S(1)} %copy-done.5, bf16[256,256]{1,0:T(8,128)(2,1)S(1)} %copy-done.1, bf16[256,256]{1,0:T(8,128)(2,1)S(1)} %copy-done.2, bf16[2,256,512]{2,1,0:T(8,128)(2,1)S(1)} %pivot_inverse.1.inverse), custom_call_target="tpu_custom_call" | custom-call | flops 268435456 | bytes 1310736 | tf_op jit(solution)/shard_map/local_rows/pallas_call | solution.py:18
  19.2 0.0 copy-done.8
  19.2 17.8 %all-to-all-done.received = bf16[16,96,256]{2,1,0:T(8,128)(2,1)S(1)} async-done(((bf16[16,96,256]{2,1,0:T(8,128)(2,1)}), bf16[16,96,256]{2,1,0:T(8,128)(2,1)S(1)}, u32[]{:S(2)}, u32[]{:S(2)}) %all-to-all-start) | async-done | bytes 786464 | tf_op jit(solution)/shard_map/all_to_all | solution.py:369
  37.0 0.0 copy-start.9
  37.0 1.0 %copy-done.9 = bf16[2,256,512]{2,1,0:T(8,128)(2,1)S(1)} copy-done((bf16[2,256,512]{2,1,0:T(8,128)(2,1)S(1)}, bf16[2,256,512]{2,1,0:T(8,128)(2,1)}, u32[]{:S(2)}) %copy-start.9) | copy-done | bytes 524312
  38.1 1.2 %solved_rows.1 = (bf16[512,512]{1,0:T(8,128)(2,1)S(1)}, bf16[12,32,256]{2,1,0:T(8,128)(2,1)S(1)}, bf16[12,32,256]{2,1,0:T(8,128)(2,1)S(1)}) custom-call(f32[1,2]{1,0:T(1,128)S(1)} %copy-done.4, bf16[16,96,256]{2,1,0:T(8,128)(2,1)S(1)} %all-to-all-done.received, bf16[2,256,512]{2,1,0:T(8,128)(2,1)S(1)} %copy-done.9), custom_call_target="tpu_custom_call" | custom-call | flops 536870912 | bytes 2228232 | tf_op jit(solution)/shard_map/solved_rows/pallas_call | solution.py:18
  39.3 1.9 %collective-permute-start = (bf16[512,512]{1,0:T(8,128)(2,1)S(1)}, bf16[512,512]{1,0:T(8,128)(2,1)S(1)}, u32[]{:S(2)}, u32[]{:S(2)}) collective-permute-start(bf16[512,512]{1,0:T(8,128)(2,1)S(1)} %get-tuple-element.21.mine), channel_id=1, source_target_pairs={{0,4},{4,0},{8,12},{12,8},{16,20},{20,16},{24,28},{28,24},{32,36},... | collective-permute-start | bytes 1572872 | tf_op jit(solution)/shard_map/ppermute | solution.py:395
  41.2 0.0 copy-done
  41.2 0.5 own_column.1.part
  41.7 1.4 %collective-permute-done.other = bf16[512,512]{1,0:T(8,128)(2,1)S(1)} collective-permute-done((bf16[512,512]{1,0:T(8,128)(2,1)S(1)}, bf16[512,512]{1,0:T(8,128)(2,1)S(1)}, u32[]{:S(2)}, u32[]{:S(2)}) %collective-permute-start) | collective-permute-done | bytes 524320 | tf_op jit(solution)/shard_map/ppermute | solution.py:395
  43.1 2.2 %column.1 = bf16[32,32,128]{2,1,0:T(8,128)(2,1)} custom-call(f32[1,2]{1,0:T(1,128)S(1)} %copy-done.5, bf16[512,512]{1,0:T(8,128)(2,1)S(1)} %collective-permute-done.other, bf16[2,16,64,256]{3,2,1,0:T(8,128)(2,1)S(1)} %bitcast.7, f32[512,256]{1,0:T(8,128)S(1)} %own_column.1.part, bf16[512,256]{1,0:T(8,128)(2,1)S(1)} %get-tuple-element.24.right, ...), custom_call_target="tpu_custom_call" | custom-call | flops 268435456 | bytes 2097152 | tf_op jit(solution)/shard_map/column/pallas_call | solution.py:405
  45.4 9.7 %all-to-all-start.1 = ((bf16[32,32,128]{2,1,0:T(8,128)(2,1)}), bf16[32,32,128]{2,1,0:T(8,128)(2,1)S(1)}, u32[]{:S(2)}, u32[]{:S(2)}) async-start(bf16[32,32,128]{2,1,0:T(8,128)(2,1)} %column.1), calls=%async_computation.1 | async-start | bytes 524288 | tf_op jit(solution)/shard_map/all_to_all | solution.py:424
  55.1 3.1 %collective-permute-start.1 = (bf16[12,32,256]{2,1,0:T(8,128)(2,1)S(1)}, bf16[12,32,256]{2,1,0:T(8,128)(2,1)S(1)}, u32[]{:S(2)}, u32[]{:S(2)}) collective-permute-start(bf16[12,32,256]{2,1,0:T(8,128)(2,1)S(1)} %get-tuple-element.26.up), channel_id=1, source_target_pairs={{0,64},{64,128},{128,192},{192,256},{256,320},{320,384},{384,448},... | collective-permute-start | bytes 589832 | tf_op jit(solution)/shard_map/ppermute | solution.py:421
  58.2 3.4 %collective-permute-start.2 = (bf16[12,32,256]{2,1,0:T(8,128)(2,1)S(1)}, bf16[12,32,256]{2,1,0:T(8,128)(2,1)S(1)}, u32[]{:S(2)}, u32[]{:S(2)}) collective-permute-start(bf16[12,32,256]{2,1,0:T(8,128)(2,1)S(1)} %get-tuple-element.27.down), channel_id=1, source_target_pairs={{0,448},{64,0},{128,64},{192,128},{256,192},{320,256},{384,320},{4... | collective-permute-start | bytes 589832 | tf_op jit(solution)/shard_map/ppermute | solution.py:422
  61.6 3.6 %all-to-all-done.1.parts = bf16[32,32,128]{2,1,0:T(8,128)(2,1)S(1)} async-done(((bf16[32,32,128]{2,1,0:T(8,128)(2,1)}), bf16[32,32,128]{2,1,0:T(8,128)(2,1)S(1)}, u32[]{:S(2)}, u32[]{:S(2)}) %all-to-all-start.1) | async-done | bytes 262176 | tf_op jit(solution)/shard_map/all_to_all | solution.py:424
  65.2 0.8 sums.1
  65.9 8.0 %all-to-all-start.2 = ((bf16[64,16,128]{2,1,0:T(8,128)(2,1)}), bf16[64,16,128]{2,1,0:T(8,128)(2,1)S(1)}, u32[]{:S(2)}, u32[]{:S(2)}) async-start(bf16[64,16,128]{2,1,0:T(8,128)(2,1)} %get-tuple-element.32), calls=%async_computation.2 | async-start | bytes 524288 | tf_op jit(solution)/shard_map/all_to_all | solution.py:444
  74.0 0.0 collective-permute-done.1.from_below
  74.0 0.0 collective-permute-done.2.from_above
  74.0 0.0 copy-start.3
  74.0 2.7 %collective-permute-start.4 = (bf16[12,32,256]{2,1,0:T(8,128)(2,1)S(1)}, bf16[12,32,256]{2,1,0:T(8,128)(2,1)S(1)}, u32[]{:S(2)}, u32[]{:S(2)}) collective-permute-start(bf16[12,32,256]{2,1,0:T(8,128)(2,1)S(1)} %get-tuple-element.29), channel_id=1, source_target_pairs={{0,64},{64,128},{128,192},{192,256},{256,320},{320,384},{384,448},... | collective-permute-start | bytes 589832 | tf_op jit(solution)/shard_map/ppermute | solution.py:442
  76.7 3.8 %collective-permute-start.3 = (bf16[12,32,256]{2,1,0:T(8,128)(2,1)S(1)}, bf16[12,32,256]{2,1,0:T(8,128)(2,1)S(1)}, u32[]{:S(2)}, u32[]{:S(2)}) collective-permute-start(bf16[12,32,256]{2,1,0:T(8,128)(2,1)S(1)} %get-tuple-element.28), channel_id=1, source_target_pairs={{0,448},{64,0},{128,64},{192,128},{256,192},{320,256},{384,320},{4... | collective-permute-start | bytes 589832 | tf_op jit(solution)/shard_map/ppermute | solution.py:443
  80.5 1.3 %update.1 = f32[16,4,16,512]{3,2,1,0:T(8,128)S(1)} custom-call(f32[1,2]{1,0:T(1,128)S(1)} %copy-done.4, bf16[256,256]{1,0:T(8,128)(2,1)S(1)} %copy-done.1, bf16[256,256]{1,0:T(8,128)(2,1)S(1)} %copy-done.2, bf16[512,512]{1,0:T(8,128)(2,1)S(1)} %get-tuple-element.21.mine, bf16[512,512]{1,0:T(8,128)(2,1)S(1)} %collective-permute-done.other), custom_call_target="tpu_custom_call" | custom-call | flops 536870912 | bytes 3407880 | tf_op jit(solution)/shard_map/update/pallas_call | solution.py:18
  81.8 0.0 copy-done.3
  81.8 1.6 %schur_first.1.begun = bf16[2,16,4,16,256]{4,3,2,1,0:T(8,128)(2,1)} custom-call(f32[1,2]{1,0:T(1,128)S(1)} %copy-done.4, s32[16,16]{1,0:T(8,128)S(1)} %copy-done.3, f32[16,4,16,512]{3,2,1,0:T(8,128)S(1)} %update.1, bf16[12,32,256]{2,1,0:T(8,128)(2,1)S(1)} %get-tuple-element.26.up, bf16[12,32,256]{2,1,0:T(8,128)(2,1)S(1)} %get-tuple-element.27.down, ...), custom_call_target="tpu_custom_call" | custom-call | bytes 3145728 | tf_op jit(solution)/shard_map/schur_first/pallas_call | solution.py:457
  83.5 0.0 collective-permute-done.4.below
  83.5 1.5 %schur_below.1.begun = bf16[2,16,4,16,256]{4,3,2,1,0:T(8,128)(2,1)} custom-call(f32[1,2]{1,0:T(1,128)S(1)} %copy-done.4, s32[16,16]{1,0:T(8,128)S(1)} %copy-done.3, f32[16,4,16,512]{3,2,1,0:T(8,128)S(1)} %update.1, bf16[12,32,256]{2,1,0:T(8,128)(2,1)S(1)} %collective-permute-done.4.below, ...), custom_call_target="tpu_custom_call", output_to_operand_aliasing={{}: (4, {})} | custom-call | bytes 3145728 | tf_op jit(solution)/shard_map/schur_below/pallas_call | solution.py:457
  85.0 0.0 collective-permute-done.3.above
  85.0 1.5 %schur_above.1 = bf16[2,16,4,16,256]{4,3,2,1,0:T(8,128)(2,1)} custom-call(f32[1,2]{1,0:T(1,128)S(1)} %copy-done.4, s32[16,16]{1,0:T(8,128)S(1)} %copy-done.3, f32[16,4,16,512]{3,2,1,0:T(8,128)S(1)} %update.1, bf16[12,32,256]{2,1,0:T(8,128)(2,1)S(1)} %collective-permute-done.3.above, ...), custom_call_target="tpu_custom_call", output_to_operand_aliasing={{}: (4, {})} | custom-call | bytes 3145728 | tf_op jit(solution)/shard_map/schur_above/pallas_call | solution.py:457
  86.4 0.0 all-to-all-done.2.parts
  86.4 0.7 pivot.1
  (1 shorter events, 0.0 us)
Async XLA Ops:
  0.6 13.7 %copy-start.4 = (f32[1,2]{1,0:T(1,128)S(1)}, f32[1,2]{1,0:T(1,128)}, u32[]{:S(2)}) copy-start(f32[1,2]{1,0:T(1,128)} %shift.13) | copy-start | bytes 28
  0.6 13.7 %copy-start.7 = (bf16[256,256]{1,0:T(8,128)(2,1)S(1)}, bf16[256,256]{1,0:T(8,128)(2,1)}, u32[]{:S(2)}) copy-start(bf16[256,256]{1,0:T(8,128)(2,1)} %pivot_s.1) | copy-start | bytes 393220
  0.7 13.7 %copy-start.6 = (bf16[256,256]{1,0:T(8,128)(2,1)S(1)}, bf16[256,256]{1,0:T(8,128)(2,1)}, u32[]{:S(2)}) copy-start(bf16[256,256]{1,0:T(8,128)(2,1)} %pivot_h.1) | copy-start | bytes 393220
  2.5 34.5 %all-to-all-start = ((bf16[16,96,256]{2,1,0:T(8,128)(2,1)}), bf16[16,96,256]{2,1,0:T(8,128)(2,1)S(1)}, u32[]{:S(2)}, u32[]{:S(2)}) async-start(bf16[16,96,256]{2,1,0:T(8,128)(2,1)} %pack.1), calls=%async_computation | async-start | bytes 1572864 | tf_op jit(solution)/shard_map/all_to_all | solution.py:369
  14.4 3.8 %copy-start.1 = (bf16[256,256]{1,0:T(8,128)(2,1)S(1)}, bf16[256,256]{1,0:T(8,128)(2,1)}, u32[]{:S(2)}) copy-start(bf16[256,256]{1,0:T(8,128)(2,1)} %panel_h.5) | copy-start | bytes 393220
  14.4 3.8 %copy-start.2 = (bf16[256,256]{1,0:T(8,128)(2,1)S(1)}, bf16[256,256]{1,0:T(8,128)(2,1)}, u32[]{:S(2)}) copy-start(bf16[256,256]{1,0:T(8,128)(2,1)} %panel_s.5) | copy-start | bytes 393220
  14.4 3.8 %copy-start.5 = (f32[1,2]{1,0:T(1,128)S(1)}, f32[1,2]{1,0:T(1,128)}, u32[]{:S(2)}) copy-start(f32[1,2]{1,0:T(1,128)} %weight.3) | copy-start | bytes 28
  18.2 1.0 %copy-start.8 = (bf16[2,256,512]{2,1,0:T(8,128)(2,1)}, bf16[2,256,512]{2,1,0:T(8,128)(2,1)S(1)}, u32[]{:S(2)}) copy-start(bf16[2,256,512]{2,1,0:T(8,128)(2,1)S(1)} %pivot_inverse.1.inverse) | copy-start | bytes 1572868
  18.2 23.0 %copy-start = (bf16[1,2,16,1,64,256]{5,4,3,2,1,0:T(8,128)(2,1)S(1)}, bf16[1,2,16,1,64,256]{5,4,3,2,1,0:T(8,128)(2,1)}, u32[]{:S(2)}) copy-start(bf16[1,2,16,1,64,256]{5,4,3,2,1,0:T(8,128)(2,1)} %param.19) | copy-start | bytes 3145732
  37.0 1.0 %copy-start.9 = (bf16[2,256,512]{2,1,0:T(8,128)(2,1)S(1)}, bf16[2,256,512]{2,1,0:T(8,128)(2,1)}, u32[]{:S(2)}) copy-start(bf16[2,256,512]{2,1,0:T(8,128)(2,1)} %copy-done.8) | copy-start | bytes 1572868
  39.3 3.8 %collective-permute-start = (bf16[512,512]{1,0:T(8,128)(2,1)S(1)}, bf16[512,512]{1,0:T(8,128)(2,1)S(1)}, u32[]{:S(2)}, u32[]{:S(2)}) collective-permute-start(bf16[512,512]{1,0:T(8,128)(2,1)S(1)} %get-tuple-element.21.mine), channel_id=1, source_target_pairs={{0,4},{4,0},{8,12},{12,8},{16,20},{20,16},{24,28},{28,24},{32,36},... | collective-permute-start | bytes 1572872 | tf_op jit(solution)/shard_map/ppermute | solution.py:395
  45.4 19.8 %all-to-all-start.1 = ((bf16[32,32,128]{2,1,0:T(8,128)(2,1)}), bf16[32,32,128]{2,1,0:T(8,128)(2,1)S(1)}, u32[]{:S(2)}, u32[]{:S(2)}) async-start(bf16[32,32,128]{2,1,0:T(8,128)(2,1)} %column.1), calls=%async_computation.1 | async-start | bytes 524288 | tf_op jit(solution)/shard_map/all_to_all | solution.py:424
  55.1 18.9 %collective-permute-start.1 = (bf16[12,32,256]{2,1,0:T(8,128)(2,1)S(1)}, bf16[12,32,256]{2,1,0:T(8,128)(2,1)S(1)}, u32[]{:S(2)}, u32[]{:S(2)}) collective-permute-start(bf16[12,32,256]{2,1,0:T(8,128)(2,1)S(1)} %get-tuple-element.26.up), channel_id=1, source_target_pairs={{0,64},{64,128},{128,192},{192,256},{256,320},{320,384},{384,448},... | collective-permute-start | bytes 589832 | tf_op jit(solution)/shard_map/ppermute | solution.py:421
  58.2 15.8 %collective-permute-start.2 = (bf16[12,32,256]{2,1,0:T(8,128)(2,1)S(1)}, bf16[12,32,256]{2,1,0:T(8,128)(2,1)S(1)}, u32[]{:S(2)}, u32[]{:S(2)}) collective-permute-start(bf16[12,32,256]{2,1,0:T(8,128)(2,1)S(1)} %get-tuple-element.27.down), channel_id=1, source_target_pairs={{0,448},{64,0},{128,64},{192,128},{256,192},{320,256},{384,320},{4... | collective-permute-start | bytes 589832 | tf_op jit(solution)/shard_map/ppermute | solution.py:422
  65.9 20.5 %all-to-all-start.2 = ((bf16[64,16,128]{2,1,0:T(8,128)(2,1)}), bf16[64,16,128]{2,1,0:T(8,128)(2,1)S(1)}, u32[]{:S(2)}, u32[]{:S(2)}) async-start(bf16[64,16,128]{2,1,0:T(8,128)(2,1)} %get-tuple-element.32), calls=%async_computation.2 | async-start | bytes 524288 | tf_op jit(solution)/shard_map/all_to_all | solution.py:444
  74.0 7.8 %copy-start.3 = (s32[16,16]{1,0:T(8,128)S(1)}, s32[16,16]{1,0:T(8,128)}, u32[]{:S(2)}) copy-start(s32[16,16]{1,0:T(8,128)} %pattern.5) | copy-start | bytes 3076
  74.0 9.5 %collective-permute-start.4 = (bf16[12,32,256]{2,1,0:T(8,128)(2,1)S(1)}, bf16[12,32,256]{2,1,0:T(8,128)(2,1)S(1)}, u32[]{:S(2)}, u32[]{:S(2)}) collective-permute-start(bf16[12,32,256]{2,1,0:T(8,128)(2,1)S(1)} %get-tuple-element.29), channel_id=1, source_target_pairs={{0,64},{64,128},{128,192},{192,256},{256,320},{320,384},{384,448},... | collective-permute-start | bytes 589832 | tf_op jit(solution)/shard_map/ppermute | solution.py:442
  76.7 8.3 %collective-permute-start.3 = (bf16[12,32,256]{2,1,0:T(8,128)(2,1)S(1)}, bf16[12,32,256]{2,1,0:T(8,128)(2,1)S(1)}, u32[]{:S(2)}, u32[]{:S(2)}) collective-permute-start(bf16[12,32,256]{2,1,0:T(8,128)(2,1)S(1)} %get-tuple-element.28), channel_id=1, source_target_pairs={{0,448},{64,0},{128,64},{192,128},{256,192},{320,256},{384,320},{4... | collective-permute-start | bytes 589832 | tf_op jit(solution)/shard_map/ppermute | solution.py:443

commit v13 on v11

--- a/solution.py
+++ b/solution.py
@@ -109,15 +109,23 @@
     return (dot(coupling, block(inverse[0])) + dot(coupling, block(inverse[1]))).astype(bf16)
 
 
-def local_body(shift, weight, panel_h, panel_s, inverse, right, base):
+def local_body(shift, weight, panel_h, panel_s, inverse, right, base, rights, bases, sems):
     size = panel_h.shape[1]
     solved = solve(panel_h[...], panel_s[...], shift, inverse)
-    right[:size] = solved[:, :size]
-    right[size:] = solved[:, size:]
+    rights[:size] = solved[:, :size]
+    rights[size:] = solved[:, size:]
     whole = inverse[0].astype(f32) + inverse[1].astype(f32)
     density = weight[0, 0] * whole[:, size:] + weight[0, 1] * whole[:, :size]
     first_device = (lax.axis_index("row") == 0) & (lax.axis_index("col") == 0)
-    base[...] = jnp.where(first_device, density.T, 0.0)
+    bases[...] = jnp.where(first_device, density.T, 0.0)
+    stores = [
+        pltpu.make_async_copy(rights, right, sems.at[0]),
+        pltpu.make_async_copy(bases, base, sems.at[1]),
+    ]
+    for store in stores:
+        store.start()
+    for store in stores:
+        store.wait()
 
 
 def pack_body(panel_h, panel_s, front_h, front_s, out, panels, fronts, buffer, sems):
@@ -158,14 +166,13 @@
         store.wait()
 
 
-def solve_body(shift, received, inverse, solved, up, down):
+def solve_body(shift, received, inverse, solved, fronts):
     strips, rows, size = received.shape
     half = solved.shape[0] // strips
     rows_h = received[:, :half].reshape(strips * half, size)
     rows_s = received[:, half : 2 * half].reshape(strips * half, size)
     solved[...] = solve(rows_h, rows_s, shift, inverse)
-    up[...] = received[: up.shape[0], 2 * half :]
-    down[...] = received[strips - down.shape[0] :, 2 * half :]
+    fronts[...] = received[:, 2 * half :]
 
 
 def ordered(mine, other):
@@ -268,14 +275,10 @@
         out[first : first + group] = update.reshape((group,) + out.shape[1:])
 
 
-def relay_body(up, down, from_below, from_above, below, above):
-    more = up.shape[0]
-    less = more // 3
-    half = more - less
-    below[:less] = down[half:]
-    below[less:] = from_below[:half]
-    above[:less] = up[:less]
-    above[less:] = from_above[less:]
+def relay_body(from_below, from_above, below, above):
+    half = below.shape[0]
+    below[...] = from_below[:half]
+    above[...] = from_above[half:]
 
 
 def schur_tiles(shift, pattern, update, members, buffer, out, sems):
@@ -300,27 +303,20 @@
         copy.wait()
 
 
-def schur_first_body(shift, pattern, update, up, down, from_below, from_above, out, buffer, sems):
-    more, less = up.shape[0], out.shape[1] - up.shape[0]
+def schur_first_body(shift, pattern, update, fronts, from_below, from_above, out, buffer, sems):
+    strips = out.shape[1]
     members = (
-        (up, 0, more, 0, 0),
-        (down, more - less, less, 0, more),
-        (from_below, 0, more, -1, 0),
-        (from_above, 0, more, 1, less),
+        (fronts, 0, strips, 0, 0),
+        (from_below, 0, strips, -1, 0),
+        (from_above, 0, strips, 1, 0),
     )
     schur_tiles(shift, pattern, update, members, buffer, out, sems)
 
 
 def schur_last_body(shift, pattern, update, below, above, begun, out, buffer, sems):
     del begun
-    half = out.shape[1] // 2
-    less = below.shape[0] - half
-    members = (
-        (below, 0, less, -1, 2 * half - less),
-        (below, less, half, -2, 0),
-        (above, 0, less, 1, 0),
-        (above, less, half, 2, half),
-    )
+    half = below.shape[0]
+    members = ((below, 0, half, -2, 0), (above, 0, half, 2, half))
     schur_tiles(shift, pattern, update, members, buffer, out, sems)
 
 
@@ -372,19 +368,26 @@
         6 * 4 * 3 * 2 * size**3,
         "pivot_inverse",
     )
-    right, base = call(
+    right, base = pl.pallas_call(
         local_body,
-        [shape(2 * size, size), shape(size, size, dtype=f32)],
-        [pole_shift, pole_weight, panel_h, panel_s, inverse],
-        2 * 8 * size**3,
-        "local_rows",
-    )
+        out_shape=[shape(2 * size, size), shape(size, size, dtype=f32)],
+        in_specs=[SMEM] * 2 + [VMEM] * 3,
+        out_specs=[pl.BlockSpec(memory_space=pltpu.HBM)] * 2,
+        scratch_shapes=[
+            pltpu.VMEM((2 * size, size), bf16),
+            pltpu.VMEM((size, size), f32),
+            pltpu.SemaphoreType.DMA((2,)),
+        ],
+        compiler_params=pltpu.CompilerParams(vmem_limit_bytes=16 * 2**20),
+        cost_estimate=pl.CostEstimate(
+            flops=2 * 8 * size**3, bytes_accessed=2**20, transcendentals=0
+        ),
+        name="local_rows",
+    )(pole_shift, pole_weight, panel_h, panel_s, inverse)
     inverse, right, base = lax.optimization_barrier((inverse, right, base))
-    less = row_count // 4
-    more = row_count - less
-    mine, up, down = call(
+    mine, fronts = call(
         solve_body,
-        [shape(row_count * half, 2 * size)] + [shape(more, 2 * share, size)] * 2,
+        [shape(row_count * half, 2 * size), shape(row_count, 2 * share, size)],
         [pole_shift, received, inverse],
         2 * 8 * row_count * half * size * size,
         "solved_rows",
@@ -414,11 +417,19 @@
 
     onward = [(i, (i + 1) % pole_count) for i in range(pole_count)]
     back = [(i, (i - 1) % pole_count) for i in range(pole_count)]
-    up, down, both = lax.optimization_barrier((up, down, both))
-    from_below = lax.ppermute(up, "pole", onward)
-    from_above = lax.ppermute(down, "pole", back)
-
+    fronts, both = lax.optimization_barrier((fronts, both))
+    from_below = lax.ppermute(fronts, "pole", onward)
+    from_above = lax.ppermute(fronts, "pole", back)
+
+    (update,) = call(
+        update_body,
+        [shape(row_count, quarters, share, 2 * size, dtype=f32)],
+        [pole_shift, panel_h, panel_s, mine, other],
+        8 * row_count * width * size * size,
+        "update",
+    )
     both = lax.all_to_all(both, ("col", "pole"), split_axis=0, concat_axis=0, tiled=True)
+    both, update = lax.optimization_barrier((both, update))
     spread, rows_out = call(
         sums_body,
         [
@@ -429,26 +440,17 @@
         0,
         "sums",
     )
-    from_below, from_above, spread = lax.optimization_barrier((from_below, from_above, spread))
     below, above = call(
         relay_body,
-        [shape(more, 2 * share, size)] * 2,
-        [up, down, from_below, from_above],
-        0,
+        [shape(row_count // 2, 2 * share, size)] * 2,
+        [from_below, from_above],
+        10**11,
         "relay",
     )
     below = lax.ppermute(below, "pole", onward)
     above = lax.ppermute(above, "pole", back)
     spread = lax.all_to_all(spread, ("row", "col"), split_axis=0, concat_axis=0, tiled=True)
     (pivot_out,) = call(pivot_body, [shape(piece, size, dtype=f32)], [spread], 0, "pivot")
-
-    (update,) = call(
-        update_body,
-        [shape(row_count, quarters, share, 2 * size, dtype=f32)],
-        [pole_shift, panel_h, panel_s, mine, other],
-        8 * row_count * width * size * size,
-        "update",
-    )
 
     def tiles(body, ins, name, begun=()):
         tile = shape(2, row_count, quarters, share, size)
@@ -465,7 +467,7 @@
         )(*ins, *begun)
 
     fixed = [pole_shift, pattern, update]
-    schur = tiles(schur_first_body, fixed + [up, down, from_below, from_above], "schur_first")
+    schur = tiles(schur_first_body, fixed + [fronts, from_below, from_above], "schur_first")
     schur = tiles(schur_last_body, fixed + [below, above], "schur_last", (schur,))
     return (schur.reshape(1, 2, row_count, 1, width, size), rows_out.T, pivot_out.T)
 

time: 88.3 us -> 87.8 us (level)
  waiting for transfers between devices: 24.7 us -> 21.3 us
  Pallas kernels: 16.5 us -> 18.7 us
    all_to_all x1, waiting for transfers between devices: 3.6 us -> 1.62 us  [shards(): lax.all_to_all(both, ('col', 'pole'), split_axis=0, concat_axis=0, tiled=...]
    ppermute x2, waiting for transfers between devices: 1.88 us -> 0.01 us  [the longest x1 0.01 us: shards(): from_below = lax.ppermute(fronts, 'pole', onward)]
    ppermute x1, starting transfers between devices: 2.3 us -> 3.76 us  [shards(): below = lax.ppermute(below, 'pole', onward)]
    ppermute x1, starting transfers between devices: 4.19 us -> 2.73 us  [shards(): above = lax.ppermute(above, 'pole', back)]
    pallas_call x0 -> x1, Pallas kernels: none -> 1.05 us  [shards(): pl.pallas_call(local_body, out_shape=[shape(2 * size, size), shape(size,...]
    pallas_call x8 -> x7, Pallas kernels: 9.29 us -> 9.95 us  [call(): pl.pallas_call(body, out_shape=outs, in_specs=[SMEM if x.size <= 256 else...]
  transfers between devices with their start and end apart: 8 -> 8, of which waited for: 5 -> 4; matrix products, arithmetic and copies ran while one was open for 0% -> 0% of each run, Pallas kernels for 12% -> 14%
where the time goes in v13:
time: 87.8 us; the launch traced here: 86.4 us
  starting transfers between devices  43.8 us (50%)
  waiting for transfers between devices  21.3 us (24%)
  Pallas kernels  18.7 us (21%)
  local copies, waits for them, and re-layouts  1.65 us (2%)
  between operations  0.93 us (1%)
    all_to_all x1, waiting for transfers between devices, shards(): lax.all_to_all(sent, 'row', split_axis=0, concat_axis=0, tiled=True)  17 us
    all_to_all x1, starting transfers between devices, shards(): lax.all_to_all(sent, 'row', split_axis=0, concat_axis=0, tiled=True)  11.8 us
    pallas_call x7, Pallas kernels, call(): pl.pallas_call(body, out_shape=outs, in_specs=[SMEM if x.size <= 256 else...  9.95 us
    all_to_all x1, starting transfers between devices, shards(): lax.all_to_all(both, ('col', 'pole'), split_axis=0, concat_axis=0, tiled=...  9.68 us
    all_to_all x1, starting transfers between devices, shards(): lax.all_to_all(spread, ('row', 'col'), split_axis=0, concat_axis=0, tiled...  7.61 us
    ppermute x1, starting transfers between devices, shards(): from_above = lax.ppermute(fronts, 'pole', back)  4.35 us
    ppermute x1, starting transfers between devices, shards(): below = lax.ppermute(below, 'pole', onward)  3.76 us
    pallas_call x2, Pallas kernels, tiles(): pl.pallas_call(body, out_shape=tile, in_specs=[SMEM] * 2 + [VMEM] * (len(...  3.6 us
  transfers between devices with their start and end apart: 8, of which 4 were waited for; matrix products, arithmetic and copies ran while one was open for 0% of the time, Pallas kernels for 14%

profile of v13, /device:TPU:1, one launch (start us, length us, event | category | flops | bytes accessed | tf_op | source)
XLA Modules:
  0.0 86.4 jit_solution(5365889785721375657)
XLA Ops:
  0.6 0.0 copy-start.7
  0.6 0.0 copy-start.10
  0.7 0.0 copy-start.9
  0.7 1.8 %pack.1 = bf16[16,96,256]{2,1,0:T(8,128)(2,1)} custom-call(bf16[256,256]{1,0:T(8,128)(2,1)} %panel_h.5, bf16[256,256]{1,0:T(8,128)(2,1)} %panel_s.5, bf16[64,4096]{1,0:T(8,128)(2,1)} %front_h.1, bf16[64,4096]{1,0:T(8,128)(2,1)} %front_s.1), custom_call_target="tpu_custom_call" | custom-call | bytes 1048576 | tf_op jit(solution)/shard_map/pack/pallas_call | solution.py:348
  2.5 11.8 %all-to-all-start = ((bf16[16,96,256]{2,1,0:T(8,128)(2,1)}), bf16[16,96,256]{2,1,0:T(8,128)(2,1)S(1)}, u32[]{:S(2)}, u32[]{:S(2)}) async-start(bf16[16,96,256]{2,1,0:T(8,128)(2,1)} %pack.1), calls=%async_computation | async-start | bytes 1572864 | tf_op jit(solution)/shard_map/all_to_all | solution.py:362
  14.3 0.0 copy-done.7
  14.4 0.0 copy-done.10
  14.4 0.0 copy-done.9
  14.4 0.0 copy-start.1
  14.4 0.0 copy-start.2
  14.4 0.0 copy-start.8
  14.4 3.8 %pivot_inverse.1.inverse = bf16[2,256,512]{2,1,0:T(8,128)(2,1)S(1)} custom-call(f32[1,2]{1,0:T(1,128)S(1)} %copy-done.7, bf16[256,256]{1,0:T(8,128)(2,1)S(1)} %copy-done.9, bf16[256,256]{1,0:T(8,128)(2,1)S(1)} %copy-done.10), custom_call_target="tpu_custom_call" | custom-call | flops 2415919104 | bytes 786440 | tf_op jit(solution)/shard_map/pivot_inverse/pallas_call | solution.py:18
  18.2 0.0 copy-done.1
  18.2 0.0 copy-done.2
  18.2 0.0 copy-done.8
  18.2 0.0 copy-start
  18.2 1.1 %local_rows.1 = (bf16[512,256]{1,0:T(8,128)(2,1)S(1)}, f32[256,256]{1,0:T(8,128)S(1)}) custom-call(f32[1,2]{1,0:T(1,128)S(1)} %copy-done.7, f32[1,2]{1,0:T(1,128)S(1)} %copy-done.8, bf16[256,256]{1,0:T(8,128)(2,1)S(1)} %copy-done.1, bf16[256,256]{1,0:T(8,128)(2,1)S(1)} %copy-done.2, bf16[2,256,512]{2,1,0:T(8,128)(2,1)S(1)} %pivot_inverse.1.inverse), custom_call_target="tpu_custom_call" | custom-call | flops 268435456 | bytes 1048576 | tf_op jit(solution)/shard_map/local_rows/pallas_call | solution.py:371
  19.3 0.0 copy-start.4
  19.3 0.7 copy-done.4
  20.0 0.0 copy-start.5
  20.0 17.0 %all-to-all-done.received = bf16[16,96,256]{2,1,0:T(8,128)(2,1)S(1)} async-done(((bf16[16,96,256]{2,1,0:T(8,128)(2,1)}), bf16[16,96,256]{2,1,0:T(8,128)(2,1)S(1)}, u32[]{:S(2)}, u32[]{:S(2)}) %all-to-all-start) | async-done | bytes 786464 | tf_op jit(solution)/shard_map/all_to_all | solution.py:362
  37.0 1.9 %solved_rows.1 = (bf16[512,512]{1,0:T(8,128)(2,1)S(1)}, bf16[16,32,256]{2,1,0:T(8,128)(2,1)}) custom-call(f32[1,2]{1,0:T(1,128)S(1)} %copy-done.7, bf16[16,96,256]{2,1,0:T(8,128)(2,1)S(1)} %all-to-all-done.received, bf16[2,256,512]{2,1,0:T(8,128)(2,1)S(1)} %pivot_inverse.1.inverse), custom_call_target="tpu_custom_call" | custom-call | flops 536870912 | bytes 2097160 | tf_op jit(solution)/shard_map/solved_rows/pallas_call | solution.py:18
  38.9 1.9 %collective-permute-start = (bf16[512,512]{1,0:T(8,128)(2,1)S(1)}, bf16[512,512]{1,0:T(8,128)(2,1)S(1)}, u32[]{:S(2)}, u32[]{:S(2)}) collective-permute-start(bf16[512,512]{1,0:T(8,128)(2,1)S(1)} %get-tuple-element.22.mine), channel_id=1, source_target_pairs={{0,4},{4,0},{8,12},{12,8},{16,20},{20,16},{24,28},{28,24},{32,36},... | collective-permute-start | bytes 1572872 | tf_op jit(solution)/shard_map/ppermute | solution.py:395
  40.8 0.0 copy-done
  40.8 0.5 own_column.1.part
  41.3 1.4 %collective-permute-done.other = bf16[512,512]{1,0:T(8,128)(2,1)S(1)} collective-permute-done((bf16[512,512]{1,0:T(8,128)(2,1)S(1)}, bf16[512,512]{1,0:T(8,128)(2,1)S(1)}, u32[]{:S(2)}, u32[]{:S(2)}) %collective-permute-start) | collective-permute-done | bytes 524320 | tf_op jit(solution)/shard_map/ppermute | solution.py:395
  42.7 0.0 copy-done.5
  42.7 2.2 %column.1 = bf16[32,32,128]{2,1,0:T(8,128)(2,1)} custom-call(f32[1,2]{1,0:T(1,128)S(1)} %copy-done.8, bf16[512,512]{1,0:T(8,128)(2,1)S(1)} %collective-permute-done.other, bf16[2,16,64,256]{3,2,1,0:T(8,128)(2,1)S(1)} %bitcast.7, f32[512,256]{1,0:T(8,128)S(1)} %own_column.1.part, bf16[512,256]{1,0:T(8,128)(2,1)S(1)} %get-tuple-element.23.right, ...), custom_call_target="tpu_custom_call" | custom-call | flops 268435456 | bytes 2097152 | tf_op jit(solution)/shard_map/column/pallas_call | solution.py:405
  44.9 9.7 %all-to-all-start.1 = ((bf16[32,32,128]{2,1,0:T(8,128)(2,1)}), bf16[32,32,128]{2,1,0:T(8,128)(2,1)S(1)}, u32[]{:S(2)}, u32[]{:S(2)}) async-start(bf16[32,32,128]{2,1,0:T(8,128)(2,1)} %column.1), calls=%async_computation.1 | async-start | bytes 524288 | tf_op jit(solution)/shard_map/all_to_all | solution.py:431
  54.6 4.4 %collective-permute-start.2 = (bf16[16,32,256]{2,1,0:T(8,128)(2,1)}, bf16[16,32,256]{2,1,0:T(8,128)(2,1)}, u32[]{:S(2)}, u32[]{:S(2)}) collective-permute-start(bf16[16,32,256]{2,1,0:T(8,128)(2,1)} %get-tuple-element.27.fronts), channel_id=1, source_target_pairs={{0,448},{64,0},{128,64},{192,128},{256,192},{320,256},{384,320},{4... | collective-permute-start | bytes 786440 | tf_op jit(solution)/shard_map/ppermute | solution.py:422
  59.0 1.9 %collective-permute-start.1 = (bf16[16,32,256]{2,1,0:T(8,128)(2,1)}, bf16[16,32,256]{2,1,0:T(8,128)(2,1)}, u32[]{:S(2)}, u32[]{:S(2)}) collective-permute-start(bf16[16,32,256]{2,1,0:T(8,128)(2,1)} %get-tuple-element.27.fronts), channel_id=1, source_target_pairs={{0,64},{64,128},{128,192},{192,256},{256,320},{320,384},{384,448},... | collective-permute-start | bytes 786440 | tf_op jit(solution)/shard_map/ppermute | solution.py:421
  60.9 0.0 copy-start.3
  60.9 0.9 %copy-done.3 = bf16[256,256]{1,0:T(8,128)(2,1)S(1)} copy-done((bf16[256,256]{1,0:T(8,128)(2,1)S(1)}, bf16[256,256]{1,0:T(8,128)(2,1)}, u32[]{:S(2)}) %copy-start.3) | copy-done | bytes 131096
  61.8 1.3 %update.1 = f32[16,4,16,512]{3,2,1,0:T(8,128)S(1)} custom-call(f32[1,2]{1,0:T(1,128)S(1)} %copy-done.7, bf16[256,256]{1,0:T(8,128)(2,1)S(1)} %copy-done.1, bf16[256,256]{1,0:T(8,128)(2,1)S(1)} %copy-done.3, bf16[512,512]{1,0:T(8,128)(2,1)S(1)} %get-tuple-element.22.mine, bf16[512,512]{1,0:T(8,128)(2,1)S(1)} %collective-permute-done.other), custom_call_target="tpu_custom_call" | custom-call | flops 536870912 | bytes 3407880 | tf_op jit(solution)/shard_map/update/pallas_call | solution.py:18
  63.1 1.6 %all-to-all-done.1.parts = bf16[32,32,128]{2,1,0:T(8,128)(2,1)S(1)} async-done(((bf16[32,32,128]{2,1,0:T(8,128)(2,1)}), bf16[32,32,128]{2,1,0:T(8,128)(2,1)S(1)}, u32[]{:S(2)}, u32[]{:S(2)}) %all-to-all-start.1) | async-done | bytes 262176 | tf_op jit(solution)/shard_map/all_to_all | solution.py:431
  64.7 0.8 sums.1
  65.5 7.6 %all-to-all-start.2 = ((bf16[64,16,128]{2,1,0:T(8,128)(2,1)}), bf16[64,16,128]{2,1,0:T(8,128)(2,1)S(1)}, u32[]{:S(2)}, u32[]{:S(2)}) async-start(bf16[64,16,128]{2,1,0:T(8,128)(2,1)} %get-tuple-element.32), calls=%async_computation.2 | async-start | bytes 524288 | tf_op jit(solution)/shard_map/all_to_all | solution.py:452
  73.1 0.0 copy-start.6
  73.1 0.0 collective-permute-done.2.from_above
  73.1 0.0 collective-permute-done.1.from_below
  73.2 1.0 %relay.1 = (bf16[8,32,256]{2,1,0:T(8,128)(2,1)S(1)}, bf16[8,32,256]{2,1,0:T(8,128)(2,1)S(1)}) custom-call(bf16[16,32,256]{2,1,0:T(8,128)(2,1)} %collective-permute-done.1.from_below, bf16[16,32,256]{2,1,0:T(8,128)(2,1)} %collective-permute-done.2.from_above), custom_call_target="tpu_custom_call" | custom-call | flops 99999997952 | bytes 786432 | tf_op jit(solution)/shard_map/relay/pallas_call | solution.py:18
  74.2 3.8 %collective-permute-start.3 = (bf16[8,32,256]{2,1,0:T(8,128)(2,1)S(1)}, bf16[8,32,256]{2,1,0:T(8,128)(2,1)S(1)}, u32[]{:S(2)}, u32[]{:S(2)}) collective-permute-start(bf16[8,32,256]{2,1,0:T(8,128)(2,1)S(1)} %get-tuple-element.28), channel_id=1, source_target_pairs={{0,64},{64,128},{128,192},{192,256},{256,320},{320,384},{384,448},... | collective-permute-start | bytes 393224 | tf_op jit(solution)/shard_map/ppermute | solution.py:450
  78.0 2.7 %collective-permute-start.4 = (bf16[8,32,256]{2,1,0:T(8,128)(2,1)S(1)}, bf16[8,32,256]{2,1,0:T(8,128)(2,1)S(1)}, u32[]{:S(2)}, u32[]{:S(2)}) collective-permute-start(bf16[8,32,256]{2,1,0:T(8,128)(2,1)S(1)} %get-tuple-element.29), channel_id=1, source_target_pairs={{0,448},{64,0},{128,64},{192,128},{256,192},{320,256},{384,320},{4... | collective-permute-start | bytes 393224 | tf_op jit(solution)/shard_map/ppermute | solution.py:451
  80.7 0.0 copy-done.6
  80.7 2.1 %schur_first.1.begun = bf16[2,16,4,16,256]{4,3,2,1,0:T(8,128)(2,1)} custom-call(f32[1,2]{1,0:T(1,128)S(1)} %copy-done.7, s32[16,16]{1,0:T(8,128)S(1)} %copy-done.6, f32[16,4,16,512]{3,2,1,0:T(8,128)S(1)} %update.1, bf16[16,32,256]{2,1,0:T(8,128)(2,1)} %get-tuple-element.27.fronts, bf16[16,32,256]{2,1,0:T(8,128)(2,1)} %collective-permute-done.1.from_below, ...), custom_call_target="tpu_custom_call" | custom-call | bytes 3145728 | tf_op jit(solution)/shard_map/schur_first/pallas_call | solution.py:457
  82.9 0.0 collective-permute-done.3.below
  82.9 1.3 %collective-permute-done.4.above = bf16[8,32,256]{2,1,0:T(8,128)(2,1)S(1)} collective-permute-done((bf16[8,32,256]{2,1,0:T(8,128)(2,1)S(1)}, bf16[8,32,256]{2,1,0:T(8,128)(2,1)S(1)}, u32[]{:S(2)}, u32[]{:S(2)}) %collective-permute-start.4) | collective-permute-done | bytes 131104 | tf_op jit(solution)/shard_map/ppermute | solution.py:451
  84.2 1.5 %schur_last.1 = bf16[2,16,4,16,256]{4,3,2,1,0:T(8,128)(2,1)} custom-call(f32[1,2]{1,0:T(1,128)S(1)} %copy-done.7, s32[16,16]{1,0:T(8,128)S(1)} %copy-done.6, f32[16,4,16,512]{3,2,1,0:T(8,128)S(1)} %update.1, bf16[8,32,256]{2,1,0:T(8,128)(2,1)S(1)} %collective-permute-done.3.below, ...), custom_call_target="tpu_custom_call", output_to_operand_aliasing={{}: (5, {})} | custom-call | bytes 3145728 | tf_op jit(solution)/shard_map/schur_last/pallas_call | solution.py:457
  85.6 0.0 all-to-all-done.2.parts
  85.7 0.7 pivot.1
Async XLA Ops:
  0.6 13.7 %copy-start.7 = (f32[1,2]{1,0:T(1,128)S(1)}, f32[1,2]{1,0:T(1,128)}, u32[]{:S(2)}) copy-start(f32[1,2]{1,0:T(1,128)} %shift.11) | copy-start | bytes 28
  0.6 13.7 %copy-start.10 = (bf16[256,256]{1,0:T(8,128)(2,1)S(1)}, bf16[256,256]{1,0:T(8,128)(2,1)}, u32[]{:S(2)}) copy-start(bf16[256,256]{1,0:T(8,128)(2,1)} %pivot_s.1) | copy-start | bytes 393220
  0.7 13.7 %copy-start.9 = (bf16[256,256]{1,0:T(8,128)(2,1)S(1)}, bf16[256,256]{1,0:T(8,128)(2,1)}, u32[]{:S(2)}) copy-start(bf16[256,256]{1,0:T(8,128)(2,1)} %pivot_h.1) | copy-start | bytes 393220
  2.5 34.5 %all-to-all-start = ((bf16[16,96,256]{2,1,0:T(8,128)(2,1)}), bf16[16,96,256]{2,1,0:T(8,128)(2,1)S(1)}, u32[]{:S(2)}, u32[]{:S(2)}) async-start(bf16[16,96,256]{2,1,0:T(8,128)(2,1)} %pack.1), calls=%async_computation | async-start | bytes 1572864 | tf_op jit(solution)/shard_map/all_to_all | solution.py:362
  14.4 3.8 %copy-start.1 = (bf16[256,256]{1,0:T(8,128)(2,1)S(1)}, bf16[256,256]{1,0:T(8,128)(2,1)}, u32[]{:S(2)}) copy-start(bf16[256,256]{1,0:T(8,128)(2,1)} %panel_h.5) | copy-start | bytes 393220
  14.4 3.8 %copy-start.2 = (bf16[256,256]{1,0:T(8,128)(2,1)S(1)}, bf16[256,256]{1,0:T(8,128)(2,1)}, u32[]{:S(2)}) copy-start(bf16[256,256]{1,0:T(8,128)(2,1)} %panel_s.5) | copy-start | bytes 393220
  14.4 3.8 %copy-start.8 = (f32[1,2]{1,0:T(1,128)S(1)}, f32[1,2]{1,0:T(1,128)}, u32[]{:S(2)}) copy-start(f32[1,2]{1,0:T(1,128)} %weight.3) | copy-start | bytes 28
  18.2 22.6 %copy-start = (bf16[1,2,16,1,64,256]{5,4,3,2,1,0:T(8,128)(2,1)S(1)}, bf16[1,2,16,1,64,256]{5,4,3,2,1,0:T(8,128)(2,1)}, u32[]{:S(2)}) copy-start(bf16[1,2,16,1,64,256]{5,4,3,2,1,0:T(8,128)(2,1)} %param.19) | copy-start | bytes 3145732
  19.3 0.7 copy-start.4
  20.0 22.7 %copy-start.5 = (f32[256,256]{1,0:T(8,128)S(1)}, f32[256,256]{1,0:T(8,128)}, u32[]{:S(2)}) copy-start(f32[256,256]{1,0:T(8,128)} %copy-done.4) | copy-start | bytes 786436
  38.9 3.8 %collective-permute-start = (bf16[512,512]{1,0:T(8,128)(2,1)S(1)}, bf16[512,512]{1,0:T(8,128)(2,1)S(1)}, u32[]{:S(2)}, u32[]{:S(2)}) collective-permute-start(bf16[512,512]{1,0:T(8,128)(2,1)S(1)} %get-tuple-element.22.mine), channel_id=1, source_target_pairs={{0,4},{4,0},{8,12},{12,8},{16,20},{20,16},{24,28},{28,24},{32,36},... | collective-permute-start | bytes 1572872 | tf_op jit(solution)/shard_map/ppermute | solution.py:395
  44.9 19.8 %all-to-all-start.1 = ((bf16[32,32,128]{2,1,0:T(8,128)(2,1)}), bf16[32,32,128]{2,1,0:T(8,128)(2,1)S(1)}, u32[]{:S(2)}, u32[]{:S(2)}) async-start(bf16[32,32,128]{2,1,0:T(8,128)(2,1)} %column.1), calls=%async_computation.1 | async-start | bytes 524288 | tf_op jit(solution)/shard_map/all_to_all | solution.py:431
  54.6 18.5 %collective-permute-start.2 = (bf16[16,32,256]{2,1,0:T(8,128)(2,1)}, bf16[16,32,256]{2,1,0:T(8,128)(2,1)}, u32[]{:S(2)}, u32[]{:S(2)}) collective-permute-start(bf16[16,32,256]{2,1,0:T(8,128)(2,1)} %get-tuple-element.27.fronts), channel_id=1, source_target_pairs={{0,448},{64,0},{128,64},{192,128},{256,192},{320,256},{384,320},{4... | collective-permute-start | bytes 786440 | tf_op jit(solution)/shard_map/ppermute | solution.py:422
  59.0 14.2 %collective-permute-start.1 = (bf16[16,32,256]{2,1,0:T(8,128)(2,1)}, bf16[16,32,256]{2,1,0:T(8,128)(2,1)}, u32[]{:S(2)}, u32[]{:S(2)}) collective-permute-start(bf16[16,32,256]{2,1,0:T(8,128)(2,1)} %get-tuple-element.27.fronts), channel_id=1, source_target_pairs={{0,64},{64,128},{128,192},{192,256},{256,320},{320,384},{384,448},... | collective-permute-start | bytes 786440 | tf_op jit(solution)/shard_map/ppermute | solution.py:421
  60.9 0.9 %copy-start.3 = (bf16[256,256]{1,0:T(8,128)(2,1)S(1)}, bf16[256,256]{1,0:T(8,128)(2,1)}, u32[]{:S(2)}) copy-start(bf16[256,256]{1,0:T(8,128)(2,1)} %panel_s.5) | copy-start | bytes 393220
  65.5 20.1 %all-to-all-start.2 = ((bf16[64,16,128]{2,1,0:T(8,128)(2,1)}), bf16[64,16,128]{2,1,0:T(8,128)(2,1)S(1)}, u32[]{:S(2)}, u32[]{:S(2)}) async-start(bf16[64,16,128]{2,1,0:T(8,128)(2,1)} %get-tuple-element.32), calls=%async_computation.2 | async-start | bytes 524288 | tf_op jit(solution)/shard_map/all_to_all | solution.py:452
  73.1 7.6 %copy-start.6 = (s32[16,16]{1,0:T(8,128)S(1)}, s32[16,16]{1,0:T(8,128)}, u32[]{:S(2)}) copy-start(s32[16,16]{1,0:T(8,128)} %pattern.3) | copy-start | bytes 3076
  74.2 8.7 %collective-permute-start.3 = (bf16[8,32,256]{2,1,0:T(8,128)(2,1)S(1)}, bf16[8,32,256]{2,1,0:T(8,128)(2,1)S(1)}, u32[]{:S(2)}, u32[]{:S(2)}) collective-permute-start(bf16[8,32,256]{2,1,0:T(8,128)(2,1)S(1)} %get-tuple-element.28), channel_id=1, source_target_pairs={{0,64},{64,128},{128,192},{192,256},{256,320},{320,384},{384,448},... | collective-permute-start | bytes 393224 | tf_op jit(solution)/shard_map/ppermute | solution.py:450
  78.0 6.2 %collective-permute-start.4 = (bf16[8,32,256]{2,1,0:T(8,128)(2,1)S(1)}, bf16[8,32,256]{2,1,0:T(8,128)(2,1)S(1)}, u32[]{:S(2)}, u32[]{:S(2)}) collective-permute-start(bf16[8,32,256]{2,1,0:T(8,128)(2,1)S(1)} %get-tuple-element.29), channel_id=1, source_target_pairs={{0,448},{64,0},{128,64},{192,128},{256,192},{320,256},{384,320},{4... | collective-permute-start | bytes 393224 | tf_op jit(solution)/shard_map/ppermute | solution.py:451

commit v14 on v13

--- a/solution.py
+++ b/solution.py
@@ -166,13 +166,16 @@
         store.wait()
 
 
-def solve_body(shift, received, inverse, solved, fronts):
+def fronts_body(received, fronts):
+    fronts[...] = received[:, received.shape[1] - fronts.shape[1] :]
+
+
+def solve_body(shift, received, inverse, solved):
     strips, rows, size = received.shape
     half = solved.shape[0] // strips
     rows_h = received[:, :half].reshape(strips * half, size)
     rows_s = received[:, half : 2 * half].reshape(strips * half, size)
     solved[...] = solve(rows_h, rows_s, shift, inverse)
-    fronts[...] = received[:, 2 * half :]
 
 
 def ordered(mine, other):
@@ -385,14 +388,17 @@
         name="local_rows",
     )(pole_shift, pole_weight, panel_h, panel_s, inverse)
     inverse, right, base = lax.optimization_barrier((inverse, right, base))
-    mine, fronts = call(
+    (mine,) = call(
         solve_body,
-        [shape(row_count * half, 2 * size), shape(row_count, 2 * share, size)],
+        [shape(row_count * half, 2 * size)],
         [pole_shift, received, inverse],
         2 * 8 * row_count * half * size * size,
         "solved_rows",
     )
     other = lax.ppermute(mine, "row", neighbour)
+    (fronts,) = call(
+        fronts_body, [shape(row_count, 2 * share, size)], [received], 0, "fronts"
+    )
     ancestor = ancestor_inverse.reshape(2, row_count, width, size)
     (part,) = call(
         own_column_body,
@@ -417,10 +423,7 @@
 
     onward = [(i, (i + 1) % pole_count) for i in range(pole_count)]
     back = [(i, (i - 1) % pole_count) for i in range(pole_count)]
-    fronts, both = lax.optimization_barrier((fronts, both))
-    from_below = lax.ppermute(fronts, "pole", onward)
-    from_above = lax.ppermute(fronts, "pole", back)
-
+    mine, other, both = lax.optimization_barrier((mine, other, both))
     (update,) = call(
         update_body,
         [shape(row_count, quarters, share, 2 * size, dtype=f32)],
@@ -428,6 +431,10 @@
         8 * row_count * width * size * size,
         "update",
     )
+    fronts, update = lax.optimization_barrier((fronts, update))
+    from_below = lax.ppermute(fronts, "pole", onward)
+    from_above = lax.ppermute(fronts, "pole", back)
+
     both = lax.all_to_all(both, ("col", "pole"), split_axis=0, concat_axis=0, tiled=True)
     both, update = lax.optimization_barrier((both, update))
     spread, rows_out = call(

time: 87.8 us -> 88.3 us (level)
  waiting for transfers between devices: 21.3 us -> 22.6 us
  Pallas kernels: 18.7 us -> 17.5 us
    pallas_call x7 -> x8, Pallas kernels: 9.95 us -> 9.25 us  [call(): pl.pallas_call(body, out_shape=outs, in_specs=[SMEM if x.size <= 256 else...]
  transfers between devices with their start and end apart: 8 -> 8, of which waited for: 4 -> 5; matrix products, arithmetic and copies ran while one was open for 0% -> 0% of each run, Pallas kernels for 14% -> 13%
where the time goes in v14:
time: 88.3 us; the launch traced here: 86.6 us
  starting transfers between devices  43.9 us (50%)
  waiting for transfers between devices  22.6 us (26%)
  Pallas kernels  17.5 us (20%)
  local copies, waits for them, and re-layouts  1.65 us (2%)
  between operations  0.94 us (1%)
    all_to_all x1, waiting for transfers between devices, shards(): lax.all_to_all(sent, 'row', split_axis=0, concat_axis=0, tiled=True)  17 us
    all_to_all x1, starting transfers between devices, shards(): lax.all_to_all(sent, 'row', split_axis=0, concat_axis=0, tiled=True)  11.8 us
    all_to_all x1, starting transfers between devices, shards(): lax.all_to_all(both, ('col', 'pole'), split_axis=0, concat_axis=0, tiled=...  9.8 us
    pallas_call x8, Pallas kernels, call(): pl.pallas_call(body, out_shape=outs, in_specs=[SMEM if x.size <= 256 else...  9.25 us
    all_to_all x1, starting transfers between devices, shards(): lax.all_to_all(spread, ('row', 'col'), split_axis=0, concat_axis=0, tiled...  7.6 us
    ppermute x1, starting transfers between devices, shards(): from_above = lax.ppermute(fronts, 'pole', back)  4.28 us
    ppermute x1, starting transfers between devices, shards(): below = lax.ppermute(below, 'pole', onward)  3.87 us
    pallas_call x2, Pallas kernels, tiles(): pl.pallas_call(body, out_shape=tile, in_specs=[SMEM] * 2 + [VMEM] * (len(...  3.16 us
  transfers between devices with their start and end apart: 8, of which 5 were waited for; matrix products, arithmetic and copies ran while one was open for 0% of the time, Pallas kernels for 13%

profile of v14, /device:TPU:1, one launch (start us, length us, event | category | flops | bytes accessed | tf_op | source)
XLA Modules:
  0.0 86.6 jit_solution(3479914416781757298)
XLA Ops:
  0.6 0.0 copy-start.7
  0.6 0.0 copy-start.10
  0.7 0.0 copy-start.9
  0.7 1.8 %pack.1 = bf16[16,96,256]{2,1,0:T(8,128)(2,1)} custom-call(bf16[256,256]{1,0:T(8,128)(2,1)} %panel_h.5, bf16[256,256]{1,0:T(8,128)(2,1)} %panel_s.5, bf16[64,4096]{1,0:T(8,128)(2,1)} %front_h.1, bf16[64,4096]{1,0:T(8,128)(2,1)} %front_s.1), custom_call_target="tpu_custom_call" | custom-call | bytes 1048576 | tf_op jit(solution)/shard_map/pack/pallas_call | solution.py:351
  2.5 11.8 %all-to-all-start = ((bf16[16,96,256]{2,1,0:T(8,128)(2,1)}), bf16[16,96,256]{2,1,0:T(8,128)(2,1)S(1)}, u32[]{:S(2)}, u32[]{:S(2)}) async-start(bf16[16,96,256]{2,1,0:T(8,128)(2,1)} %pack.1), calls=%async_computation | async-start | bytes 1572864 | tf_op jit(solution)/shard_map/all_to_all | solution.py:365
  14.3 0.0 copy-done.7
  14.4 0.0 copy-done.10
  14.4 0.0 copy-done.9
  14.4 0.0 copy-start.1
  14.4 0.0 copy-start.2
  14.4 0.0 copy-start.8
  14.4 3.8 %pivot_inverse.1.inverse = bf16[2,256,512]{2,1,0:T(8,128)(2,1)S(1)} custom-call(f32[1,2]{1,0:T(1,128)S(1)} %copy-done.7, bf16[256,256]{1,0:T(8,128)(2,1)S(1)} %copy-done.9, bf16[256,256]{1,0:T(8,128)(2,1)S(1)} %copy-done.10), custom_call_target="tpu_custom_call" | custom-call | flops 2415919104 | bytes 786440 | tf_op jit(solution)/shard_map/pivot_inverse/pallas_call | solution.py:18
  18.2 0.0 copy-done.1
  18.2 0.0 copy-done.2
  18.2 0.0 copy-done.8
  18.2 0.0 copy-start
  18.2 1.1 %local_rows.1 = (bf16[512,256]{1,0:T(8,128)(2,1)S(1)}, f32[256,256]{1,0:T(8,128)S(1)}) custom-call(f32[1,2]{1,0:T(1,128)S(1)} %copy-done.7, f32[1,2]{1,0:T(1,128)S(1)} %copy-done.8, bf16[256,256]{1,0:T(8,128)(2,1)S(1)} %copy-done.1, bf16[256,256]{1,0:T(8,128)(2,1)S(1)} %copy-done.2, bf16[2,256,512]{2,1,0:T(8,128)(2,1)S(1)} %pivot_inverse.1.inverse), custom_call_target="tpu_custom_call" | custom-call | flops 268435456 | bytes 1048576 | tf_op jit(solution)/shard_map/local_rows/pallas_call | solution.py:374
  19.3 0.0 copy-start.4
  19.3 0.7 copy-done.4
  20.0 0.0 copy-start.5
  20.0 17.0 %all-to-all-done.received = bf16[16,96,256]{2,1,0:T(8,128)(2,1)S(1)} async-done(((bf16[16,96,256]{2,1,0:T(8,128)(2,1)}), bf16[16,96,256]{2,1,0:T(8,128)(2,1)S(1)}, u32[]{:S(2)}, u32[]{:S(2)}) %all-to-all-start) | async-done | bytes 786464 | tf_op jit(solution)/shard_map/all_to_all | solution.py:365
  37.0 1.3 %solved_rows.1.mine = bf16[512,512]{1,0:T(8,128)(2,1)S(1)} custom-call(f32[1,2]{1,0:T(1,128)S(1)} %copy-done.7, bf16[16,96,256]{2,1,0:T(8,128)(2,1)S(1)} %all-to-all-done.received, bf16[2,256,512]{2,1,0:T(8,128)(2,1)S(1)} %pivot_inverse.1.inverse), custom_call_target="tpu_custom_call" | custom-call | flops 536870912 | bytes 1835016 | tf_op jit(solution)/shard_map/solved_rows/pallas_call | solution.py:18
  38.3 1.9 %collective-permute-start = (bf16[512,512]{1,0:T(8,128)(2,1)S(1)}, bf16[512,512]{1,0:T(8,128)(2,1)S(1)}, u32[]{:S(2)}, u32[]{:S(2)}) collective-permute-start(bf16[512,512]{1,0:T(8,128)(2,1)S(1)} %solved_rows.1.mine), channel_id=1, source_target_pairs={{0,4},{4,0},{8,12},{12,8},{16,20},{20,16},{24,28},{28,24},{32,36},... | collective-permute-start | bytes 1572872 | tf_op jit(solution)/shard_map/ppermute | solution.py:398
  40.2 0.0 copy-done
  40.2 0.5 own_column.1.part
  40.7 1.4 %collective-permute-done.other = bf16[512,512]{1,0:T(8,128)(2,1)S(1)} collective-permute-done((bf16[512,512]{1,0:T(8,128)(2,1)S(1)}, bf16[512,512]{1,0:T(8,128)(2,1)S(1)}, u32[]{:S(2)}, u32[]{:S(2)}) %collective-permute-start) | collective-permute-done | bytes 524320 | tf_op jit(solution)/shard_map/ppermute | solution.py:398
  42.1 0.0 copy-done.5
  42.1 2.2 %column.1 = bf16[32,32,128]{2,1,0:T(8,128)(2,1)} custom-call(f32[1,2]{1,0:T(1,128)S(1)} %copy-done.8, bf16[512,512]{1,0:T(8,128)(2,1)S(1)} %collective-permute-done.other, bf16[2,16,64,256]{3,2,1,0:T(8,128)(2,1)S(1)} %bitcast.7, f32[512,256]{1,0:T(8,128)S(1)} %own_column.1.part, bf16[512,256]{1,0:T(8,128)(2,1)S(1)} %get-tuple-element.22.right, ...), custom_call_target="tpu_custom_call" | custom-call | flops 268435456 | bytes 2097152 | tf_op jit(solution)/shard_map/column/pallas_call | solution.py:411
  44.3 9.8 %all-to-all-start.1 = ((bf16[32,32,128]{2,1,0:T(8,128)(2,1)}), bf16[32,32,128]{2,1,0:T(8,128)(2,1)}, u32[]{:S(2)}, u32[]{:S(2)}) async-start(bf16[32,32,128]{2,1,0:T(8,128)(2,1)} %column.1), calls=%async_computation.1 | async-start | bytes 524288 | tf_op jit(solution)/shard_map/all_to_all | solution.py:438
  54.2 0.0 copy-start.3
  54.2 0.9 %copy-done.3 = bf16[256,256]{1,0:T(8,128)(2,1)S(1)} copy-done((bf16[256,256]{1,0:T(8,128)(2,1)S(1)}, bf16[256,256]{1,0:T(8,128)(2,1)}, u32[]{:S(2)}) %copy-start.3) | copy-done | bytes 131096
  55.1 1.3 %update.1 = f32[16,4,16,512]{3,2,1,0:T(8,128)S(1)} custom-call(f32[1,2]{1,0:T(1,128)S(1)} %copy-done.7, bf16[256,256]{1,0:T(8,128)(2,1)S(1)} %copy-done.1, bf16[256,256]{1,0:T(8,128)(2,1)S(1)} %copy-done.3, bf16[512,512]{1,0:T(8,128)(2,1)S(1)} %solved_rows.1.mine, bf16[512,512]{1,0:T(8,128)(2,1)S(1)} %collective-permute-done.other), custom_call_target="tpu_custom_call" | custom-call | flops 536870912 | bytes 3407880 | tf_op jit(solution)/shard_map/update/pallas_call | solution.py:18
  56.4 4.3 %collective-permute-start.2 = (bf16[16,32,256]{2,1,0:T(8,128)(2,1)S(1)}, bf16[16,32,256]{2,1,0:T(8,128)(2,1)S(1)}, u32[]{:S(2)}, u32[]{:S(2)}) collective-permute-start(bf16[16,32,256]{2,1,0:T(8,128)(2,1)S(1)} %fronts.1), channel_id=1, source_target_pairs={{0,448},{64,0},{128,64},{192,128},{256,192},{320,256},{384,320},{4... | collective-permute-start | bytes 786440 | tf_op jit(solution)/shard_map/ppermute | solution.py:436
  60.6 1.9 %collective-permute-start.1 = (bf16[16,32,256]{2,1,0:T(8,128)(2,1)S(1)}, bf16[16,32,256]{2,1,0:T(8,128)(2,1)S(1)}, u32[]{:S(2)}, u32[]{:S(2)}) collective-permute-start(bf16[16,32,256]{2,1,0:T(8,128)(2,1)S(1)} %fronts.1), channel_id=1, source_target_pairs={{0,64},{64,128},{128,192},{192,256},{256,320},{320,384},{384,448},... | collective-permute-start | bytes 786440 | tf_op jit(solution)/shard_map/ppermute | solution.py:435
  62.6 1.6 %all-to-all-done.1.parts = bf16[32,32,128]{2,1,0:T(8,128)(2,1)} async-done(((bf16[32,32,128]{2,1,0:T(8,128)(2,1)}), bf16[32,32,128]{2,1,0:T(8,128)(2,1)}, u32[]{:S(2)}, u32[]{:S(2)}) %all-to-all-start.1) | async-done | bytes 262176 | tf_op jit(solution)/shard_map/all_to_all | solution.py:438
  64.2 1.7 %sums.1 = (bf16[64,16,128]{2,1,0:T(8,128)(2,1)}, f32[32,64]{1,0:T(8,128)}) custom-call(bf16[32,32,128]{2,1,0:T(8,128)(2,1)} %all-to-all-done.1.parts), custom_call_target="tpu_custom_call" | custom-call | bytes 532480 | tf_op jit(solution)/shard_map/sums/pallas_call | solution.py:18
  65.9 7.6 %all-to-all-start.2 = ((bf16[64,16,128]{2,1,0:T(8,128)(2,1)}), bf16[64,16,128]{2,1,0:T(8,128)(2,1)S(1)}, u32[]{:S(2)}, u32[]{:S(2)}) async-start(bf16[64,16,128]{2,1,0:T(8,128)(2,1)} %get-tuple-element.34), calls=%async_computation.2 | async-start | bytes 524288 | tf_op jit(solution)/shard_map/all_to_all | solution.py:459
  73.5 0.0 copy-start.6
  73.6 0.0 collective-permute-done.2.from_above
  73.6 0.0 collective-permute-done.1.from_below
  73.6 3.9 %collective-permute-start.3 = (bf16[8,32,256]{2,1,0:T(8,128)(2,1)S(1)}, bf16[8,32,256]{2,1,0:T(8,128)(2,1)S(1)}, u32[]{:S(2)}, u32[]{:S(2)}) collective-permute-start(bf16[8,32,256]{2,1,0:T(8,128)(2,1)S(1)} %get-tuple-element.30), channel_id=1, source_target_pairs={{0,64},{64,128},{128,192},{192,256},{256,320},{320,384},{384,448},... | collective-permute-start | bytes 393224 | tf_op jit(solution)/shard_map/ppermute | solution.py:457
  77.5 2.6 %collective-permute-start.4 = (bf16[8,32,256]{2,1,0:T(8,128)(2,1)S(1)}, bf16[8,32,256]{2,1,0:T(8,128)(2,1)S(1)}, u32[]{:S(2)}, u32[]{:S(2)}) collective-permute-start(bf16[8,32,256]{2,1,0:T(8,128)(2,1)S(1)} %get-tuple-element.31), channel_id=1, source_target_pairs={{0,448},{64,0},{128,64},{192,128},{256,192},{320,256},{384,320},{4... | collective-permute-start | bytes 393224 | tf_op jit(solution)/shard_map/ppermute | solution.py:458
  80.1 0.0 copy-done.6
  80.1 1.7 %schur_first.1.begun = bf16[2,16,4,16,256]{4,3,2,1,0:T(8,128)(2,1)} custom-call(f32[1,2]{1,0:T(1,128)S(1)} %copy-done.7, s32[16,16]{1,0:T(8,128)S(1)} %copy-done.6, f32[16,4,16,512]{3,2,1,0:T(8,128)S(1)} %update.1, bf16[16,32,256]{2,1,0:T(8,128)(2,1)S(1)} %fronts.1, bf16[16,32,256]{2,1,0:T(8,128)(2,1)S(1)} %collective-permute-done.1.from_below, ...), custom_call_target="tpu_custom_call" | custom-call | bytes 3145728 | tf_op jit(solution)/shard_map/schur_first/pallas_call | solution.py:464
  81.8 0.0 collective-permute-done.3.below
  81.8 1.8 %collective-permute-done.4.above = bf16[8,32,256]{2,1,0:T(8,128)(2,1)S(1)} collective-permute-done((bf16[8,32,256]{2,1,0:T(8,128)(2,1)S(1)}, bf16[8,32,256]{2,1,0:T(8,128)(2,1)S(1)}, u32[]{:S(2)}, u32[]{:S(2)}) %collective-permute-start.4) | collective-permute-done | bytes 131104 | tf_op jit(solution)/shard_map/ppermute | solution.py:458
  83.7 1.5 %schur_last.1 = bf16[2,16,4,16,256]{4,3,2,1,0:T(8,128)(2,1)} custom-call(f32[1,2]{1,0:T(1,128)S(1)} %copy-done.7, s32[16,16]{1,0:T(8,128)S(1)} %copy-done.6, f32[16,4,16,512]{3,2,1,0:T(8,128)S(1)} %update.1, bf16[8,32,256]{2,1,0:T(8,128)(2,1)S(1)} %collective-permute-done.3.below, ...), custom_call_target="tpu_custom_call", output_to_operand_aliasing={{}: (5, {})} | custom-call | bytes 3145728 | tf_op jit(solution)/shard_map/schur_last/pallas_call | solution.py:464
  85.1 0.7 all-to-all-done.2.parts
  85.8 0.7 pivot.1
  (2 shorter events, 0.0 us)
Async XLA Ops:
  0.6 13.7 %copy-start.7 = (f32[1,2]{1,0:T(1,128)S(1)}, f32[1,2]{1,0:T(1,128)}, u32[]{:S(2)}) copy-start(f32[1,2]{1,0:T(1,128)} %shift.11) | copy-start | bytes 28
  0.6 13.7 %copy-start.10 = (bf16[256,256]{1,0:T(8,128)(2,1)S(1)}, bf16[256,256]{1,0:T(8,128)(2,1)}, u32[]{:S(2)}) copy-start(bf16[256,256]{1,0:T(8,128)(2,1)} %pivot_s.1) | copy-start | bytes 393220
  0.7 13.7 %copy-start.9 = (bf16[256,256]{1,0:T(8,128)(2,1)S(1)}, bf16[256,256]{1,0:T(8,128)(2,1)}, u32[]{:S(2)}) copy-start(bf16[256,256]{1,0:T(8,128)(2,1)} %pivot_h.1) | copy-start | bytes 393220
  2.5 34.5 %all-to-all-start = ((bf16[16,96,256]{2,1,0:T(8,128)(2,1)}), bf16[16,96,256]{2,1,0:T(8,128)(2,1)S(1)}, u32[]{:S(2)}, u32[]{:S(2)}) async-start(bf16[16,96,256]{2,1,0:T(8,128)(2,1)} %pack.1), calls=%async_computation | async-start | bytes 1572864 | tf_op jit(solution)/shard_map/all_to_all | solution.py:365
  14.4 3.8 %copy-start.1 = (bf16[256,256]{1,0:T(8,128)(2,1)S(1)}, bf16[256,256]{1,0:T(8,128)(2,1)}, u32[]{:S(2)}) copy-start(bf16[256,256]{1,0:T(8,128)(2,1)} %panel_h.5) | copy-start | bytes 393220
  14.4 3.8 %copy-start.2 = (bf16[256,256]{1,0:T(8,128)(2,1)S(1)}, bf16[256,256]{1,0:T(8,128)(2,1)}, u32[]{:S(2)}) copy-start(bf16[256,256]{1,0:T(8,128)(2,1)} %panel_s.5) | copy-start | bytes 393220
  14.4 3.8 %copy-start.8 = (f32[1,2]{1,0:T(1,128)S(1)}, f32[1,2]{1,0:T(1,128)}, u32[]{:S(2)}) copy-start(f32[1,2]{1,0:T(1,128)} %weight.3) | copy-start | bytes 28
  18.2 22.0 %copy-start = (bf16[1,2,16,1,64,256]{5,4,3,2,1,0:T(8,128)(2,1)S(1)}, bf16[1,2,16,1,64,256]{5,4,3,2,1,0:T(8,128)(2,1)}, u32[]{:S(2)}) copy-start(bf16[1,2,16,1,64,256]{5,4,3,2,1,0:T(8,128)(2,1)} %param.19) | copy-start | bytes 3145732
  19.3 0.7 copy-start.4
  20.0 22.1 %copy-start.5 = (f32[256,256]{1,0:T(8,128)S(1)}, f32[256,256]{1,0:T(8,128)}, u32[]{:S(2)}) copy-start(f32[256,256]{1,0:T(8,128)} %copy-done.4) | copy-start | bytes 786436
  38.3 3.8 %collective-permute-start = (bf16[512,512]{1,0:T(8,128)(2,1)S(1)}, bf16[512,512]{1,0:T(8,128)(2,1)S(1)}, u32[]{:S(2)}, u32[]{:S(2)}) collective-permute-start(bf16[512,512]{1,0:T(8,128)(2,1)S(1)} %solved_rows.1.mine), channel_id=1, source_target_pairs={{0,4},{4,0},{8,12},{12,8},{16,20},{20,16},{24,28},{28,24},{32,36},... | collective-permute-start | bytes 1572872 | tf_op jit(solution)/shard_map/ppermute | solution.py:398
  44.3 19.9 %all-to-all-start.1 = ((bf16[32,32,128]{2,1,0:T(8,128)(2,1)}), bf16[32,32,128]{2,1,0:T(8,128)(2,1)}, u32[]{:S(2)}, u32[]{:S(2)}) async-start(bf16[32,32,128]{2,1,0:T(8,128)(2,1)} %column.1), calls=%async_computation.1 | async-start | bytes 524288 | tf_op jit(solution)/shard_map/all_to_all | solution.py:438
  54.2 0.9 %copy-start.3 = (bf16[256,256]{1,0:T(8,128)(2,1)S(1)}, bf16[256,256]{1,0:T(8,128)(2,1)}, u32[]{:S(2)}) copy-start(bf16[256,256]{1,0:T(8,128)(2,1)} %panel_s.5) | copy-start | bytes 393220
  56.4 17.2 %collective-permute-start.2 = (bf16[16,32,256]{2,1,0:T(8,128)(2,1)S(1)}, bf16[16,32,256]{2,1,0:T(8,128)(2,1)S(1)}, u32[]{:S(2)}, u32[]{:S(2)}) collective-permute-start(bf16[16,32,256]{2,1,0:T(8,128)(2,1)S(1)} %fronts.1), channel_id=1, source_target_pairs={{0,448},{64,0},{128,64},{192,128},{256,192},{320,256},{384,320},{4... | collective-permute-start | bytes 786440 | tf_op jit(solution)/shard_map/ppermute | solution.py:436
  60.6 12.9 %collective-permute-start.1 = (bf16[16,32,256]{2,1,0:T(8,128)(2,1)S(1)}, bf16[16,32,256]{2,1,0:T(8,128)(2,1)S(1)}, u32[]{:S(2)}, u32[]{:S(2)}) collective-permute-start(bf16[16,32,256]{2,1,0:T(8,128)(2,1)S(1)} %fronts.1), channel_id=1, source_target_pairs={{0,64},{64,128},{128,192},{192,256},{256,320},{320,384},{384,448},... | collective-permute-start | bytes 786440 | tf_op jit(solution)/shard_map/ppermute | solution.py:435
  65.9 19.9 %all-to-all-start.2 = ((bf16[64,16,128]{2,1,0:T(8,128)(2,1)}), bf16[64,16,128]{2,1,0:T(8,128)(2,1)S(1)}, u32[]{:S(2)}, u32[]{:S(2)}) async-start(bf16[64,16,128]{2,1,0:T(8,128)(2,1)} %get-tuple-element.34), calls=%async_computation.2 | async-start | bytes 524288 | tf_op jit(solution)/shard_map/all_to_all | solution.py:459
  73.5 6.6 %copy-start.6 = (s32[16,16]{1,0:T(8,128)S(1)}, s32[16,16]{1,0:T(8,128)}, u32[]{:S(2)}) copy-start(s32[16,16]{1,0:T(8,128)} %pattern.3) | copy-start | bytes 3076
  73.6 8.2 %collective-permute-start.3 = (bf16[8,32,256]{2,1,0:T(8,128)(2,1)S(1)}, bf16[8,32,256]{2,1,0:T(8,128)(2,1)S(1)}, u32[]{:S(2)}, u32[]{:S(2)}) collective-permute-start(bf16[8,32,256]{2,1,0:T(8,128)(2,1)S(1)} %get-tuple-element.30), channel_id=1, source_target_pairs={{0,64},{64,128},{128,192},{192,256},{256,320},{320,384},{384,448},... | collective-permute-start | bytes 393224 | tf_op jit(solution)/shard_map/ppermute | solution.py:457
  77.5 6.2 %collective-permute-start.4 = (bf16[8,32,256]{2,1,0:T(8,128)(2,1)S(1)}, bf16[8,32,256]{2,1,0:T(8,128)(2,1)S(1)}, u32[]{:S(2)}, u32[]{:S(2)}) collective-permute-start(bf16[8,32,256]{2,1,0:T(8,128)(2,1)S(1)} %get-tuple-element.31), channel_id=1, source_target_pairs={{0,448},{64,0},{128,64},{192,128},{256,192},{320,256},{384,320},{4... | collective-permute-start | bytes 393224 | tf_op jit(solution)/shard_map/ppermute | solution.py:458

commit v15 on v11

--- a/solution.py
+++ b/solution.py
@@ -107,17 +107,6 @@
 def solve(rows_h, rows_s, shift, inverse):
     coupling = jnp.concatenate(couple(rows_h, rows_s, shift[0, 0], shift[0, 1]), axis=1)
     return (dot(coupling, block(inverse[0])) + dot(coupling, block(inverse[1]))).astype(bf16)
-
-
-def local_body(shift, weight, panel_h, panel_s, inverse, right, base):
-    size = panel_h.shape[1]
-    solved = solve(panel_h[...], panel_s[...], shift, inverse)
-    right[:size] = solved[:, :size]
-    right[size:] = solved[:, size:]
-    whole = inverse[0].astype(f32) + inverse[1].astype(f32)
-    density = weight[0, 0] * whole[:, size:] + weight[0, 1] * whole[:, :size]
-    first_device = (lax.axis_index("row") == 0) & (lax.axis_index("col") == 0)
-    base[...] = jnp.where(first_device, density.T, 0.0)
 
 
 def pack_body(panel_h, panel_s, front_h, front_s, out, panels, fronts, buffer, sems):
@@ -199,9 +188,18 @@
     return by_real[:size] - by_imag[size:], by_real[size:] + by_imag[:size]
 
 
-def own_column_body(mine, ancestor, part):
+def own_column_body(
+    shift, weight, panel_h, panel_s, inverse, mine, ancestor, part, right, base
+):
     size = part.shape[1]
     part[:size], part[size:] = half_column(mine, ancestor, lax.rem(lax.axis_index("row"), 2))
+    solved = solve(panel_h[...], panel_s[...], shift, inverse)
+    right[:size] = solved[:, :size]
+    right[size:] = solved[:, size:]
+    whole = inverse[0].astype(f32) + inverse[1].astype(f32)
+    density = weight[0, 0] * whole[:, size:] + weight[0, 1] * whole[:, :size]
+    first_device = (lax.axis_index("row") == 0) & (lax.axis_index("col") == 0)
+    base[...] = jnp.where(first_device, density.T, 0.0)
 
 
 def column_body(weight, other, ancestor, part, right, base, out, buffer, sems):
@@ -372,14 +370,6 @@
         6 * 4 * 3 * 2 * size**3,
         "pivot_inverse",
     )
-    right, base = call(
-        local_body,
-        [shape(2 * size, size), shape(size, size, dtype=f32)],
-        [pole_shift, pole_weight, panel_h, panel_s, inverse],
-        2 * 8 * size**3,
-        "local_rows",
-    )
-    inverse, right, base = lax.optimization_barrier((inverse, right, base))
     less = row_count // 4
     more = row_count - less
     mine, up, down = call(
@@ -391,11 +381,15 @@
     )
     other = lax.ppermute(mine, "row", neighbour)
     ancestor = ancestor_inverse.reshape(2, row_count, width, size)
-    (part,) = call(
+    part, right, base = call(
         own_column_body,
-        [shape(2 * size, size, dtype=f32)],
-        [mine, ancestor],
-        4 * row_count * width * size * size,
+        [
+            shape(2 * size, size, dtype=f32),
+            shape(2 * size, size),
+            shape(size, size, dtype=f32),
+        ],
+        [pole_shift, pole_weight, panel_h, panel_s, inverse, mine, ancestor],
+        4 * row_count * width * size * size + 2 * 8 * size**3,
         "own_column",
     )
     folded = (col_count * pole_count, piece, 128)
@@ -429,12 +423,11 @@
         0,
         "sums",
     )
-    from_below, from_above, spread = lax.optimization_barrier((from_below, from_above, spread))
     below, above = call(
         relay_body,
         [shape(more, 2 * share, size)] * 2,
         [up, down, from_below, from_above],
-        0,
+        10**11,
         "relay",
     )
     below = lax.ppermute(below, "pole", onward)

time: 88.3 us -> 87.4 us (0.990)
  starting transfers between devices: 43.5 us -> 45 us
  waiting for transfers between devices: 24.7 us -> 23.2 us
    all_to_all x1, waiting for transfers between devices: 16.4 us -> 18.8 us  [shards(): lax.all_to_all(sent, 'row', split_axis=0, concat_axis=0, tiled=True)]
    ppermute x1, waiting for transfers between devices: 1.88 us -> 0.01 us  [shards(): from_below = lax.ppermute(up, 'pole', onward)]
    all_to_all x1, starting transfers between devices: 7.04 us -> 8.57 us  [shards(): lax.all_to_all(spread, ('row', 'col'), split_axis=0, concat_axis=0, tiled...]
    ppermute x1, waiting for transfers between devices: 1.39 us -> 0.01 us  [shards(): other = lax.ppermute(mine, 'row', neighbour)]
    pallas_call x8 -> x7, Pallas kernels: 9.29 us -> 9.12 us  [call(): pl.pallas_call(body, out_shape=outs, in_specs=[SMEM if x.size <= 256 else...]
  transfers between devices with their start and end apart: 8 -> 8, of which waited for: 5 -> 4; matrix products, arithmetic and copies ran while one was open for 0% -> 0% of each run, Pallas kernels for 12% -> 12%
where the time goes in v15:
time: 87.4 us; the launch traced here: 86.6 us
  starting transfers between devices  45 us (51%)
  waiting for transfers between devices  23.2 us (27%)
  Pallas kernels  16.4 us (19%)
  local copies, waits for them, and re-layouts  1.08 us (1%)
  between operations  0.94 us (1%)
    all_to_all x1, waiting for transfers between devices, shards(): lax.all_to_all(sent, 'row', split_axis=0, concat_axis=0, tiled=True)  18.8 us
    all_to_all x1, starting transfers between devices, shards(): lax.all_to_all(sent, 'row', split_axis=0, concat_axis=0, tiled=True)  11.8 us
    all_to_all x1, starting transfers between devices, shards(): lax.all_to_all(both, ('col', 'pole'), split_axis=0, concat_axis=0, tiled=...  9.67 us
    pallas_call x7, Pallas kernels, call(): pl.pallas_call(body, out_shape=outs, in_specs=[SMEM if x.size <= 256 else...  9.12 us
    all_to_all x1, starting transfers between devices, shards(): lax.all_to_all(spread, ('row', 'col'), split_axis=0, concat_axis=0, tiled...  8.57 us
    ppermute x1, starting transfers between devices, shards(): above = lax.ppermute(above, 'pole', back)  3.56 us
    ppermute x1, starting transfers between devices, shards(): from_above = lax.ppermute(down, 'pole', back)  3.36 us
    all_to_all x1, waiting for transfers between devices, shards(): lax.all_to_all(both, ('col', 'pole'), split_axis=0, concat_axis=0, tiled=...  3.17 us
  transfers between devices with their start and end apart: 8, of which 4 were waited for; matrix products, arithmetic and copies ran while one was open for 0% of the time, Pallas kernels for 12%

profile of v15, /device:TPU:1, one launch (start us, length us, event | category | flops | bytes accessed | tf_op | source)
XLA Modules:
  0.0 86.6 jit_solution(14551739088763668550)
XLA Ops:
  0.6 0.0 copy-start.6
  0.6 0.0 copy-start.9
  0.7 0.0 copy-start.8
  0.7 1.8 %pack.1 = bf16[16,96,256]{2,1,0:T(8,128)(2,1)} custom-call(bf16[256,256]{1,0:T(8,128)(2,1)} %panel_h.5, bf16[256,256]{1,0:T(8,128)(2,1)} %panel_s.5, bf16[64,4096]{1,0:T(8,128)(2,1)} %front_h.1, bf16[64,4096]{1,0:T(8,128)(2,1)} %front_s.1), custom_call_target="tpu_custom_call" | custom-call | bytes 1048576 | tf_op jit(solution)/shard_map/pack/pallas_call | solution.py:350
  2.5 11.8 %all-to-all-start = ((bf16[16,96,256]{2,1,0:T(8,128)(2,1)}), bf16[16,96,256]{2,1,0:T(8,128)(2,1)S(1)}, u32[]{:S(2)}, u32[]{:S(2)}) async-start(bf16[16,96,256]{2,1,0:T(8,128)(2,1)} %pack.1), calls=%async_computation | async-start | bytes 1572864 | tf_op jit(solution)/shard_map/all_to_all | solution.py:364
  14.3 0.0 copy-done.6
  14.4 0.0 copy-done.9
  14.4 0.0 copy-done.8
  14.4 0.0 copy-start.1
  14.4 0.0 copy-start.2
  14.4 0.0 copy-start.7
  14.4 3.8 %pivot_inverse.1.inverse = bf16[2,256,512]{2,1,0:T(8,128)(2,1)S(1)} custom-call(f32[1,2]{1,0:T(1,128)S(1)} %copy-done.6, bf16[256,256]{1,0:T(8,128)(2,1)S(1)} %copy-done.8, bf16[256,256]{1,0:T(8,128)(2,1)S(1)} %copy-done.9), custom_call_target="tpu_custom_call" | custom-call | flops 2415919104 | bytes 786440 | tf_op jit(solution)/shard_map/pivot_inverse/pallas_call | solution.py:18
  18.2 0.0 copy-start.3
  18.2 0.0 copy-start
  18.2 18.8 %all-to-all-done.received = bf16[16,96,256]{2,1,0:T(8,128)(2,1)S(1)} async-done(((bf16[16,96,256]{2,1,0:T(8,128)(2,1)}), bf16[16,96,256]{2,1,0:T(8,128)(2,1)S(1)}, u32[]{:S(2)}, u32[]{:S(2)}) %all-to-all-start) | async-done | bytes 786464 | tf_op jit(solution)/shard_map/all_to_all | solution.py:364
  37.0 1.3 %solved_rows.1 = (bf16[512,512]{1,0:T(8,128)(2,1)S(1)}, bf16[12,32,256]{2,1,0:T(8,128)(2,1)S(1)}, bf16[12,32,256]{2,1,0:T(8,128)(2,1)S(1)}) custom-call(f32[1,2]{1,0:T(1,128)S(1)} %copy-done.6, bf16[16,96,256]{2,1,0:T(8,128)(2,1)S(1)} %all-to-all-done.received, bf16[2,256,512]{2,1,0:T(8,128)(2,1)S(1)} %pivot_inverse.1.inverse), custom_call_target="tpu_custom_call" | custom-call | flops 536870912 | bytes 2228232 | tf_op jit(solution)/shard_map/solved_rows/pallas_call | solution.py:18
  38.3 0.0 copy-done.3
  38.3 1.9 %collective-permute-start = (bf16[512,512]{1,0:T(8,128)(2,1)S(1)}, bf16[512,512]{1,0:T(8,128)(2,1)S(1)}, u32[]{:S(2)}, u32[]{:S(2)}) collective-permute-start(bf16[512,512]{1,0:T(8,128)(2,1)S(1)} %get-tuple-element.16.mine), channel_id=1, source_target_pairs={{0,4},{4,0},{8,12},{12,8},{16,20},{20,16},{24,28},{28,24},{32,36},... | collective-permute-start | bytes 1572872 | tf_op jit(solution)/shard_map/ppermute | solution.py:382
  40.2 0.0 copy-done.1
  40.2 0.0 copy-done.2
  40.2 0.0 copy-done.7
  40.2 0.0 copy-done
  40.2 0.0 copy-start.4
  40.3 1.0 %copy-done.4 = bf16[2,256,512]{2,1,0:T(8,128)(2,1)S(1)} copy-done((bf16[2,256,512]{2,1,0:T(8,128)(2,1)S(1)}, bf16[2,256,512]{2,1,0:T(8,128)(2,1)}, u32[]{:S(2)}) %copy-start.4) | copy-done | bytes 524312
  41.3 1.3 %own_column.1 = (f32[512,256]{1,0:T(8,128)S(1)}, bf16[512,256]{1,0:T(8,128)(2,1)S(1)}, f32[256,256]{1,0:T(8,128)S(1)}) custom-call(f32[1,2]{1,0:T(1,128)S(1)} %copy-done.6, f32[1,2]{1,0:T(1,128)S(1)} %copy-done.7, bf16[256,256]{1,0:T(8,128)(2,1)S(1)} %copy-done.1, bf16[256,256]{1,0:T(8,128)(2,1)S(1)} %copy-done.2, bf16[2,256,512]{2,1,0:T(8,128)(2,1)S(1)} %copy-done.4, ...), custom_call_target="tpu_custom_call" | custom-call | flops 536870912 | bytes 3407888 | tf_op jit(solution)/shard_map/own_column/pallas_call | solution.py:18
  42.6 0.0 collective-permute-done.other
  42.6 2.3 %column.1 = bf16[32,32,128]{2,1,0:T(8,128)(2,1)} custom-call(f32[1,2]{1,0:T(1,128)S(1)} %copy-done.7, bf16[512,512]{1,0:T(8,128)(2,1)S(1)} %collective-permute-done.other, bf16[2,16,64,256]{3,2,1,0:T(8,128)(2,1)S(1)} %bitcast.7, f32[512,256]{1,0:T(8,128)S(1)} %get-tuple-element.19.part, bf16[512,256]{1,0:T(8,128)(2,1)S(1)} %get-tuple-element.20.right, ...), custom_call_target="tpu_custom_call" | custom-call | flops 268435456 | bytes 2097152 | tf_op jit(solution)/shard_map/column/pallas_call | solution.py:396
  44.9 9.7 %all-to-all-start.1 = ((bf16[32,32,128]{2,1,0:T(8,128)(2,1)}), bf16[32,32,128]{2,1,0:T(8,128)(2,1)S(1)}, u32[]{:S(2)}, u32[]{:S(2)}) async-start(bf16[32,32,128]{2,1,0:T(8,128)(2,1)} %column.1), calls=%async_computation.1 | async-start | bytes 524288 | tf_op jit(solution)/shard_map/all_to_all | solution.py:415
  54.5 3.1 %collective-permute-start.1 = (bf16[12,32,256]{2,1,0:T(8,128)(2,1)S(1)}, bf16[12,32,256]{2,1,0:T(8,128)(2,1)S(1)}, u32[]{:S(2)}, u32[]{:S(2)}) collective-permute-start(bf16[12,32,256]{2,1,0:T(8,128)(2,1)S(1)} %get-tuple-element.22.up), channel_id=1, source_target_pairs={{0,64},{64,128},{128,192},{192,256},{256,320},{320,384},{384,448},... | collective-permute-start | bytes 589832 | tf_op jit(solution)/shard_map/ppermute | solution.py:412
  57.7 3.4 %collective-permute-start.2 = (bf16[12,32,256]{2,1,0:T(8,128)(2,1)S(1)}, bf16[12,32,256]{2,1,0:T(8,128)(2,1)S(1)}, u32[]{:S(2)}, u32[]{:S(2)}) collective-permute-start(bf16[12,32,256]{2,1,0:T(8,128)(2,1)S(1)} %get-tuple-element.23.down), channel_id=1, source_target_pairs={{0,448},{64,0},{128,64},{192,128},{256,192},{320,256},{384,320},{4... | collective-permute-start | bytes 589832 | tf_op jit(solution)/shard_map/ppermute | solution.py:413
  61.0 3.2 %all-to-all-done.1.parts = bf16[32,32,128]{2,1,0:T(8,128)(2,1)S(1)} async-done(((bf16[32,32,128]{2,1,0:T(8,128)(2,1)}), bf16[32,32,128]{2,1,0:T(8,128)(2,1)S(1)}, u32[]{:S(2)}, u32[]{:S(2)}) %all-to-all-start.1) | async-done | bytes 262176 | tf_op jit(solution)/shard_map/all_to_all | solution.py:415
  64.2 0.8 sums.1
  65.0 8.6 %all-to-all-start.2 = ((bf16[64,16,128]{2,1,0:T(8,128)(2,1)}), bf16[64,16,128]{2,1,0:T(8,128)(2,1)S(1)}, u32[]{:S(2)}, u32[]{:S(2)}) async-start(bf16[64,16,128]{2,1,0:T(8,128)(2,1)} %get-tuple-element.28), calls=%async_computation.2 | async-start | bytes 524288 | tf_op jit(solution)/shard_map/all_to_all | solution.py:435
  73.6 0.0 collective-permute-done.1.from_below
  73.6 0.0 collective-permute-done.2.from_above
  73.6 0.0 copy-start.5
  73.6 2.9 %collective-permute-start.3 = (bf16[12,32,256]{2,1,0:T(8,128)(2,1)S(1)}, bf16[12,32,256]{2,1,0:T(8,128)(2,1)S(1)}, u32[]{:S(2)}, u32[]{:S(2)}) collective-permute-start(bf16[12,32,256]{2,1,0:T(8,128)(2,1)S(1)} %get-tuple-element.24), channel_id=1, source_target_pairs={{0,64},{64,128},{128,192},{192,256},{256,320},{320,384},{384,448},... | collective-permute-start | bytes 589832 | tf_op jit(solution)/shard_map/ppermute | solution.py:433
  76.6 3.6 %collective-permute-start.4 = (bf16[12,32,256]{2,1,0:T(8,128)(2,1)S(1)}, bf16[12,32,256]{2,1,0:T(8,128)(2,1)S(1)}, u32[]{:S(2)}, u32[]{:S(2)}) collective-permute-start(bf16[12,32,256]{2,1,0:T(8,128)(2,1)S(1)} %get-tuple-element.25), channel_id=1, source_target_pairs={{0,448},{64,0},{128,64},{192,128},{256,192},{320,256},{384,320},{4... | collective-permute-start | bytes 589832 | tf_op jit(solution)/shard_map/ppermute | solution.py:434
  80.2 1.3 %update.1 = f32[16,4,16,512]{3,2,1,0:T(8,128)S(1)} custom-call(f32[1,2]{1,0:T(1,128)S(1)} %copy-done.6, bf16[256,256]{1,0:T(8,128)(2,1)S(1)} %copy-done.1, bf16[256,256]{1,0:T(8,128)(2,1)S(1)} %copy-done.2, bf16[512,512]{1,0:T(8,128)(2,1)S(1)} %get-tuple-element.16.mine, bf16[512,512]{1,0:T(8,128)(2,1)S(1)} %collective-permute-done.other), custom_call_target="tpu_custom_call" | custom-call | flops 536870912 | bytes 3407880 | tf_op jit(solution)/shard_map/update/pallas_call | solution.py:18
  81.4 0.0 copy-done.5
  81.5 1.6 %schur_first.1.begun = bf16[2,16,4,16,256]{4,3,2,1,0:T(8,128)(2,1)} custom-call(f32[1,2]{1,0:T(1,128)S(1)} %copy-done.6, s32[16,16]{1,0:T(8,128)S(1)} %copy-done.5, f32[16,4,16,512]{3,2,1,0:T(8,128)S(1)} %update.1, bf16[12,32,256]{2,1,0:T(8,128)(2,1)S(1)} %get-tuple-element.22.up, bf16[12,32,256]{2,1,0:T(8,128)(2,1)S(1)} %get-tuple-element.23.down, ...), custom_call_target="tpu_custom_call" | custom-call | bytes 3145728 | tf_op jit(solution)/shard_map/schur_first/pallas_call | solution.py:448
  83.1 0.0 collective-permute-done.3.below
  83.1 1.1 %collective-permute-done.4.above = bf16[12,32,256]{2,1,0:T(8,128)(2,1)S(1)} collective-permute-done((bf16[12,32,256]{2,1,0:T(8,128)(2,1)S(1)}, bf16[12,32,256]{2,1,0:T(8,128)(2,1)S(1)}, u32[]{:S(2)}, u32[]{:S(2)}) %collective-permute-start.4) | collective-permute-done | bytes 196640 | tf_op jit(solution)/shard_map/ppermute | solution.py:434
  84.2 1.5 %schur_last.1 = bf16[2,16,4,16,256]{4,3,2,1,0:T(8,128)(2,1)} custom-call(f32[1,2]{1,0:T(1,128)S(1)} %copy-done.6, s32[16,16]{1,0:T(8,128)S(1)} %copy-done.5, f32[16,4,16,512]{3,2,1,0:T(8,128)S(1)} %update.1, bf16[12,32,256]{2,1,0:T(8,128)(2,1)S(1)} %collective-permute-done.3.below, ...), custom_call_target="tpu_custom_call", output_to_operand_aliasing={{}: (5, {})} | custom-call | bytes 3145728 | tf_op jit(solution)/shard_map/schur_last/pallas_call | solution.py:448
  85.7 0.2 all-to-all-done.2.parts
  85.9 0.7 pivot.1
  (1 shorter events, 0.0 us)
Async XLA Ops:
  0.6 13.7 %copy-start.6 = (f32[1,2]{1,0:T(1,128)S(1)}, f32[1,2]{1,0:T(1,128)}, u32[]{:S(2)}) copy-start(f32[1,2]{1,0:T(1,128)} %shift.11) | copy-start | bytes 28
  0.6 13.7 %copy-start.9 = (bf16[256,256]{1,0:T(8,128)(2,1)S(1)}, bf16[256,256]{1,0:T(8,128)(2,1)}, u32[]{:S(2)}) copy-start(bf16[256,256]{1,0:T(8,128)(2,1)} %pivot_s.1) | copy-start | bytes 393220
  0.7 13.7 %copy-start.8 = (bf16[256,256]{1,0:T(8,128)(2,1)S(1)}, bf16[256,256]{1,0:T(8,128)(2,1)}, u32[]{:S(2)}) copy-start(bf16[256,256]{1,0:T(8,128)(2,1)} %pivot_h.1) | copy-start | bytes 393220
  2.5 34.5 %all-to-all-start = ((bf16[16,96,256]{2,1,0:T(8,128)(2,1)}), bf16[16,96,256]{2,1,0:T(8,128)(2,1)S(1)}, u32[]{:S(2)}, u32[]{:S(2)}) async-start(bf16[16,96,256]{2,1,0:T(8,128)(2,1)} %pack.1), calls=%async_computation | async-start | bytes 1572864 | tf_op jit(solution)/shard_map/all_to_all | solution.py:364
  14.4 25.8 %copy-start.1 = (bf16[256,256]{1,0:T(8,128)(2,1)S(1)}, bf16[256,256]{1,0:T(8,128)(2,1)}, u32[]{:S(2)}) copy-start(bf16[256,256]{1,0:T(8,128)(2,1)} %panel_h.5) | copy-start | bytes 393220
  14.4 25.8 %copy-start.2 = (bf16[256,256]{1,0:T(8,128)(2,1)S(1)}, bf16[256,256]{1,0:T(8,128)(2,1)}, u32[]{:S(2)}) copy-start(bf16[256,256]{1,0:T(8,128)(2,1)} %panel_s.5) | copy-start | bytes 393220
  14.4 25.8 %copy-start.7 = (f32[1,2]{1,0:T(1,128)S(1)}, f32[1,2]{1,0:T(1,128)}, u32[]{:S(2)}) copy-start(f32[1,2]{1,0:T(1,128)} %weight.3) | copy-start | bytes 28
  18.2 20.1 %copy-start.3 = (bf16[2,256,512]{2,1,0:T(8,128)(2,1)}, bf16[2,256,512]{2,1,0:T(8,128)(2,1)S(1)}, u32[]{:S(2)}) copy-start(bf16[2,256,512]{2,1,0:T(8,128)(2,1)S(1)} %pivot_inverse.1.inverse) | copy-start | bytes 1572868
  18.2 22.0 %copy-start = (bf16[1,2,16,1,64,256]{5,4,3,2,1,0:T(8,128)(2,1)S(1)}, bf16[1,2,16,1,64,256]{5,4,3,2,1,0:T(8,128)(2,1)}, u32[]{:S(2)}) copy-start(bf16[1,2,16,1,64,256]{5,4,3,2,1,0:T(8,128)(2,1)} %param.19) | copy-start | bytes 3145732
  38.3 4.3 %collective-permute-start = (bf16[512,512]{1,0:T(8,128)(2,1)S(1)}, bf16[512,512]{1,0:T(8,128)(2,1)S(1)}, u32[]{:S(2)}, u32[]{:S(2)}) collective-permute-start(bf16[512,512]{1,0:T(8,128)(2,1)S(1)} %get-tuple-element.16.mine), channel_id=1, source_target_pairs={{0,4},{4,0},{8,12},{12,8},{16,20},{20,16},{24,28},{28,24},{32,36},... | collective-permute-start | bytes 1572872 | tf_op jit(solution)/shard_map/ppermute | solution.py:382
  40.2 1.0 %copy-start.4 = (bf16[2,256,512]{2,1,0:T(8,128)(2,1)S(1)}, bf16[2,256,512]{2,1,0:T(8,128)(2,1)}, u32[]{:S(2)}) copy-start(bf16[2,256,512]{2,1,0:T(8,128)(2,1)} %copy-done.3) | copy-start | bytes 1572868
  44.9 19.4 %all-to-all-start.1 = ((bf16[32,32,128]{2,1,0:T(8,128)(2,1)}), bf16[32,32,128]{2,1,0:T(8,128)(2,1)S(1)}, u32[]{:S(2)}, u32[]{:S(2)}) async-start(bf16[32,32,128]{2,1,0:T(8,128)(2,1)} %column.1), calls=%async_computation.1 | async-start | bytes 524288 | tf_op jit(solution)/shard_map/all_to_all | solution.py:415
  54.5 19.0 %collective-permute-start.1 = (bf16[12,32,256]{2,1,0:T(8,128)(2,1)S(1)}, bf16[12,32,256]{2,1,0:T(8,128)(2,1)S(1)}, u32[]{:S(2)}, u32[]{:S(2)}) collective-permute-start(bf16[12,32,256]{2,1,0:T(8,128)(2,1)S(1)} %get-tuple-element.22.up), channel_id=1, source_target_pairs={{0,64},{64,128},{128,192},{192,256},{256,320},{320,384},{384,448},... | collective-permute-start | bytes 589832 | tf_op jit(solution)/shard_map/ppermute | solution.py:412
  57.7 15.9 %collective-permute-start.2 = (bf16[12,32,256]{2,1,0:T(8,128)(2,1)S(1)}, bf16[12,32,256]{2,1,0:T(8,128)(2,1)S(1)}, u32[]{:S(2)}, u32[]{:S(2)}) collective-permute-start(bf16[12,32,256]{2,1,0:T(8,128)(2,1)S(1)} %get-tuple-element.23.down), channel_id=1, source_target_pairs={{0,448},{64,0},{128,64},{192,128},{256,192},{320,256},{384,320},{4... | collective-permute-start | bytes 589832 | tf_op jit(solution)/shard_map/ppermute | solution.py:413
  65.0 20.9 %all-to-all-start.2 = ((bf16[64,16,128]{2,1,0:T(8,128)(2,1)}), bf16[64,16,128]{2,1,0:T(8,128)(2,1)S(1)}, u32[]{:S(2)}, u32[]{:S(2)}) async-start(bf16[64,16,128]{2,1,0:T(8,128)(2,1)} %get-tuple-element.28), calls=%async_computation.2 | async-start | bytes 524288 | tf_op jit(solution)/shard_map/all_to_all | solution.py:435
  73.6 7.8 %copy-start.5 = (s32[16,16]{1,0:T(8,128)S(1)}, s32[16,16]{1,0:T(8,128)}, u32[]{:S(2)}) copy-start(s32[16,16]{1,0:T(8,128)} %pattern.3) | copy-start | bytes 3076
  73.6 9.5 %collective-permute-start.3 = (bf16[12,32,256]{2,1,0:T(8,128)(2,1)S(1)}, bf16[12,32,256]{2,1,0:T(8,128)(2,1)S(1)}, u32[]{:S(2)}, u32[]{:S(2)}) collective-permute-start(bf16[12,32,256]{2,1,0:T(8,128)(2,1)S(1)} %get-tuple-element.24), channel_id=1, source_target_pairs={{0,64},{64,128},{128,192},{192,256},{256,320},{320,384},{384,448},... | collective-permute-start | bytes 589832 | tf_op jit(solution)/shard_map/ppermute | solution.py:433
  76.6 7.6 %collective-permute-start.4 = (bf16[12,32,256]{2,1,0:T(8,128)(2,1)S(1)}, bf16[12,32,256]{2,1,0:T(8,128)(2,1)S(1)}, u32[]{:S(2)}, u32[]{:S(2)}) collective-permute-start(bf16[12,32,256]{2,1,0:T(8,128)(2,1)S(1)} %get-tuple-element.25), channel_id=1, source_target_pairs={{0,448},{64,0},{128,64},{192,128},{256,192},{320,256},{384,320},{4... | collective-permute-start | bytes 589832 | tf_op jit(solution)/shard_map/ppermute | solution.py:434

commit v16 on v15

--- a/solution.py
+++ b/solution.py
@@ -18,7 +18,7 @@
     return pl.pallas_call(
         body,
         out_shape=outs,
-        in_specs=[SMEM if x.size <= 256 else VMEM for x in ins],
+        in_specs=[VMEM] * len(ins),
         out_specs=[VMEM] * len(outs),
         compiler_params=pltpu.CompilerParams(vmem_limit_bytes=grant * 2**20),
         cost_estimate=pl.CostEstimate(flops=flops, bytes_accessed=moved, transcendentals=0),
@@ -67,7 +67,7 @@
 
 def invert_body(shift, pivot_h, pivot_s, inverse):
     size = pivot_h.shape[0]
-    shift_real, shift_imag = shift[0, 0], shift[0, 1]
+    shift_real, shift_imag = shift[:, 0:1], shift[:, 1:2]
     margin = pivot_s[...].astype(f32)
     real = pivot_h[...].astype(f32) - shift_real * margin
     imag = -shift_imag * margin
@@ -105,7 +105,7 @@
 
 
 def solve(rows_h, rows_s, shift, inverse):
-    coupling = jnp.concatenate(couple(rows_h, rows_s, shift[0, 0], shift[0, 1]), axis=1)
+    coupling = jnp.concatenate(couple(rows_h, rows_s, shift[:, 0:1], shift[:, 1:2]), axis=1)
     return (dot(coupling, block(inverse[0])) + dot(coupling, block(inverse[1]))).astype(bf16)
 
 
@@ -197,7 +197,7 @@
     right[:size] = solved[:, :size]
     right[size:] = solved[:, size:]
     whole = inverse[0].astype(f32) + inverse[1].astype(f32)
-    density = weight[0, 0] * whole[:, size:] + weight[0, 1] * whole[:, :size]
+    density = weight[:, 0:1] * whole[:, size:] + weight[:, 1:2] * whole[:, :size]
     first_device = (lax.axis_index("row") == 0) & (lax.axis_index("col") == 0)
     base[...] = jnp.where(first_device, density.T, 0.0)
 
@@ -212,7 +212,7 @@
         pltpu.make_async_copy(buffer.at[:, rows], out.at[:, rows], sems.at[index])
         for index, rows in enumerate((pl.ds(0, half), pl.ds(half, half)))
     ]
-    weight_real, weight_imag = weight[0, 0], weight[0, 1]
+    weight_real, weight_imag = weight[:, 0:1], weight[:, 1:2]
     density = -(weight_real * part_imag + weight_imag * part_real)
     fold(density, buffer, 0)
     stores[0].start()
@@ -249,7 +249,7 @@
     half = mine.shape[0] // strips
     group = 4
     top, bottom = ordered(mine[...], other[...])
-    real, imag = couple(panel_h[...], panel_s[...], shift[0, 0], shift[0, 1])
+    real, imag = couple(panel_h[...], panel_s[...], shift[:, 0:1], shift[:, 1:2])
     wide = jnp.concatenate(
         [jnp.concatenate([real, -imag], axis=1), jnp.concatenate([imag, real], axis=1)], axis=0
     )
@@ -280,7 +280,7 @@
     strips, count, share, size = out.shape[1:]
     pole = lax.axis_index("pole")
     row = lax.axis_index("row")
-    shift_real, shift_imag = shift[0, 0], shift[0, 1]
+    shift_real, shift_imag = shift[:, 0:1], shift[:, 1:2]
     copies = []
     for member, start, length, step, first in members:
         at = lax.rem(pole + count + step, count)
@@ -396,7 +396,7 @@
     (both,) = pl.pallas_call(
         column_body,
         out_shape=[shape(*folded)],
-        in_specs=[SMEM] + [VMEM] * 5,
+        in_specs=[VMEM] * 6,
         out_specs=[pl.BlockSpec(memory_space=pl.ANY)],
         scratch_shapes=[pltpu.VMEM(folded, bf16), pltpu.SemaphoreType.DMA((2,))],
         compiler_params=pltpu.CompilerParams(vmem_limit_bytes=16 * 2**20),
@@ -448,7 +448,7 @@
         return pl.pallas_call(
             body,
             out_shape=tile,
-            in_specs=[SMEM] * 2 + [VMEM] * (len(ins) - 2) + [pl.BlockSpec(memory_space=pl.ANY)] * len(begun),
+            in_specs=[VMEM, SMEM] + [VMEM] * (len(ins) - 2) + [pl.BlockSpec(memory_space=pl.ANY)] * len(begun),
             out_specs=pl.BlockSpec(memory_space=pl.ANY),
             input_output_aliases={len(ins): 0} if begun else {},
             scratch_shapes=[pltpu.VMEM(tile.shape, bf16), pltpu.SemaphoreType.DMA((4,))],

time: 87.4 us -> 85.9 us (0.983)
  Pallas kernels: 16.4 us -> 14 us
    pallas_call x10, Pallas kernels: 14.5 us -> 12.2 us  [the longest x7 7.26 us: call(): pl.pallas_call(body, out_shape=outs, in_specs=[VMEM] * len(ins), out_spec...]
  transfers between devices with their start and end apart: 8 -> 8, of which waited for: 4 -> 5; matrix products, arithmetic and copies ran while one was open for 0% -> 0% of each run, Pallas kernels for 12% -> 11%
where the time goes in v16:
time: 85.9 us; the launch traced here: 85.1 us
  starting transfers between devices  45 us (52%)
  waiting for transfers between devices  24 us (28%)
  Pallas kernels  14 us (16%)
  local copies, waits for them, and re-layouts  1.08 us (1%)
  between operations  0.93 us (1%)
    all_to_all x1, waiting for transfers between devices, shards(): lax.all_to_all(sent, 'row', split_axis=0, concat_axis=0, tiled=True)  19.2 us
    all_to_all x1, starting transfers between devices, shards(): lax.all_to_all(sent, 'row', split_axis=0, concat_axis=0, tiled=True)  11.8 us
    all_to_all x1, starting transfers between devices, shards(): lax.all_to_all(both, ('col', 'pole'), split_axis=0, concat_axis=0, tiled=...  9.67 us
    all_to_all x1, starting transfers between devices, shards(): lax.all_to_all(spread, ('row', 'col'), split_axis=0, concat_axis=0, tiled...  8.57 us
    pallas_call x7, Pallas kernels, call(): pl.pallas_call(body, out_shape=outs, in_specs=[VMEM] * len(ins), out_spec...  7.26 us
    ppermute x1, starting transfers between devices, shards(): above = lax.ppermute(above, 'pole', back)  3.56 us
    ppermute x1, starting transfers between devices, shards(): from_above = lax.ppermute(down, 'pole', back)  3.36 us
    pallas_call x2, Pallas kernels, tiles(): pl.pallas_call(body, out_shape=tile, in_specs=[VMEM, SMEM] + [VMEM] * (le...  3.22 us
  transfers between devices with their start and end apart: 8, of which 5 were waited for; matrix products, arithmetic and copies ran while one was open for 0% of the time, Pallas kernels for 11%

profile of v16, /device:TPU:1, one launch (start us, length us, event | category | flops | bytes accessed | tf_op | source)
XLA Modules:
  0.0 85.1 jit_solution(5704043445043824761)
XLA Ops:
  0.6 0.0 copy-start.6
  0.6 0.0 copy-start.9
  0.7 0.0 copy-start.8
  0.7 1.8 %pack.1 = bf16[16,96,256]{2,1,0:T(8,128)(2,1)} custom-call(bf16[256,256]{1,0:T(8,128)(2,1)} %panel_h.5, bf16[256,256]{1,0:T(8,128)(2,1)} %panel_s.5, bf16[64,4096]{1,0:T(8,128)(2,1)} %front_h.1, bf16[64,4096]{1,0:T(8,128)(2,1)} %front_s.1), custom_call_target="tpu_custom_call" | custom-call | bytes 1048576 | tf_op jit(solution)/shard_map/pack/pallas_call | solution.py:350
  2.5 11.8 %all-to-all-start = ((bf16[16,96,256]{2,1,0:T(8,128)(2,1)}), bf16[16,96,256]{2,1,0:T(8,128)(2,1)S(1)}, u32[]{:S(2)}, u32[]{:S(2)}) async-start(bf16[16,96,256]{2,1,0:T(8,128)(2,1)} %pack.1), calls=%async_computation | async-start | bytes 1572864 | tf_op jit(solution)/shard_map/all_to_all | solution.py:364
  14.3 0.0 copy-done.6
  14.4 0.0 copy-done.9
  14.4 0.0 copy-done.8
  14.4 0.0 copy-start.1
  14.4 0.0 copy-start.2
  14.4 0.0 copy-start.7
  14.4 3.3 %pivot_inverse.1.inverse = bf16[2,256,512]{2,1,0:T(8,128)(2,1)S(1)} custom-call(f32[1,2]{1,0:T(1,128)S(1)} %copy-done.6, bf16[256,256]{1,0:T(8,128)(2,1)S(1)} %copy-done.8, bf16[256,256]{1,0:T(8,128)(2,1)S(1)} %copy-done.9), custom_call_target="tpu_custom_call" | custom-call | flops 2415919104 | bytes 786440 | tf_op jit(solution)/shard_map/pivot_inverse/pallas_call | solution.py:18
  17.7 0.0 copy-start.3
  17.8 0.0 copy-start
  17.8 19.2 %all-to-all-done.received = bf16[16,96,256]{2,1,0:T(8,128)(2,1)S(1)} async-done(((bf16[16,96,256]{2,1,0:T(8,128)(2,1)}), bf16[16,96,256]{2,1,0:T(8,128)(2,1)S(1)}, u32[]{:S(2)}, u32[]{:S(2)}) %all-to-all-start) | async-done | bytes 786464 | tf_op jit(solution)/shard_map/all_to_all | solution.py:364
  37.0 0.8 solved_rows.1
  37.8 0.0 copy-done.3
  37.8 1.9 %collective-permute-start = (bf16[512,512]{1,0:T(8,128)(2,1)S(1)}, bf16[512,512]{1,0:T(8,128)(2,1)S(1)}, u32[]{:S(2)}, u32[]{:S(2)}) collective-permute-start(bf16[512,512]{1,0:T(8,128)(2,1)S(1)} %get-tuple-element.16.mine), channel_id=1, source_target_pairs={{0,4},{4,0},{8,12},{12,8},{16,20},{20,16},{24,28},{28,24},{32,36},... | collective-permute-start | bytes 1572872 | tf_op jit(solution)/shard_map/ppermute | solution.py:382
  39.7 0.0 copy-done.1
  39.7 0.0 copy-done.2
  39.7 0.0 copy-done.7
  39.7 0.0 copy-done
  39.8 0.0 copy-start.4
  39.8 1.0 %copy-done.4 = bf16[2,256,512]{2,1,0:T(8,128)(2,1)S(1)} copy-done((bf16[2,256,512]{2,1,0:T(8,128)(2,1)S(1)}, bf16[2,256,512]{2,1,0:T(8,128)(2,1)}, u32[]{:S(2)}) %copy-start.4) | copy-done | bytes 524312
  40.8 0.8 own_column.1
  41.6 0.0 collective-permute-done.other
  41.6 1.7 %column.1 = bf16[32,32,128]{2,1,0:T(8,128)(2,1)} custom-call(f32[1,2]{1,0:T(1,128)S(1)} %copy-done.7, bf16[512,512]{1,0:T(8,128)(2,1)S(1)} %collective-permute-done.other, bf16[2,16,64,256]{3,2,1,0:T(8,128)(2,1)S(1)} %bitcast.7, f32[512,256]{1,0:T(8,128)S(1)} %get-tuple-element.19.part, bf16[512,256]{1,0:T(8,128)(2,1)S(1)} %get-tuple-element.20.right, ...), custom_call_target="tpu_custom_call" | custom-call | flops 268435456 | bytes 2097152 | tf_op jit(solution)/shard_map/column/pallas_call | solution.py:396
  43.3 9.7 %all-to-all-start.1 = ((bf16[32,32,128]{2,1,0:T(8,128)(2,1)}), bf16[32,32,128]{2,1,0:T(8,128)(2,1)S(1)}, u32[]{:S(2)}, u32[]{:S(2)}) async-start(bf16[32,32,128]{2,1,0:T(8,128)(2,1)} %column.1), calls=%async_computation.1 | async-start | bytes 524288 | tf_op jit(solution)/shard_map/all_to_all | solution.py:415
  53.0 3.1 %collective-permute-start.1 = (bf16[12,32,256]{2,1,0:T(8,128)(2,1)S(1)}, bf16[12,32,256]{2,1,0:T(8,128)(2,1)S(1)}, u32[]{:S(2)}, u32[]{:S(2)}) collective-permute-start(bf16[12,32,256]{2,1,0:T(8,128)(2,1)S(1)} %get-tuple-element.22.up), channel_id=1, source_target_pairs={{0,64},{64,128},{128,192},{192,256},{256,320},{320,384},{384,448},... | collective-permute-start | bytes 589832 | tf_op jit(solution)/shard_map/ppermute | solution.py:412
  56.2 3.4 %collective-permute-start.2 = (bf16[12,32,256]{2,1,0:T(8,128)(2,1)S(1)}, bf16[12,32,256]{2,1,0:T(8,128)(2,1)S(1)}, u32[]{:S(2)}, u32[]{:S(2)}) collective-permute-start(bf16[12,32,256]{2,1,0:T(8,128)(2,1)S(1)} %get-tuple-element.23.down), channel_id=1, source_target_pairs={{0,448},{64,0},{128,64},{192,128},{256,192},{320,256},{384,320},{4... | collective-permute-start | bytes 589832 | tf_op jit(solution)/shard_map/ppermute | solution.py:413
  59.5 3.2 %all-to-all-done.1.parts = bf16[32,32,128]{2,1,0:T(8,128)(2,1)S(1)} async-done(((bf16[32,32,128]{2,1,0:T(8,128)(2,1)}), bf16[32,32,128]{2,1,0:T(8,128)(2,1)S(1)}, u32[]{:S(2)}, u32[]{:S(2)}) %all-to-all-start.1) | async-done | bytes 262176 | tf_op jit(solution)/shard_map/all_to_all | solution.py:415
  62.7 0.8 sums.1
  63.5 8.6 %all-to-all-start.2 = ((bf16[64,16,128]{2,1,0:T(8,128)(2,1)}), bf16[64,16,128]{2,1,0:T(8,128)(2,1)S(1)}, u32[]{:S(2)}, u32[]{:S(2)}) async-start(bf16[64,16,128]{2,1,0:T(8,128)(2,1)} %get-tuple-element.28), calls=%async_computation.2 | async-start | bytes 524288 | tf_op jit(solution)/shard_map/all_to_all | solution.py:435
  72.1 0.0 collective-permute-done.1.from_below
  72.1 0.0 collective-permute-done.2.from_above
  72.1 0.0 copy-start.5
  72.1 2.9 %collective-permute-start.3 = (bf16[12,32,256]{2,1,0:T(8,128)(2,1)S(1)}, bf16[12,32,256]{2,1,0:T(8,128)(2,1)S(1)}, u32[]{:S(2)}, u32[]{:S(2)}) collective-permute-start(bf16[12,32,256]{2,1,0:T(8,128)(2,1)S(1)} %get-tuple-element.24), channel_id=1, source_target_pairs={{0,64},{64,128},{128,192},{192,256},{256,320},{320,384},{384,448},... | collective-permute-start | bytes 589832 | tf_op jit(solution)/shard_map/ppermute | solution.py:433
  75.1 3.6 %collective-permute-start.4 = (bf16[12,32,256]{2,1,0:T(8,128)(2,1)S(1)}, bf16[12,32,256]{2,1,0:T(8,128)(2,1)S(1)}, u32[]{:S(2)}, u32[]{:S(2)}) collective-permute-start(bf16[12,32,256]{2,1,0:T(8,128)(2,1)S(1)} %get-tuple-element.25), channel_id=1, source_target_pairs={{0,448},{64,0},{128,64},{192,128},{256,192},{320,256},{384,320},{4... | collective-permute-start | bytes 589832 | tf_op jit(solution)/shard_map/ppermute | solution.py:434
  78.6 0.8 update.1
  79.5 0.0 copy-done.5
  79.5 1.7 %schur_first.1.begun = bf16[2,16,4,16,256]{4,3,2,1,0:T(8,128)(2,1)} custom-call(f32[1,2]{1,0:T(1,128)S(1)} %copy-done.6, s32[16,16]{1,0:T(8,128)S(1)} %copy-done.5, f32[16,4,16,512]{3,2,1,0:T(8,128)S(1)} %update.1, bf16[12,32,256]{2,1,0:T(8,128)(2,1)S(1)} %get-tuple-element.22.up, bf16[12,32,256]{2,1,0:T(8,128)(2,1)S(1)} %get-tuple-element.23.down, ...), custom_call_target="tpu_custom_call" | custom-call | bytes 3145728 | tf_op jit(solution)/shard_map/schur_first/pallas_call | solution.py:448
  81.2 0.1 collective-permute-done.3.below
  81.2 1.4 %collective-permute-done.4.above = bf16[12,32,256]{2,1,0:T(8,128)(2,1)S(1)} collective-permute-done((bf16[12,32,256]{2,1,0:T(8,128)(2,1)S(1)}, bf16[12,32,256]{2,1,0:T(8,128)(2,1)S(1)}, u32[]{:S(2)}, u32[]{:S(2)}) %collective-permute-start.4) | collective-permute-done | bytes 196640 | tf_op jit(solution)/shard_map/ppermute | solution.py:434
  82.7 1.6 %schur_last.1 = bf16[2,16,4,16,256]{4,3,2,1,0:T(8,128)(2,1)} custom-call(f32[1,2]{1,0:T(1,128)S(1)} %copy-done.6, s32[16,16]{1,0:T(8,128)S(1)} %copy-done.5, f32[16,4,16,512]{3,2,1,0:T(8,128)S(1)} %update.1, bf16[12,32,256]{2,1,0:T(8,128)(2,1)S(1)} %collective-permute-done.3.below, ...), custom_call_target="tpu_custom_call", output_to_operand_aliasing={{}: (5, {})} | custom-call | bytes 3145728 | tf_op jit(solution)/shard_map/schur_last/pallas_call | solution.py:448
  84.2 0.1 all-to-all-done.2.parts
  84.3 0.7 pivot.1
  (1 shorter events, 0.0 us)
Async XLA Ops:
  0.6 13.7 %copy-start.6 = (f32[1,2]{1,0:T(1,128)S(1)}, f32[1,2]{1,0:T(1,128)}, u32[]{:S(2)}) copy-start(f32[1,2]{1,0:T(1,128)} %shift.11) | copy-start | bytes 28
  0.6 13.7 %copy-start.9 = (bf16[256,256]{1,0:T(8,128)(2,1)S(1)}, bf16[256,256]{1,0:T(8,128)(2,1)}, u32[]{:S(2)}) copy-start(bf16[256,256]{1,0:T(8,128)(2,1)} %pivot_s.1) | copy-start | bytes 393220
  0.7 13.7 %copy-start.8 = (bf16[256,256]{1,0:T(8,128)(2,1)S(1)}, bf16[256,256]{1,0:T(8,128)(2,1)}, u32[]{:S(2)}) copy-start(bf16[256,256]{1,0:T(8,128)(2,1)} %pivot_h.1) | copy-start | bytes 393220
  2.5 34.5 %all-to-all-start = ((bf16[16,96,256]{2,1,0:T(8,128)(2,1)}), bf16[16,96,256]{2,1,0:T(8,128)(2,1)S(1)}, u32[]{:S(2)}, u32[]{:S(2)}) async-start(bf16[16,96,256]{2,1,0:T(8,128)(2,1)} %pack.1), calls=%async_computation | async-start | bytes 1572864 | tf_op jit(solution)/shard_map/all_to_all | solution.py:364
  14.4 25.3 %copy-start.1 = (bf16[256,256]{1,0:T(8,128)(2,1)S(1)}, bf16[256,256]{1,0:T(8,128)(2,1)}, u32[]{:S(2)}) copy-start(bf16[256,256]{1,0:T(8,128)(2,1)} %panel_h.5) | copy-start | bytes 393220
  14.4 25.3 %copy-start.2 = (bf16[256,256]{1,0:T(8,128)(2,1)S(1)}, bf16[256,256]{1,0:T(8,128)(2,1)}, u32[]{:S(2)}) copy-start(bf16[256,256]{1,0:T(8,128)(2,1)} %panel_s.5) | copy-start | bytes 393220
  14.4 25.3 %copy-start.7 = (f32[1,2]{1,0:T(1,128)S(1)}, f32[1,2]{1,0:T(1,128)}, u32[]{:S(2)}) copy-start(f32[1,2]{1,0:T(1,128)} %weight.3) | copy-start | bytes 28
  17.7 20.0 %copy-start.3 = (bf16[2,256,512]{2,1,0:T(8,128)(2,1)}, bf16[2,256,512]{2,1,0:T(8,128)(2,1)S(1)}, u32[]{:S(2)}) copy-start(bf16[2,256,512]{2,1,0:T(8,128)(2,1)S(1)} %pivot_inverse.1.inverse) | copy-start | bytes 1572868
  17.8 22.0 %copy-start = (bf16[1,2,16,1,64,256]{5,4,3,2,1,0:T(8,128)(2,1)S(1)}, bf16[1,2,16,1,64,256]{5,4,3,2,1,0:T(8,128)(2,1)}, u32[]{:S(2)}) copy-start(bf16[1,2,16,1,64,256]{5,4,3,2,1,0:T(8,128)(2,1)} %param.19) | copy-start | bytes 3145732
  37.8 3.8 %collective-permute-start = (bf16[512,512]{1,0:T(8,128)(2,1)S(1)}, bf16[512,512]{1,0:T(8,128)(2,1)S(1)}, u32[]{:S(2)}, u32[]{:S(2)}) collective-permute-start(bf16[512,512]{1,0:T(8,128)(2,1)S(1)} %get-tuple-element.16.mine), channel_id=1, source_target_pairs={{0,4},{4,0},{8,12},{12,8},{16,20},{20,16},{24,28},{28,24},{32,36},... | collective-permute-start | bytes 1572872 | tf_op jit(solution)/shard_map/ppermute | solution.py:382
  39.8 1.0 %copy-start.4 = (bf16[2,256,512]{2,1,0:T(8,128)(2,1)S(1)}, bf16[2,256,512]{2,1,0:T(8,128)(2,1)}, u32[]{:S(2)}) copy-start(bf16[2,256,512]{2,1,0:T(8,128)(2,1)} %copy-done.3) | copy-start | bytes 1572868
  43.3 19.4 %all-to-all-start.1 = ((bf16[32,32,128]{2,1,0:T(8,128)(2,1)}), bf16[32,32,128]{2,1,0:T(8,128)(2,1)S(1)}, u32[]{:S(2)}, u32[]{:S(2)}) async-start(bf16[32,32,128]{2,1,0:T(8,128)(2,1)} %column.1), calls=%async_computation.1 | async-start | bytes 524288 | tf_op jit(solution)/shard_map/all_to_all | solution.py:415
  53.0 19.0 %collective-permute-start.1 = (bf16[12,32,256]{2,1,0:T(8,128)(2,1)S(1)}, bf16[12,32,256]{2,1,0:T(8,128)(2,1)S(1)}, u32[]{:S(2)}, u32[]{:S(2)}) collective-permute-start(bf16[12,32,256]{2,1,0:T(8,128)(2,1)S(1)} %get-tuple-element.22.up), channel_id=1, source_target_pairs={{0,64},{64,128},{128,192},{192,256},{256,320},{320,384},{384,448},... | collective-permute-start | bytes 589832 | tf_op jit(solution)/shard_map/ppermute | solution.py:412
  56.2 15.9 %collective-permute-start.2 = (bf16[12,32,256]{2,1,0:T(8,128)(2,1)S(1)}, bf16[12,32,256]{2,1,0:T(8,128)(2,1)S(1)}, u32[]{:S(2)}, u32[]{:S(2)}) collective-permute-start(bf16[12,32,256]{2,1,0:T(8,128)(2,1)S(1)} %get-tuple-element.23.down), channel_id=1, source_target_pairs={{0,448},{64,0},{128,64},{192,128},{256,192},{320,256},{384,320},{4... | collective-permute-start | bytes 589832 | tf_op jit(solution)/shard_map/ppermute | solution.py:413
  63.5 20.9 %all-to-all-start.2 = ((bf16[64,16,128]{2,1,0:T(8,128)(2,1)}), bf16[64,16,128]{2,1,0:T(8,128)(2,1)S(1)}, u32[]{:S(2)}, u32[]{:S(2)}) async-start(bf16[64,16,128]{2,1,0:T(8,128)(2,1)} %get-tuple-element.28), calls=%async_computation.2 | async-start | bytes 524288 | tf_op jit(solution)/shard_map/all_to_all | solution.py:435
  72.1 7.4 %copy-start.5 = (s32[16,16]{1,0:T(8,128)S(1)}, s32[16,16]{1,0:T(8,128)}, u32[]{:S(2)}) copy-start(s32[16,16]{1,0:T(8,128)} %pattern.3) | copy-start | bytes 3076
  72.1 9.1 %collective-permute-start.3 = (bf16[12,32,256]{2,1,0:T(8,128)(2,1)S(1)}, bf16[12,32,256]{2,1,0:T(8,128)(2,1)S(1)}, u32[]{:S(2)}, u32[]{:S(2)}) collective-permute-start(bf16[12,32,256]{2,1,0:T(8,128)(2,1)S(1)} %get-tuple-element.24), channel_id=1, source_target_pairs={{0,64},{64,128},{128,192},{192,256},{256,320},{320,384},{384,448},... | collective-permute-start | bytes 589832 | tf_op jit(solution)/shard_map/ppermute | solution.py:433
  75.1 7.6 %collective-permute-start.4 = (bf16[12,32,256]{2,1,0:T(8,128)(2,1)S(1)}, bf16[12,32,256]{2,1,0:T(8,128)(2,1)S(1)}, u32[]{:S(2)}, u32[]{:S(2)}) collective-permute-start(bf16[12,32,256]{2,1,0:T(8,128)(2,1)S(1)} %get-tuple-element.25), channel_id=1, source_target_pairs={{0,448},{64,0},{128,64},{192,128},{256,192},{320,256},{384,320},{4... | collective-permute-start | bytes 589832 | tf_op jit(solution)/shard_map/ppermute | solution.py:434

commit v17 on v16

--- a/solution.py
+++ b/solution.py
@@ -10,7 +10,6 @@
 bf16 = jnp.bfloat16
 f32 = jnp.float32
 VMEM = pl.BlockSpec(memory_space=pltpu.VMEM)
-SMEM = pl.BlockSpec(memory_space=pltpu.SMEM)
 
 
 def call(body, outs, ins, flops, name, grant=16):
@@ -244,7 +243,10 @@
         out[index * half : (index + 1) * half] = jnp.concatenate(strips, axis=1)
 
 
-def update_body(shift, panel_h, panel_s, mine, other, out):
+def update_body(shift, pattern, panel_h, panel_s, mine, other, out, mask):
+    here = lax.broadcasted_iota(jnp.int32, pattern.shape, 1) == lax.axis_index("row")
+    column = jnp.sum(jnp.where(here, pattern[...], 0).astype(f32), axis=1, keepdims=True)
+    mask[...] = jnp.broadcast_to(column, mask.shape)
     strips, rows = out.shape[0], out.shape[1] * out.shape[2]
     half = mine.shape[0] // strips
     group = 4
@@ -276,19 +278,18 @@
     above[less:] = from_above[less:]
 
 
-def schur_tiles(shift, pattern, update, members, buffer, out, sems):
+def schur_tiles(shift, mask, update, members, buffer, out, sems):
     strips, count, share, size = out.shape[1:]
     pole = lax.axis_index("pole")
-    row = lax.axis_index("row")
     shift_real, shift_imag = shift[:, 0:1], shift[:, 1:2]
     copies = []
     for member, start, length, step, first in members:
         at = lax.rem(pole + count + step, count)
         for index in range(length):
             strip = first + index
-            mask = pattern[strip, row].astype(f32)
-            margin = mask * member[start + index, share:].astype(f32)
-            real = mask * member[start + index, :share].astype(f32) - shift_real * margin
+            here = mask[strip : strip + 1, :]
+            margin = here * member[start + index, share:].astype(f32)
+            real = here * member[start + index, :share].astype(f32) - shift_real * margin
             buffer[0, strip, at] = (real - update[strip, at, :, :size]).astype(bf16)
             buffer[1, strip, at] = (-shift_imag * margin - update[strip, at, :, size:]).astype(bf16)
         where = (slice(None), pl.ds(first, length), at)
@@ -298,7 +299,7 @@
         copy.wait()
 
 
-def schur_first_body(shift, pattern, update, up, down, from_below, from_above, out, buffer, sems):
+def schur_first_body(shift, mask, update, up, down, from_below, from_above, out, buffer, sems):
     more, less = up.shape[0], out.shape[1] - up.shape[0]
     members = (
         (up, 0, more, 0, 0),
@@ -306,10 +307,10 @@
         (from_below, 0, more, -1, 0),
         (from_above, 0, more, 1, less),
     )
-    schur_tiles(shift, pattern, update, members, buffer, out, sems)
-
-
-def schur_last_body(shift, pattern, update, below, above, begun, out, buffer, sems):
+    schur_tiles(shift, mask, update, members, buffer, out, sems)
+
+
+def schur_last_body(shift, mask, update, below, above, begun, out, buffer, sems):
     del begun
     half = out.shape[1] // 2
     less = below.shape[0] - half
@@ -319,7 +320,7 @@
         (above, 0, less, 1, 0),
         (above, less, half, 2, half),
     )
-    schur_tiles(shift, pattern, update, members, buffer, out, sems)
+    schur_tiles(shift, mask, update, members, buffer, out, sems)
 
 
 def shards(
@@ -435,10 +436,13 @@
     spread = lax.all_to_all(spread, ("row", "col"), split_axis=0, concat_axis=0, tiled=True)
     (pivot_out,) = call(pivot_body, [shape(piece, size, dtype=f32)], [spread], 0, "pivot")
 
-    (update,) = call(
+    update, mask = call(
         update_body,
-        [shape(row_count, quarters, share, 2 * size, dtype=f32)],
-        [pole_shift, panel_h, panel_s, mine, other],
+        [
+            shape(row_count, quarters, share, 2 * size, dtype=f32),
+            shape(row_count, size, dtype=f32),
+        ],
+        [pole_shift, pattern, panel_h, panel_s, mine, other],
         8 * row_count * width * size * size,
         "update",
     )
@@ -448,7 +452,7 @@
         return pl.pallas_call(
             body,
             out_shape=tile,
-            in_specs=[VMEM, SMEM] + [VMEM] * (len(ins) - 2) + [pl.BlockSpec(memory_space=pl.ANY)] * len(begun),
+            in_specs=[VMEM] * len(ins) + [pl.BlockSpec(memory_space=pl.ANY)] * len(begun),
             out_specs=pl.BlockSpec(memory_space=pl.ANY),
             input_output_aliases={len(ins): 0} if begun else {},
             scratch_shapes=[pltpu.VMEM(tile.shape, bf16), pltpu.SemaphoreType.DMA((4,))],
@@ -457,7 +461,7 @@
             name=name,
         )(*ins, *begun)
 
-    fixed = [pole_shift, pattern, update]
+    fixed = [pole_shift, mask, update]
     schur = tiles(schur_first_body, fixed + [up, down, from_below, from_above], "schur_first")
     schur = tiles(schur_last_body, fixed + [below, above], "schur_last", (schur,))
     return (schur.reshape(1, 2, row_count, 1, width, size), rows_out.T, pivot_out.T)

time: 85.9 us -> 85.6 us (level)
  waiting for transfers between devices: 24 us -> 27 us
  Pallas kernels: 14 us -> 12.6 us
  local copies, waits for them, and re-layouts: 1.08 us -> 0.04 us
    pallas_call x2, Pallas kernels: 3.22 us -> 1.9 us  [tiles(): pl.pallas_call(body, out_shape=tile, in_specs=[VMEM] * len(ins) + [pl.Blo...]
    all_to_all x1, waiting for transfers between devices: 0.12 us -> 1.29 us  [shards(): lax.all_to_all(spread, ('row', 'col'), split_axis=0, concat_axis=0, tiled...]
    ppermute x1, waiting for transfers between devices: 0.01 us -> 1.06 us  [shards(): other = lax.ppermute(mine, 'row', neighbour)]
    unnamed x20 -> x16, local copies, waits for them, and re-layouts: 1.08 us -> 0.04 us
  transfers between devices with their start and end apart: 8 -> 8, of which waited for: 5 -> 6; matrix products, arithmetic and copies ran while one was open for 0% -> 0% of each run, Pallas kernels for 11% -> 9%
where the time goes in v17:
time: 85.6 us; the launch traced here: 85.1 us
  starting transfers between devices  44.4 us (52%)
  waiting for transfers between devices  27 us (32%)
  Pallas kernels  12.6 us (15%)
  between operations  0.9 us (1%)
    all_to_all x1, waiting for transfers between devices, shards(): lax.all_to_all(sent, 'row', split_axis=0, concat_axis=0, tiled=True)  19.3 us
    all_to_all x1, starting transfers between devices, shards(): lax.all_to_all(sent, 'row', split_axis=0, concat_axis=0, tiled=True)  11.8 us
    all_to_all x1, starting transfers between devices, shards(): lax.all_to_all(both, ('col', 'pole'), split_axis=0, concat_axis=0, tiled=...  9.68 us
    all_to_all x1, starting transfers between devices, shards(): lax.all_to_all(spread, ('row', 'col'), split_axis=0, concat_axis=0, tiled...  8.02 us
    pallas_call x7, Pallas kernels, call(): pl.pallas_call(body, out_shape=outs, in_specs=[VMEM] * len(ins), out_spec...  7.18 us
    ppermute x1, starting transfers between devices, shards(): above = lax.ppermute(above, 'pole', back)  3.85 us
    all_to_all x1, waiting for transfers between devices, shards(): lax.all_to_all(both, ('col', 'pole'), split_axis=0, concat_axis=0, tiled=...  3.6 us
    ppermute x1, starting transfers between devices, shards(): from_above = lax.ppermute(down, 'pole', back)  3.36 us
  transfers between devices with their start and end apart: 8, of which 6 were waited for; matrix products, arithmetic and copies ran while one was open for 0% of the time, Pallas kernels for 9%

profile of v17, /device:TPU:1, one launch (start us, length us, event | category | flops | bytes accessed | tf_op | source)
XLA Modules:
  0.0 85.1 jit_solution(5197029933717813759)
XLA Ops:
  0.6 0.0 copy-start.3
  0.6 0.0 copy-start.6
  0.7 0.0 copy-start.5
  0.7 1.8 %pack.1 = bf16[16,96,256]{2,1,0:T(8,128)(2,1)} custom-call(bf16[256,256]{1,0:T(8,128)(2,1)} %panel_h.5, bf16[256,256]{1,0:T(8,128)(2,1)} %panel_s.5, bf16[64,4096]{1,0:T(8,128)(2,1)} %front_h.1, bf16[64,4096]{1,0:T(8,128)(2,1)} %front_s.1), custom_call_target="tpu_custom_call" | custom-call | bytes 1048576 | tf_op jit(solution)/shard_map/pack/pallas_call | solution.py:351
  2.5 11.8 %all-to-all-start = ((bf16[16,96,256]{2,1,0:T(8,128)(2,1)}), bf16[16,96,256]{2,1,0:T(8,128)(2,1)S(1)}, u32[]{:S(2)}, u32[]{:S(2)}) async-start(bf16[16,96,256]{2,1,0:T(8,128)(2,1)} %pack.1), calls=%async_computation | async-start | bytes 1572864 | tf_op jit(solution)/shard_map/all_to_all | solution.py:365
  14.3 0.0 copy-done.3
  14.4 0.0 copy-done.6
  14.4 0.0 copy-done.5
  14.4 0.0 copy-start.1
  14.4 0.0 copy-start.2
  14.4 0.0 copy-start.4
  14.4 3.3 %pivot_inverse.1.inverse = bf16[2,256,512]{2,1,0:T(8,128)(2,1)S(1)} custom-call(f32[1,2]{1,0:T(1,128)S(1)} %copy-done.3, bf16[256,256]{1,0:T(8,128)(2,1)S(1)} %copy-done.5, bf16[256,256]{1,0:T(8,128)(2,1)S(1)} %copy-done.6), custom_call_target="tpu_custom_call" | custom-call | flops 2415919104 | bytes 786440 | tf_op jit(solution)/shard_map/pivot_inverse/pallas_call | solution.py:17
  17.7 0.0 copy-start
  17.7 19.3 %all-to-all-done.received = bf16[16,96,256]{2,1,0:T(8,128)(2,1)S(1)} async-done(((bf16[16,96,256]{2,1,0:T(8,128)(2,1)}), bf16[16,96,256]{2,1,0:T(8,128)(2,1)S(1)}, u32[]{:S(2)}, u32[]{:S(2)}) %all-to-all-start) | async-done | bytes 786464 | tf_op jit(solution)/shard_map/all_to_all | solution.py:365
  37.0 0.8 solved_rows.1
  37.8 1.9 %collective-permute-start = (bf16[512,512]{1,0:T(8,128)(2,1)S(1)}, bf16[512,512]{1,0:T(8,128)(2,1)S(1)}, u32[]{:S(2)}, u32[]{:S(2)}) collective-permute-start(bf16[512,512]{1,0:T(8,128)(2,1)S(1)} %get-tuple-element.18.mine), channel_id=1, source_target_pairs={{0,4},{4,0},{8,12},{12,8},{16,20},{20,16},{24,28},{28,24},{32,36},... | collective-permute-start | bytes 1572872 | tf_op jit(solution)/shard_map/ppermute | solution.py:383
  39.7 0.0 copy-done.1
  39.7 0.0 copy-done.2
  39.7 0.0 copy-done.4
  39.7 0.0 copy-done
  39.7 0.8 own_column.1
  40.5 1.1 %collective-permute-done.other = bf16[512,512]{1,0:T(8,128)(2,1)S(1)} collective-permute-done((bf16[512,512]{1,0:T(8,128)(2,1)S(1)}, bf16[512,512]{1,0:T(8,128)(2,1)S(1)}, u32[]{:S(2)}, u32[]{:S(2)}) %collective-permute-start) | collective-permute-done | bytes 524320 | tf_op jit(solution)/shard_map/ppermute | solution.py:383
  41.6 1.7 %column.1 = bf16[32,32,128]{2,1,0:T(8,128)(2,1)} custom-call(f32[1,2]{1,0:T(1,128)S(1)} %copy-done.4, bf16[512,512]{1,0:T(8,128)(2,1)S(1)} %collective-permute-done.other, bf16[2,16,64,256]{3,2,1,0:T(8,128)(2,1)S(1)} %bitcast.7, f32[512,256]{1,0:T(8,128)S(1)} %get-tuple-element.23.part, bf16[512,256]{1,0:T(8,128)(2,1)S(1)} %get-tuple-element.24.right, ...), custom_call_target="tpu_custom_call" | custom-call | flops 268435456 | bytes 2097152 | tf_op jit(solution)/shard_map/column/pallas_call | solution.py:397
  43.3 9.7 %all-to-all-start.1 = ((bf16[32,32,128]{2,1,0:T(8,128)(2,1)}), bf16[32,32,128]{2,1,0:T(8,128)(2,1)S(1)}, u32[]{:S(2)}, u32[]{:S(2)}) async-start(bf16[32,32,128]{2,1,0:T(8,128)(2,1)} %column.1), calls=%async_computation.1 | async-start | bytes 524288 | tf_op jit(solution)/shard_map/all_to_all | solution.py:416
  53.0 3.1 %collective-permute-start.1 = (bf16[12,32,256]{2,1,0:T(8,128)(2,1)S(1)}, bf16[12,32,256]{2,1,0:T(8,128)(2,1)S(1)}, u32[]{:S(2)}, u32[]{:S(2)}) collective-permute-start(bf16[12,32,256]{2,1,0:T(8,128)(2,1)S(1)} %get-tuple-element.26.up), channel_id=1, source_target_pairs={{0,64},{64,128},{128,192},{192,256},{256,320},{320,384},{384,448},... | collective-permute-start | bytes 589832 | tf_op jit(solution)/shard_map/ppermute | solution.py:413
  56.1 3.4 %collective-permute-start.2 = (bf16[12,32,256]{2,1,0:T(8,128)(2,1)S(1)}, bf16[12,32,256]{2,1,0:T(8,128)(2,1)S(1)}, u32[]{:S(2)}, u32[]{:S(2)}) collective-permute-start(bf16[12,32,256]{2,1,0:T(8,128)(2,1)S(1)} %get-tuple-element.27.down), channel_id=1, source_target_pairs={{0,448},{64,0},{128,64},{192,128},{256,192},{320,256},{384,320},{4... | collective-permute-start | bytes 589832 | tf_op jit(solution)/shard_map/ppermute | solution.py:414
  59.5 3.6 %all-to-all-done.1.parts = bf16[32,32,128]{2,1,0:T(8,128)(2,1)S(1)} async-done(((bf16[32,32,128]{2,1,0:T(8,128)(2,1)}), bf16[32,32,128]{2,1,0:T(8,128)(2,1)S(1)}, u32[]{:S(2)}, u32[]{:S(2)}) %all-to-all-start.1) | async-done | bytes 262176 | tf_op jit(solution)/shard_map/all_to_all | solution.py:416
  63.1 0.8 sums.1
  63.8 8.0 %all-to-all-start.2 = ((bf16[64,16,128]{2,1,0:T(8,128)(2,1)}), bf16[64,16,128]{2,1,0:T(8,128)(2,1)S(1)}, u32[]{:S(2)}, u32[]{:S(2)}) async-start(bf16[64,16,128]{2,1,0:T(8,128)(2,1)} %get-tuple-element.32), calls=%async_computation.2 | async-start | bytes 524288 | tf_op jit(solution)/shard_map/all_to_all | solution.py:436
  71.9 0.0 copy-start.7
  71.9 0.0 collective-permute-done.1.from_below
  71.9 0.0 collective-permute-done.2.from_above
  71.9 2.6 %collective-permute-start.3 = (bf16[12,32,256]{2,1,0:T(8,128)(2,1)S(1)}, bf16[12,32,256]{2,1,0:T(8,128)(2,1)S(1)}, u32[]{:S(2)}, u32[]{:S(2)}) collective-permute-start(bf16[12,32,256]{2,1,0:T(8,128)(2,1)S(1)} %get-tuple-element.28), channel_id=1, source_target_pairs={{0,64},{64,128},{128,192},{192,256},{256,320},{320,384},{384,448},... | collective-permute-start | bytes 589832 | tf_op jit(solution)/shard_map/ppermute | solution.py:434
  74.6 3.8 %collective-permute-start.4 = (bf16[12,32,256]{2,1,0:T(8,128)(2,1)S(1)}, bf16[12,32,256]{2,1,0:T(8,128)(2,1)S(1)}, u32[]{:S(2)}, u32[]{:S(2)}) collective-permute-start(bf16[12,32,256]{2,1,0:T(8,128)(2,1)S(1)} %get-tuple-element.29), channel_id=1, source_target_pairs={{0,448},{64,0},{128,64},{192,128},{256,192},{320,256},{384,320},{4... | collective-permute-start | bytes 589832 | tf_op jit(solution)/shard_map/ppermute | solution.py:435
  78.5 0.0 copy-done.7
  78.5 0.8 update.1
  79.3 1.0 %schur_first.1.begun = bf16[2,16,4,16,256]{4,3,2,1,0:T(8,128)(2,1)} custom-call(f32[1,2]{1,0:T(1,128)S(1)} %copy-done.3, f32[16,256]{1,0:T(8,128)S(1)} %get-tuple-element.19.mask, f32[16,4,16,512]{3,2,1,0:T(8,128)S(1)} %get-tuple-element.20.update, bf16[12,32,256]{2,1,0:T(8,128)(2,1)S(1)} %get-tuple-element.26.up, ...), custom_call_target="tpu_custom_call" | custom-call | bytes 3145728 | tf_op jit(solution)/shard_map/schur_first/pallas_call | solution.py:452
  80.3 0.6 collective-permute-done.3.below
  81.0 1.2 %collective-permute-done.4.above = bf16[12,32,256]{2,1,0:T(8,128)(2,1)S(1)} collective-permute-done((bf16[12,32,256]{2,1,0:T(8,128)(2,1)S(1)}, bf16[12,32,256]{2,1,0:T(8,128)(2,1)S(1)}, u32[]{:S(2)}, u32[]{:S(2)}) %collective-permute-start.4) | collective-permute-done | bytes 196640 | tf_op jit(solution)/shard_map/ppermute | solution.py:435
  82.1 0.9 %schur_last.1 = bf16[2,16,4,16,256]{4,3,2,1,0:T(8,128)(2,1)} custom-call(f32[1,2]{1,0:T(1,128)S(1)} %copy-done.3, f32[16,256]{1,0:T(8,128)S(1)} %get-tuple-element.19.mask, f32[16,4,16,512]{3,2,1,0:T(8,128)S(1)} %get-tuple-element.20.update, bf16[12,32,256]{2,1,0:T(8,128)(2,1)S(1)} %collective-permute-done.3.below, ...), custom_call_target="tpu_custom_call", output_to_operand_aliasing={{}: (5, {})} | custom-call | bytes 3145728 | tf_op jit(solution)/shard_map/schur_last/pallas_call | solution.py:452
  83.0 1.3 %all-to-all-done.2.parts = bf16[64,16,128]{2,1,0:T(8,128)(2,1)S(1)} async-done(((bf16[64,16,128]{2,1,0:T(8,128)(2,1)}), bf16[64,16,128]{2,1,0:T(8,128)(2,1)S(1)}, u32[]{:S(2)}, u32[]{:S(2)}) %all-to-all-start.2) | async-done | bytes 262176 | tf_op jit(solution)/shard_map/all_to_all | solution.py:436
  84.3 0.7 pivot.1
  (1 shorter events, 0.0 us)
Async XLA Ops:
  0.6 13.7 %copy-start.3 = (f32[1,2]{1,0:T(1,128)S(1)}, f32[1,2]{1,0:T(1,128)}, u32[]{:S(2)}) copy-start(f32[1,2]{1,0:T(1,128)} %shift.11) | copy-start | bytes 28
  0.6 13.7 %copy-start.6 = (bf16[256,256]{1,0:T(8,128)(2,1)S(1)}, bf16[256,256]{1,0:T(8,128)(2,1)}, u32[]{:S(2)}) copy-start(bf16[256,256]{1,0:T(8,128)(2,1)} %pivot_s.1) | copy-start | bytes 393220
  0.7 13.7 %copy-start.5 = (bf16[256,256]{1,0:T(8,128)(2,1)S(1)}, bf16[256,256]{1,0:T(8,128)(2,1)}, u32[]{:S(2)}) copy-start(bf16[256,256]{1,0:T(8,128)(2,1)} %pivot_h.1) | copy-start | bytes 393220
  2.5 34.5 %all-to-all-start = ((bf16[16,96,256]{2,1,0:T(8,128)(2,1)}), bf16[16,96,256]{2,1,0:T(8,128)(2,1)S(1)}, u32[]{:S(2)}, u32[]{:S(2)}) async-start(bf16[16,96,256]{2,1,0:T(8,128)(2,1)} %pack.1), calls=%async_computation | async-start | bytes 1572864 | tf_op jit(solution)/shard_map/all_to_all | solution.py:365
  14.4 25.3 %copy-start.1 = (bf16[256,256]{1,0:T(8,128)(2,1)S(1)}, bf16[256,256]{1,0:T(8,128)(2,1)}, u32[]{:S(2)}) copy-start(bf16[256,256]{1,0:T(8,128)(2,1)} %panel_h.5) | copy-start | bytes 393220
  14.4 25.3 %copy-start.2 = (bf16[256,256]{1,0:T(8,128)(2,1)S(1)}, bf16[256,256]{1,0:T(8,128)(2,1)}, u32[]{:S(2)}) copy-start(bf16[256,256]{1,0:T(8,128)(2,1)} %panel_s.5) | copy-start | bytes 393220
  14.4 25.3 %copy-start.4 = (f32[1,2]{1,0:T(1,128)S(1)}, f32[1,2]{1,0:T(1,128)}, u32[]{:S(2)}) copy-start(f32[1,2]{1,0:T(1,128)} %weight.3) | copy-start | bytes 28
  17.7 22.0 %copy-start = (bf16[1,2,16,1,64,256]{5,4,3,2,1,0:T(8,128)(2,1)S(1)}, bf16[1,2,16,1,64,256]{5,4,3,2,1,0:T(8,128)(2,1)}, u32[]{:S(2)}) copy-start(bf16[1,2,16,1,64,256]{5,4,3,2,1,0:T(8,128)(2,1)} %param.19) | copy-start | bytes 3145732
  37.8 3.8 %collective-permute-start = (bf16[512,512]{1,0:T(8,128)(2,1)S(1)}, bf16[512,512]{1,0:T(8,128)(2,1)S(1)}, u32[]{:S(2)}, u32[]{:S(2)}) collective-permute-start(bf16[512,512]{1,0:T(8,128)(2,1)S(1)} %get-tuple-element.18.mine), channel_id=1, source_target_pairs={{0,4},{4,0},{8,12},{12,8},{16,20},{20,16},{24,28},{28,24},{32,36},... | collective-permute-start | bytes 1572872 | tf_op jit(solution)/shard_map/ppermute | solution.py:383
  43.3 19.8 %all-to-all-start.1 = ((bf16[32,32,128]{2,1,0:T(8,128)(2,1)}), bf16[32,32,128]{2,1,0:T(8,128)(2,1)S(1)}, u32[]{:S(2)}, u32[]{:S(2)}) async-start(bf16[32,32,128]{2,1,0:T(8,128)(2,1)} %column.1), calls=%async_computation.1 | async-start | bytes 524288 | tf_op jit(solution)/shard_map/all_to_all | solution.py:416
  53.0 18.9 %collective-permute-start.1 = (bf16[12,32,256]{2,1,0:T(8,128)(2,1)S(1)}, bf16[12,32,256]{2,1,0:T(8,128)(2,1)S(1)}, u32[]{:S(2)}, u32[]{:S(2)}) collective-permute-start(bf16[12,32,256]{2,1,0:T(8,128)(2,1)S(1)} %get-tuple-element.26.up), channel_id=1, source_target_pairs={{0,64},{64,128},{128,192},{192,256},{256,320},{320,384},{384,448},... | collective-permute-start | bytes 589832 | tf_op jit(solution)/shard_map/ppermute | solution.py:413
  56.1 15.8 %collective-permute-start.2 = (bf16[12,32,256]{2,1,0:T(8,128)(2,1)S(1)}, bf16[12,32,256]{2,1,0:T(8,128)(2,1)S(1)}, u32[]{:S(2)}, u32[]{:S(2)}) collective-permute-start(bf16[12,32,256]{2,1,0:T(8,128)(2,1)S(1)} %get-tuple-element.27.down), channel_id=1, source_target_pairs={{0,448},{64,0},{128,64},{192,128},{256,192},{320,256},{384,320},{4... | collective-permute-start | bytes 589832 | tf_op jit(solution)/shard_map/ppermute | solution.py:414
  63.8 20.5 %all-to-all-start.2 = ((bf16[64,16,128]{2,1,0:T(8,128)(2,1)}), bf16[64,16,128]{2,1,0:T(8,128)(2,1)S(1)}, u32[]{:S(2)}, u32[]{:S(2)}) async-start(bf16[64,16,128]{2,1,0:T(8,128)(2,1)} %get-tuple-element.32), calls=%async_computation.2 | async-start | bytes 524288 | tf_op jit(solution)/shard_map/all_to_all | solution.py:436
  71.9 6.6 %copy-start.7 = (s32[16,16]{1,0:T(8,128)S(1)}, s32[16,16]{1,0:T(8,128)}, u32[]{:S(2)}) copy-start(s32[16,16]{1,0:T(8,128)} %pattern.1) | copy-start | bytes 3076
  71.9 9.0 %collective-permute-start.3 = (bf16[12,32,256]{2,1,0:T(8,128)(2,1)S(1)}, bf16[12,32,256]{2,1,0:T(8,128)(2,1)S(1)}, u32[]{:S(2)}, u32[]{:S(2)}) collective-permute-start(bf16[12,32,256]{2,1,0:T(8,128)(2,1)S(1)} %get-tuple-element.28), channel_id=1, source_target_pairs={{0,64},{64,128},{128,192},{192,256},{256,320},{320,384},{384,448},... | collective-permute-start | bytes 589832 | tf_op jit(solution)/shard_map/ppermute | solution.py:434
  74.6 7.5 %collective-permute-start.4 = (bf16[12,32,256]{2,1,0:T(8,128)(2,1)S(1)}, bf16[12,32,256]{2,1,0:T(8,128)(2,1)S(1)}, u32[]{:S(2)}, u32[]{:S(2)}) collective-permute-start(bf16[12,32,256]{2,1,0:T(8,128)(2,1)S(1)} %get-tuple-element.29), channel_id=1, source_target_pairs={{0,448},{64,0},{128,64},{192,128},{256,192},{320,256},{384,320},{4... | collective-permute-start | bytes 589832 | tf_op jit(solution)/shard_map/ppermute | solution.py:435

commit v18 on v17

--- a/solution.py
+++ b/solution.py
@@ -270,12 +270,12 @@
 
 def relay_body(up, down, from_below, from_above, below, above):
     more = up.shape[0]
-    less = more // 3
-    half = more - less
-    below[:less] = down[half:]
+    less = below.shape[0] - (below.shape[0] + more) // 3
+    half = below.shape[0] - less
+    below[:less] = down[more - less :]
     below[less:] = from_below[:half]
     above[:less] = up[:less]
-    above[less:] = from_above[less:]
+    above[less:] = from_above[more - half :]
 
 
 def schur_tiles(shift, mask, update, members, buffer, out, sems):
@@ -371,7 +371,7 @@
         6 * 4 * 3 * 2 * size**3,
         "pivot_inverse",
     )
-    less = row_count // 4
+    less = 3 * row_count // 8
     more = row_count - less
     mine, up, down = call(
         solve_body,
@@ -426,7 +426,7 @@
     )
     below, above = call(
         relay_body,
-        [shape(more, 2 * share, size)] * 2,
+        [shape(less + row_count // 2, 2 * share, size)] * 2,
         [up, down, from_below, from_above],
         10**11,
         "relay",

time: 85.6 us -> 85.6 us (level)
  no operation moved by 1% of the time
where the time goes in v18:
time: 85.6 us; the launch traced here: 85.1 us
  starting transfers between devices  44.5 us (52%)
  waiting for transfers between devices  27 us (32%)
  Pallas kernels  12.6 us (15%)
  between operations  0.9 us (1%)
    all_to_all x1, waiting for transfers between devices, shards(): lax.all_to_all(sent, 'row', split_axis=0, concat_axis=0, tiled=True)  19.3 us
    all_to_all x1, starting transfers between devices, shards(): lax.all_to_all(sent, 'row', split_axis=0, concat_axis=0, tiled=True)  11.8 us
    all_to_all x1, starting transfers between devices, shards(): lax.all_to_all(both, ('col', 'pole'), split_axis=0, concat_axis=0, tiled=...  9.68 us
    all_to_all x1, starting transfers between devices, shards(): lax.all_to_all(spread, ('row', 'col'), split_axis=0, concat_axis=0, tiled...  8.02 us
    pallas_call x7, Pallas kernels, call(): pl.pallas_call(body, out_shape=outs, in_specs=[VMEM] * len(ins), out_spec...  7.2 us
    ppermute x1, starting transfers between devices, shards(): above = lax.ppermute(above, 'pole', back)  3.85 us
    all_to_all x1, waiting for transfers between devices, shards(): lax.all_to_all(both, ('col', 'pole'), split_axis=0, concat_axis=0, tiled=...  3.6 us
    ppermute x1, starting transfers between devices, shards(): from_above = lax.ppermute(down, 'pole', back)  3.36 us
  transfers between devices with their start and end apart: 8, of which 6 were waited for; matrix products, arithmetic and copies ran while one was open for 0% of the time, Pallas kernels for 9%

profile of v18, /device:TPU:1, one launch (start us, length us, event | category | flops | bytes accessed | tf_op | source)
XLA Modules:
  0.0 85.1 jit_solution(14155106691307798782)
XLA Ops:
  0.6 0.0 copy-start.3
  0.6 0.0 copy-start.6
  0.7 0.0 copy-start.5
  0.7 1.8 %pack.1 = bf16[16,96,256]{2,1,0:T(8,128)(2,1)} custom-call(bf16[256,256]{1,0:T(8,128)(2,1)} %panel_h.5, bf16[256,256]{1,0:T(8,128)(2,1)} %panel_s.5, bf16[64,4096]{1,0:T(8,128)(2,1)} %front_h.1, bf16[64,4096]{1,0:T(8,128)(2,1)} %front_s.1), custom_call_target="tpu_custom_call" | custom-call | bytes 1048576 | tf_op jit(solution)/shard_map/pack/pallas_call | solution.py:351
  2.5 11.8 %all-to-all-start = ((bf16[16,96,256]{2,1,0:T(8,128)(2,1)}), bf16[16,96,256]{2,1,0:T(8,128)(2,1)S(1)}, u32[]{:S(2)}, u32[]{:S(2)}) async-start(bf16[16,96,256]{2,1,0:T(8,128)(2,1)} %pack.1), calls=%async_computation | async-start | bytes 1572864 | tf_op jit(solution)/shard_map/all_to_all | solution.py:365
  14.3 0.0 copy-done.3
  14.4 0.0 copy-done.6
  14.4 0.0 copy-done.5
  14.4 0.0 copy-start.1
  14.4 0.0 copy-start.2
  14.4 0.0 copy-start.4
  14.4 3.3 %pivot_inverse.1.inverse = bf16[2,256,512]{2,1,0:T(8,128)(2,1)S(1)} custom-call(f32[1,2]{1,0:T(1,128)S(1)} %copy-done.3, bf16[256,256]{1,0:T(8,128)(2,1)S(1)} %copy-done.5, bf16[256,256]{1,0:T(8,128)(2,1)S(1)} %copy-done.6), custom_call_target="tpu_custom_call" | custom-call | flops 2415919104 | bytes 786440 | tf_op jit(solution)/shard_map/pivot_inverse/pallas_call | solution.py:17
  17.7 0.0 copy-start
  17.7 19.3 %all-to-all-done.received = bf16[16,96,256]{2,1,0:T(8,128)(2,1)S(1)} async-done(((bf16[16,96,256]{2,1,0:T(8,128)(2,1)}), bf16[16,96,256]{2,1,0:T(8,128)(2,1)S(1)}, u32[]{:S(2)}, u32[]{:S(2)}) %all-to-all-start) | async-done | bytes 786464 | tf_op jit(solution)/shard_map/all_to_all | solution.py:365
  37.0 0.8 solved_rows.1
  37.8 1.9 %collective-permute-start = (bf16[512,512]{1,0:T(8,128)(2,1)S(1)}, bf16[512,512]{1,0:T(8,128)(2,1)S(1)}, u32[]{:S(2)}, u32[]{:S(2)}) collective-permute-start(bf16[512,512]{1,0:T(8,128)(2,1)S(1)} %get-tuple-element.18.mine), channel_id=1, source_target_pairs={{0,4},{4,0},{8,12},{12,8},{16,20},{20,16},{24,28},{28,24},{32,36},... | collective-permute-start | bytes 1572872 | tf_op jit(solution)/shard_map/ppermute | solution.py:383
  39.7 0.0 copy-done.1
  39.7 0.0 copy-done.2
  39.7 0.0 copy-done.4
  39.7 0.0 copy-done
  39.7 0.8 own_column.1
  40.5 1.1 %collective-permute-done.other = bf16[512,512]{1,0:T(8,128)(2,1)S(1)} collective-permute-done((bf16[512,512]{1,0:T(8,128)(2,1)S(1)}, bf16[512,512]{1,0:T(8,128)(2,1)S(1)}, u32[]{:S(2)}, u32[]{:S(2)}) %collective-permute-start) | collective-permute-done | bytes 524320 | tf_op jit(solution)/shard_map/ppermute | solution.py:383
  41.6 1.7 %column.1 = bf16[32,32,128]{2,1,0:T(8,128)(2,1)} custom-call(f32[1,2]{1,0:T(1,128)S(1)} %copy-done.4, bf16[512,512]{1,0:T(8,128)(2,1)S(1)} %collective-permute-done.other, bf16[2,16,64,256]{3,2,1,0:T(8,128)(2,1)S(1)} %bitcast.7, f32[512,256]{1,0:T(8,128)S(1)} %get-tuple-element.23.part, bf16[512,256]{1,0:T(8,128)(2,1)S(1)} %get-tuple-element.24.right, ...), custom_call_target="tpu_custom_call" | custom-call | flops 268435456 | bytes 2097152 | tf_op jit(solution)/shard_map/column/pallas_call | solution.py:397
  43.3 9.7 %all-to-all-start.1 = ((bf16[32,32,128]{2,1,0:T(8,128)(2,1)}), bf16[32,32,128]{2,1,0:T(8,128)(2,1)S(1)}, u32[]{:S(2)}, u32[]{:S(2)}) async-start(bf16[32,32,128]{2,1,0:T(8,128)(2,1)} %column.1), calls=%async_computation.1 | async-start | bytes 524288 | tf_op jit(solution)/shard_map/all_to_all | solution.py:416
  53.0 3.1 %collective-permute-start.1 = (bf16[10,32,256]{2,1,0:T(8,128)(2,1)S(1)}, bf16[10,32,256]{2,1,0:T(8,128)(2,1)S(1)}, u32[]{:S(2)}, u32[]{:S(2)}) collective-permute-start(bf16[10,32,256]{2,1,0:T(8,128)(2,1)S(1)} %get-tuple-element.26.up), channel_id=1, source_target_pairs={{0,64},{64,128},{128,192},{192,256},{256,320},{320,384},{384,448},... | collective-permute-start | bytes 491528 | tf_op jit(solution)/shard_map/ppermute | solution.py:413
  56.1 3.4 %collective-permute-start.2 = (bf16[10,32,256]{2,1,0:T(8,128)(2,1)S(1)}, bf16[10,32,256]{2,1,0:T(8,128)(2,1)S(1)}, u32[]{:S(2)}, u32[]{:S(2)}) collective-permute-start(bf16[10,32,256]{2,1,0:T(8,128)(2,1)S(1)} %get-tuple-element.27.down), channel_id=1, source_target_pairs={{0,448},{64,0},{128,64},{192,128},{256,192},{320,256},{384,320},{4... | collective-permute-start | bytes 491528 | tf_op jit(solution)/shard_map/ppermute | solution.py:414
  59.5 3.6 %all-to-all-done.1.parts = bf16[32,32,128]{2,1,0:T(8,128)(2,1)S(1)} async-done(((bf16[32,32,128]{2,1,0:T(8,128)(2,1)}), bf16[32,32,128]{2,1,0:T(8,128)(2,1)S(1)}, u32[]{:S(2)}, u32[]{:S(2)}) %all-to-all-start.1) | async-done | bytes 262176 | tf_op jit(solution)/shard_map/all_to_all | solution.py:416
  63.1 0.8 sums.1
  63.8 8.0 %all-to-all-start.2 = ((bf16[64,16,128]{2,1,0:T(8,128)(2,1)}), bf16[64,16,128]{2,1,0:T(8,128)(2,1)S(1)}, u32[]{:S(2)}, u32[]{:S(2)}) async-start(bf16[64,16,128]{2,1,0:T(8,128)(2,1)} %get-tuple-element.32), calls=%async_computation.2 | async-start | bytes 524288 | tf_op jit(solution)/shard_map/all_to_all | solution.py:436
  71.9 0.0 copy-start.7
  71.9 0.0 collective-permute-done.1.from_below
  71.9 0.0 collective-permute-done.2.from_above
  71.9 2.6 %collective-permute-start.3 = (bf16[14,32,256]{2,1,0:T(8,128)(2,1)S(1)}, bf16[14,32,256]{2,1,0:T(8,128)(2,1)S(1)}, u32[]{:S(2)}, u32[]{:S(2)}) collective-permute-start(bf16[14,32,256]{2,1,0:T(8,128)(2,1)S(1)} %get-tuple-element.28), channel_id=1, source_target_pairs={{0,64},{64,128},{128,192},{192,256},{256,320},{320,384},{384,448},... | collective-permute-start | bytes 688136 | tf_op jit(solution)/shard_map/ppermute | solution.py:434
  74.6 3.8 %collective-permute-start.4 = (bf16[14,32,256]{2,1,0:T(8,128)(2,1)S(1)}, bf16[14,32,256]{2,1,0:T(8,128)(2,1)S(1)}, u32[]{:S(2)}, u32[]{:S(2)}) collective-permute-start(bf16[14,32,256]{2,1,0:T(8,128)(2,1)S(1)} %get-tuple-element.29), channel_id=1, source_target_pairs={{0,448},{64,0},{128,64},{192,128},{256,192},{320,256},{384,320},{4... | collective-permute-start | bytes 688136 | tf_op jit(solution)/shard_map/ppermute | solution.py:435
  78.5 0.0 copy-done.7
  78.5 0.8 update.1
  79.3 1.0 %schur_first.1.begun = bf16[2,16,4,16,256]{4,3,2,1,0:T(8,128)(2,1)} custom-call(f32[1,2]{1,0:T(1,128)S(1)} %copy-done.3, f32[16,256]{1,0:T(8,128)S(1)} %get-tuple-element.19.mask, f32[16,4,16,512]{3,2,1,0:T(8,128)S(1)} %get-tuple-element.20.update, bf16[10,32,256]{2,1,0:T(8,128)(2,1)S(1)} %get-tuple-element.26.up, ...), custom_call_target="tpu_custom_call" | custom-call | bytes 3145728 | tf_op jit(solution)/shard_map/schur_first/pallas_call | solution.py:452
  80.3 1.4 %collective-permute-done.3.below = bf16[14,32,256]{2,1,0:T(8,128)(2,1)S(1)} collective-permute-done((bf16[14,32,256]{2,1,0:T(8,128)(2,1)S(1)}, bf16[14,32,256]{2,1,0:T(8,128)(2,1)S(1)}, u32[]{:S(2)}, u32[]{:S(2)}) %collective-permute-start.3) | collective-permute-done | bytes 229408 | tf_op jit(solution)/shard_map/ppermute | solution.py:434
  81.7 1.2 %collective-permute-done.4.above = bf16[14,32,256]{2,1,0:T(8,128)(2,1)S(1)} collective-permute-done((bf16[14,32,256]{2,1,0:T(8,128)(2,1)S(1)}, bf16[14,32,256]{2,1,0:T(8,128)(2,1)S(1)}, u32[]{:S(2)}, u32[]{:S(2)}) %collective-permute-start.4) | collective-permute-done | bytes 229408 | tf_op jit(solution)/shard_map/ppermute | solution.py:435
  82.8 0.9 %schur_last.1 = bf16[2,16,4,16,256]{4,3,2,1,0:T(8,128)(2,1)} custom-call(f32[1,2]{1,0:T(1,128)S(1)} %copy-done.3, f32[16,256]{1,0:T(8,128)S(1)} %get-tuple-element.19.mask, f32[16,4,16,512]{3,2,1,0:T(8,128)S(1)} %get-tuple-element.20.update, bf16[14,32,256]{2,1,0:T(8,128)(2,1)S(1)} %collective-permute-done.3.below, ...), custom_call_target="tpu_custom_call", output_to_operand_aliasing={{}: (5, {})} | custom-call | bytes 3145728 | tf_op jit(solution)/shard_map/schur_last/pallas_call | solution.py:452
  83.8 0.6 all-to-all-done.2.parts
  84.3 0.7 pivot.1
  (1 shorter events, 0.0 us)
Async XLA Ops:
  0.6 13.7 %copy-start.3 = (f32[1,2]{1,0:T(1,128)S(1)}, f32[1,2]{1,0:T(1,128)}, u32[]{:S(2)}) copy-start(f32[1,2]{1,0:T(1,128)} %shift.11) | copy-start | bytes 28
  0.6 13.7 %copy-start.6 = (bf16[256,256]{1,0:T(8,128)(2,1)S(1)}, bf16[256,256]{1,0:T(8,128)(2,1)}, u32[]{:S(2)}) copy-start(bf16[256,256]{1,0:T(8,128)(2,1)} %pivot_s.1) | copy-start | bytes 393220
  0.7 13.7 %copy-start.5 = (bf16[256,256]{1,0:T(8,128)(2,1)S(1)}, bf16[256,256]{1,0:T(8,128)(2,1)}, u32[]{:S(2)}) copy-start(bf16[256,256]{1,0:T(8,128)(2,1)} %pivot_h.1) | copy-start | bytes 393220
  2.5 34.5 %all-to-all-start = ((bf16[16,96,256]{2,1,0:T(8,128)(2,1)}), bf16[16,96,256]{2,1,0:T(8,128)(2,1)S(1)}, u32[]{:S(2)}, u32[]{:S(2)}) async-start(bf16[16,96,256]{2,1,0:T(8,128)(2,1)} %pack.1), calls=%async_computation | async-start | bytes 1572864 | tf_op jit(solution)/shard_map/all_to_all | solution.py:365
  14.4 25.3 %copy-start.1 = (bf16[256,256]{1,0:T(8,128)(2,1)S(1)}, bf16[256,256]{1,0:T(8,128)(2,1)}, u32[]{:S(2)}) copy-start(bf16[256,256]{1,0:T(8,128)(2,1)} %panel_h.5) | copy-start | bytes 393220
  14.4 25.3 %copy-start.2 = (bf16[256,256]{1,0:T(8,128)(2,1)S(1)}, bf16[256,256]{1,0:T(8,128)(2,1)}, u32[]{:S(2)}) copy-start(bf16[256,256]{1,0:T(8,128)(2,1)} %panel_s.5) | copy-start | bytes 393220
  14.4 25.3 %copy-start.4 = (f32[1,2]{1,0:T(1,128)S(1)}, f32[1,2]{1,0:T(1,128)}, u32[]{:S(2)}) copy-start(f32[1,2]{1,0:T(1,128)} %weight.3) | copy-start | bytes 28
  17.7 22.0 %copy-start = (bf16[1,2,16,1,64,256]{5,4,3,2,1,0:T(8,128)(2,1)S(1)}, bf16[1,2,16,1,64,256]{5,4,3,2,1,0:T(8,128)(2,1)}, u32[]{:S(2)}) copy-start(bf16[1,2,16,1,64,256]{5,4,3,2,1,0:T(8,128)(2,1)} %param.19) | copy-start | bytes 3145732
  37.8 3.8 %collective-permute-start = (bf16[512,512]{1,0:T(8,128)(2,1)S(1)}, bf16[512,512]{1,0:T(8,128)(2,1)S(1)}, u32[]{:S(2)}, u32[]{:S(2)}) collective-permute-start(bf16[512,512]{1,0:T(8,128)(2,1)S(1)} %get-tuple-element.18.mine), channel_id=1, source_target_pairs={{0,4},{4,0},{8,12},{12,8},{16,20},{20,16},{24,28},{28,24},{32,36},... | collective-permute-start | bytes 1572872 | tf_op jit(solution)/shard_map/ppermute | solution.py:383
  43.3 19.8 %all-to-all-start.1 = ((bf16[32,32,128]{2,1,0:T(8,128)(2,1)}), bf16[32,32,128]{2,1,0:T(8,128)(2,1)S(1)}, u32[]{:S(2)}, u32[]{:S(2)}) async-start(bf16[32,32,128]{2,1,0:T(8,128)(2,1)} %column.1), calls=%async_computation.1 | async-start | bytes 524288 | tf_op jit(solution)/shard_map/all_to_all | solution.py:416
  53.0 18.9 %collective-permute-start.1 = (bf16[10,32,256]{2,1,0:T(8,128)(2,1)S(1)}, bf16[10,32,256]{2,1,0:T(8,128)(2,1)S(1)}, u32[]{:S(2)}, u32[]{:S(2)}) collective-permute-start(bf16[10,32,256]{2,1,0:T(8,128)(2,1)S(1)} %get-tuple-element.26.up), channel_id=1, source_target_pairs={{0,64},{64,128},{128,192},{192,256},{256,320},{320,384},{384,448},... | collective-permute-start | bytes 491528 | tf_op jit(solution)/shard_map/ppermute | solution.py:413
  56.1 15.8 %collective-permute-start.2 = (bf16[10,32,256]{2,1,0:T(8,128)(2,1)S(1)}, bf16[10,32,256]{2,1,0:T(8,128)(2,1)S(1)}, u32[]{:S(2)}, u32[]{:S(2)}) collective-permute-start(bf16[10,32,256]{2,1,0:T(8,128)(2,1)S(1)} %get-tuple-element.27.down), channel_id=1, source_target_pairs={{0,448},{64,0},{128,64},{192,128},{256,192},{320,256},{384,320},{4... | collective-permute-start | bytes 491528 | tf_op jit(solution)/shard_map/ppermute | solution.py:414
  63.8 20.5 %all-to-all-start.2 = ((bf16[64,16,128]{2,1,0:T(8,128)(2,1)}), bf16[64,16,128]{2,1,0:T(8,128)(2,1)S(1)}, u32[]{:S(2)}, u32[]{:S(2)}) async-start(bf16[64,16,128]{2,1,0:T(8,128)(2,1)} %get-tuple-element.32), calls=%async_computation.2 | async-start | bytes 524288 | tf_op jit(solution)/shard_map/all_to_all | solution.py:436
  71.9 6.6 %copy-start.7 = (s32[16,16]{1,0:T(8,128)S(1)}, s32[16,16]{1,0:T(8,128)}, u32[]{:S(2)}) copy-start(s32[16,16]{1,0:T(8,128)} %pattern.1) | copy-start | bytes 3076
  71.9 9.7 %collective-permute-start.3 = (bf16[14,32,256]{2,1,0:T(8,128)(2,1)S(1)}, bf16[14,32,256]{2,1,0:T(8,128)(2,1)S(1)}, u32[]{:S(2)}, u32[]{:S(2)}) collective-permute-start(bf16[14,32,256]{2,1,0:T(8,128)(2,1)S(1)} %get-tuple-element.28), channel_id=1, source_target_pairs={{0,64},{64,128},{128,192},{192,256},{256,320},{320,384},{384,448},... | collective-permute-start | bytes 688136 | tf_op jit(solution)/shard_map/ppermute | solution.py:434
  74.6 8.2 %collective-permute-start.4 = (bf16[14,32,256]{2,1,0:T(8,128)(2,1)S(1)}, bf16[14,32,256]{2,1,0:T(8,128)(2,1)S(1)}, u32[]{:S(2)}, u32[]{:S(2)}) collective-permute-start(bf16[14,32,256]{2,1,0:T(8,128)(2,1)S(1)} %get-tuple-element.29), channel_id=1, source_target_pairs={{0,448},{64,0},{128,64},{192,128},{256,192},{320,256},{384,320},{4... | collective-permute-start | bytes 688136 | tf_op jit(solution)/shard_map/ppermute | solution.py:435

commit v19 on v18

--- a/solution.py
+++ b/solution.py
@@ -120,28 +120,35 @@
         pltpu.make_async_copy(front_h.at[of], fronts.at[0], sems.at[2]),
         pltpu.make_async_copy(front_s.at[of], fronts.at[1], sems.at[3]),
     ]
-    panel_rows, front_rows = pl.ds(0, 2 * half), pl.ds(2 * half, 2 * share)
-    stores = [
-        pltpu.make_async_copy(buffer.at[:, rows], out.at[:, rows], sems.at[4 + index])
-        for index, rows in enumerate((panel_rows, front_rows))
-    ]
+    rows = out.shape[0] // 2
+    stores = []
+
+    def send(first, low, height):
+        where = (pl.ds(first, rows), pl.ds(low, height))
+        stores.append(
+            pltpu.make_async_copy(buffer.at[where], out.at[where], sems.at[4 + len(stores)])
+        )
+        stores[-1].start()
+
     for load in loads:
         load.start()
     loads[0].wait()
     loads[1].wait()
-    for row in range(out.shape[0]):
-        core = row % 2
-        for part in range(2):
-            low = part * half
-            buffer[row, low : low + half] = panels[part, core * half : (core + 1) * half]
-    stores[0].start()
+    for first in (0, rows):
+        for row in range(first, first + rows):
+            core = row % 2
+            for part in range(2):
+                low = part * half
+                buffer[row, low : low + half] = panels[part, core * half : (core + 1) * half]
+        send(first, 0, 2 * half)
     loads[2].wait()
     loads[3].wait()
-    for row in range(out.shape[0]):
-        for part in range(2):
-            low = 2 * half + part * share
-            buffer[row, low : low + share] = fronts[part, :, row * size : (row + 1) * size]
-    stores[1].start()
+    for first in (0, rows):
+        for row in range(first, first + rows):
+            for part in range(2):
+                low = 2 * half + part * share
+                buffer[row, low : low + share] = fronts[part, :, row * size : (row + 1) * size]
+        send(first, 2 * half, 2 * share)
     for store in stores:
         store.wait()
 
@@ -224,12 +231,21 @@
         store.wait()
 
 
-def sums_body(parts, spread, rows):
+def sums_body(parts, spread, rows, copies, shares, sems):
     half, width = parts.shape[1] // 2, rows.shape[1]
-    total = jnp.sum(parts[...].astype(f32), axis=0)
-    rows[:half] = total[:half, :width]
-    rows[half:] = total[:half, width:]
-    spread[...] = jnp.broadcast_to(total[None, half:].astype(spread.dtype), spread.shape)
+    total = jnp.sum(parts[:, half:].astype(f32), axis=0)
+    copies[...] = jnp.broadcast_to(total[None].astype(copies.dtype), copies.shape)
+    stores = [
+        pltpu.make_async_copy(copies, spread, sems.at[0]),
+        pltpu.make_async_copy(shares, rows, sems.at[1]),
+    ]
+    stores[0].start()
+    total = jnp.sum(parts[:, :half].astype(f32), axis=0)
+    shares[:half] = total[:, :width]
+    shares[half:] = total[:, width:]
+    stores[1].start()
+    for store in stores:
+        store.wait()
 
 
 def pivot_body(parts, out):
@@ -357,7 +373,7 @@
             pltpu.VMEM((2, width, size), bf16),
             pltpu.VMEM((2, share, row_count * size), bf16),
             pltpu.VMEM((row_count, width + 2 * share, size), bf16),
-            pltpu.SemaphoreType.DMA((6,)),
+            pltpu.SemaphoreType.DMA((8,)),
         ],
         cost_estimate=pl.CostEstimate(flops=0, bytes_accessed=2**20, transcendentals=0),
         name="pack",
@@ -414,16 +430,21 @@
     from_above = lax.ppermute(down, "pole", back)
 
     both = lax.all_to_all(both, ("col", "pole"), split_axis=0, concat_axis=0, tiled=True)
-    spread, rows_out = call(
+    sums = [
+        shape(row_count * col_count, piece // 2, 128),
+        shape(piece, width, dtype=f32),
+    ]
+    spread, rows_out = pl.pallas_call(
         sums_body,
-        [
-            shape(row_count * col_count, piece // 2, 128),
-            shape(piece, width, dtype=f32),
-        ],
-        [both],
-        0,
-        "sums",
-    )
+        out_shape=sums,
+        in_specs=[VMEM],
+        out_specs=[pl.BlockSpec(memory_space=pl.ANY)] * 2,
+        scratch_shapes=[pltpu.VMEM(x.shape, x.dtype) for x in sums]
+        + [pltpu.SemaphoreType.DMA((2,))],
+        compiler_params=pltpu.CompilerParams(vmem_limit_bytes=16 * 2**20),
+        cost_estimate=pl.CostEstimate(flops=0, bytes_accessed=2**19, transcendentals=0),
+        name="sums",
+    )(both)
     below, above = call(
         relay_body,
         [shape(less + row_count // 2, 2 * share, size)] * 2,

time: 85.6 us -> 85.6 us (level)
    pallas_call x7 -> x6, Pallas kernels: 7.2 us -> 6.43 us  [call(): pl.pallas_call(body, out_shape=outs, in_specs=[VMEM] * len(ins), out_spec...]
where the time goes in v19:
time: 85.6 us; the launch traced here: 85.1 us
  starting transfers between devices  44.5 us (52%)
  waiting for transfers between devices  27 us (32%)
  Pallas kernels  12.6 us (15%)
  between operations  0.9 us (1%)
    all_to_all x1, waiting for transfers between devices, shards(): lax.all_to_all(sent, 'row', split_axis=0, concat_axis=0, tiled=True)  19.3 us
    all_to_all x1, starting transfers between devices, shards(): lax.all_to_all(sent, 'row', split_axis=0, concat_axis=0, tiled=True)  11.8 us
    all_to_all x1, starting transfers between devices, shards(): lax.all_to_all(both, ('col', 'pole'), split_axis=0, concat_axis=0, tiled=...  9.68 us
    all_to_all x1, starting transfers between devices, shards(): lax.all_to_all(spread, ('row', 'col'), split_axis=0, concat_axis=0, tiled...  8.04 us
    pallas_call x6, Pallas kernels, call(): pl.pallas_call(body, out_shape=outs, in_specs=[VMEM] * len(ins), out_spec...  6.43 us
    ppermute x1, starting transfers between devices, shards(): above = lax.ppermute(above, 'pole', back)  3.84 us
    all_to_all x1, waiting for transfers between devices, shards(): lax.all_to_all(both, ('col', 'pole'), split_axis=0, concat_axis=0, tiled=...  3.6 us
    ppermute x1, starting transfers between devices, shards(): from_above = lax.ppermute(down, 'pole', back)  3.36 us
  transfers between devices with their start and end apart: 8, of which 6 were waited for; matrix products, arithmetic and copies ran while one was open for 0% of the time, Pallas kernels for 9%

profile of v19, /device:TPU:1, one launch (start us, length us, event | category | flops | bytes accessed | tf_op | source)
XLA Modules:
  0.0 85.1 jit_solution(8656121951672960987)
XLA Ops:
  0.6 0.0 copy-start.3
  0.6 0.0 copy-start.6
  0.7 0.0 copy-start.5
  0.7 1.8 %pack.1 = bf16[16,96,256]{2,1,0:T(8,128)(2,1)} custom-call(bf16[256,256]{1,0:T(8,128)(2,1)} %panel_h.5, bf16[256,256]{1,0:T(8,128)(2,1)} %panel_s.5, bf16[64,4096]{1,0:T(8,128)(2,1)} %front_h.1, bf16[64,4096]{1,0:T(8,128)(2,1)} %front_s.1), custom_call_target="tpu_custom_call" | custom-call | bytes 1048576 | tf_op jit(solution)/shard_map/pack/pallas_call | solution.py:367
  2.5 11.8 %all-to-all-start = ((bf16[16,96,256]{2,1,0:T(8,128)(2,1)}), bf16[16,96,256]{2,1,0:T(8,128)(2,1)S(1)}, u32[]{:S(2)}, u32[]{:S(2)}) async-start(bf16[16,96,256]{2,1,0:T(8,128)(2,1)} %pack.1), calls=%async_computation | async-start | bytes 1572864 | tf_op jit(solution)/shard_map/all_to_all | solution.py:381
  14.4 0.0 copy-done.3
  14.4 0.0 copy-done.6
  14.4 0.0 copy-done.5
  14.4 0.0 copy-start.1
  14.4 0.0 copy-start.2
  14.4 0.0 copy-start.4
  14.4 3.3 %pivot_inverse.1.inverse = bf16[2,256,512]{2,1,0:T(8,128)(2,1)S(1)} custom-call(f32[1,2]{1,0:T(1,128)S(1)} %copy-done.3, bf16[256,256]{1,0:T(8,128)(2,1)S(1)} %copy-done.5, bf16[256,256]{1,0:T(8,128)(2,1)S(1)} %copy-done.6), custom_call_target="tpu_custom_call" | custom-call | flops 2415919104 | bytes 786440 | tf_op jit(solution)/shard_map/pivot_inverse/pallas_call | solution.py:17
  17.7 0.0 copy-start
  17.8 19.3 %all-to-all-done.received = bf16[16,96,256]{2,1,0:T(8,128)(2,1)S(1)} async-done(((bf16[16,96,256]{2,1,0:T(8,128)(2,1)}), bf16[16,96,256]{2,1,0:T(8,128)(2,1)S(1)}, u32[]{:S(2)}, u32[]{:S(2)}) %all-to-all-start) | async-done | bytes 786464 | tf_op jit(solution)/shard_map/all_to_all | solution.py:381
  37.0 0.7 solved_rows.1
  37.8 1.9 %collective-permute-start = (bf16[512,512]{1,0:T(8,128)(2,1)S(1)}, bf16[512,512]{1,0:T(8,128)(2,1)S(1)}, u32[]{:S(2)}, u32[]{:S(2)}) collective-permute-start(bf16[512,512]{1,0:T(8,128)(2,1)S(1)} %get-tuple-element.18.mine), channel_id=1, source_target_pairs={{0,4},{4,0},{8,12},{12,8},{16,20},{20,16},{24,28},{28,24},{32,36},... | collective-permute-start | bytes 1572872 | tf_op jit(solution)/shard_map/ppermute | solution.py:399
  39.7 0.0 copy-done.1
  39.7 0.0 copy-done.2
  39.7 0.0 copy-done.4
  39.7 0.0 copy-done
  39.7 0.8 own_column.1
  40.5 1.1 %collective-permute-done.other = bf16[512,512]{1,0:T(8,128)(2,1)S(1)} collective-permute-done((bf16[512,512]{1,0:T(8,128)(2,1)S(1)}, bf16[512,512]{1,0:T(8,128)(2,1)S(1)}, u32[]{:S(2)}, u32[]{:S(2)}) %collective-permute-start) | collective-permute-done | bytes 524320 | tf_op jit(solution)/shard_map/ppermute | solution.py:399
  41.6 1.7 %column.1 = bf16[32,32,128]{2,1,0:T(8,128)(2,1)} custom-call(f32[1,2]{1,0:T(1,128)S(1)} %copy-done.4, bf16[512,512]{1,0:T(8,128)(2,1)S(1)} %collective-permute-done.other, bf16[2,16,64,256]{3,2,1,0:T(8,128)(2,1)S(1)} %bitcast.7, f32[512,256]{1,0:T(8,128)S(1)} %get-tuple-element.23.part, bf16[512,256]{1,0:T(8,128)(2,1)S(1)} %get-tuple-element.24.right, ...), custom_call_target="tpu_custom_call" | custom-call | flops 268435456 | bytes 2097152 | tf_op jit(solution)/shard_map/column/pallas_call | solution.py:413
  43.3 9.7 %all-to-all-start.1 = ((bf16[32,32,128]{2,1,0:T(8,128)(2,1)}), bf16[32,32,128]{2,1,0:T(8,128)(2,1)S(1)}, u32[]{:S(2)}, u32[]{:S(2)}) async-start(bf16[32,32,128]{2,1,0:T(8,128)(2,1)} %column.1), calls=%async_computation.1 | async-start | bytes 524288 | tf_op jit(solution)/shard_map/all_to_all | solution.py:432
  53.0 3.1 %collective-permute-start.1 = (bf16[10,32,256]{2,1,0:T(8,128)(2,1)S(1)}, bf16[10,32,256]{2,1,0:T(8,128)(2,1)S(1)}, u32[]{:S(2)}, u32[]{:S(2)}) collective-permute-start(bf16[10,32,256]{2,1,0:T(8,128)(2,1)S(1)} %get-tuple-element.26.up), channel_id=1, source_target_pairs={{0,64},{64,128},{128,192},{192,256},{256,320},{320,384},{384,448},... | collective-permute-start | bytes 491528 | tf_op jit(solution)/shard_map/ppermute | solution.py:429
  56.1 3.4 %collective-permute-start.2 = (bf16[10,32,256]{2,1,0:T(8,128)(2,1)S(1)}, bf16[10,32,256]{2,1,0:T(8,128)(2,1)S(1)}, u32[]{:S(2)}, u32[]{:S(2)}) collective-permute-start(bf16[10,32,256]{2,1,0:T(8,128)(2,1)S(1)} %get-tuple-element.27.down), channel_id=1, source_target_pairs={{0,448},{64,0},{128,64},{192,128},{256,192},{320,256},{384,320},{4... | collective-permute-start | bytes 491528 | tf_op jit(solution)/shard_map/ppermute | solution.py:430
  59.5 3.6 %all-to-all-done.1.parts = bf16[32,32,128]{2,1,0:T(8,128)(2,1)S(1)} async-done(((bf16[32,32,128]{2,1,0:T(8,128)(2,1)}), bf16[32,32,128]{2,1,0:T(8,128)(2,1)S(1)}, u32[]{:S(2)}, u32[]{:S(2)}) %all-to-all-start.1) | async-done | bytes 262176 | tf_op jit(solution)/shard_map/all_to_all | solution.py:432
  63.1 0.8 sums.1
  63.9 8.0 %all-to-all-start.2 = ((bf16[64,16,128]{2,1,0:T(8,128)(2,1)}), bf16[64,16,128]{2,1,0:T(8,128)(2,1)S(1)}, u32[]{:S(2)}, u32[]{:S(2)}) async-start(bf16[64,16,128]{2,1,0:T(8,128)(2,1)} %get-tuple-element.32), calls=%async_computation.2 | async-start | bytes 524288 | tf_op jit(solution)/shard_map/all_to_all | solution.py:457
  71.9 0.0 copy-start.7
  71.9 0.0 collective-permute-done.1.from_below
  71.9 0.0 collective-permute-done.2.from_above
  72.0 2.7 %collective-permute-start.3 = (bf16[14,32,256]{2,1,0:T(8,128)(2,1)S(1)}, bf16[14,32,256]{2,1,0:T(8,128)(2,1)S(1)}, u32[]{:S(2)}, u32[]{:S(2)}) collective-permute-start(bf16[14,32,256]{2,1,0:T(8,128)(2,1)S(1)} %get-tuple-element.28), channel_id=1, source_target_pairs={{0,64},{64,128},{128,192},{192,256},{256,320},{320,384},{384,448},... | collective-permute-start | bytes 688136 | tf_op jit(solution)/shard_map/ppermute | solution.py:455
  74.6 3.8 %collective-permute-start.4 = (bf16[14,32,256]{2,1,0:T(8,128)(2,1)S(1)}, bf16[14,32,256]{2,1,0:T(8,128)(2,1)S(1)}, u32[]{:S(2)}, u32[]{:S(2)}) collective-permute-start(bf16[14,32,256]{2,1,0:T(8,128)(2,1)S(1)} %get-tuple-element.29), channel_id=1, source_target_pairs={{0,448},{64,0},{128,64},{192,128},{256,192},{320,256},{384,320},{4... | collective-permute-start | bytes 688136 | tf_op jit(solution)/shard_map/ppermute | solution.py:456
  78.5 0.0 copy-done.7
  78.5 0.8 update.1
  79.3 1.0 %schur_first.1.begun = bf16[2,16,4,16,256]{4,3,2,1,0:T(8,128)(2,1)} custom-call(f32[1,2]{1,0:T(1,128)S(1)} %copy-done.3, f32[16,256]{1,0:T(8,128)S(1)} %get-tuple-element.19.mask, f32[16,4,16,512]{3,2,1,0:T(8,128)S(1)} %get-tuple-element.20.update, bf16[10,32,256]{2,1,0:T(8,128)(2,1)S(1)} %get-tuple-element.26.up, ...), custom_call_target="tpu_custom_call" | custom-call | bytes 3145728 | tf_op jit(solution)/shard_map/schur_first/pallas_call | solution.py:473
  80.3 1.4 %collective-permute-done.3.below = bf16[14,32,256]{2,1,0:T(8,128)(2,1)S(1)} collective-permute-done((bf16[14,32,256]{2,1,0:T(8,128)(2,1)S(1)}, bf16[14,32,256]{2,1,0:T(8,128)(2,1)S(1)}, u32[]{:S(2)}, u32[]{:S(2)}) %collective-permute-start.3) | collective-permute-done | bytes 229408 | tf_op jit(solution)/shard_map/ppermute | solution.py:455
  81.7 1.2 %collective-permute-done.4.above = bf16[14,32,256]{2,1,0:T(8,128)(2,1)S(1)} collective-permute-done((bf16[14,32,256]{2,1,0:T(8,128)(2,1)S(1)}, bf16[14,32,256]{2,1,0:T(8,128)(2,1)S(1)}, u32[]{:S(2)}, u32[]{:S(2)}) %collective-permute-start.4) | collective-permute-done | bytes 229408 | tf_op jit(solution)/shard_map/ppermute | solution.py:456
  82.9 0.9 %schur_last.1 = bf16[2,16,4,16,256]{4,3,2,1,0:T(8,128)(2,1)} custom-call(f32[1,2]{1,0:T(1,128)S(1)} %copy-done.3, f32[16,256]{1,0:T(8,128)S(1)} %get-tuple-element.19.mask, f32[16,4,16,512]{3,2,1,0:T(8,128)S(1)} %get-tuple-element.20.update, bf16[14,32,256]{2,1,0:T(8,128)(2,1)S(1)} %collective-permute-done.3.below, ...), custom_call_target="tpu_custom_call", output_to_operand_aliasing={{}: (5, {})} | custom-call | bytes 3145728 | tf_op jit(solution)/shard_map/schur_last/pallas_call | solution.py:473
  83.8 0.5 all-to-all-done.2.parts
  84.4 0.7 pivot.1
  (1 shorter events, 0.0 us)
Async XLA Ops:
  0.6 13.7 %copy-start.3 = (f32[1,2]{1,0:T(1,128)S(1)}, f32[1,2]{1,0:T(1,128)}, u32[]{:S(2)}) copy-start(f32[1,2]{1,0:T(1,128)} %shift.11) | copy-start | bytes 28
  0.6 13.7 %copy-start.6 = (bf16[256,256]{1,0:T(8,128)(2,1)S(1)}, bf16[256,256]{1,0:T(8,128)(2,1)}, u32[]{:S(2)}) copy-start(bf16[256,256]{1,0:T(8,128)(2,1)} %pivot_s.1) | copy-start | bytes 393220
  0.7 13.7 %copy-start.5 = (bf16[256,256]{1,0:T(8,128)(2,1)S(1)}, bf16[256,256]{1,0:T(8,128)(2,1)}, u32[]{:S(2)}) copy-start(bf16[256,256]{1,0:T(8,128)(2,1)} %pivot_h.1) | copy-start | bytes 393220
  2.5 34.5 %all-to-all-start = ((bf16[16,96,256]{2,1,0:T(8,128)(2,1)}), bf16[16,96,256]{2,1,0:T(8,128)(2,1)S(1)}, u32[]{:S(2)}, u32[]{:S(2)}) async-start(bf16[16,96,256]{2,1,0:T(8,128)(2,1)} %pack.1), calls=%async_computation | async-start | bytes 1572864 | tf_op jit(solution)/shard_map/all_to_all | solution.py:381
  14.4 25.3 %copy-start.1 = (bf16[256,256]{1,0:T(8,128)(2,1)S(1)}, bf16[256,256]{1,0:T(8,128)(2,1)}, u32[]{:S(2)}) copy-start(bf16[256,256]{1,0:T(8,128)(2,1)} %panel_h.5) | copy-start | bytes 393220
  14.4 25.3 %copy-start.2 = (bf16[256,256]{1,0:T(8,128)(2,1)S(1)}, bf16[256,256]{1,0:T(8,128)(2,1)}, u32[]{:S(2)}) copy-start(bf16[256,256]{1,0:T(8,128)(2,1)} %panel_s.5) | copy-start | bytes 393220
  14.4 25.3 %copy-start.4 = (f32[1,2]{1,0:T(1,128)S(1)}, f32[1,2]{1,0:T(1,128)}, u32[]{:S(2)}) copy-start(f32[1,2]{1,0:T(1,128)} %weight.3) | copy-start | bytes 28
  17.7 22.0 %copy-start = (bf16[1,2,16,1,64,256]{5,4,3,2,1,0:T(8,128)(2,1)S(1)}, bf16[1,2,16,1,64,256]{5,4,3,2,1,0:T(8,128)(2,1)}, u32[]{:S(2)}) copy-start(bf16[1,2,16,1,64,256]{5,4,3,2,1,0:T(8,128)(2,1)} %param.19) | copy-start | bytes 3145732
  37.8 3.8 %collective-permute-start = (bf16[512,512]{1,0:T(8,128)(2,1)S(1)}, bf16[512,512]{1,0:T(8,128)(2,1)S(1)}, u32[]{:S(2)}, u32[]{:S(2)}) collective-permute-start(bf16[512,512]{1,0:T(8,128)(2,1)S(1)} %get-tuple-element.18.mine), channel_id=1, source_target_pairs={{0,4},{4,0},{8,12},{12,8},{16,20},{20,16},{24,28},{28,24},{32,36},... | collective-permute-start | bytes 1572872 | tf_op jit(solution)/shard_map/ppermute | solution.py:399
  43.3 19.8 %all-to-all-start.1 = ((bf16[32,32,128]{2,1,0:T(8,128)(2,1)}), bf16[32,32,128]{2,1,0:T(8,128)(2,1)S(1)}, u32[]{:S(2)}, u32[]{:S(2)}) async-start(bf16[32,32,128]{2,1,0:T(8,128)(2,1)} %column.1), calls=%async_computation.1 | async-start | bytes 524288 | tf_op jit(solution)/shard_map/all_to_all | solution.py:432
  53.0 18.9 %collective-permute-start.1 = (bf16[10,32,256]{2,1,0:T(8,128)(2,1)S(1)}, bf16[10,32,256]{2,1,0:T(8,128)(2,1)S(1)}, u32[]{:S(2)}, u32[]{:S(2)}) collective-permute-start(bf16[10,32,256]{2,1,0:T(8,128)(2,1)S(1)} %get-tuple-element.26.up), channel_id=1, source_target_pairs={{0,64},{64,128},{128,192},{192,256},{256,320},{320,384},{384,448},... | collective-permute-start | bytes 491528 | tf_op jit(solution)/shard_map/ppermute | solution.py:429
  56.1 15.8 %collective-permute-start.2 = (bf16[10,32,256]{2,1,0:T(8,128)(2,1)S(1)}, bf16[10,32,256]{2,1,0:T(8,128)(2,1)S(1)}, u32[]{:S(2)}, u32[]{:S(2)}) collective-permute-start(bf16[10,32,256]{2,1,0:T(8,128)(2,1)S(1)} %get-tuple-element.27.down), channel_id=1, source_target_pairs={{0,448},{64,0},{128,64},{192,128},{256,192},{320,256},{384,320},{4... | collective-permute-start | bytes 491528 | tf_op jit(solution)/shard_map/ppermute | solution.py:430
  63.9 20.5 %all-to-all-start.2 = ((bf16[64,16,128]{2,1,0:T(8,128)(2,1)}), bf16[64,16,128]{2,1,0:T(8,128)(2,1)S(1)}, u32[]{:S(2)}, u32[]{:S(2)}) async-start(bf16[64,16,128]{2,1,0:T(8,128)(2,1)} %get-tuple-element.32), calls=%async_computation.2 | async-start | bytes 524288 | tf_op jit(solution)/shard_map/all_to_all | solution.py:457
  71.9 6.6 %copy-start.7 = (s32[16,16]{1,0:T(8,128)S(1)}, s32[16,16]{1,0:T(8,128)}, u32[]{:S(2)}) copy-start(s32[16,16]{1,0:T(8,128)} %pattern.1) | copy-start | bytes 3076
  72.0 9.7 %collective-permute-start.3 = (bf16[14,32,256]{2,1,0:T(8,128)(2,1)S(1)}, bf16[14,32,256]{2,1,0:T(8,128)(2,1)S(1)}, u32[]{:S(2)}, u32[]{:S(2)}) collective-permute-start(bf16[14,32,256]{2,1,0:T(8,128)(2,1)S(1)} %get-tuple-element.28), channel_id=1, source_target_pairs={{0,64},{64,128},{128,192},{192,256},{256,320},{320,384},{384,448},... | collective-permute-start | bytes 688136 | tf_op jit(solution)/shard_map/ppermute | solution.py:455
  74.6 8.3 %collective-permute-start.4 = (bf16[14,32,256]{2,1,0:T(8,128)(2,1)S(1)}, bf16[14,32,256]{2,1,0:T(8,128)(2,1)S(1)}, u32[]{:S(2)}, u32[]{:S(2)}) collective-permute-start(bf16[14,32,256]{2,1,0:T(8,128)(2,1)S(1)} %get-tuple-element.29), channel_id=1, source_target_pairs={{0,448},{64,0},{128,64},{192,128},{256,192},{320,256},{384,320},{4... | collective-permute-start | bytes 688136 | tf_op jit(solution)/shard_map/ppermute | solution.py:456
